TPU v7x, 32 devices: a whole 2x2x4 slice. The times are simulated.
32 devices in a mesh: groups: 2 (over y), expert: 4 (over z), dp: 4 (over x, core).
Axes of the slice: x: 2, y: 2, z: 4, core: 2. Of those that a mesh axis runs over, the one named last changes fastest.
Arguments:
- hidden_rows: bfloat16 [256, 4096], P(('groups', 'expert', 'dp')), parts along dimension 0, may hold values from -6 to 6
- expert_ids: int32 [256, 8], P(('groups', 'expert', 'dp')), parts along dimension 0, may hold values from 0 to 15, as said below
- gate_values: float32 [256, 8], P(('groups', 'expert', 'dp')), parts along dimension 0, may hold values from 0.1 to 0.6
- gate_proj: bfloat16 [16, 4096, 1024], P('expert', None, 'dp'), may hold values from -0.09375 to 0.09375
- up_proj: bfloat16 [16, 4096, 1024], P('expert', None, 'dp'), may hold values from -0.09375 to 0.09375
- down_proj: bfloat16 [16, 1024, 4096], P('expert', None, 'dp'), may hold values from -0.1875 to 0.1875
- queries: bfloat16 [64, 128, 576], P(('groups', 'expert', 'dp')), parts along dimension 0, may hold values from -16 to 16
- latent_cache: bfloat16 [64, 512, 576], P(('groups', 'expert', 'dp')), parts along dimension 0, may hold values from -8 to 8
- cache_lengths: int32 [64], P(('groups', 'expert', 'dp')), parts along dimension 0, may hold values from 2 to 512, as said below
Outputs:
- mixed_rows: bfloat16 [256, 4096], P(('groups', 'expert', 'dp')), parts along dimension 0
- attention_latent: bfloat16 [64, 128, 512], P(('groups', 'expert', 'dp')), parts along dimension 0
There are 2 independent parts, one for each index of `groups`. A program takes and returns all parts, laid end to end along the dimension named above; an argument that names none is the same for every part. Nothing has to cross between parts.
Inputs may be any that keep to these rules, and one draw needn't show every extreme that they name: `expert_ids`: each row names 8 different experts. Within the rows of one device (aligned blocks of 8 rows) no expert is named by more than 6 rows, and one expert, the same for every block, is named by exactly 6 rows in each block. `cache_lengths`: some row has length 512.
All inputs are finite; a program needn't handle non-finite values.
Results may differ from a plain program's by a relative error of at most 0.0057.
Values may be sent and summed in bfloat16 or wider, within the bound.
No kernel may reach another device: no remote copies, remote signals or barrier semaphores. Data moves between devices by JAX's collectives and lax.ppermute only.
A program may use at most 128 MiB of HBM per device.

v0:
```python
import jax
import jax.numpy as jnp
from jax import lax
from jax.sharding import PartitionSpec as P

LATENT = 512


softmax_scale = 192.0 ** (-0.5)


def attend(queries, latent_cache, cache_lengths):
    scores = (
        jnp.einsum("rhc,rtc->rht", queries, latent_cache, preferred_element_type=jnp.float32)
        * softmax_scale
    )
    usable = (
        jnp.arange(latent_cache.shape[1], dtype=jnp.int32)[None, None, :]
        < cache_lengths[:, None, None]
    )
    scores = jnp.where(usable, scores, -1e30)
    highest = jnp.max(scores, axis=2, keepdims=True)
    weights = jnp.exp(scores - highest)
    weights = weights / jnp.sum(weights, axis=2, keepdims=True)
    latent_values = latent_cache[:, :, :LATENT]
    return jnp.einsum(
        "rht,rtv->rhv",
        weights.astype(jnp.bfloat16),
        latent_values,
        preferred_element_type=jnp.float32,
    ).astype(jnp.bfloat16)


def local(
    hidden_rows,
    expert_ids,
    gate_values,
    gate_proj,
    up_proj,
    down_proj,
    queries,
    latent_cache,
    cache_lengths,
):
    attended = attend(queries, latent_cache, cache_lengths)
    rows_dev, feature_count = hidden_rows.shape
    top_count = expert_ids.shape[1]
    local_experts = gate_proj.shape[0]
    slice_width = down_proj.shape[2]
    owners = lax.axis_size("expert")
    members = lax.axis_size("dp")
    experts_all = local_experts * owners
    capacity = max(2, 3 * rows_dev * top_count // (2 * experts_all))
    selected = expert_ids[:, :, None] == jnp.arange(experts_all, dtype=jnp.int32)[None, None, :]
    naming = jnp.sum(selected.astype(jnp.int32), axis=1)
    before = jnp.cumsum(naming, axis=0) - naming
    placer = (
        (naming[:, :, None] == 1)
        & (before[:, :, None] == jnp.arange(capacity, dtype=jnp.int32)[None, None, :])
    ).astype(jnp.bfloat16)
    outgoing = jnp.einsum(
        "rjc,rd->jcd", placer, hidden_rows, preferred_element_type=jnp.float32
    ).astype(jnp.bfloat16)
    outgoing = outgoing.reshape(owners, local_experts, capacity, feature_count)
    copies = jnp.broadcast_to(
        outgoing[:, :, :, None, :], (owners, local_experts, capacity, members, feature_count)
    )
    arrived = lax.all_to_all(
        lax.all_to_all(copies, "expert", split_axis=0, concat_axis=0, tiled=True),
        "dp",
        split_axis=3,
        concat_axis=2,
        tiled=True,
    )
    row_block = arrived.reshape(owners, local_experts, members * capacity, feature_count)
    gate_pre = jnp.einsum(
        "olmd,ldf->olmf", row_block, gate_proj, preferred_element_type=jnp.float32
    )
    up_pre = jnp.einsum("olmd,ldf->olmf", row_block, up_proj, preferred_element_type=jnp.float32)
    hidden_share = (jax.nn.silu(gate_pre) * up_pre).astype(jnp.bfloat16)
    produced = jnp.einsum(
        "olmf,lfd->olmd",
        lax.all_gather(hidden_share, "dp", axis=3, tiled=True),
        down_proj,
        preferred_element_type=jnp.float32,
    ).astype(jnp.bfloat16)
    produced = produced.reshape(owners, local_experts, members, capacity, 1, slice_width)
    returned = lax.all_to_all(
        lax.all_to_all(produced, "expert", split_axis=0, concat_axis=0, tiled=True),
        "dp",
        split_axis=2,
        concat_axis=4,
        tiled=True,
    )
    returned = returned.reshape(experts_all, capacity, feature_count)
    position = jnp.take_along_axis(before, expert_ids, axis=1)
    picked = returned[expert_ids, position]
    blended = jnp.sum(gate_values[:, :, None] * picked.astype(jnp.float32), axis=1).astype(
        jnp.bfloat16
    )
    return (blended, attended)


def solution(mesh):
    return jax.shard_map(
        local,
        mesh=mesh,
        in_specs=(
            P(("groups", "expert", "dp"), None),
            P(("groups", "expert", "dp"), None),
            P(("groups", "expert", "dp"), None),
            P("expert", None, "dp"),
            P("expert", None, "dp"),
            P("expert", None, "dp"),
            P(("groups", "expert", "dp"), None, None),
            P(("groups", "expert", "dp"), None, None),
            P(("groups", "expert", "dp")),
        ),
        out_specs=(P(("groups", "expert", "dp"), None), P(("groups", "expert", "dp"), None, None)),
        check_vma=False,
    )
```

profile of v0, /device:TPU:0, one launch (start us, length us, event | category | flops | bytes accessed | tf_op | source)
XLA Modules:
  0.0 188.9 jit_solution(7463616457518171517)
XLA Ops:
  0.6 0.0 copy-start
  0.6 0.8 convert_reduce_fusion
  1.5 1.2 convolution_convert_fusion
  2.8 0.3 broadcast_in_dim.22
  3.0 0.4 copy.38
  3.5 1.5 broadcast_in_dim.23
  5.0 76.8 %all_to_all.40 = bf16[4,4,6,4,4096]{4,1,2,3,0:T(4,128)(2,1)S(1)} all-to-all(bf16[4,4,6,4,4096]{4,1,2,3,0:T(4,128)(2,1)S(1)} %broadcast_in_dim.23), channel_id=1, replica_groups=mesh['groups'=2,'expert'=4,'dp'=4] {'expert'}, dimensions={0} | all-to-all | bytes 6291456 | tf_op jit(solution)/shard_map/all_to_all | solution.py:69
  81.8 0.0 slice-start.2
  81.8 2.6 %copy.39 = bf16[4,4,6,4,4096]{4,1,2,0,3:T(4,128)(2,1)S(1)} copy(bf16[4,4,6,4,4096]{4,1,2,3,0:T(4,128)(2,1)S(1)} %all_to_all.40) | data formatting | bytes 6291456 | tf_op jit(solution)/shard_map/all_to_all | solution.py:69
  84.4 0.0 slice-start.3
  84.4 0.0 slice-start.4
  84.5 39.8 %all_to_all.41 = bf16[4,4,6,4,4096]{4,1,2,0,3:T(4,128)(2,1)S(1)} all-to-all(bf16[4,4,6,4,4096]{4,1,2,0,3:T(4,128)(2,1)S(1)} %copy.39), channel_id=1, replica_groups=mesh['groups'=2,'expert'=4,'dp'=4] {'dp'}, dimensions={3} | all-to-all | bytes 6291456 | tf_op jit(solution)/shard_map/all_to_all | solution.py:68
  124.3 0.0 slice-start.5
  124.3 2.6 %copy.40 = bf16[4,4,4,6,1,4096]{5,1,3,2,0,4:T(4,128)(2,1)S(1)} copy(bf16[4,4,4,6,1,4096]{5,1,3,0,2,4:T(4,128)(2,1)S(1)} %bitcast.66) | data formatting | bytes 6291456 | tf_op jit(solution)/shard_map/all_to_all | solution.py:68
  126.9 0.0 slice-done.2
  127.0 0.0 slice-done.3
  127.0 0.0 slice-start
  127.0 2.8 %fusion.18 = f32[4,4,24,256]{3,2,0,1:T(8,128)S(1)} fusion(bf16[4,4096,256]{2,1,0:T(8,128)(2,1)S(1)} %bitcast.72, bf16[4,4,24,4096]{3,1,2,0:T(4,128)(2,1)S(1)} %bitcast.67), kind=kOutput, calls=%fused_computation.19 | convolution fusion | flops 805306368 | bytes 11927552 | tf_op jit(solution)/shard_map/olmd,ldf->olmf/dot_general | solution.py:76
  129.8 0.0 slice-done.4
  129.8 0.0 slice-done.5
  129.8 0.0 slice-start.1
  129.8 2.8 %fusion.33 = bf16[4,4,24,256]{3,2,0,1:T(8,128)(2,1)S(1)} fusion(bf16[4,4096,256]{2,1,0:T(8,128)(2,1)S(1)} %bitcast.75, bf16[4,4,24,4096]{3,1,2,0:T(4,128)(2,1)S(1)} %bitcast.68, f32[4,4,24,256]{3,2,0,1:T(8,128)S(1)} %fusion.18), kind=kOutput, calls=%fused_computation.22 | convolution fusion | flops 805896192 | bytes 12124160 | tf_op jit(solution)/shard_map/olmd,ldf->olmf/dot_general | solution.py:79
  132.6 8.0 %all_gather.3 = bf16[4,4,24,1024]{3,2,0,1:T(8,128)(2,1)S(1)} all-gather(bf16[4,4,24,256]{3,2,0,1:T(8,128)(2,1)S(1)} %fusion.33), channel_id=1, replica_groups=mesh['groups'=2,'expert'=4,'dp'=4] {'dp'}, dimensions={3}, use_global_device_ids=true | all-gather | bytes 983040 | tf_op jit(solution)/shard_map/all_gather | solution.py:83
  140.6 0.0 slice-done
  140.6 0.0 slice-done.1
  140.6 1.5 fusion.12
  142.1 0.0 copy-start.2
  142.1 1.5 copy.43
  143.6 0.0 copy-start.4
  143.6 3.6 %all-to-all-start.2 = ((bf16[4,4,4,6,1,1024]{5,1,3,2,4,0:T(4,128)(2,1)}), bf16[4,4,4,6,1,1024]{5,1,3,2,4,0:T(4,128)(2,1)S(1)}, u32[]{:S(2)}, u32[]{:S(2)}) async-start(bf16[4,4,4,6,1,1024]{5,1,3,2,4,0:T(4,128)(2,1)} %bitcast.14), calls=%async_computation.2 | async-start | bytes 1572864 | tf_op jit(solution)/shard_map/all_to_all | solution.py:89
  147.3 0.0 copy-done.2
  147.3 0.1 reshape.70
  147.4 0.0 copy-start.1
  147.4 0.7 gather_fusion.1
  148.1 0.1 reshape.73
  148.2 0.1 reshape.64
  148.3 0.0 copy-done.4
  148.3 0.1 iota_compare_fusion.2
  148.4 19.8 %all-to-all-done.2 = bf16[4,4,4,6,1,1024]{5,1,3,2,4,0:T(4,128)(2,1)S(1)} async-done(((bf16[4,4,4,6,1,1024]{5,1,3,2,4,0:T(4,128)(2,1)}), bf16[4,4,4,6,1,1024]{5,1,3,2,4,0:T(4,128)(2,1)S(1)}, u32[]{:S(2)}, u32[]{:S(2)}) %all-to-all-start.2) | async-done | bytes 786464 | tf_op jit(solution)/shard_map/all_to_all | solution.py:89
  168.1 1.2 copy.45
  169.3 3.5 %all-to-all-start.3 = ((bf16[4,4,4,6,1,1024]{5,1,3,0,4,2:T(4,128)(2,1)}), bf16[4,4,4,6,1,1024]{5,1,3,0,4,2:T(4,128)(2,1)S(1)}, u32[]{:S(2)}, u32[]{:S(2)}) async-start(bf16[4,4,4,6,1,1024]{5,1,3,0,4,2:T(4,128)(2,1)} %copy.45), calls=%async_computation.3 | async-start | bytes 1572864 | tf_op jit(solution)/shard_map/all_to_all | solution.py:88
  172.8 0.0 copy-done
  172.8 0.0 copy-done.1
  172.8 0.4 fusion.16
  173.3 0.2 fusion.50
  173.5 1.3 convolution_convert_fusion.1
  174.8 9.6 %all-to-all-done.3 = bf16[4,4,4,6,1,1024]{5,1,3,0,4,2:T(4,128)(2,1)S(1)} async-done(((bf16[4,4,4,6,1,1024]{5,1,3,0,4,2:T(4,128)(2,1)}), bf16[4,4,4,6,1,1024]{5,1,3,0,4,2:T(4,128)(2,1)S(1)}, u32[]{:S(2)}, u32[]{:S(2)}) %all-to-all-start.3) | async-done | bytes 786464 | tf_op jit(solution)/shard_map/all_to_all | solution.py:88
  184.4 0.6 copy.46
  185.1 0.0 copy-start.3
  185.1 0.6 reshape.63
  185.6 2.2 %gather_fusion = bf16[64,4096]{1,0:T(8,128)(2,1)S(1)} fusion(bf16[16,6,4096]{2,0,1:T(8,128)(2,1)S(1)} %reshape.63, s32[64]{0:T(128)S(1)} %reshape.64), kind=kCustom, calls=%fused_computation | custom fusion | bytes 1049088 | tf_op jit(solution)/shard_map/gather | solution.py:97
  187.9 0.0 copy-done.3
  187.9 1.1 fusion.38
  (8 shorter events, 0.1 us)
Async XLA Ops:
  0.6 172.2 %copy-start = (bf16[2,128,576]{1,2,0:T(8,128)(2,1)S(1)}, bf16[2,128,576]{1,2,0:T(8,128)(2,1)}, u32[]{:S(2)}) copy-start(bf16[2,128,576]{1,2,0:T(8,128)(2,1)} %param.15) | copy-start | bytes 884740
  81.8 45.2 %slice-start.2 = ((s8[8388608]{0:T(1024)(128)(4,1)}), s8[4194304]{0:T(1024)(128)(4,1)S(1)}, s32[]{:S(2)}) async-start(s8[8388608]{0:T(1024)(128)(4,1)} %bitcast.71), calls=%async_computation.6 | async-start | bytes 8388608
  84.4 42.5 %slice-start.3 = ((s8[8388608]{0:T(1024)(128)(4,1)}), s8[4194304]{0:T(1024)(128)(4,1)S(1)}, s32[]{:S(2)}) async-start(s8[8388608]{0:T(1024)(128)(4,1)} %bitcast.71), calls=%async_computation.7 | async-start | bytes 8388608
  84.4 45.3 %slice-start.4 = ((s8[8388608]{0:T(1024)(128)(4,1)}), s8[4194304]{0:T(1024)(128)(4,1)S(1)}, s32[]{:S(2)}) async-start(s8[8388608]{0:T(1024)(128)(4,1)} %bitcast.74), calls=%async_computation.8 | async-start | bytes 8388608
  124.3 5.5 %slice-start.5 = ((s8[8388608]{0:T(1024)(128)(4,1)}), s8[4194304]{0:T(1024)(128)(4,1)S(1)}, s32[]{:S(2)}) async-start(s8[8388608]{0:T(1024)(128)(4,1)} %bitcast.74), calls=%async_computation.9 | async-start | bytes 8388608
  127.0 13.6 %slice-start = ((s8[8388608]{0:T(1024)(128)(4,1)}), s8[4194304]{0:T(1024)(128)(4,1)S(1)}, s32[]{:S(2)}) async-start(s8[8388608]{0:T(1024)(128)(4,1)} %bitcast.69), calls=%async_computation.4 | async-start | bytes 8388608
  129.8 10.8 %slice-start.1 = ((s8[8388608]{0:T(1024)(128)(4,1)}), s8[4194304]{0:T(1024)(128)(4,1)S(1)}, s32[]{:S(2)}) async-start(s8[8388608]{0:T(1024)(128)(4,1)} %bitcast.69), calls=%async_computation.5 | async-start | bytes 8388608
  142.1 5.1 %copy-start.2 = (s32[8,8]{1,0:T(8,128)S(1)}, s32[8,8]{1,0:T(8,128)}, u32[]{:S(2)}) copy-start(s32[8,8]{1,0:T(8,128)} %param.10) | copy-start | bytes 772
  143.6 4.7 %copy-start.4 = (s32[2]{0:T(128)S(1)}, s32[2]{0:T(128)}, u32[]{:S(2)}) copy-start(s32[2]{0:T(128)} %param.17) | copy-start | bytes 28
  143.6 24.5 %all-to-all-start.2 = ((bf16[4,4,4,6,1,1024]{5,1,3,2,4,0:T(4,128)(2,1)}), bf16[4,4,4,6,1,1024]{5,1,3,2,4,0:T(4,128)(2,1)S(1)}, u32[]{:S(2)}, u32[]{:S(2)}) async-start(bf16[4,4,4,6,1,1024]{5,1,3,2,4,0:T(4,128)(2,1)} %bitcast.14), calls=%async_computation.2 | async-start | bytes 1572864 | tf_op jit(solution)/shard_map/all_to_all | solution.py:89
  147.4 25.5 %copy-start.1 = (bf16[2,512,576]{1,2,0:T(8,128)(2,1)S(1)}, bf16[2,512,576]{1,2,0:T(8,128)(2,1)}, u32[]{:S(2)}) copy-start(bf16[2,512,576]{1,2,0:T(8,128)(2,1)} %param.16) | copy-start | bytes 3538948
  169.3 15.1 %all-to-all-start.3 = ((bf16[4,4,4,6,1,1024]{5,1,3,0,4,2:T(4,128)(2,1)}), bf16[4,4,4,6,1,1024]{5,1,3,0,4,2:T(4,128)(2,1)S(1)}, u32[]{:S(2)}, u32[]{:S(2)}) async-start(bf16[4,4,4,6,1,1024]{5,1,3,0,4,2:T(4,128)(2,1)} %copy.45), calls=%async_computation.3 | async-start | bytes 1572864 | tf_op jit(solution)/shard_map/all_to_all | solution.py:88
  185.1 2.8 %copy-start.3 = (f32[8,8]{1,0:T(8,128)S(1)}, f32[8,8]{1,0:T(8,128)}, u32[]{:S(2)}) copy-start(f32[8,8]{1,0:T(8,128)} %param.11) | copy-start | bytes 772
where the time goes:
time: 189 us
  blocking collectives  125 us (66%)
  waiting for transfers between devices  29.4 us (16%)
  local copies, waits for them, and re-layouts  14.6 us (8%)
  matrix products  10.1 us (5%)
  starting transfers between devices  7.12 us (4%)
  other arithmetic  2.26 us (1%)
    all_to_all x1, blocking collectives, local(): lax.all_to_all(copies, 'expert', split_axis=0, concat_axis=0, tiled=True)  76.8 us
    all_to_all x1, blocking collectives, local(): lax.all_to_all(lax.all_to_all(copies, 'expert', split_axis=0, concat_axis...  39.8 us
    all_to_all x1, waiting for transfers between devices, local(): lax.all_to_all(produced, 'expert', split_axis=0, concat_axis=0, tiled=True)  19.8 us
    all_to_all x1, waiting for transfers between devices, local(): lax.all_to_all(lax.all_to_all(produced, 'expert', split_axis=0, concat_ax...  9.59 us
    all_gather x1, blocking collectives, local(): lax.all_gather(hidden_share, 'dp', axis=3, tiled=True)  8.02 us
  transfers between devices with their start and end apart: 2, of which 2 were waited for; matrix products, arithmetic and copies ran while one was open for 2% of the time, Pallas kernels for 0%

commit v1 on v0

v1 whole, which is shorter than its diff:
```python
import jax
import jax.numpy as jnp
from jax import lax
from jax.experimental import pallas as pl
from jax.experimental.pallas import tpu as pltpu
from jax.sharding import PartitionSpec as P

LATENT = 512
F32 = jnp.float32
BF16 = jnp.bfloat16
VMEM = pltpu.VMEM
MIB = 1024 * 1024


softmax_scale = 192.0 ** (-0.5)


def attend_kernel(lengths_ref, queries_ref, cache_ref, out_ref):
    length = lengths_ref[pl.program_id(0)]
    cache = cache_ref[0]
    scores = (
        lax.dot_general(
            queries_ref[0], cache, (((1,), (1,)), ((), ())), preferred_element_type=F32
        )
        * softmax_scale
    )
    usable = lax.broadcasted_iota(jnp.int32, scores.shape, 1) < length
    scores = jnp.where(usable, scores, -1e30)
    weights = jnp.exp(scores - jnp.max(scores, axis=1, keepdims=True))
    weights = weights / jnp.sum(weights, axis=1, keepdims=True)
    out_ref[0] = jnp.dot(
        weights.astype(BF16), cache[:, :LATENT], preferred_element_type=F32
    ).astype(BF16)


def attend(queries, latent_cache, cache_lengths):
    rows, heads, width = queries.shape
    positions = latent_cache.shape[1]
    return pl.pallas_call(
        attend_kernel,
        grid_spec=pltpu.PrefetchScalarGridSpec(
            num_scalar_prefetch=1,
            grid=(rows,),
            in_specs=[
                pl.BlockSpec((1, heads, width), lambda r, n: (r, 0, 0)),
                pl.BlockSpec((1, positions, width), lambda r, n: (r, 0, 0)),
            ],
            out_specs=pl.BlockSpec((1, heads, LATENT), lambda r, n: (r, 0, 0)),
        ),
        out_shape=jax.ShapeDtypeStruct((rows, heads, LATENT), BF16),
        compiler_params=pltpu.CompilerParams(vmem_limit_bytes=16 * MIB),
        cost_estimate=pl.CostEstimate(
            flops=2 * rows * heads * positions * (width + LATENT),
            bytes_accessed=2 * rows * (positions * width + heads * (width + LATENT)),
            transcendentals=rows * heads * positions,
        ),
    )(cache_lengths, queries, latent_cache)


def gate_table(expert_ids, gate_values, experts_all):
    chosen = expert_ids[:, :, None] == jnp.arange(experts_all, dtype=jnp.int32)[None, None, :]
    return jnp.sum(jnp.where(chosen, gate_values[:, :, None], 0.0), axis=1)


def in_parts(table):
    high = table.astype(BF16)
    rest = table - high.astype(F32)
    middle = rest.astype(BF16)
    low = (rest - middle.astype(F32)).astype(BF16)
    return [high, middle, low]


def gate_up_kernel(rows_ref, gate_ref, up_ref, out_ref):
    rows = rows_ref[...]
    for e in range(gate_ref.shape[0]):
        gate = jnp.dot(rows, gate_ref[e], preferred_element_type=F32)
        up = jnp.dot(rows, up_ref[e], preferred_element_type=F32)
        out_ref[e] = (gate / (1.0 + jnp.exp(-gate)) * up).astype(BF16)


def gate_up(rows, gate_proj, up_proj):
    experts, depth, share = gate_proj.shape
    whole = pl.BlockSpec(memory_space=VMEM)
    return pl.pallas_call(
        gate_up_kernel,
        in_specs=[whole] * 3,
        out_specs=whole,
        out_shape=jax.ShapeDtypeStruct((experts, rows.shape[0], share), BF16),
        compiler_params=pltpu.CompilerParams(vmem_limit_bytes=40 * MIB),
        cost_estimate=pl.CostEstimate(
            flops=4 * experts * rows.shape[0] * depth * share,
            bytes_accessed=4 * experts * depth * share,
            transcendentals=experts * rows.shape[0] * share,
        ),
    )(
        rows,
        pltpu.with_memory_space_constraint(gate_proj, VMEM),
        pltpu.with_memory_space_constraint(up_proj, VMEM),
    )


def swap_halves(value, half):
    pieces = []
    for start in range(0, value.shape[0], 2 * half):
        pieces.append(value[start + half : start + 2 * half])
        pieces.append(value[start : start + half])
    return jnp.concatenate(pieces, axis=0)


def down_kernel(place_ref, table_ref, h0_ref, h1_ref, h2_ref, h3_ref, down_ref, *out_refs):
    place = place_ref[0]
    share = h0_ref.shape[2]
    width = down_ref.shape[2]
    tile = 256
    rows_z = out_refs[0].shape[0]
    experts = down_ref.shape[0]
    for start in range(0, width, tile):
        total = jnp.zeros((h0_ref.shape[1], tile), F32)
        for e in range(experts):
            made = jnp.zeros((h0_ref.shape[1], tile), F32)
            for k, ref in enumerate((h0_ref, h1_ref, h2_ref, h3_ref)):
                hidden = ref[e]
                if k >= 2:
                    hidden = swap_halves(hidden, rows_z // 2)
                owner = jnp.bitwise_xor(place, k)
                weights = down_ref[e, pl.ds(pl.multiple_of(owner * share, share), share), start : start + tile]
                made += jnp.dot(hidden, weights, preferred_element_type=F32)
            total += table_ref[:, e : e + 1] * made.astype(BF16).astype(F32)
        done = total.astype(BF16)
        for k, ref in enumerate(out_refs):
            ref[:, start : start + tile] = done[k * rows_z : (k + 1) * rows_z]


def down(place, table, hidden, down_proj):
    experts, depth, width = down_proj.shape
    rows = hidden[0].shape[1]
    whole = pl.BlockSpec(memory_space=VMEM)
    return pl.pallas_call(
        down_kernel,
        in_specs=[pl.BlockSpec(memory_space=pltpu.SMEM)] + [whole] * 6,
        out_specs=[whole] * 4,
        out_shape=[jax.ShapeDtypeStruct((rows // 4, width), BF16)] * 4,
        compiler_params=pltpu.CompilerParams(vmem_limit_bytes=40 * MIB),
        cost_estimate=pl.CostEstimate(
            flops=2 * experts * rows * depth * width,
            bytes_accessed=2 * experts * depth * width,
            transcendentals=0,
        ),
    )(place, table, *hidden, pltpu.with_memory_space_constraint(down_proj, VMEM))


def swap(value, axis, bit):
    size = lax.axis_size(axis)
    return lax.ppermute(value, axis, [(i, i ^ bit) for i in range(size)])


def routed_four(hidden_rows, expert_ids, gate_values, gate_proj, up_proj, down_proj):
    rows_dev, feature_count = hidden_rows.shape
    local_experts = gate_proj.shape[0]
    width = down_proj.shape[2]
    experts_all = local_experts * 4
    layer = lax.axis_index("expert")
    place = lax.axis_index("dp")
    core = place % 2
    x_side = place // 2

    parts = in_parts(gate_table(expert_ids, gate_values, experts_all))
    pad = -3 * experts_all % 128
    sent = jnp.concatenate([hidden_rows] + parts + [jnp.zeros((rows_dev, pad), BF16)], axis=1)
    total_width = sent.shape[1]
    along_z = [sent] + [swap(sent, "expert", k) for k in (1, 2, 3)]
    along_x = [swap(block, "dp", 2) for block in along_z]
    mine = jnp.stack([jnp.stack(along_z), jnp.stack(along_x)], axis=1)
    other_z = swap(jnp.stack(along_z), "dp", 1)
    other_x = swap(jnp.stack(along_x), "dp", 1)
    other = jnp.stack([other_z, other_x], axis=1)
    gathered = jnp.where(
        core == 0, jnp.stack([mine, other], axis=2), jnp.stack([other, mine], axis=2)
    ).reshape(16 * rows_dev, total_width)
    rows = gathered[:, :feature_count]
    coded = gathered[:, feature_count : feature_count + 3 * experts_all].astype(F32)
    table = coded[:, :experts_all] + coded[:, experts_all : 2 * experts_all] + coded[:, 2 * experts_all :]
    table = lax.dynamic_slice_in_dim(table, layer * local_experts, local_experts, axis=1)

    hidden = gate_up(rows, gate_proj, up_proj)
    hidden_x = swap(hidden, "dp", 2)
    hidden_c = swap(hidden, "dp", 1)
    hidden_xc = swap(hidden_x, "dp", 1)
    partial = down(
        place.astype(jnp.int32).reshape(1),
        table,
        (hidden, hidden_c, hidden_x, hidden_xc),
        down_proj,
    )
    arrived = [partial[0]] + [swap(partial[k], "expert", k) for k in (1, 2, 3)]
    summed = sum(block.astype(F32) for block in arrived).astype(BF16)
    summed = summed.reshape(2, 2, rows_dev, width)
    both = jnp.stack([summed[0], swap(summed[1], "dp", 2)])
    kept = jnp.where(core == 0, both[:, 0], both[:, 1])
    given = jnp.where(core == 0, both[:, 1], both[:, 0])
    taken = swap(given, "dp", 1)
    by_core = jnp.where(core == 0, jnp.stack([kept, taken], 1), jnp.stack([taken, kept], 1))
    by_place = jnp.where(x_side == 0, by_core, by_core[::-1]).reshape(4, rows_dev, width)
    return jnp.transpose(by_place, (1, 0, 2)).reshape(rows_dev, 4 * width)


def routed_any(hidden_rows, expert_ids, gate_values, gate_proj, up_proj, down_proj):
    rows_dev, feature_count = hidden_rows.shape
    local_experts = gate_proj.shape[0]
    width = down_proj.shape[2]
    owners = lax.axis_size("expert")
    members = lax.axis_size("dp")
    experts_all = local_experts * owners
    table = gate_table(expert_ids, gate_values, experts_all)
    rows = lax.all_gather(hidden_rows, ("expert", "dp"), axis=0, tiled=True)
    table = lax.all_gather(table, ("expert", "dp"), axis=0, tiled=True)
    table = lax.dynamic_slice_in_dim(
        table, lax.axis_index("expert") * local_experts, local_experts, axis=1
    )
    total = jnp.zeros((rows.shape[0], width), F32)
    for e in range(local_experts):
        gate = jnp.dot(rows, gate_proj[e], preferred_element_type=F32)
        up = jnp.dot(rows, up_proj[e], preferred_element_type=F32)
        share = (jax.nn.silu(gate) * up).astype(BF16)
        hidden = lax.all_gather(share, "dp", axis=1, tiled=True)
        made = jnp.dot(hidden, down_proj[e], preferred_element_type=F32).astype(BF16)
        total += table[:, e : e + 1] * made.astype(F32)
    partial = total.astype(BF16).reshape(owners, members, rows_dev, width)
    returned = lax.all_to_all(
        lax.all_to_all(partial, "expert", split_axis=0, concat_axis=0, tiled=True),
        "dp",
        split_axis=1,
        concat_axis=1,
        tiled=True,
    )
    blended = jnp.sum(returned.astype(F32), axis=0).astype(BF16)
    return jnp.transpose(blended, (1, 0, 2)).reshape(rows_dev, members * width)


def local(
    hidden_rows,
    expert_ids,
    gate_values,
    gate_proj,
    up_proj,
    down_proj,
    queries,
    latent_cache,
    cache_lengths,
):
    attended = attend(queries, latent_cache, cache_lengths)
    four = lax.axis_size("expert") == 4 and lax.axis_size("dp") == 4
    routed = routed_four if four else routed_any
    blended = routed(hidden_rows, expert_ids, gate_values, gate_proj, up_proj, down_proj)
    return (blended, attended)


def solution(mesh):
    return jax.shard_map(
        local,
        mesh=mesh,
        in_specs=(
            P(("groups", "expert", "dp"), None),
            P(("groups", "expert", "dp"), None),
            P(("groups", "expert", "dp"), None),
            P("expert", None, "dp"),
            P("expert", None, "dp"),
            P("expert", None, "dp"),
            P(("groups", "expert", "dp"), None, None),
            P(("groups", "expert", "dp"), None, None),
            P(("groups", "expert", "dp")),
        ),
        out_specs=(P(("groups", "expert", "dp"), None), P(("groups", "expert", "dp"), None, None)),
        check_vma=False,
    )
```

time: 189 us -> 62.8 us (0.33)
  blocking collectives: 125 us -> 0 us
  starting transfers between devices: 7.12 us -> 18.3 us
  matrix products: 10.1 us -> 0 us
  Pallas kernels: 0 us -> 8.46 us
  waiting for transfers between devices: 29.4 us -> 21.1 us
  local copies, waits for them, and re-layouts: 14.6 us -> 11.7 us
    all_to_all x2 -> x0, blocking collectives: 117 us -> none  [the longest x1 76.8 us: local(): lax.all_to_all(copies, 'expert', split_axis=0, concat_axis=0, tiled=True)]
    all_to_all x2 -> x0, waiting for transfers between devices: 29.4 us -> none  [the longest x1 19.8 us: local(): lax.all_to_all(produced, 'expert', split_axis=0, concat_axis=0, tiled=True)]
    ppermute x0 -> x17, waiting for transfers between devices: none -> 21.1 us  [swap(): return lax.ppermute(value, axis, [(i, i ^ bit) for i in range(size)])]
    ppermute x0 -> x17, starting transfers between devices: none -> 18.3 us  [swap(): return lax.ppermute(value, axis, [(i, i ^ bit) for i in range(size)])]
    dot_general x6 -> x0, matrix products: 10.1 us -> none  [the longest x1 2.81 us: local(): jnp.einsum('olmd,ldf->olmf', row_block, up_proj, preferred_element_type=j...]
    unnamed x22 -> x16, local copies, waits for them, and re-layouts: 0.07 us -> 9.43 us
    pallas_call x0 -> x3, Pallas kernels: none -> 8.46 us  [the longest x1 4.28 us: gate_up(): pl.pallas_call(gate_up_kernel, in_specs=[whole] * 3, out_specs=whole, out...]
    all_gather x1 -> x0, blocking collectives: 8.02 us -> none  [local(): lax.all_gather(hidden_share, 'dp', axis=3, tiled=True)]
  transfers between devices with their start and end apart: 2 -> 17, of which waited for: 2 -> 10; matrix products, arithmetic and copies ran while one was open for 2% -> 2% of each run, Pallas kernels for 0% -> 4%
where the time goes in v1:
time: 62.8 us; the launch traced here: 62.4 us
  waiting for transfers between devices  21.1 us (34%)
  starting transfers between devices  18.3 us (29%)
  local copies, waits for them, and re-layouts  11.7 us (19%)
  Pallas kernels  8.46 us (13%)
  other arithmetic  2.04 us (3%)
  between operations  0.85 us (1%)
    ppermute x17, waiting for transfers between devices, swap(): return lax.ppermute(value, axis, [(i, i ^ bit) for i in range(size)])  21.1 us
    ppermute x17, starting transfers between devices, swap(): return lax.ppermute(value, axis, [(i, i ^ bit) for i in range(size)])  18.3 us
    unnamed x16, local copies, waits for them, and re-layouts  9.43 us
    pallas_call x1, Pallas kernels, gate_up(): pl.pallas_call(gate_up_kernel, in_specs=[whole] * 3, out_specs=whole, out...  4.28 us
    pallas_call x1, Pallas kernels, attend(): pl.pallas_call(attend_kernel, grid_spec=pltpu.PrefetchScalarGridSpec(num_...  2.62 us
    pallas_call x1, Pallas kernels, down(): pl.pallas_call(down_kernel, in_specs=[pl.BlockSpec(memory_space=pltpu.SME...  1.55 us
  transfers between devices with their start and end apart: 17, of which 10 were waited for; matrix products, arithmetic and copies ran while one was open for 2% of the time, Pallas kernels for 4%

profile of v1, /device:TPU:0, one launch (start us, length us, event | category | flops | bytes accessed | tf_op | source)
XLA Modules:
  0.0 62.4 jit_solution(7706545295469042892)
XLA Ops:
  0.6 0.8 %select_reduce_fusion = f32[8,16]{1,0:T(8,128)S(1)} fusion(f32[8,8]{1,0:T(8,128)} %param.11, s32[8,8]{1,0:T(8,128)} %param.10), kind=kLoop, calls=%fused_computation.19 | loop fusion | flops 2944 | bytes 1024 | tf_op jit(solution)/shard_map/reduce_sum | solution.py:62
  1.5 0.9 %concatenate.3 = bf16[8,4224]{1,0:T(8,128)(2,1)S(1)} concatenate(bf16[8,4096]{1,0:T(8,128)(2,1)} %param.9, bf16[8,16]{1,0:T(8,128)(2,1)S(1)} %get-tuple-element.21, bf16[8,16]{1,0:T(8,128)(2,1)S(1)} %get-tuple-element.20, bf16[8,16]{1,0:T(8,128)(2,1)S(1)} %get-tuple-element.19, bf16[8,80]{1,0:T(8,128)(2,1)S(1)} %broadcast_in_dim.20), dimensions={1} | concatenate | bytes 135168 | tf_op jit(solution)/shard_map/concatenate | solution.py:169
  2.4 5.0 %collective-permute-start.2 = (bf16[8,4224]{1,0:T(8,128)(2,1)S(1)}, bf16[8,4224]{1,0:T(8,128)(2,1)S(1)}, u32[]{:S(2)}, u32[]{:S(2)}) collective-permute-start(bf16[8,4224]{1,0:T(8,128)(2,1)S(1)} %concatenate.3), channel_id=1, source_target_pairs={{0,12},{4,8},{8,4},{12,0},{1,13},{5,9},{9,5},{13,1},{2,14},{6,10},... | collective-permute-start | bytes 202760 | tf_op jit(solution)/shard_map/ppermute | solution.py:154
  7.4 0.0 collective-permute-start.1
  7.4 0.6 %collective-permute-start = (bf16[8,4224]{1,0:T(8,128)(2,1)S(1)}, bf16[8,4224]{1,0:T(8,128)(2,1)S(1)}, u32[]{:S(2)}, u32[]{:S(2)}) collective-permute-start(bf16[8,4224]{1,0:T(8,128)(2,1)S(1)} %concatenate.3), channel_id=1, source_target_pairs={{0,4},{4,0},{8,12},{12,8},{1,5},{5,1},{9,13},{13,9},{2,6},{6,2},{1... | collective-permute-start | bytes 202760 | tf_op jit(solution)/shard_map/ppermute | solution.py:154
  8.1 1.6 %collective-permute-start.3 = (bf16[8,4224]{1,0:T(8,128)(2,1)S(1)}, bf16[8,4224]{1,0:T(8,128)(2,1)S(1)}, u32[]{:S(2)}, u32[]{:S(2)}) collective-permute-start(bf16[8,4224]{1,0:T(8,128)(2,1)S(1)} %concatenate.3), channel_id=1, source_target_pairs={{0,2},{1,3},{2,0},{3,1},{4,6},{5,7},{6,4},{7,5},{8,10},{9,11},{10,... | collective-permute-start | bytes 202760 | tf_op jit(solution)/shard_map/ppermute | solution.py:154
  9.7 0.3 collective-permute-done.2
  10.0 1.9 %collective-permute-start.6 = (bf16[8,4224]{1,0:T(8,128)(2,1)S(1)}, bf16[8,4224]{1,0:T(8,128)(2,1)S(1)}, u32[]{:S(2)}, u32[]{:S(2)}) collective-permute-start(bf16[8,4224]{1,0:T(8,128)(2,1)S(1)} %collective-permute-done.2), channel_id=1, source_target_pairs={{0,2},{1,3},{2,0},{3,1},{4,6},{5,7},{6,4},{7,5},{8,10},{9,11},{10,... | collective-permute-start | bytes 202760 | tf_op jit(solution)/shard_map/ppermute | solution.py:154
  11.9 1.3 %collective-permute-done.1 = bf16[8,4224]{1,0:T(8,128)(2,1)S(1)} collective-permute-done((bf16[8,4224]{1,0:T(8,128)(2,1)S(1)}, bf16[8,4224]{1,0:T(8,128)(2,1)S(1)}, u32[]{:S(2)}, u32[]{:S(2)}) %collective-permute-start.1) | collective-permute-done | bytes 67616 | tf_op jit(solution)/shard_map/ppermute | solution.py:154
  13.2 1.5 %collective-permute-start.5 = (bf16[8,4224]{1,0:T(8,128)(2,1)S(1)}, bf16[8,4224]{1,0:T(8,128)(2,1)S(1)}, u32[]{:S(2)}, u32[]{:S(2)}) collective-permute-start(bf16[8,4224]{1,0:T(8,128)(2,1)S(1)} %collective-permute-done.1), channel_id=1, source_target_pairs={{0,2},{1,3},{2,0},{3,1},{4,6},{5,7},{6,4},{7,5},{8,10},{9,11},{10,... | collective-permute-start | bytes 202760 | tf_op jit(solution)/shard_map/ppermute | solution.py:154
  14.7 0.0 collective-permute-done
  14.7 0.5 collective-permute-start.4
  15.2 0.1 fusion.3
  15.3 0.1 collective-permute-start.7
  15.4 0.0 collective-permute-done.3
  15.4 0.0 collective-permute-done.6
  15.4 2.7 %collective-permute-done.5 = bf16[8,4224]{1,0:T(8,128)(2,1)S(1)} collective-permute-done((bf16[8,4224]{1,0:T(8,128)(2,1)S(1)}, bf16[8,4224]{1,0:T(8,128)(2,1)S(1)}, u32[]{:S(2)}, u32[]{:S(2)}) %collective-permute-start.5) | collective-permute-done | bytes 67616 | tf_op jit(solution)/shard_map/ppermute | solution.py:154
  18.1 0.9 %collective-permute-done.4 = bf16[8,4224]{1,0:T(8,128)(2,1)S(1)} collective-permute-done((bf16[8,4224]{1,0:T(8,128)(2,1)S(1)}, bf16[8,4224]{1,0:T(8,128)(2,1)S(1)}, u32[]{:S(2)}, u32[]{:S(2)}) %collective-permute-start.4) | collective-permute-done | bytes 67616 | tf_op jit(solution)/shard_map/ppermute | solution.py:154
  19.0 0.1 fusion.2
  19.0 0.1 collective-permute-start.8
  19.1 0.0 copy-start.1
  19.1 0.1 maximum_bitcast_fusion
  19.2 0.0 collective-permute-done.7
  19.2 1.4 %collective-permute-done.8 = bf16[4,8,4224]{2,1,0:T(8,128)(2,1)S(1)} collective-permute-done((bf16[4,8,4224]{2,1,0:T(8,128)(2,1)S(1)}, bf16[4,8,4224]{2,1,0:T(8,128)(2,1)S(1)}, u32[]{:S(2)}, u32[]{:S(2)}) %collective-permute-start.8) | collective-permute-done | bytes 270368 | tf_op jit(solution)/shard_map/ppermute | solution.py:154
  20.6 0.1 maximum_bitcast_fusion.1
  20.7 0.2 maximum_select_fusion
  20.9 0.1 copy.25
  21.0 1.1 %slice.47.rows_ref = bf16[128,4096]{1,0:T(8,128)(2,1)} slice(bf16[128,4224]{1,0:T(8,128)(2,1)S(1)} %bitcast.41), slice={[0:128], [0:4096]} | slice | bytes 2097152 | tf_op jit(solution)/shard_map/slice | solution.py:180
  22.1 0.8 %copy-done.1 = bf16[4,4096,256]{2,1,0:T(8,128)(2,1)S(1)} copy-done((bf16[4,4096,256]{2,1,0:T(8,128)(2,1)S(1)}, bf16[4,4096,256]{2,1,0:T(8,128)(2,1)}, u32[]{:S(2)}) %copy-start.1) | copy-done | bytes 8388632
  22.9 0.0 copy-start.2
  22.9 3.4 %copy-done.2 = bf16[4,4096,256]{2,1,0:T(8,128)(2,1)S(1)} copy-done((bf16[4,4096,256]{2,1,0:T(8,128)(2,1)S(1)}, bf16[4,4096,256]{2,1,0:T(8,128)(2,1)}, u32[]{:S(2)}) %copy-start.2) | copy-done | bytes 8388632
  26.3 4.3 %shard_map.104.h0_ref = bf16[4,128,256]{2,1,0:T(8,128)(2,1)} custom-call(bf16[128,4096]{1,0:T(8,128)(2,1)} %slice.47.rows_ref, bf16[4,4096,256]{2,1,0:T(8,128)(2,1)S(1)} %copy-done.1, bf16[4,4096,256]{2,1,0:T(8,128)(2,1)S(1)} %copy-done.2), custom_call_target="tpu_custom_call" | custom-call | flops 2147483648 | bytes 16777216 | tf_op jit(solution)/shard_map/pallas_call | solution.py:84
  30.5 1.1 %collective-permute-start.10 = (bf16[4,128,256]{2,1,0:T(8,128)(2,1)}, bf16[4,128,256]{2,1,0:T(8,128)(2,1)S(1)}, u32[]{:S(2)}, u32[]{:S(2)}) collective-permute-start(bf16[4,128,256]{2,1,0:T(8,128)(2,1)} %shard_map.104.h0_ref), channel_id=1, source_target_pairs={{0,2},{1,3},{2,0},{3,1},{4,6},{5,7},{6,4},{7,5},{8,10},{9,11},{10,... | collective-permute-start | bytes 786440 | tf_op jit(solution)/shard_map/ppermute | solution.py:154
  31.6 0.2 collective-permute-start.9
  31.8 7.6 %collective-permute-done.10.h2_ref = bf16[4,128,256]{2,1,0:T(8,128)(2,1)S(1)} collective-permute-done((bf16[4,128,256]{2,1,0:T(8,128)(2,1)}, bf16[4,128,256]{2,1,0:T(8,128)(2,1)S(1)}, u32[]{:S(2)}, u32[]{:S(2)}) %collective-permute-start.10) | collective-permute-done | bytes 262176 | tf_op jit(solution)/shard_map/ppermute | solution.py:154
  39.5 0.0 collective-permute-start.11
  39.5 0.1 fusion.4
  39.6 0.1 dynamic-slice_add_fusion.table_ref
  39.7 0.0 collective-permute-done.9.h1_ref
  39.7 1.3 %collective-permute-done.11.h3_ref = bf16[4,128,256]{2,1,0:T(8,128)(2,1)S(1)} collective-permute-done((bf16[4,128,256]{2,1,0:T(8,128)(2,1)S(1)}, bf16[4,128,256]{2,1,0:T(8,128)(2,1)S(1)}, u32[]{:S(2)}, u32[]{:S(2)}) %collective-permute-start.11) | collective-permute-done | bytes 262176 | tf_op jit(solution)/shard_map/ppermute | solution.py:154
  41.0 0.0 copy-start
  41.0 3.4 %copy-done = bf16[4,1024,1024]{2,1,0:T(8,128)(2,1)S(1)} copy-done((bf16[4,1024,1024]{2,1,0:T(8,128)(2,1)S(1)}, bf16[4,1024,1024]{2,1,0:T(8,128)(2,1)}, u32[]{:S(2)}) %copy-start) | copy-done | bytes 8388632
  44.4 0.0 copy-start.3
  44.4 0.9 %copy-done.3 = bf16[4,128,256]{2,1,0:T(8,128)(2,1)S(1)} copy-done((bf16[4,128,256]{2,1,0:T(8,128)(2,1)S(1)}, bf16[4,128,256]{2,1,0:T(8,128)(2,1)}, u32[]{:S(2)}) %copy-start.3) | copy-done | bytes 262168
  45.3 0.0 copy-start.6
  45.3 1.6 %shard_map.105 = (bf16[32,1024]{1,0:T(8,128)(2,1)S(1)}, bf16[32,1024]{1,0:T(8,128)(2,1)S(1)}, bf16[32,1024]{1,0:T(8,128)(2,1)S(1)}, bf16[32,1024]{1,0:T(8,128)(2,1)S(1)}) custom-call(s32[1]{0:T(128)} %bitcast.1.place_ref, f32[128,4]{1,0:T(8,128)S(1)} %dynamic-slice_add_fusion.table_ref, bf16[4,128,256]{2,1,0:T(8,128)(2,1)S(1)} %copy-done.3, ...), custom_call_target="tpu_custom_call" | custom-call | flops 1073741824 | bytes 8388608 | tf_op jit(solution)/shard_map/pallas_call | solution.py:138
  46.9 2.8 %collective-permute-start.14 = (bf16[32,1024]{1,0:T(8,128)(2,1)S(1)}, bf16[32,1024]{1,0:T(8,128)(2,1)S(1)}, u32[]{:S(2)}, u32[]{:S(2)}) collective-permute-start(bf16[32,1024]{1,0:T(8,128)(2,1)S(1)} %get-tuple-element.9), channel_id=1, source_target_pairs={{0,12},{4,8},{8,4},{12,0},{1,13},{5,9},{9,5},{13,1},{2,14},{6,10},... | collective-permute-start | bytes 196616 | tf_op jit(solution)/shard_map/ppermute | solution.py:154
  49.7 0.0 collective-permute-start.13
  49.7 1.7 %collective-permute-start.12 = (bf16[32,1024]{1,0:T(8,128)(2,1)S(1)}, bf16[32,1024]{1,0:T(8,128)(2,1)S(1)}, u32[]{:S(2)}, u32[]{:S(2)}) collective-permute-start(bf16[32,1024]{1,0:T(8,128)(2,1)S(1)} %get-tuple-element.7), channel_id=1, source_target_pairs={{0,4},{4,0},{8,12},{12,8},{1,5},{5,1},{9,13},{13,9},{2,6},{6,2},{1... | collective-permute-start | bytes 196616 | tf_op jit(solution)/shard_map/ppermute | solution.py:154
  51.3 2.3 %collective-permute-done.14 = bf16[32,1024]{1,0:T(8,128)(2,1)S(1)} collective-permute-done((bf16[32,1024]{1,0:T(8,128)(2,1)S(1)}, bf16[32,1024]{1,0:T(8,128)(2,1)S(1)}, u32[]{:S(2)}, u32[]{:S(2)}) %collective-permute-start.14) | collective-permute-done | bytes 65568 | tf_op jit(solution)/shard_map/ppermute | solution.py:154
  53.6 2.0 %collective-permute-done.13 = bf16[32,1024]{1,0:T(8,128)(2,1)S(1)} collective-permute-done((bf16[32,1024]{1,0:T(8,128)(2,1)S(1)}, bf16[32,1024]{1,0:T(8,128)(2,1)S(1)}, u32[]{:S(2)}, u32[]{:S(2)}) %collective-permute-start.13) | collective-permute-done | bytes 65568 | tf_op jit(solution)/shard_map/ppermute | solution.py:154
  55.7 0.0 collective-permute-done.12
  55.7 1.1 %collective-permute-start.15 = (bf16[2,8,1024]{2,1,0:T(8,128)(2,1)S(1)}, bf16[2,8,1024]{2,1,0:T(8,128)(2,1)S(1)}, u32[]{:S(2)}, u32[]{:S(2)}) collective-permute-start(bf16[2,8,1024]{2,1,0:T(8,128)(2,1)S(1)} %get-tuple-element.15), channel_id=1, source_target_pairs={{0,2},{1,3},{2,0},{3,1},{4,6},{5,7},{6,4},{7,5},{8,10},{9,11},{10,... | collective-permute-start | bytes 98312 | tf_op jit(solution)/shard_map/ppermute | solution.py:154
  56.9 0.0 copy-done.6
  56.9 0.2 copy.30.queries_ref
  57.1 0.0 copy-done.5
  57.1 0.0 copy-start.4
  57.1 0.7 %copy.31.cache_ref = bf16[2,512,576]{2,1,0:T(8,128)(2,1)S(1)} copy(bf16[2,512,576]{1,2,0:T(8,128)(2,1)S(1)} %copy-done.5) | data formatting | bytes 2359296 | tf_op args[7]
  57.8 0.0 copy-done.4
  57.8 2.6 %shard_map.106 = bf16[2,128,512]{2,1,0:T(8,128)(2,1)} custom-call(s32[2]{0:T(128)S(1)} %copy-done.4, bf16[2,128,576]{2,1,0:T(8,128)(2,1)S(1)} %copy.30.queries_ref, bf16[2,512,576]{2,1,0:T(8,128)(2,1)S(1)} %copy.31.cache_ref), custom_call_target="tpu_custom_call" | custom-call | flops 285212672 | bytes 1736704 | tf_op jit(solution)/shard_map/pallas_call | solution.py:39
  60.5 0.0 collective-permute-done.15
  60.5 0.1 collective-permute-start.16
  60.6 1.2 %collective-permute-done.16 = bf16[2,8,1024]{2,1,0:T(8,128)(2,1)S(1)} collective-permute-done((bf16[2,8,1024]{2,1,0:T(8,128)(2,1)S(1)}, bf16[2,8,1024]{2,1,0:T(8,128)(2,1)S(1)}, u32[]{:S(2)}, u32[]{:S(2)}) %collective-permute-start.16) | collective-permute-done | bytes 32800 | tf_op jit(solution)/shard_map/ppermute | solution.py:154
  61.8 0.6 %reverse_select_fusion = bf16[2,2,8,1024]{3,2,1,0:T(8,128)(2,1)} fusion(bf16[2,2,8,1024]{3,2,1,0:T(8,128)(2,1)S(1)} %maximum_select_fusion.1, pred[]{:T(512)S(6)} %eq.12), kind=kLoop, calls=%fused_computation.6 | loop fusion | flops 32768 | bytes 131073 | tf_op jit(solution)/shard_map/jit(_where)/select_n | solution.py:203
  (9 shorter events, 0.1 us)
Async XLA Ops:
  2.4 7.7 %collective-permute-start.2 = (bf16[8,4224]{1,0:T(8,128)(2,1)S(1)}, bf16[8,4224]{1,0:T(8,128)(2,1)S(1)}, u32[]{:S(2)}, u32[]{:S(2)}) collective-permute-start(bf16[8,4224]{1,0:T(8,128)(2,1)S(1)} %concatenate.3), channel_id=1, source_target_pairs={{0,12},{4,8},{8,4},{12,0},{1,13},{5,9},{9,5},{13,1},{2,14},{6,10},... | collective-permute-start | bytes 202760 | tf_op jit(solution)/shard_map/ppermute | solution.py:154
  7.4 5.8 %collective-permute-start.1 = (bf16[8,4224]{1,0:T(8,128)(2,1)S(1)}, bf16[8,4224]{1,0:T(8,128)(2,1)S(1)}, u32[]{:S(2)}, u32[]{:S(2)}) collective-permute-start(bf16[8,4224]{1,0:T(8,128)(2,1)S(1)} %concatenate.3), channel_id=1, source_target_pairs={{0,8},{4,12},{8,0},{12,4},{1,9},{5,13},{9,1},{13,5},{2,10},{6,14},... | collective-permute-start | bytes 202760 | tf_op jit(solution)/shard_map/ppermute | solution.py:154
  7.4 7.2 %collective-permute-start = (bf16[8,4224]{1,0:T(8,128)(2,1)S(1)}, bf16[8,4224]{1,0:T(8,128)(2,1)S(1)}, u32[]{:S(2)}, u32[]{:S(2)}) collective-permute-start(bf16[8,4224]{1,0:T(8,128)(2,1)S(1)} %concatenate.3), channel_id=1, source_target_pairs={{0,4},{4,0},{8,12},{12,8},{1,5},{5,1},{9,13},{13,9},{2,6},{6,2},{1... | collective-permute-start | bytes 202760 | tf_op jit(solution)/shard_map/ppermute | solution.py:154
  8.1 7.3 %collective-permute-start.3 = (bf16[8,4224]{1,0:T(8,128)(2,1)S(1)}, bf16[8,4224]{1,0:T(8,128)(2,1)S(1)}, u32[]{:S(2)}, u32[]{:S(2)}) collective-permute-start(bf16[8,4224]{1,0:T(8,128)(2,1)S(1)} %concatenate.3), channel_id=1, source_target_pairs={{0,2},{1,3},{2,0},{3,1},{4,6},{5,7},{6,4},{7,5},{8,10},{9,11},{10,... | collective-permute-start | bytes 202760 | tf_op jit(solution)/shard_map/ppermute | solution.py:154
  10.0 5.3 %collective-permute-start.6 = (bf16[8,4224]{1,0:T(8,128)(2,1)S(1)}, bf16[8,4224]{1,0:T(8,128)(2,1)S(1)}, u32[]{:S(2)}, u32[]{:S(2)}) collective-permute-start(bf16[8,4224]{1,0:T(8,128)(2,1)S(1)} %collective-permute-done.2), channel_id=1, source_target_pairs={{0,2},{1,3},{2,0},{3,1},{4,6},{5,7},{6,4},{7,5},{8,10},{9,11},{10,... | collective-permute-start | bytes 202760 | tf_op jit(solution)/shard_map/ppermute | solution.py:154
  13.2 4.9 %collective-permute-start.5 = (bf16[8,4224]{1,0:T(8,128)(2,1)S(1)}, bf16[8,4224]{1,0:T(8,128)(2,1)S(1)}, u32[]{:S(2)}, u32[]{:S(2)}) collective-permute-start(bf16[8,4224]{1,0:T(8,128)(2,1)S(1)} %collective-permute-done.1), channel_id=1, source_target_pairs={{0,2},{1,3},{2,0},{3,1},{4,6},{5,7},{6,4},{7,5},{8,10},{9,11},{10,... | collective-permute-start | bytes 202760 | tf_op jit(solution)/shard_map/ppermute | solution.py:154
  14.7 4.3 %collective-permute-start.4 = (bf16[8,4224]{1,0:T(8,128)(2,1)S(1)}, bf16[8,4224]{1,0:T(8,128)(2,1)S(1)}, u32[]{:S(2)}, u32[]{:S(2)}) collective-permute-start(bf16[8,4224]{1,0:T(8,128)(2,1)S(1)} %collective-permute-done), channel_id=1, source_target_pairs={{0,2},{1,3},{2,0},{3,1},{4,6},{5,7},{6,4},{7,5},{8,10},{9,11},{10,... | collective-permute-start | bytes 202760 | tf_op jit(solution)/shard_map/ppermute | solution.py:154
  15.3 3.9 %collective-permute-start.7 = (bf16[4,8,4224]{2,1,0:T(8,128)(2,1)S(1)}, bf16[4,8,4224]{2,1,0:T(8,128)(2,1)S(1)}, u32[]{:S(2)}, u32[]{:S(2)}) collective-permute-start(bf16[4,8,4224]{2,1,0:T(8,128)(2,1)S(1)} %get-tuple-element.11), channel_id=1, source_target_pairs={{0,1},{1,0},{2,3},{3,2},{4,5},{5,4},{6,7},{7,6},{8,9},{9,8},{10,11... | collective-permute-start | bytes 811016 | tf_op jit(solution)/shard_map/ppermute | solution.py:154
  19.0 1.6 %collective-permute-start.8 = (bf16[4,8,4224]{2,1,0:T(8,128)(2,1)S(1)}, bf16[4,8,4224]{2,1,0:T(8,128)(2,1)S(1)}, u32[]{:S(2)}, u32[]{:S(2)}) collective-permute-start(bf16[4,8,4224]{2,1,0:T(8,128)(2,1)S(1)} %get-tuple-element.13), channel_id=1, source_target_pairs={{0,1},{1,0},{2,3},{3,2},{4,5},{5,4},{6,7},{7,6},{8,9},{9,8},{10,11... | collective-permute-start | bytes 811016 | tf_op jit(solution)/shard_map/ppermute | solution.py:154
  19.1 3.8 %copy-start.1 = (bf16[4,4096,256]{2,1,0:T(8,128)(2,1)S(1)}, bf16[4,4096,256]{2,1,0:T(8,128)(2,1)}, u32[]{:S(2)}) copy-start(bf16[4,4096,256]{2,1,0:T(8,128)(2,1)} %gate_ref.1) | copy-start | bytes 25165828
  22.9 3.4 %copy-start.2 = (bf16[4,4096,256]{2,1,0:T(8,128)(2,1)S(1)}, bf16[4,4096,256]{2,1,0:T(8,128)(2,1)}, u32[]{:S(2)}) copy-start(bf16[4,4096,256]{2,1,0:T(8,128)(2,1)} %up_ref.1) | copy-start | bytes 25165828
  30.5 8.9 %collective-permute-start.10 = (bf16[4,128,256]{2,1,0:T(8,128)(2,1)}, bf16[4,128,256]{2,1,0:T(8,128)(2,1)S(1)}, u32[]{:S(2)}, u32[]{:S(2)}) collective-permute-start(bf16[4,128,256]{2,1,0:T(8,128)(2,1)} %shard_map.104.h0_ref), channel_id=1, source_target_pairs={{0,2},{1,3},{2,0},{3,1},{4,6},{5,7},{6,4},{7,5},{8,10},{9,11},{10,... | collective-permute-start | bytes 786440 | tf_op jit(solution)/shard_map/ppermute | solution.py:154
  31.6 8.1 %collective-permute-start.9 = (bf16[4,128,256]{2,1,0:T(8,128)(2,1)}, bf16[4,128,256]{2,1,0:T(8,128)(2,1)S(1)}, u32[]{:S(2)}, u32[]{:S(2)}) collective-permute-start(bf16[4,128,256]{2,1,0:T(8,128)(2,1)} %shard_map.104.h0_ref), channel_id=1, source_target_pairs={{0,1},{1,0},{2,3},{3,2},{4,5},{5,4},{6,7},{7,6},{8,9},{9,8},{10,11... | collective-permute-start | bytes 786440 | tf_op jit(solution)/shard_map/ppermute | solution.py:154
  39.5 1.5 %collective-permute-start.11 = (bf16[4,128,256]{2,1,0:T(8,128)(2,1)S(1)}, bf16[4,128,256]{2,1,0:T(8,128)(2,1)S(1)}, u32[]{:S(2)}, u32[]{:S(2)}) collective-permute-start(bf16[4,128,256]{2,1,0:T(8,128)(2,1)S(1)} %collective-permute-done.10.h2_ref), channel_id=1, source_target_pairs={{0,1},{1,0},{2,3},{3,2},{4,5},{5,4},{6,7},{7,6},{8,9},{9,8},{10,11... | collective-permute-start | bytes 786440 | tf_op jit(solution)/shard_map/ppermute | solution.py:154
  41.0 3.4 %copy-start = (bf16[4,1024,1024]{2,1,0:T(8,128)(2,1)S(1)}, bf16[4,1024,1024]{2,1,0:T(8,128)(2,1)}, u32[]{:S(2)}) copy-start(bf16[4,1024,1024]{2,1,0:T(8,128)(2,1)} %down_ref.1) | copy-start | bytes 25165828
  44.4 0.9 %copy-start.3 = (bf16[4,128,256]{2,1,0:T(8,128)(2,1)S(1)}, bf16[4,128,256]{2,1,0:T(8,128)(2,1)}, u32[]{:S(2)}) copy-start(bf16[4,128,256]{2,1,0:T(8,128)(2,1)} %shard_map.104.h0_ref) | copy-start | bytes 786436
  45.3 11.5 %copy-start.6 = (bf16[2,128,576]{1,2,0:T(8,128)(2,1)S(1)}, bf16[2,128,576]{1,2,0:T(8,128)(2,1)}, u32[]{:S(2)}) copy-start(bf16[2,128,576]{1,2,0:T(8,128)(2,1)} %param.15) | copy-start | bytes 884740
  45.3 11.8 %copy-start.5 = (bf16[2,512,576]{1,2,0:T(8,128)(2,1)S(1)}, bf16[2,512,576]{1,2,0:T(8,128)(2,1)}, u32[]{:S(2)}) copy-start(bf16[2,512,576]{1,2,0:T(8,128)(2,1)} %param.16) | copy-start | bytes 3538948
  46.9 6.8 %collective-permute-start.14 = (bf16[32,1024]{1,0:T(8,128)(2,1)S(1)}, bf16[32,1024]{1,0:T(8,128)(2,1)S(1)}, u32[]{:S(2)}, u32[]{:S(2)}) collective-permute-start(bf16[32,1024]{1,0:T(8,128)(2,1)S(1)} %get-tuple-element.9), channel_id=1, source_target_pairs={{0,12},{4,8},{8,4},{12,0},{1,13},{5,9},{9,5},{13,1},{2,14},{6,10},... | collective-permute-start | bytes 196616 | tf_op jit(solution)/shard_map/ppermute | solution.py:154
  49.7 6.0 %collective-permute-start.13 = (bf16[32,1024]{1,0:T(8,128)(2,1)S(1)}, bf16[32,1024]{1,0:T(8,128)(2,1)S(1)}, u32[]{:S(2)}, u32[]{:S(2)}) collective-permute-start(bf16[32,1024]{1,0:T(8,128)(2,1)S(1)} %get-tuple-element.8), channel_id=1, source_target_pairs={{0,8},{4,12},{8,0},{12,4},{1,9},{5,13},{9,1},{13,5},{2,10},{6,14},... | collective-permute-start | bytes 196616 | tf_op jit(solution)/shard_map/ppermute | solution.py:154
  49.7 6.0 %collective-permute-start.12 = (bf16[32,1024]{1,0:T(8,128)(2,1)S(1)}, bf16[32,1024]{1,0:T(8,128)(2,1)S(1)}, u32[]{:S(2)}, u32[]{:S(2)}) collective-permute-start(bf16[32,1024]{1,0:T(8,128)(2,1)S(1)} %get-tuple-element.7), channel_id=1, source_target_pairs={{0,4},{4,0},{8,12},{12,8},{1,5},{5,1},{9,13},{13,9},{2,6},{6,2},{1... | collective-permute-start | bytes 196616 | tf_op jit(solution)/shard_map/ppermute | solution.py:154
  55.7 4.7 %collective-permute-start.15 = (bf16[2,8,1024]{2,1,0:T(8,128)(2,1)S(1)}, bf16[2,8,1024]{2,1,0:T(8,128)(2,1)S(1)}, u32[]{:S(2)}, u32[]{:S(2)}) collective-permute-start(bf16[2,8,1024]{2,1,0:T(8,128)(2,1)S(1)} %get-tuple-element.15), channel_id=1, source_target_pairs={{0,2},{1,3},{2,0},{3,1},{4,6},{5,7},{6,4},{7,5},{8,10},{9,11},{10,... | collective-permute-start | bytes 98312 | tf_op jit(solution)/shard_map/ppermute | solution.py:154
  57.1 0.7 %copy-start.4 = (s32[2]{0:T(128)S(1)}, s32[2]{0:T(128)}, u32[]{:S(2)}) copy-start(s32[2]{0:T(128)} %lengths_ref.1) | copy-start | bytes 28
  60.5 1.3 %collective-permute-start.16 = (bf16[2,8,1024]{2,1,0:T(8,128)(2,1)S(1)}, bf16[2,8,1024]{2,1,0:T(8,128)(2,1)S(1)}, u32[]{:S(2)}, u32[]{:S(2)}) collective-permute-start(bf16[2,8,1024]{2,1,0:T(8,128)(2,1)S(1)} %select_bitcast_fusion), channel_id=1, source_target_pairs={{0,1},{1,0},{2,3},{3,2},{4,5},{5,4},{6,7},{7,6},{8,9},{9,8},{10,11... | collective-permute-start | bytes 98312 | tf_op jit(solution)/shard_map/ppermute | solution.py:154

commit v2 on v1

v2 whole, which is shorter than its diff:
```python
import jax
import jax.numpy as jnp
from jax import lax
from jax.experimental import pallas as pl
from jax.experimental.pallas import tpu as pltpu
from jax.sharding import PartitionSpec as P

LATENT = 512
F32 = jnp.float32
BF16 = jnp.bfloat16
VMEM = pltpu.VMEM
MIB = 1024 * 1024


softmax_scale = 192.0 ** (-0.5)


def attend_rows(lengths_ref, queries_ref, cache_ref, out_ref):
    for r in range(queries_ref.shape[0]):
        queries = queries_ref[r].T
        cache = cache_ref[r]
        scores = jnp.dot(queries, cache, preferred_element_type=F32) * softmax_scale
        usable = lax.broadcasted_iota(jnp.int32, scores.shape, 1) < lengths_ref[r]
        scores = jnp.where(usable, scores, -1e30)
        weights = jnp.exp(scores - jnp.max(scores, axis=1, keepdims=True))
        weights = weights / jnp.sum(weights, axis=1, keepdims=True)
        out_ref[r] = lax.dot_general(
            weights.astype(BF16),
            cache[:LATENT],
            (((1,), (1,)), ((), ())),
            preferred_element_type=F32,
        ).astype(BF16)


def attend_cost(queries, latent_cache):
    rows, heads, width = queries.shape
    positions = latent_cache.shape[1]
    return pl.CostEstimate(
        flops=2 * rows * heads * positions * (width + LATENT),
        bytes_accessed=2 * rows * (positions * width + heads * (width + LATENT)),
        transcendentals=rows * heads * positions,
    )


def in_hbm(array):
    return pltpu.with_memory_space_constraint(array, pltpu.HBM)


def in_vmem(array):
    return pltpu.with_memory_space_constraint(array, VMEM)


def whole(space=VMEM):
    return pl.BlockSpec(memory_space=space)


def attend(queries, latent_cache, cache_lengths):
    rows, heads, _ = queries.shape
    return pl.pallas_call(
        attend_rows,
        in_specs=[whole(pltpu.SMEM), whole(), whole()],
        out_specs=whole(),
        out_shape=jax.ShapeDtypeStruct((rows, heads, LATENT), BF16),
        compiler_params=pltpu.CompilerParams(vmem_limit_bytes=16 * MIB),
        cost_estimate=attend_cost(queries, latent_cache),
    )(cache_lengths, jnp.swapaxes(queries, 1, 2), jnp.swapaxes(latent_cache, 1, 2))


def attend_and_fetch_kernel(
    lengths_ref, queries_ref, cache_ref, source_ref, after_ref, out_ref, held_ref, sem
):
    copy = pltpu.make_async_copy(source_ref, held_ref, sem)
    copy.start()
    attend_rows(lengths_ref, queries_ref, cache_ref, out_ref)
    copy.wait()


def attend_and_fetch(queries, latent_cache, cache_lengths, weights, after):
    rows, heads, _ = queries.shape
    return pl.pallas_call(
        attend_and_fetch_kernel,
        in_specs=[whole(pltpu.SMEM), whole(), whole(), whole(pltpu.HBM), whole(pl.ANY)],
        out_specs=[whole(), whole()],
        out_shape=[
            jax.ShapeDtypeStruct((rows, heads, LATENT), BF16),
            VMEM(weights.shape, weights.dtype),
        ],
        scratch_shapes=[pltpu.SemaphoreType.DMA],
        compiler_params=pltpu.CompilerParams(vmem_limit_bytes=12 * MIB),
        cost_estimate=attend_cost(queries, latent_cache),
    )(
        cache_lengths,
        jnp.swapaxes(queries, 1, 2),
        jnp.swapaxes(latent_cache, 1, 2),
        in_hbm(weights),
        after,
    )


def once_done(value, other):
    return pl.pallas_call(
        lambda *refs: None,
        in_specs=[whole(pl.ANY)] * 2,
        out_specs=whole(pl.ANY),
        out_shape=VMEM(value.shape, value.dtype),
        input_output_aliases={0: 0},
        compiler_params=pltpu.CompilerParams(vmem_limit_bytes=MIB),
        cost_estimate=pl.CostEstimate(flops=0, bytes_accessed=0, transcendentals=0),
    )(value, other)


def fetch_kernel(source_ref, *refs):
    count = len(refs) - 3
    piece_refs, (held_ref, stack_ref, sems) = refs[:count], refs[count:]
    copies = [
        pltpu.make_async_copy(source_ref.at[e], held_ref.at[e], sems.at[e])
        for e in range(source_ref.shape[0])
    ]
    for copy in copies:
        copy.start()
    for k, piece_ref in enumerate(piece_refs):
        stack_ref[k] = piece_ref[...]
    for copy in copies:
        copy.wait()


def fetch(weights, pieces):
    return pl.pallas_call(
        fetch_kernel,
        in_specs=[whole(pltpu.HBM)] + [whole()] * len(pieces),
        out_specs=[whole(), whole()],
        out_shape=[
            VMEM(weights.shape, weights.dtype),
            VMEM((len(pieces),) + pieces[0].shape, pieces[0].dtype),
        ],
        scratch_shapes=[pltpu.SemaphoreType.DMA((weights.shape[0],))],
        compiler_params=pltpu.CompilerParams(vmem_limit_bytes=2 * MIB),
        cost_estimate=pl.CostEstimate(
            flops=0, bytes_accessed=2 * weights.size, transcendentals=0
        ),
    )(in_hbm(weights), *pieces)


def gate_table(expert_ids, gate_values, experts_all):
    chosen = expert_ids[:, :, None] == jnp.arange(experts_all, dtype=jnp.int32)[None, None, :]
    return jnp.sum(jnp.where(chosen, gate_values[:, :, None], 0.0), axis=1)


def pack_kernel(experts_all, rows_in, ids_in, gates_in, out_ref, ids_ref, gates_ref, sems):
    rows, feature_count = rows_in.shape
    copies = [
        pltpu.make_async_copy(ids_in, ids_ref, sems.at[0]),
        pltpu.make_async_copy(gates_in, gates_ref, sems.at[1]),
        pltpu.make_async_copy(rows_in, out_ref.at[:, :feature_count], sems.at[2]),
    ]
    for copy in copies:
        copy.start()
    copies[0].wait()
    copies[1].wait()
    lane = lax.broadcasted_iota(jnp.int32, (rows, out_ref.shape[1] - feature_count), 1)
    expert = lax.rem(lane, experts_all)
    table = jnp.zeros(lane.shape, F32)
    for k in range(ids_ref.shape[1]):
        table += jnp.where(ids_ref[:, k : k + 1] == expert, gates_ref[:, k : k + 1], 0.0)
    high = table.astype(BF16).astype(F32)
    middle = (table - high).astype(BF16).astype(F32)
    low = table - high - middle
    coded = jnp.where(
        lane < experts_all,
        high,
        jnp.where(
            lane < 2 * experts_all, middle, jnp.where(lane < 3 * experts_all, low, 0.0)
        ),
    )
    out_ref[:, feature_count:] = coded.astype(BF16)
    copies[2].wait()


def pack(hidden_rows, expert_ids, gate_values, experts_all):
    rows, feature_count = hidden_rows.shape
    return pl.pallas_call(
        lambda *refs: pack_kernel(experts_all, *refs),
        in_specs=[whole(pltpu.HBM)] * 3,
        out_specs=whole(),
        out_shape=VMEM((rows, feature_count + 128), BF16),
        scratch_shapes=[
            VMEM(expert_ids.shape, jnp.int32),
            VMEM(gate_values.shape, F32),
            pltpu.SemaphoreType.DMA((3,)),
        ],
        compiler_params=pltpu.CompilerParams(vmem_limit_bytes=2 * MIB),
        cost_estimate=pl.CostEstimate(
            flops=0, bytes_accessed=4 * rows * feature_count, transcendentals=0
        ),
    )(in_hbm(hidden_rows), in_hbm(expert_ids), in_hbm(gate_values))


def gate_up_kernel(
    slots,
    experts_all,
    mine_z_ref,
    mine_x_ref,
    other_z_ref,
    other_x_ref,
    gate_ref,
    up_ref,
    hidden_ref,
    table_ref,
    slot_ref,
    rows_ref,
    coded_ref,
):
    layer = lax.axis_index("expert")
    member = lax.axis_index("dp")
    x_side, core = jnp.right_shift(member, 1), jnp.bitwise_and(member, 1)
    layers, rows_dev, _ = mine_z_ref.shape
    experts, feature_count, _ = gate_ref.shape
    count = rows_ref.shape[0]
    first = core == 0
    for z in range(layers):
        for x, (mine_ref, other_ref) in enumerate(
            ((mine_z_ref, other_z_ref), (mine_x_ref, other_x_ref))
        ):
            at = (2 * z + x) * 2 * rows_dev
            mine, other = mine_ref[z], other_ref[z]
            pair = jnp.concatenate(
                [jnp.where(first, mine, other), jnp.where(first, other, mine)], axis=0
            )
            rows_ref[at : at + 2 * rows_dev] = pair[:, :feature_count]
            coded_ref[at : at + 2 * rows_dev] = pair[:, feature_count:]
    lanes = coded_ref.shape[1]
    source = lax.broadcasted_iota(jnp.int32, (lanes, lanes), 0)
    target = lax.broadcasted_iota(jnp.int32, (lanes, lanes), 1)
    selector = (
        (lax.rem(source, experts_all) == layer * experts + target)
        & (target < experts)
        & (source < 3 * experts_all)
    )
    table = jnp.dot(
        coded_ref[...], selector.astype(F32).astype(BF16), preferred_element_type=F32
    )
    table_ref[...] = table
    chosen = (table > 0.0).astype(F32).astype(BF16)
    row = lax.broadcasted_iota(jnp.int32, (count, count), 0)
    column = lax.broadcasted_iota(jnp.int32, (count, count), 1)
    turn = x_side * (2 * rows_dev)
    ahead = jnp.bitwise_xor(column, turn) < jnp.bitwise_xor(row, turn)
    rank = jnp.dot(ahead.astype(F32).astype(BF16), chosen, preferred_element_type=F32)
    rank = jnp.where(table > 0.0, rank, -1.0)
    slot = lax.broadcasted_iota(jnp.int32, (count, slot_ref.shape[2]), 1).astype(F32)
    rows = rows_ref[...]
    for e in range(experts):
        in_slot = (rank[:, e : e + 1] == slot).astype(F32).astype(BF16)
        slot_ref[e] = in_slot
        gate = jnp.dot(rows, gate_ref[e], preferred_element_type=F32)
        up = jnp.dot(rows, up_ref[e], preferred_element_type=F32)
        made = (gate / (1.0 + jnp.exp(-gate)) * up).astype(BF16)
        hidden_ref[e] = lax.dot_general(
            in_slot, made, (((0,), (0,)), ((), ())), preferred_element_type=F32
        )[:slots].astype(BF16)


def gate_up(pieces, gate_proj, up_proj, slots, experts_all):
    experts, depth, share = gate_proj.shape
    layers, rows_dev, total_width = pieces[0].shape
    count = 4 * layers * rows_dev
    extra = total_width - depth
    return pl.pallas_call(
        lambda *refs: gate_up_kernel(slots, experts_all, *refs),
        in_specs=[whole()] * 6,
        out_specs=[whole()] * 3,
        out_shape=[
            VMEM((experts, slots, share), BF16),
            VMEM((count, extra), F32),
            VMEM((experts, count, 128), BF16),
        ],
        scratch_shapes=[VMEM((count, depth), BF16), VMEM((count, extra), BF16)],
        compiler_params=pltpu.CompilerParams(vmem_limit_bytes=24 * MIB),
        cost_estimate=pl.CostEstimate(
            flops=4 * experts * count * depth * share,
            bytes_accessed=4 * experts * depth * share,
            transcendentals=experts * count * share,
        ),
    )(*pieces, in_vmem(gate_proj), in_vmem(up_proj))


def down_kernel(
    table_ref, slot_ref, h0_ref, h1_ref, h2_ref, h3_ref, down_ref, *out_refs
):
    place = lax.axis_index("dp")
    experts, slots, share = h0_ref.shape
    width = down_ref.shape[2]
    count = table_ref.shape[0]
    tile = 256
    rows_z = out_refs[0].shape[0]
    for start in range(0, width, tile):
        total = jnp.zeros((count, tile), F32)
        for e in range(experts):
            made = jnp.zeros((slots, tile), F32)
            for k, ref in enumerate((h0_ref, h1_ref, h2_ref, h3_ref)):
                owner = jnp.bitwise_xor(place, k)
                weights = down_ref[
                    e, pl.ds(pl.multiple_of(owner * share, share), share), start : start + tile
                ]
                made += jnp.dot(ref[e], weights, preferred_element_type=F32)
            spread = jnp.dot(
                slot_ref[e][:, :slots], made.astype(BF16), preferred_element_type=F32
            )
            total += table_ref[:, e : e + 1] * spread
        done = total.astype(BF16)
        for k, ref in enumerate(out_refs):
            ref[:, start : start + tile] = done[k * rows_z : (k + 1) * rows_z]


def down(table, slot, hidden, down_proj):
    experts, depth, width = down_proj.shape
    rows = table.shape[0]
    return pl.pallas_call(
        down_kernel,
        in_specs=[whole()] * 7,
        out_specs=[whole()] * 4,
        out_shape=[VMEM((rows // 4, width), BF16)] * 4,
        compiler_params=pltpu.CompilerParams(vmem_limit_bytes=16 * MIB),
        cost_estimate=pl.CostEstimate(
            flops=2 * experts * rows * depth * width,
            bytes_accessed=2 * experts * depth * width,
            transcendentals=0,
        ),
    )(table, slot, *hidden, in_vmem(down_proj))


def swap(value, axis, bit):
    size = lax.axis_size(axis)
    return lax.ppermute(value, axis, [(i, i ^ bit) for i in range(size)])


def routed_four(
    hidden_rows,
    expert_ids,
    gate_values,
    gate_proj,
    up_proj,
    down_proj,
    queries,
    latent_cache,
    cache_lengths,
):
    rows_dev, feature_count = hidden_rows.shape
    local_experts = gate_proj.shape[0]
    width = down_proj.shape[2]
    experts_all = local_experts * 4
    capacity = max(2, 3 * rows_dev * expert_ids.shape[1] // (2 * experts_all))
    member = lax.axis_index("dp").astype(jnp.int32)
    core = jnp.bitwise_and(member, 1)
    x_side = jnp.right_shift(member, 1)

    sent = pack(hidden_rows, expert_ids, gate_values, experts_all)
    along_z = [sent] + [swap(sent, "expert", k) for k in (1, 2, 3)]
    along_x = [swap(sent, "dp", 2)]
    gate_held, passed = fetch(gate_proj, along_z[1:2])
    along_z[1] = passed[0]
    along_x += [swap(block, "dp", 2) for block in along_z[1:]]
    up_held, mine_z = fetch(up_proj, along_z)
    mine_x = jnp.stack(along_x)
    other_z = swap(mine_z, "dp", 1)
    other_x = swap(mine_x, "dp", 1)

    hidden, table, slot = gate_up(
        (mine_z, mine_x, other_z, other_x),
        gate_held,
        up_held,
        16 * capacity,
        experts_all,
    )
    hidden_x = swap(hidden, "dp", 2)
    hidden_c = swap(hidden, "dp", 1)
    attended, down_held = attend_and_fetch(
        queries, latent_cache, cache_lengths, down_proj, hidden
    )
    hidden_x = once_done(hidden_x, down_held)
    hidden_xc = swap(hidden_x, "dp", 1)
    partial = down(table, slot, (hidden, hidden_c, hidden_x, hidden_xc), down_held)
    arrived = [partial[0]] + [swap(partial[k], "expert", k) for k in (1, 2, 3)]
    summed = sum(block.astype(F32) for block in arrived).astype(BF16)
    summed = summed.reshape(2, 2, rows_dev, width)
    both = jnp.stack([summed[0], swap(summed[1], "dp", 2)])
    kept = jnp.where(core == 0, both[:, 0], both[:, 1])
    given = jnp.where(core == 0, both[:, 1], both[:, 0])
    taken = swap(given, "dp", 1)
    by_core = jnp.where(core == 0, jnp.stack([kept, taken], 1), jnp.stack([taken, kept], 1))
    by_place = jnp.where(x_side == 0, by_core, by_core[::-1]).reshape(4, rows_dev, width)
    blended = jnp.transpose(by_place, (1, 0, 2)).reshape(rows_dev, 4 * width)
    return blended, attended


def routed_any(hidden_rows, expert_ids, gate_values, gate_proj, up_proj, down_proj):
    rows_dev, feature_count = hidden_rows.shape
    local_experts = gate_proj.shape[0]
    width = down_proj.shape[2]
    owners = lax.axis_size("expert")
    members = lax.axis_size("dp")
    experts_all = local_experts * owners
    table = gate_table(expert_ids, gate_values, experts_all)
    rows = lax.all_gather(hidden_rows, ("expert", "dp"), axis=0, tiled=True)
    table = lax.all_gather(table, ("expert", "dp"), axis=0, tiled=True)
    table = lax.dynamic_slice_in_dim(
        table, lax.axis_index("expert") * local_experts, local_experts, axis=1
    )
    total = jnp.zeros((rows.shape[0], width), F32)
    for e in range(local_experts):
        gate = jnp.dot(rows, gate_proj[e], preferred_element_type=F32)
        up = jnp.dot(rows, up_proj[e], preferred_element_type=F32)
        share = (jax.nn.silu(gate) * up).astype(BF16)
        hidden = lax.all_gather(share, "dp", axis=1, tiled=True)
        made = jnp.dot(hidden, down_proj[e], preferred_element_type=F32).astype(BF16)
        total += table[:, e : e + 1] * made.astype(F32)
    partial = total.astype(BF16).reshape(owners, members, rows_dev, width)
    returned = lax.all_to_all(
        lax.all_to_all(partial, "expert", split_axis=0, concat_axis=0, tiled=True),
        "dp",
        split_axis=1,
        concat_axis=1,
        tiled=True,
    )
    blended = jnp.sum(returned.astype(F32), axis=0).astype(BF16)
    return jnp.transpose(blended, (1, 0, 2)).reshape(rows_dev, members * width)


def local(
    hidden_rows,
    expert_ids,
    gate_values,
    gate_proj,
    up_proj,
    down_proj,
    queries,
    latent_cache,
    cache_lengths,
):
    routing = (hidden_rows, expert_ids, gate_values, gate_proj, up_proj, down_proj)
    attention = (queries, latent_cache, cache_lengths)
    four = lax.axis_size("expert") == 4 and lax.axis_size("dp") == 4
    if four and hidden_rows.shape[0] == 8 and 12 * gate_proj.shape[0] <= 128:
        return routed_four(*routing, *attention)
    return routed_any(*routing), attend(*attention)


def solution(mesh):
    return jax.shard_map(
        local,
        mesh=mesh,
        in_specs=(
            P(("groups", "expert", "dp"), None),
            P(("groups", "expert", "dp"), None),
            P(("groups", "expert", "dp"), None),
            P("expert", None, "dp"),
            P("expert", None, "dp"),
            P("expert", None, "dp"),
            P(("groups", "expert", "dp"), None, None),
            P(("groups", "expert", "dp"), None, None),
            P(("groups", "expert", "dp")),
        ),
        out_specs=(P(("groups", "expert", "dp"), None), P(("groups", "expert", "dp"), None, None)),
        check_vma=False,
    )
```

time: 62.8 us -> 53.4 us (0.85)
  local copies, waits for them, and re-layouts: 11.7 us -> 0.02 us
  Pallas kernels: 8.46 us -> 20.1 us
  waiting for transfers between devices: 21.1 us -> 13.6 us
  other arithmetic: 2.04 us -> 0.76 us
    pallas_call x3 -> x7, Pallas kernels: 8.46 us -> 20.1 us  [the longest x2 7 us: fetch(): pl.pallas_call(fetch_kernel, in_specs=[whole(pltpu.HBM)] + [whole()] * le...]
    unnamed x16 -> x6, local copies, waits for them, and re-layouts: 9.43 us -> 0.01 us
    ppermute x17, waiting for transfers between devices: 21.1 us -> 13.6 us  [swap(): return lax.ppermute(value, axis, [(i, i ^ bit) for i in range(size)])]
    slice x2 -> x0, local copies, waits for them, and re-layouts: 1.2 us -> none  [the longest x1 1.11 us: routed_four(): rows = gathered[:, :feature_count]]
    concatenate x1 -> x0, local copies, waits for them, and re-layouts: 0.93 us -> none  [routed_four(): jnp.concatenate([hidden_rows] + parts + [jnp.zeros((rows_dev, pad), BF16)...]
    reduce_sum x1 -> x0, other arithmetic: 0.79 us -> none  [gate_table(): return jnp.sum(jnp.where(chosen, gate_values[:, :, None], 0.0), axis=1)]
  transfers between devices with their start and end apart: 17 -> 17, of which waited for: 10 -> 9; matrix products, arithmetic and copies ran while one was open for 2% -> 0% of each run, Pallas kernels for 4% -> 22%
where the time goes in v2:
time: 53.4 us; the launch traced here: 53.2 us
  Pallas kernels  20.1 us (38%)
  starting transfers between devices  17.9 us (34%)
  waiting for transfers between devices  13.6 us (25%)
  between operations  0.77 us (1%)
  other arithmetic  0.76 us (1%)
    ppermute x17, starting transfers between devices, swap(): return lax.ppermute(value, axis, [(i, i ^ bit) for i in range(size)])  17.9 us
    ppermute x17, waiting for transfers between devices, swap(): return lax.ppermute(value, axis, [(i, i ^ bit) for i in range(size)])  13.6 us
    pallas_call x2, Pallas kernels, fetch(): pl.pallas_call(fetch_kernel, in_specs=[whole(pltpu.HBM)] + [whole()] * le...  7 us
    pallas_call x1, Pallas kernels, attend_and_fetch(): pl.pallas_call(attend_and_fetch_kernel, in_specs=[whole(pltpu.SMEM), whol...  4.63 us
    pallas_call x1, Pallas kernels, down(): pl.pallas_call(down_kernel, in_specs=[whole()] * 7, out_specs=[whole()] *...  4.49 us
    pallas_call x1, Pallas kernels, gate_up(): pl.pallas_call(lambda *refs: gate_up_kernel(slots, experts_all, *refs), i...  3.09 us
  transfers between devices with their start and end apart: 17, of which 9 were waited for; matrix products, arithmetic and copies ran while one was open for 0% of the time, Pallas kernels for 22%

profile of v2, /device:TPU:0, one launch (start us, length us, event | category | flops | bytes accessed | tf_op | source)
XLA Modules:
  0.0 53.2 jit_solution(5862449364479454805)
XLA Ops:
  0.6 0.9 %shard_map.104.refs_0_ = bf16[8,4224]{1,0:T(8,128)(2,1)S(1)} custom-call(bf16[8,4096]{1,0:T(8,128)(2,1)} %refs_0_.1, s32[8,8]{1,0:T(8,128)} %refs_1_.1, f32[8,8]{1,0:T(8,128)} %refs_2_.1), custom_call_target="tpu_custom_call" | custom-call | bytes 131072 | tf_op jit(solution)/shard_map/pallas_call | solution.py:181
  1.5 3.1 %collective-permute-start = (bf16[8,4224]{1,0:T(8,128)(2,1)S(1)}, bf16[8,4224]{1,0:T(8,128)(2,1)S(1)}, u32[]{:S(2)}, u32[]{:S(2)}) collective-permute-start(bf16[8,4224]{1,0:T(8,128)(2,1)S(1)} %shard_map.104.refs_0_), channel_id=1, source_target_pairs={{0,4},{4,0},{8,12},{12,8},{1,5},{5,1},{9,13},{13,9},{2,6},{6,2},{1... | collective-permute-start | bytes 202760 | tf_op jit(solution)/shard_map/ppermute | solution.py:334
  4.6 2.6 %collective-permute-start.1 = (bf16[8,4224]{1,0:T(8,128)(2,1)S(1)}, bf16[8,4224]{1,0:T(8,128)(2,1)S(1)}, u32[]{:S(2)}, u32[]{:S(2)}) collective-permute-start(bf16[8,4224]{1,0:T(8,128)(2,1)S(1)} %shard_map.104.refs_0_), channel_id=1, source_target_pairs={{0,8},{4,12},{8,0},{12,4},{1,9},{5,13},{9,1},{13,5},{2,10},{6,14},... | collective-permute-start | bytes 202760 | tf_op jit(solution)/shard_map/ppermute | solution.py:334
  7.2 0.0 collective-permute-start.2
  7.2 1.7 %collective-permute-start.3 = (bf16[8,4224]{1,0:T(8,128)(2,1)S(1)}, bf16[8,4224]{1,0:T(8,128)(2,1)S(1)}, u32[]{:S(2)}, u32[]{:S(2)}) collective-permute-start(bf16[8,4224]{1,0:T(8,128)(2,1)S(1)} %shard_map.104.refs_0_), channel_id=1, source_target_pairs={{0,2},{1,3},{2,0},{3,1},{4,6},{5,7},{6,4},{7,5},{8,10},{9,11},{10,... | collective-permute-start | bytes 202760 | tf_op jit(solution)/shard_map/ppermute | solution.py:334
  8.9 0.0 collective-permute-done.refs_0_
  8.9 3.5 %shard_map.105 = (bf16[4,4096,256]{2,1,0:T(8,128)(2,1)S(1)}, bf16[1,8,4224]{2,1,0:T(8,128)(2,1)S(1)}) custom-call(bf16[4,4096,256]{2,1,0:T(8,128)(2,1)} %source_ref.3, bf16[8,4224]{1,0:T(8,128)(2,1)S(1)} %collective-permute-done.refs_0_), custom_call_target="tpu_custom_call" | custom-call | bytes 8388608 | tf_op jit(solution)/shard_map/pallas_call | solution.py:128
  12.4 0.4 collective-permute-start.4
  12.8 0.0 collective-permute-done.1.refs_2_
  12.8 1.7 %collective-permute-start.5 = (bf16[8,4224]{1,0:T(8,128)(2,1)S(1)}, bf16[8,4224]{1,0:T(8,128)(2,1)S(1)}, u32[]{:S(2)}, u32[]{:S(2)}) collective-permute-start(bf16[8,4224]{1,0:T(8,128)(2,1)S(1)} %collective-permute-done.1.refs_2_), channel_id=1, source_target_pairs={{0,2},{1,3},{2,0},{3,1},{4,6},{5,7},{6,4},{7,5},{8,10},{9,11},{10,... | collective-permute-start | bytes 202760 | tf_op jit(solution)/shard_map/ppermute | solution.py:334
  14.5 0.0 collective-permute-done.2.refs_3_
  14.5 0.4 collective-permute-start.6
  14.9 3.5 %shard_map.106 = (bf16[4,4096,256]{2,1,0:T(8,128)(2,1)S(1)}, bf16[4,8,4224]{2,1,0:T(8,128)(2,1)S(1)}) custom-call(bf16[4,4096,256]{2,1,0:T(8,128)(2,1)} %source_ref.4, bf16[8,4224]{1,0:T(8,128)(2,1)S(1)} %shard_map.104.refs_0_, bf16[8,4224]{1,0:T(8,128)(2,1)S(1)} %bitcast.31, bf16[8,4224]{1,0:T(8,128)(2,1)S(1)} %collective-permute-done.1.refs_2_, ...), custom_call_target="tpu_custom_call" | custom-call | bytes 8388608 | tf_op jit(solution)/shard_map/pallas_call | solution.py:128
  18.4 0.1 collective-permute-start.7
  18.5 0.0 collective-permute-done.3
  18.5 0.0 collective-permute-done.4
  18.5 0.0 collective-permute-done.5
  18.5 0.3 collective-permute-done.6
  18.9 0.2 collective-permute-start.8
  19.1 0.9 %collective-permute-done.7.refs_2_ = bf16[4,8,4224]{2,1,0:T(8,128)(2,1)S(1)} collective-permute-done((bf16[4,8,4224]{2,1,0:T(8,128)(2,1)S(1)}, bf16[4,8,4224]{2,1,0:T(8,128)(2,1)S(1)}, u32[]{:S(2)}, u32[]{:S(2)}) %collective-permute-start.7) | collective-permute-done | bytes 270368 | tf_op jit(solution)/shard_map/ppermute | solution.py:334
  20.0 0.5 collective-permute-done.8.refs_3_
  20.5 0.0 copy-start
  20.5 0.0 copy-start.1
  20.5 0.0 copy-start.2
  20.5 3.1 %shard_map.107 = (bf16[4,96,256]{2,1,0:T(8,128)(2,1)S(1)}, f32[128,128]{1,0:T(8,128)S(1)}, bf16[4,128,128]{2,1,0:T(8,128)(2,1)S(1)}) custom-call(bf16[4,8,4224]{2,1,0:T(8,128)(2,1)S(1)} %get-tuple-element.16.refs_0_, bf16[4,8,4224]{2,1,0:T(8,128)(2,1)S(1)} %pad_maximum_fusion.refs_1_, bf16[4,8,4224]{2,1,0:T(8,128)(2,1)S(1)} %collective-permute-done.7.refs_2_, ...), custom_call_target="tpu_custom_call" | custom-call | flops 2147483648 | bytes 16777216 | tf_op jit(solution)/shard_map/pallas_call | solution.py:268
  23.6 1.6 %collective-permute-start.10 = (bf16[4,96,256]{2,1,0:T(8,128)(2,1)S(1)}, bf16[4,96,256]{2,1,0:T(8,128)(2,1)S(1)}, u32[]{:S(2)}, u32[]{:S(2)}) collective-permute-start(bf16[4,96,256]{2,1,0:T(8,128)(2,1)S(1)} %get-tuple-element.21.after_ref.h0_ref), channel_id=1, source_target_pairs={{0,2},{1,3},{2,0},{3,1},{4,6},{5,7},{6,4},{7,5},{8,10},{9,11},{10,... | collective-permute-start | bytes 589832 | tf_op jit(solution)/shard_map/ppermute | solution.py:334
  25.2 0.0 collective-permute-start.9
  25.2 0.0 copy-done
  25.2 0.0 copy-done.1
  25.3 0.0 copy-done.2
  25.3 4.6 %shard_map.108 = (bf16[2,128,512]{2,1,0:T(8,128)(2,1)}, bf16[4,1024,1024]{2,1,0:T(8,128)(2,1)S(1)}) custom-call(s32[2]{0:T(128)S(1)} %copy-done.2, bf16[2,576,128]{2,1,0:T(8,128)(2,1)S(1)} %bitcast.29, bf16[2,576,512]{2,1,0:T(8,128)(2,1)S(1)} %bitcast.28, bf16[4,1024,1024]{2,1,0:T(8,128)(2,1)} %source_ref.5, ...), custom_call_target="tpu_custom_call" | custom-call | flops 285212672 | bytes 1736704 | tf_op jit(solution)/shard_map/pallas_call | solution.py:80
  29.9 0.7 %collective-permute-done.10.refs_0_ = bf16[4,96,256]{2,1,0:T(8,128)(2,1)S(1)} collective-permute-done((bf16[4,96,256]{2,1,0:T(8,128)(2,1)S(1)}, bf16[4,96,256]{2,1,0:T(8,128)(2,1)S(1)}, u32[]{:S(2)}, u32[]{:S(2)}) %collective-permute-start.10) | collective-permute-done | bytes 196640 | tf_op jit(solution)/shard_map/ppermute | solution.py:334
  30.6 0.0 collective-permute-start.11
  30.7 0.0 collective-permute-done.9.h1_ref
  30.7 1.4 %collective-permute-done.11.h3_ref = bf16[4,96,256]{2,1,0:T(8,128)(2,1)S(1)} collective-permute-done((bf16[4,96,256]{2,1,0:T(8,128)(2,1)S(1)}, bf16[4,96,256]{2,1,0:T(8,128)(2,1)S(1)}, u32[]{:S(2)}, u32[]{:S(2)}) %collective-permute-start.11) | collective-permute-done | bytes 196640 | tf_op jit(solution)/shard_map/ppermute | solution.py:334
  32.1 4.5 %shard_map.110 = (bf16[32,1024]{1,0:T(8,128)(2,1)S(1)}, bf16[32,1024]{1,0:T(8,128)(2,1)S(1)}, bf16[32,1024]{1,0:T(8,128)(2,1)S(1)}, bf16[32,1024]{1,0:T(8,128)(2,1)S(1)}) custom-call(f32[128,128]{1,0:T(8,128)S(1)} %get-tuple-element.19.table_ref, bf16[4,128,128]{2,1,0:T(8,128)(2,1)S(1)} %get-tuple-element.20.slot_ref, ...), custom_call_target="tpu_custom_call" | custom-call | flops 1073741824 | bytes 8388608 | tf_op jit(solution)/shard_map/pallas_call | solution.py:318
  36.6 1.2 %collective-permute-start.12 = (bf16[32,1024]{1,0:T(8,128)(2,1)S(1)}, bf16[32,1024]{1,0:T(8,128)(2,1)S(1)}, u32[]{:S(2)}, u32[]{:S(2)}) collective-permute-start(bf16[32,1024]{1,0:T(8,128)(2,1)S(1)} %get-tuple-element.24), channel_id=1, source_target_pairs={{0,4},{4,0},{8,12},{12,8},{1,5},{5,1},{9,13},{13,9},{2,6},{6,2},{1... | collective-permute-start | bytes 196616 | tf_op jit(solution)/shard_map/ppermute | solution.py:334
  37.8 3.2 %collective-permute-start.13 = (bf16[32,1024]{1,0:T(8,128)(2,1)S(1)}, bf16[32,1024]{1,0:T(8,128)(2,1)S(1)}, u32[]{:S(2)}, u32[]{:S(2)}) collective-permute-start(bf16[32,1024]{1,0:T(8,128)(2,1)S(1)} %get-tuple-element.25), channel_id=1, source_target_pairs={{0,8},{4,12},{8,0},{12,4},{1,9},{5,13},{9,1},{13,5},{2,10},{6,14},... | collective-permute-start | bytes 196616 | tf_op jit(solution)/shard_map/ppermute | solution.py:334
  41.0 0.0 collective-permute-start.14
  41.0 0.0 collective-permute-done.12
  41.0 4.0 %collective-permute-done.13 = bf16[32,1024]{1,0:T(8,128)(2,1)S(1)} collective-permute-done((bf16[32,1024]{1,0:T(8,128)(2,1)S(1)}, bf16[32,1024]{1,0:T(8,128)(2,1)S(1)}, u32[]{:S(2)}, u32[]{:S(2)}) %collective-permute-start.13) | collective-permute-done | bytes 65568 | tf_op jit(solution)/shard_map/ppermute | solution.py:334
  45.1 2.1 %collective-permute-done.14 = bf16[32,1024]{1,0:T(8,128)(2,1)S(1)} collective-permute-done((bf16[32,1024]{1,0:T(8,128)(2,1)S(1)}, bf16[32,1024]{1,0:T(8,128)(2,1)S(1)}, u32[]{:S(2)}, u32[]{:S(2)}) %collective-permute-start.14) | collective-permute-done | bytes 65568 | tf_op jit(solution)/shard_map/ppermute | solution.py:334
  47.2 1.5 %collective-permute-start.15 = (bf16[2,8,1024]{2,1,0:T(8,128)(2,1)S(1)}, bf16[2,8,1024]{2,1,0:T(8,128)(2,1)S(1)}, u32[]{:S(2)}, u32[]{:S(2)}) collective-permute-start(bf16[2,8,1024]{2,1,0:T(8,128)(2,1)S(1)} %get-tuple-element.29), channel_id=1, source_target_pairs={{0,2},{1,3},{2,0},{3,1},{4,6},{5,7},{6,4},{7,5},{8,10},{9,11},{10,... | collective-permute-start | bytes 98312 | tf_op jit(solution)/shard_map/ppermute | solution.py:334
  48.8 2.4 %collective-permute-done.15 = bf16[2,8,1024]{2,1,0:T(8,128)(2,1)S(1)} collective-permute-done((bf16[2,8,1024]{2,1,0:T(8,128)(2,1)S(1)}, bf16[2,8,1024]{2,1,0:T(8,128)(2,1)S(1)}, u32[]{:S(2)}, u32[]{:S(2)}) %collective-permute-start.15) | collective-permute-done | bytes 32800 | tf_op jit(solution)/shard_map/ppermute | solution.py:334
  51.2 0.1 collective-permute-start.16
  51.3 1.2 %collective-permute-done.16 = bf16[2,8,1024]{2,1,0:T(8,128)(2,1)S(1)} collective-permute-done((bf16[2,8,1024]{2,1,0:T(8,128)(2,1)S(1)}, bf16[2,8,1024]{2,1,0:T(8,128)(2,1)S(1)}, u32[]{:S(2)}, u32[]{:S(2)}) %collective-permute-start.16) | collective-permute-done | bytes 32800 | tf_op jit(solution)/shard_map/ppermute | solution.py:334
  52.5 0.6 %reverse_select_fusion = bf16[2,2,8,1024]{3,2,1,0:T(8,128)(2,1)} fusion(bf16[2,2,8,1024]{3,2,1,0:T(8,128)(2,1)S(1)} %maximum_select_fusion, pred[]{:T(512)S(6)} %eq.8), kind=kLoop, calls=%fused_computation.2 | loop fusion | flops 32768 | bytes 131073 | tf_op jit(solution)/shard_map/jit(_where)/select_n | solution.py:391
  (7 shorter events, 0.1 us)
Async XLA Ops:
  1.5 7.4 %collective-permute-start = (bf16[8,4224]{1,0:T(8,128)(2,1)S(1)}, bf16[8,4224]{1,0:T(8,128)(2,1)S(1)}, u32[]{:S(2)}, u32[]{:S(2)}) collective-permute-start(bf16[8,4224]{1,0:T(8,128)(2,1)S(1)} %shard_map.104.refs_0_), channel_id=1, source_target_pairs={{0,4},{4,0},{8,12},{12,8},{1,5},{5,1},{9,13},{13,9},{2,6},{6,2},{1... | collective-permute-start | bytes 202760 | tf_op jit(solution)/shard_map/ppermute | solution.py:334
  4.6 8.2 %collective-permute-start.1 = (bf16[8,4224]{1,0:T(8,128)(2,1)S(1)}, bf16[8,4224]{1,0:T(8,128)(2,1)S(1)}, u32[]{:S(2)}, u32[]{:S(2)}) collective-permute-start(bf16[8,4224]{1,0:T(8,128)(2,1)S(1)} %shard_map.104.refs_0_), channel_id=1, source_target_pairs={{0,8},{4,12},{8,0},{12,4},{1,9},{5,13},{9,1},{13,5},{2,10},{6,14},... | collective-permute-start | bytes 202760 | tf_op jit(solution)/shard_map/ppermute | solution.py:334
  7.2 7.3 %collective-permute-start.2 = (bf16[8,4224]{1,0:T(8,128)(2,1)S(1)}, bf16[8,4224]{1,0:T(8,128)(2,1)S(1)}, u32[]{:S(2)}, u32[]{:S(2)}) collective-permute-start(bf16[8,4224]{1,0:T(8,128)(2,1)S(1)} %shard_map.104.refs_0_), channel_id=1, source_target_pairs={{0,12},{4,8},{8,4},{12,0},{1,13},{5,9},{9,5},{13,1},{2,14},{6,10},... | collective-permute-start | bytes 202760 | tf_op jit(solution)/shard_map/ppermute | solution.py:334
  7.2 11.3 %collective-permute-start.3 = (bf16[8,4224]{1,0:T(8,128)(2,1)S(1)}, bf16[8,4224]{1,0:T(8,128)(2,1)S(1)}, u32[]{:S(2)}, u32[]{:S(2)}) collective-permute-start(bf16[8,4224]{1,0:T(8,128)(2,1)S(1)} %shard_map.104.refs_0_), channel_id=1, source_target_pairs={{0,2},{1,3},{2,0},{3,1},{4,6},{5,7},{6,4},{7,5},{8,10},{9,11},{10,... | collective-permute-start | bytes 202760 | tf_op jit(solution)/shard_map/ppermute | solution.py:334
  12.4 6.1 %collective-permute-start.4 = (bf16[8,4224]{1,0:T(8,128)(2,1)S(1)}, bf16[8,4224]{1,0:T(8,128)(2,1)S(1)}, u32[]{:S(2)}, u32[]{:S(2)}) collective-permute-start(bf16[8,4224]{1,0:T(8,128)(2,1)S(1)} %bitcast.30), channel_id=1, source_target_pairs={{0,2},{1,3},{2,0},{3,1},{4,6},{5,7},{6,4},{7,5},{8,10},{9,11},{10,... | collective-permute-start | bytes 202760 | tf_op jit(solution)/shard_map/ppermute | solution.py:334
  12.8 5.7 %collective-permute-start.5 = (bf16[8,4224]{1,0:T(8,128)(2,1)S(1)}, bf16[8,4224]{1,0:T(8,128)(2,1)S(1)}, u32[]{:S(2)}, u32[]{:S(2)}) collective-permute-start(bf16[8,4224]{1,0:T(8,128)(2,1)S(1)} %collective-permute-done.1.refs_2_), channel_id=1, source_target_pairs={{0,2},{1,3},{2,0},{3,1},{4,6},{5,7},{6,4},{7,5},{8,10},{9,11},{10,... | collective-permute-start | bytes 202760 | tf_op jit(solution)/shard_map/ppermute | solution.py:334
  14.5 4.3 %collective-permute-start.6 = (bf16[8,4224]{1,0:T(8,128)(2,1)S(1)}, bf16[8,4224]{1,0:T(8,128)(2,1)S(1)}, u32[]{:S(2)}, u32[]{:S(2)}) collective-permute-start(bf16[8,4224]{1,0:T(8,128)(2,1)S(1)} %collective-permute-done.2.refs_3_), channel_id=1, source_target_pairs={{0,2},{1,3},{2,0},{3,1},{4,6},{5,7},{6,4},{7,5},{8,10},{9,11},{10,... | collective-permute-start | bytes 202760 | tf_op jit(solution)/shard_map/ppermute | solution.py:334
  18.4 1.6 %collective-permute-start.7 = (bf16[4,8,4224]{2,1,0:T(8,128)(2,1)S(1)}, bf16[4,8,4224]{2,1,0:T(8,128)(2,1)S(1)}, u32[]{:S(2)}, u32[]{:S(2)}) collective-permute-start(bf16[4,8,4224]{2,1,0:T(8,128)(2,1)S(1)} %get-tuple-element.16.refs_0_), channel_id=1, source_target_pairs={{0,1},{1,0},{2,3},{3,2},{4,5},{5,4},{6,7},{7,6},{8,9},{9,8},{10,11... | collective-permute-start | bytes 811016 | tf_op jit(solution)/shard_map/ppermute | solution.py:334
  18.9 1.6 %collective-permute-start.8 = (bf16[4,8,4224]{2,1,0:T(8,128)(2,1)S(1)}, bf16[4,8,4224]{2,1,0:T(8,128)(2,1)S(1)}, u32[]{:S(2)}, u32[]{:S(2)}) collective-permute-start(bf16[4,8,4224]{2,1,0:T(8,128)(2,1)S(1)} %pad_maximum_fusion.refs_1_), channel_id=1, source_target_pairs={{0,1},{1,0},{2,3},{3,2},{4,5},{5,4},{6,7},{7,6},{8,9},{9,8},{10,11... | collective-permute-start | bytes 811016 | tf_op jit(solution)/shard_map/ppermute | solution.py:334
  20.5 4.8 %copy-start = (bf16[2,512,576]{1,2,0:T(8,128)(2,1)S(1)}, bf16[2,512,576]{1,2,0:T(8,128)(2,1)}, u32[]{:S(2)}) copy-start(bf16[2,512,576]{1,2,0:T(8,128)(2,1)} %param.16) | copy-start | bytes 3538948
  20.5 4.8 %copy-start.1 = (bf16[2,128,576]{1,2,0:T(8,128)(2,1)S(1)}, bf16[2,128,576]{1,2,0:T(8,128)(2,1)}, u32[]{:S(2)}) copy-start(bf16[2,128,576]{1,2,0:T(8,128)(2,1)} %param.15) | copy-start | bytes 884740
  20.5 4.8 %copy-start.2 = (s32[2]{0:T(128)S(1)}, s32[2]{0:T(128)}, u32[]{:S(2)}) copy-start(s32[2]{0:T(128)} %lengths_ref.1) | copy-start | bytes 28
  23.6 7.1 %collective-permute-start.10 = (bf16[4,96,256]{2,1,0:T(8,128)(2,1)S(1)}, bf16[4,96,256]{2,1,0:T(8,128)(2,1)S(1)}, u32[]{:S(2)}, u32[]{:S(2)}) collective-permute-start(bf16[4,96,256]{2,1,0:T(8,128)(2,1)S(1)} %get-tuple-element.21.after_ref.h0_ref), channel_id=1, source_target_pairs={{0,2},{1,3},{2,0},{3,1},{4,6},{5,7},{6,4},{7,5},{8,10},{9,11},{10,... | collective-permute-start | bytes 589832 | tf_op jit(solution)/shard_map/ppermute | solution.py:334
  25.2 5.4 %collective-permute-start.9 = (bf16[4,96,256]{2,1,0:T(8,128)(2,1)S(1)}, bf16[4,96,256]{2,1,0:T(8,128)(2,1)S(1)}, u32[]{:S(2)}, u32[]{:S(2)}) collective-permute-start(bf16[4,96,256]{2,1,0:T(8,128)(2,1)S(1)} %get-tuple-element.21.after_ref.h0_ref), channel_id=1, source_target_pairs={{0,1},{1,0},{2,3},{3,2},{4,5},{5,4},{6,7},{7,6},{8,9},{9,8},{10,11... | collective-permute-start | bytes 589832 | tf_op jit(solution)/shard_map/ppermute | solution.py:334
  30.6 1.4 %collective-permute-start.11 = (bf16[4,96,256]{2,1,0:T(8,128)(2,1)S(1)}, bf16[4,96,256]{2,1,0:T(8,128)(2,1)S(1)}, u32[]{:S(2)}, u32[]{:S(2)}) collective-permute-start(bf16[4,96,256]{2,1,0:T(8,128)(2,1)S(1)} %shard_map.109.h2_ref), channel_id=1, source_target_pairs={{0,1},{1,0},{2,3},{3,2},{4,5},{5,4},{6,7},{7,6},{8,9},{9,8},{10,11... | collective-permute-start | bytes 589832 | tf_op jit(solution)/shard_map/ppermute | solution.py:334
  36.6 4.5 %collective-permute-start.12 = (bf16[32,1024]{1,0:T(8,128)(2,1)S(1)}, bf16[32,1024]{1,0:T(8,128)(2,1)S(1)}, u32[]{:S(2)}, u32[]{:S(2)}) collective-permute-start(bf16[32,1024]{1,0:T(8,128)(2,1)S(1)} %get-tuple-element.24), channel_id=1, source_target_pairs={{0,4},{4,0},{8,12},{12,8},{1,5},{5,1},{9,13},{13,9},{2,6},{6,2},{1... | collective-permute-start | bytes 196616 | tf_op jit(solution)/shard_map/ppermute | solution.py:334
  37.8 7.3 %collective-permute-start.13 = (bf16[32,1024]{1,0:T(8,128)(2,1)S(1)}, bf16[32,1024]{1,0:T(8,128)(2,1)S(1)}, u32[]{:S(2)}, u32[]{:S(2)}) collective-permute-start(bf16[32,1024]{1,0:T(8,128)(2,1)S(1)} %get-tuple-element.25), channel_id=1, source_target_pairs={{0,8},{4,12},{8,0},{12,4},{1,9},{5,13},{9,1},{13,5},{2,10},{6,14},... | collective-permute-start | bytes 196616 | tf_op jit(solution)/shard_map/ppermute | solution.py:334
  41.0 6.2 %collective-permute-start.14 = (bf16[32,1024]{1,0:T(8,128)(2,1)S(1)}, bf16[32,1024]{1,0:T(8,128)(2,1)S(1)}, u32[]{:S(2)}, u32[]{:S(2)}) collective-permute-start(bf16[32,1024]{1,0:T(8,128)(2,1)S(1)} %get-tuple-element.26), channel_id=1, source_target_pairs={{0,12},{4,8},{8,4},{12,0},{1,13},{5,9},{9,5},{13,1},{2,14},{6,10},... | collective-permute-start | bytes 196616 | tf_op jit(solution)/shard_map/ppermute | solution.py:334
  47.2 4.0 %collective-permute-start.15 = (bf16[2,8,1024]{2,1,0:T(8,128)(2,1)S(1)}, bf16[2,8,1024]{2,1,0:T(8,128)(2,1)S(1)}, u32[]{:S(2)}, u32[]{:S(2)}) collective-permute-start(bf16[2,8,1024]{2,1,0:T(8,128)(2,1)S(1)} %get-tuple-element.29), channel_id=1, source_target_pairs={{0,2},{1,3},{2,0},{3,1},{4,6},{5,7},{6,4},{7,5},{8,10},{9,11},{10,... | collective-permute-start | bytes 98312 | tf_op jit(solution)/shard_map/ppermute | solution.py:334
  51.2 1.3 %collective-permute-start.16 = (bf16[2,8,1024]{2,1,0:T(8,128)(2,1)S(1)}, bf16[2,8,1024]{2,1,0:T(8,128)(2,1)S(1)}, u32[]{:S(2)}, u32[]{:S(2)}) collective-permute-start(bf16[2,8,1024]{2,1,0:T(8,128)(2,1)S(1)} %select_bitcast_fusion), channel_id=1, source_target_pairs={{0,1},{1,0},{2,3},{3,2},{4,5},{5,4},{6,7},{7,6},{8,9},{9,8},{10,11... | collective-permute-start | bytes 98312 | tf_op jit(solution)/shard_map/ppermute | solution.py:334

commit v3 on v2

--- a/solution.py
+++ b/solution.py
@@ -109,13 +109,14 @@
     )(value, other)
 
 
-def fetch_kernel(source_ref, *refs):
-    count = len(refs) - 3
-    piece_refs, (held_ref, stack_ref, sems) = refs[:count], refs[count:]
-    copies = [
-        pltpu.make_async_copy(source_ref.at[e], held_ref.at[e], sems.at[e])
-        for e in range(source_ref.shape[0])
-    ]
+def fetch_kernel(gate_ref, up_ref, *refs):
+    *piece_refs, gate_held_ref, up_held_ref, stack_ref, sems = refs
+    copies = []
+    for source_ref, held_ref in ((gate_ref, gate_held_ref), (up_ref, up_held_ref)):
+        for e in range(held_ref.shape[0]):
+            copies.append(
+                pltpu.make_async_copy(source_ref.at[e], held_ref.at[e], sems.at[len(copies)])
+            )
     for copy in copies:
         copy.start()
     for k, piece_ref in enumerate(piece_refs):
@@ -124,21 +125,21 @@
         copy.wait()
 
 
-def fetch(weights, pieces):
+def fetch(gate_proj, up_proj, count, pieces):
+    held = VMEM((count,) + gate_proj.shape[1:], gate_proj.dtype)
     return pl.pallas_call(
         fetch_kernel,
-        in_specs=[whole(pltpu.HBM)] + [whole()] * len(pieces),
-        out_specs=[whole(), whole()],
-        out_shape=[
-            VMEM(weights.shape, weights.dtype),
-            VMEM((len(pieces),) + pieces[0].shape, pieces[0].dtype),
-        ],
-        scratch_shapes=[pltpu.SemaphoreType.DMA((weights.shape[0],))],
+        in_specs=[whole(pltpu.HBM)] * 2 + [whole()] * len(pieces),
+        out_specs=[whole()] * 3,
+        out_shape=[held, held, VMEM((len(pieces),) + pieces[0].shape, pieces[0].dtype)],
+        scratch_shapes=[pltpu.SemaphoreType.DMA((2 * count,))],
         compiler_params=pltpu.CompilerParams(vmem_limit_bytes=2 * MIB),
         cost_estimate=pl.CostEstimate(
-            flops=0, bytes_accessed=2 * weights.size, transcendentals=0
-        ),
-    )(in_hbm(weights), *pieces)
+            flops=0,
+            bytes_accessed=4 * count * gate_proj[0].size,
+            transcendentals=0,
+        ),
+    )(in_hbm(gate_proj), in_hbm(up_proj), *pieces)
 
 
 def gate_table(expert_ids, gate_values, experts_all):
@@ -202,14 +203,32 @@
     mine_x_ref,
     other_z_ref,
     other_x_ref,
+    gate_held_ref,
+    up_held_ref,
     gate_ref,
     up_ref,
     hidden_ref,
-    table_ref,
-    slot_ref,
+    spread_ref,
     rows_ref,
     coded_ref,
+    gate_late_ref,
+    up_late_ref,
+    sems,
 ):
+    ready = gate_held_ref.shape[0]
+    late = gate_late_ref.shape[0]
+    copies = []
+    for e in range(late):
+        for m, (source_ref, late_ref) in enumerate(
+            ((gate_ref, gate_late_ref), (up_ref, up_late_ref))
+        ):
+            copies.append(
+                pltpu.make_async_copy(
+                    source_ref.at[ready + e], late_ref.at[e], sems.at[2 * e + m]
+                )
+            )
+    for copy in copies:
+        copy.start()
     layer = lax.axis_index("expert")
     member = lax.axis_index("dp")
     x_side, core = jnp.right_shift(member, 1), jnp.bitwise_and(member, 1)
@@ -239,7 +258,6 @@
     table = jnp.dot(
         coded_ref[...], selector.astype(F32).astype(BF16), preferred_element_type=F32
     )
-    table_ref[...] = table
     chosen = (table > 0.0).astype(F32).astype(BF16)
     row = lax.broadcasted_iota(jnp.int32, (count, count), 0)
     column = lax.broadcasted_iota(jnp.int32, (count, count), 1)
@@ -247,86 +265,152 @@
     ahead = jnp.bitwise_xor(column, turn) < jnp.bitwise_xor(row, turn)
     rank = jnp.dot(ahead.astype(F32).astype(BF16), chosen, preferred_element_type=F32)
     rank = jnp.where(table > 0.0, rank, -1.0)
-    slot = lax.broadcasted_iota(jnp.int32, (count, slot_ref.shape[2]), 1).astype(F32)
+    slot = lax.broadcasted_iota(jnp.int32, (count, count), 1).astype(F32)
     rows = rows_ref[...]
     for e in range(experts):
-        in_slot = (rank[:, e : e + 1] == slot).astype(F32).astype(BF16)
-        slot_ref[e] = in_slot
-        gate = jnp.dot(rows, gate_ref[e], preferred_element_type=F32)
-        up = jnp.dot(rows, up_ref[e], preferred_element_type=F32)
+        hit = rank[:, e : e + 1] == slot
+        in_slot = hit.astype(F32).astype(BF16)
+        value = jnp.where(hit, table[:, e : e + 1], 0.0)
+        high = value.astype(BF16)
+        spread_ref[:count, e * count : (e + 1) * count] = high
+        spread_ref[count:, e * count : (e + 1) * count] = (value - high.astype(F32)).astype(BF16)
+        if e < ready:
+            gate_matrix, up_matrix = gate_held_ref[e], up_held_ref[e]
+        else:
+            copies[2 * (e - ready)].wait()
+            copies[2 * (e - ready) + 1].wait()
+            gate_matrix, up_matrix = gate_late_ref[e - ready], up_late_ref[e - ready]
+        gate = jnp.dot(rows, gate_matrix, preferred_element_type=F32)
+        up = jnp.dot(rows, up_matrix, preferred_element_type=F32)
         made = (gate / (1.0 + jnp.exp(-gate)) * up).astype(BF16)
         hidden_ref[e] = lax.dot_general(
             in_slot, made, (((0,), (0,)), ((), ())), preferred_element_type=F32
         )[:slots].astype(BF16)
 
 
-def gate_up(pieces, gate_proj, up_proj, slots, experts_all):
+def gate_up(pieces, gate_held, up_held, gate_proj, up_proj, slots, experts_all):
     experts, depth, share = gate_proj.shape
     layers, rows_dev, total_width = pieces[0].shape
     count = 4 * layers * rows_dev
+    late = experts - gate_held.shape[0]
     extra = total_width - depth
     return pl.pallas_call(
         lambda *refs: gate_up_kernel(slots, experts_all, *refs),
-        in_specs=[whole()] * 6,
-        out_specs=[whole()] * 3,
+        in_specs=[whole()] * 6 + [whole(pltpu.HBM)] * 2,
+        out_specs=[whole()] * 2,
         out_shape=[
             VMEM((experts, slots, share), BF16),
-            VMEM((count, extra), F32),
-            VMEM((experts, count, 128), BF16),
+            VMEM((2 * count, experts * count), BF16),
         ],
-        scratch_shapes=[VMEM((count, depth), BF16), VMEM((count, extra), BF16)],
+        scratch_shapes=[
+            VMEM((count, depth), BF16),
+            VMEM((count, extra), BF16),
+            VMEM((late, depth, share), BF16),
+            VMEM((late, depth, share), BF16),
+            pltpu.SemaphoreType.DMA((2 * late,)),
+        ],
         compiler_params=pltpu.CompilerParams(vmem_limit_bytes=24 * MIB),
         cost_estimate=pl.CostEstimate(
             flops=4 * experts * count * depth * share,
             bytes_accessed=4 * experts * depth * share,
             transcendentals=experts * count * share,
         ),
-    )(*pieces, in_vmem(gate_proj), in_vmem(up_proj))
+    )(*pieces, gate_held, up_held, in_hbm(gate_proj), in_hbm(up_proj))
 
 
 def down_kernel(
-    table_ref, slot_ref, h0_ref, h1_ref, h2_ref, h3_ref, down_ref, *out_refs
+    spread_ref, h0_ref, h1_ref, h2_ref, h3_ref, down_ref, o0_ref, o1_ref, o2_ref, o3_ref, made_ref
 ):
     place = lax.axis_index("dp")
     experts, slots, share = h0_ref.shape
     width = down_ref.shape[2]
-    count = table_ref.shape[0]
+    count = spread_ref.shape[0] // 2
+    rows_z = o0_ref.shape[0]
     tile = 256
-    rows_z = out_refs[0].shape[0]
+    for e in range(experts):
+        if slots < count:
+            made_ref[e * count + slots : (e + 1) * count] = jnp.zeros(
+                (count - slots, width), BF16
+            )
+        made = jnp.zeros((slots, width), F32)
+        for k, ref in enumerate((h0_ref, h1_ref, h2_ref, h3_ref)):
+            owner = jnp.bitwise_xor(place, k)
+            weights = down_ref[e, pl.ds(pl.multiple_of(owner * share, share), share)]
+            made += jnp.dot(ref[e], weights, preferred_element_type=F32)
+        made_ref[e * count : e * count + slots] = made.astype(BF16)
+    spread = spread_ref[...]
     for start in range(0, width, tile):
-        total = jnp.zeros((count, tile), F32)
-        for e in range(experts):
-            made = jnp.zeros((slots, tile), F32)
-            for k, ref in enumerate((h0_ref, h1_ref, h2_ref, h3_ref)):
-                owner = jnp.bitwise_xor(place, k)
-                weights = down_ref[
-                    e, pl.ds(pl.multiple_of(owner * share, share), share), start : start + tile
-                ]
-                made += jnp.dot(ref[e], weights, preferred_element_type=F32)
-            spread = jnp.dot(
-                slot_ref[e][:, :slots], made.astype(BF16), preferred_element_type=F32
-            )
-            total += table_ref[:, e : e + 1] * spread
-        done = total.astype(BF16)
-        for k, ref in enumerate(out_refs):
+        both = jnp.dot(spread, made_ref[:, start : start + tile], preferred_element_type=F32)
+        done = (both[:count] + both[count:]).astype(BF16)
+        for k, ref in enumerate((o0_ref, o1_ref, o2_ref, o3_ref)):
             ref[:, start : start + tile] = done[k * rows_z : (k + 1) * rows_z]
 
 
-def down(table, slot, hidden, down_proj):
+def down(spread, hidden, down_proj):
     experts, depth, width = down_proj.shape
-    rows = table.shape[0]
+    count = spread.shape[0] // 2
     return pl.pallas_call(
         down_kernel,
-        in_specs=[whole()] * 7,
+        in_specs=[whole()] * 6,
+        out_specs=[whole()] * 4,
+        out_shape=[VMEM((count // 4, width), BF16)] * 4,
+        scratch_shapes=[VMEM((experts * count, width), BF16)],
+        compiler_params=pltpu.CompilerParams(vmem_limit_bytes=16 * MIB),
+        cost_estimate=pl.CostEstimate(
+            flops=2 * experts * count * depth * width,
+            bytes_accessed=2 * experts * depth * width,
+            transcendentals=0,
+        ),
+    )(spread, *hidden, in_vmem(down_proj))
+
+
+def collect_kernel(p0_ref, p1_ref, p2_ref, p3_ref, own_ref, core_ref, x_ref, far_ref):
+    total = p0_ref[...].astype(F32)
+    for ref in (p1_ref, p2_ref, p3_ref):
+        total += ref[...].astype(F32)
+    rows = own_ref.shape[0]
+    first = jnp.bitwise_and(lax.axis_index("dp"), 1) == 0
+    near = [total[k * rows : (k + 1) * rows] for k in range(4)]
+    own_ref[...] = jnp.where(first, near[0], near[1]).astype(BF16)
+    core_ref[...] = jnp.where(first, near[1], near[0]).astype(BF16)
+    x_ref[...] = jnp.where(first, near[2], near[3]).astype(BF16)
+    far_ref[...] = jnp.where(first, near[3], near[2]).astype(BF16)
+
+
+def collect(partials):
+    rows, width = partials[0].shape
+    return pl.pallas_call(
+        collect_kernel,
+        in_specs=[whole()] * 4,
         out_specs=[whole()] * 4,
         out_shape=[VMEM((rows // 4, width), BF16)] * 4,
-        compiler_params=pltpu.CompilerParams(vmem_limit_bytes=16 * MIB),
+        compiler_params=pltpu.CompilerParams(vmem_limit_bytes=2 * MIB),
         cost_estimate=pl.CostEstimate(
-            flops=2 * experts * rows * depth * width,
-            bytes_accessed=2 * experts * depth * width,
-            transcendentals=0,
-        ),
-    )(table, slot, *hidden, in_vmem(down_proj))
+            flops=4 * rows * width, bytes_accessed=8 * rows * width, transcendentals=0
+        ),
+    )(*partials)
+
+
+def place_kernel(p0_ref, p1_ref, p2_ref, p3_ref, out_ref):
+    place = lax.axis_index("dp")
+    width = p0_ref.shape[1]
+    for k, ref in enumerate((p0_ref, p1_ref, p2_ref, p3_ref)):
+        at = pl.multiple_of(jnp.bitwise_xor(place, k) * width, width)
+        out_ref[:, pl.ds(at, width)] = ref[...]
+
+
+def place_all(pieces):
+    rows, width = pieces[0].shape
+    return pl.pallas_call(
+        place_kernel,
+        in_specs=[whole()] * 4,
+        out_specs=whole(),
+        out_shape=jax.ShapeDtypeStruct((rows, 4 * width), BF16),
+        compiler_params=pltpu.CompilerParams(vmem_limit_bytes=2 * MIB),
+        cost_estimate=pl.CostEstimate(
+            flops=0, bytes_accessed=16 * rows * width, transcendentals=0
+        ),
+    )(*pieces)
 
 
 def swap(value, axis, bit):
@@ -350,25 +434,20 @@
     width = down_proj.shape[2]
     experts_all = local_experts * 4
     capacity = max(2, 3 * rows_dev * expert_ids.shape[1] // (2 * experts_all))
-    member = lax.axis_index("dp").astype(jnp.int32)
-    core = jnp.bitwise_and(member, 1)
-    x_side = jnp.right_shift(member, 1)
-
     sent = pack(hidden_rows, expert_ids, gate_values, experts_all)
     along_z = [sent] + [swap(sent, "expert", k) for k in (1, 2, 3)]
-    along_x = [swap(sent, "dp", 2)]
-    gate_held, passed = fetch(gate_proj, along_z[1:2])
-    along_z[1] = passed[0]
-    along_x += [swap(block, "dp", 2) for block in along_z[1:]]
-    up_held, mine_z = fetch(up_proj, along_z)
+    along_x = [swap(block, "dp", 2) for block in along_z]
+    gate_held, up_held, mine_z = fetch(gate_proj, up_proj, local_experts // 2, along_z)
     mine_x = jnp.stack(along_x)
     other_z = swap(mine_z, "dp", 1)
     other_x = swap(mine_x, "dp", 1)
 
-    hidden, table, slot = gate_up(
+    hidden, spread = gate_up(
         (mine_z, mine_x, other_z, other_x),
         gate_held,
         up_held,
+        gate_proj,
+        up_proj,
         16 * capacity,
         experts_all,
     )
@@ -379,17 +458,11 @@
     )
     hidden_x = once_done(hidden_x, down_held)
     hidden_xc = swap(hidden_x, "dp", 1)
-    partial = down(table, slot, (hidden, hidden_c, hidden_x, hidden_xc), down_held)
+    partial = down(spread, (hidden, hidden_c, hidden_x, hidden_xc), down_held)
     arrived = [partial[0]] + [swap(partial[k], "expert", k) for k in (1, 2, 3)]
-    summed = sum(block.astype(F32) for block in arrived).astype(BF16)
-    summed = summed.reshape(2, 2, rows_dev, width)
-    both = jnp.stack([summed[0], swap(summed[1], "dp", 2)])
-    kept = jnp.where(core == 0, both[:, 0], both[:, 1])
-    given = jnp.where(core == 0, both[:, 1], both[:, 0])
-    taken = swap(given, "dp", 1)
-    by_core = jnp.where(core == 0, jnp.stack([kept, taken], 1), jnp.stack([taken, kept], 1))
-    by_place = jnp.where(x_side == 0, by_core, by_core[::-1]).reshape(4, rows_dev, width)
-    blended = jnp.transpose(by_place, (1, 0, 2)).reshape(rows_dev, 4 * width)
+    own, to_core, to_x, to_far = collect(arrived)
+    far = swap(to_far, "dp", 3)
+    blended = place_all((own, swap(to_core, "dp", 1), swap(to_x, "dp", 2), far))
     return blended, attended
 
 

time: 53.4 us -> 51.3 us (0.961)
  Pallas kernels: 20.1 us -> 17.3 us
  starting transfers between devices: 17.9 us -> 19.7 us
  other arithmetic: 0.76 us -> 0.05 us
    pallas_call x3 -> x4, Pallas kernels: 11.5 us -> 5.97 us  [the longest x1 3.5 us: fetch(): pl.pallas_call(fetch_kernel, in_specs=[whole(pltpu.HBM)] * 2 + [whole()]...]
    pallas_call x1, Pallas kernels: 3.09 us -> 5.79 us  [gate_up(): pl.pallas_call(lambda *refs: gate_up_kernel(slots, experts_all, *refs), i...]
    ppermute x17 -> x18, starting transfers between devices: 17.9 us -> 19.7 us  [swap(): return lax.ppermute(value, axis, [(i, i ^ bit) for i in range(size)])]
    select_n x4 -> x0, other arithmetic: 0.67 us -> none  [the longest x1 0.65 us: routed_four(): jnp.where(x_side == 0, by_core, by_core[::-1]).reshape(4, rows_dev, width)]
    ppermute x17 -> x18, waiting for transfers between devices: 13.6 us -> 13.3 us  [swap(): return lax.ppermute(value, axis, [(i, i ^ bit) for i in range(size)])]
  transfers between devices with their start and end apart: 17 -> 18, of which waited for: 9 -> 11; matrix products, arithmetic and copies ran while one was open for 0% -> 0% of each run, Pallas kernels for 22% -> 16%
where the time goes in v3:
time: 51.3 us; the launch traced here: 51.1 us
  starting transfers between devices  19.7 us (38%)
  Pallas kernels  17.3 us (34%)
  waiting for transfers between devices  13.3 us (26%)
  between operations  0.75 us (1%)
    ppermute x18, starting transfers between devices, swap(): return lax.ppermute(value, axis, [(i, i ^ bit) for i in range(size)])  19.7 us
    ppermute x18, waiting for transfers between devices, swap(): return lax.ppermute(value, axis, [(i, i ^ bit) for i in range(size)])  13.3 us
    pallas_call x1, Pallas kernels, gate_up(): pl.pallas_call(lambda *refs: gate_up_kernel(slots, experts_all, *refs), i...  5.79 us
    pallas_call x1, Pallas kernels, attend_and_fetch(): pl.pallas_call(attend_and_fetch_kernel, in_specs=[whole(pltpu.SMEM), whol...  4.63 us
    pallas_call x1, Pallas kernels, fetch(): pl.pallas_call(fetch_kernel, in_specs=[whole(pltpu.HBM)] * 2 + [whole()]...  3.5 us
    pallas_call x1, Pallas kernels, down(): pl.pallas_call(down_kernel, in_specs=[whole()] * 6, out_specs=[whole()] *...  1.79 us
  transfers between devices with their start and end apart: 18, of which 11 were waited for; matrix products, arithmetic and copies ran while one was open for 0% of the time, Pallas kernels for 16%

profile of v3, /device:TPU:0, one launch (start us, length us, event | category | flops | bytes accessed | tf_op | source)
XLA Modules:
  0.0 51.1 jit_solution(1756691022685300645)
XLA Ops:
  0.6 0.9 %shard_map.104.refs_0_ = bf16[8,4224]{1,0:T(8,128)(2,1)S(1)} custom-call(bf16[8,4096]{1,0:T(8,128)(2,1)} %refs_0_.1, s32[8,8]{1,0:T(8,128)} %refs_1_.1, f32[8,8]{1,0:T(8,128)} %refs_2_.1), custom_call_target="tpu_custom_call" | custom-call | bytes 131072 | tf_op jit(solution)/shard_map/pallas_call | solution.py:182
  1.5 5.1 %collective-permute-start.2 = (bf16[8,4224]{1,0:T(8,128)(2,1)S(1)}, bf16[8,4224]{1,0:T(8,128)(2,1)S(1)}, u32[]{:S(2)}, u32[]{:S(2)}) collective-permute-start(bf16[8,4224]{1,0:T(8,128)(2,1)S(1)} %shard_map.104.refs_0_), channel_id=1, source_target_pairs={{0,12},{4,8},{8,4},{12,0},{1,13},{5,9},{9,5},{13,1},{2,14},{6,10},... | collective-permute-start | bytes 202760 | tf_op jit(solution)/shard_map/ppermute | solution.py:418
  6.7 0.0 collective-permute-start.1
  6.7 0.6 %collective-permute-start = (bf16[8,4224]{1,0:T(8,128)(2,1)S(1)}, bf16[8,4224]{1,0:T(8,128)(2,1)S(1)}, u32[]{:S(2)}, u32[]{:S(2)}) collective-permute-start(bf16[8,4224]{1,0:T(8,128)(2,1)S(1)} %shard_map.104.refs_0_), channel_id=1, source_target_pairs={{0,4},{4,0},{8,12},{12,8},{1,5},{5,1},{9,13},{13,9},{2,6},{6,2},{1... | collective-permute-start | bytes 202760 | tf_op jit(solution)/shard_map/ppermute | solution.py:418
  7.3 1.6 %collective-permute-start.3 = (bf16[8,4224]{1,0:T(8,128)(2,1)S(1)}, bf16[8,4224]{1,0:T(8,128)(2,1)S(1)}, u32[]{:S(2)}, u32[]{:S(2)}) collective-permute-start(bf16[8,4224]{1,0:T(8,128)(2,1)S(1)} %shard_map.104.refs_0_), channel_id=1, source_target_pairs={{0,2},{1,3},{2,0},{3,1},{4,6},{5,7},{6,4},{7,5},{8,10},{9,11},{10,... | collective-permute-start | bytes 202760 | tf_op jit(solution)/shard_map/ppermute | solution.py:418
  8.9 0.3 collective-permute-done.2.refs_3_
  9.3 1.9 %collective-permute-start.6 = (bf16[8,4224]{1,0:T(8,128)(2,1)S(1)}, bf16[8,4224]{1,0:T(8,128)(2,1)S(1)}, u32[]{:S(2)}, u32[]{:S(2)}) collective-permute-start(bf16[8,4224]{1,0:T(8,128)(2,1)S(1)} %collective-permute-done.2.refs_3_), channel_id=1, source_target_pairs={{0,2},{1,3},{2,0},{3,1},{4,6},{5,7},{6,4},{7,5},{8,10},{9,11},{10,... | collective-permute-start | bytes 202760 | tf_op jit(solution)/shard_map/ppermute | solution.py:418
  11.1 1.3 %collective-permute-done.1.refs_2_ = bf16[8,4224]{1,0:T(8,128)(2,1)S(1)} collective-permute-done((bf16[8,4224]{1,0:T(8,128)(2,1)S(1)}, bf16[8,4224]{1,0:T(8,128)(2,1)S(1)}, u32[]{:S(2)}, u32[]{:S(2)}) %collective-permute-start.1) | collective-permute-done | bytes 67616 | tf_op jit(solution)/shard_map/ppermute | solution.py:418
  12.4 1.5 %collective-permute-start.5 = (bf16[8,4224]{1,0:T(8,128)(2,1)S(1)}, bf16[8,4224]{1,0:T(8,128)(2,1)S(1)}, u32[]{:S(2)}, u32[]{:S(2)}) collective-permute-start(bf16[8,4224]{1,0:T(8,128)(2,1)S(1)} %collective-permute-done.1.refs_2_), channel_id=1, source_target_pairs={{0,2},{1,3},{2,0},{3,1},{4,6},{5,7},{6,4},{7,5},{8,10},{9,11},{10,... | collective-permute-start | bytes 202760 | tf_op jit(solution)/shard_map/ppermute | solution.py:418
  13.9 0.0 collective-permute-done.refs_1_
  13.9 0.5 %collective-permute-start.4 = (bf16[8,4224]{1,0:T(8,128)(2,1)S(1)}, bf16[8,4224]{1,0:T(8,128)(2,1)S(1)}, u32[]{:S(2)}, u32[]{:S(2)}) collective-permute-start(bf16[8,4224]{1,0:T(8,128)(2,1)S(1)} %collective-permute-done.refs_1_), channel_id=1, source_target_pairs={{0,2},{1,3},{2,0},{3,1},{4,6},{5,7},{6,4},{7,5},{8,10},{9,11},{10,... | collective-permute-start | bytes 202760 | tf_op jit(solution)/shard_map/ppermute | solution.py:418
  14.4 3.5 %shard_map.105 = (bf16[2,4096,256]{2,1,0:T(8,128)(2,1)S(1)}, bf16[2,4096,256]{2,1,0:T(8,128)(2,1)S(1)}, bf16[4,8,4224]{2,1,0:T(8,128)(2,1)S(1)}) custom-call(bf16[4,4096,256]{2,1,0:T(8,128)(2,1)} %refs_6_.1, bf16[4,4096,256]{2,1,0:T(8,128)(2,1)} %refs_7_.1, bf16[8,4224]{1,0:T(8,128)(2,1)S(1)} %shard_map.104.refs_0_, ...), custom_call_target="tpu_custom_call" | custom-call | bytes 8388608 | tf_op jit(solution)/shard_map/pallas_call | solution.py:130
  17.9 0.1 collective-permute-start.7
  18.0 0.0 collective-permute-done.3
  18.0 0.0 collective-permute-done.6
  18.0 0.0 collective-permute-done.5
  18.1 0.1 collective-permute-done.4
  18.2 0.4 collective-permute-start.8
  18.7 0.9 %collective-permute-done.7.refs_2_ = bf16[4,8,4224]{2,1,0:T(8,128)(2,1)S(1)} collective-permute-done((bf16[4,8,4224]{2,1,0:T(8,128)(2,1)S(1)}, bf16[4,8,4224]{2,1,0:T(8,128)(2,1)S(1)}, u32[]{:S(2)}, u32[]{:S(2)}) %collective-permute-start.7) | collective-permute-done | bytes 270368 | tf_op jit(solution)/shard_map/ppermute | solution.py:418
  19.6 0.4 collective-permute-done.8.refs_3_
  19.9 0.0 copy-start
  19.9 0.0 copy-start.1
  20.0 0.0 copy-start.2
  20.0 5.8 %shard_map.106 = (bf16[4,96,256]{2,1,0:T(8,128)(2,1)S(1)}, bf16[256,512]{1,0:T(8,128)(2,1)S(1)}) custom-call(bf16[4,8,4224]{2,1,0:T(8,128)(2,1)S(1)} %get-tuple-element.17.refs_0_, bf16[4,8,4224]{2,1,0:T(8,128)(2,1)S(1)} %pad_maximum_fusion.refs_1_, bf16[4,8,4224]{2,1,0:T(8,128)(2,1)S(1)} %collective-permute-done.7.refs_2_, ...), custom_call_target="tpu_custom_call" | custom-call | flops 2147483648 | bytes 16777216 | tf_op jit(solution)/shard_map/pallas_call | solution.py:297
  25.8 1.6 %collective-permute-start.10 = (bf16[4,96,256]{2,1,0:T(8,128)(2,1)S(1)}, bf16[4,96,256]{2,1,0:T(8,128)(2,1)S(1)}, u32[]{:S(2)}, u32[]{:S(2)}) collective-permute-start(bf16[4,96,256]{2,1,0:T(8,128)(2,1)S(1)} %get-tuple-element.21.after_ref.h0_ref), channel_id=1, source_target_pairs={{0,2},{1,3},{2,0},{3,1},{4,6},{5,7},{6,4},{7,5},{8,10},{9,11},{10,... | collective-permute-start | bytes 589832 | tf_op jit(solution)/shard_map/ppermute | solution.py:418
  27.3 0.0 collective-permute-start.9
  27.3 0.0 copy-done
  27.3 0.0 copy-done.1
  27.3 0.0 copy-done.2
  27.3 4.6 %shard_map.107 = (bf16[2,128,512]{2,1,0:T(8,128)(2,1)}, bf16[4,1024,1024]{2,1,0:T(8,128)(2,1)S(1)}) custom-call(s32[2]{0:T(128)S(1)} %copy-done.2, bf16[2,576,128]{2,1,0:T(8,128)(2,1)S(1)} %bitcast.7, bf16[2,576,512]{2,1,0:T(8,128)(2,1)S(1)} %bitcast.6, bf16[4,1024,1024]{2,1,0:T(8,128)(2,1)} %source_ref.1, ...), custom_call_target="tpu_custom_call" | custom-call | flops 285212672 | bytes 1736704 | tf_op jit(solution)/shard_map/pallas_call | solution.py:80
  32.0 0.9 %collective-permute-done.10.refs_0_ = bf16[4,96,256]{2,1,0:T(8,128)(2,1)S(1)} collective-permute-done((bf16[4,96,256]{2,1,0:T(8,128)(2,1)S(1)}, bf16[4,96,256]{2,1,0:T(8,128)(2,1)S(1)}, u32[]{:S(2)}, u32[]{:S(2)}) %collective-permute-start.10) | collective-permute-done | bytes 196640 | tf_op jit(solution)/shard_map/ppermute | solution.py:418
  32.9 0.0 collective-permute-start.11
  32.9 0.0 collective-permute-done.9.h1_ref
  32.9 1.4 %collective-permute-done.11.h3_ref = bf16[4,96,256]{2,1,0:T(8,128)(2,1)S(1)} collective-permute-done((bf16[4,96,256]{2,1,0:T(8,128)(2,1)S(1)}, bf16[4,96,256]{2,1,0:T(8,128)(2,1)S(1)}, u32[]{:S(2)}, u32[]{:S(2)}) %collective-permute-start.11) | collective-permute-done | bytes 196640 | tf_op jit(solution)/shard_map/ppermute | solution.py:418
  34.3 1.8 %shard_map.109 = (bf16[32,1024]{1,0:T(8,128)(2,1)S(1)}, bf16[32,1024]{1,0:T(8,128)(2,1)S(1)}, bf16[32,1024]{1,0:T(8,128)(2,1)S(1)}, bf16[32,1024]{1,0:T(8,128)(2,1)S(1)}) custom-call(bf16[256,512]{1,0:T(8,128)(2,1)S(1)} %get-tuple-element.20.spread_ref, bf16[4,96,256]{2,1,0:T(8,128)(2,1)S(1)} %get-tuple-element.21.after_ref.h0_ref, ...), custom_call_target="tpu_custom_call" | custom-call | flops 1073741824 | bytes 8388608 | tf_op jit(solution)/shard_map/pallas_call | solution.py:352
  36.1 0.9 %collective-permute-start.12 = (bf16[32,1024]{1,0:T(8,128)(2,1)S(1)}, bf16[32,1024]{1,0:T(8,128)(2,1)S(1)}, u32[]{:S(2)}, u32[]{:S(2)}) collective-permute-start(bf16[32,1024]{1,0:T(8,128)(2,1)S(1)} %get-tuple-element.24), channel_id=1, source_target_pairs={{0,4},{4,0},{8,12},{12,8},{1,5},{5,1},{9,13},{13,9},{2,6},{6,2},{1... | collective-permute-start | bytes 196616 | tf_op jit(solution)/shard_map/ppermute | solution.py:418
  37.1 2.4 %collective-permute-start.13 = (bf16[32,1024]{1,0:T(8,128)(2,1)S(1)}, bf16[32,1024]{1,0:T(8,128)(2,1)S(1)}, u32[]{:S(2)}, u32[]{:S(2)}) collective-permute-start(bf16[32,1024]{1,0:T(8,128)(2,1)S(1)} %get-tuple-element.25), channel_id=1, source_target_pairs={{0,8},{4,12},{8,0},{12,4},{1,9},{5,13},{9,1},{13,5},{2,10},{6,14},... | collective-permute-start | bytes 196616 | tf_op jit(solution)/shard_map/ppermute | solution.py:418
  39.5 1.1 %collective-permute-start.14 = (bf16[32,1024]{1,0:T(8,128)(2,1)S(1)}, bf16[32,1024]{1,0:T(8,128)(2,1)S(1)}, u32[]{:S(2)}, u32[]{:S(2)}) collective-permute-start(bf16[32,1024]{1,0:T(8,128)(2,1)S(1)} %get-tuple-element.26), channel_id=1, source_target_pairs={{0,12},{4,8},{8,4},{12,0},{1,13},{5,9},{9,5},{13,1},{2,14},{6,10},... | collective-permute-start | bytes 196616 | tf_op jit(solution)/shard_map/ppermute | solution.py:418
  40.6 0.0 collective-permute-done.12.p1_ref
  40.6 4.0 %collective-permute-done.13.p2_ref = bf16[32,1024]{1,0:T(8,128)(2,1)S(1)} collective-permute-done((bf16[32,1024]{1,0:T(8,128)(2,1)S(1)}, bf16[32,1024]{1,0:T(8,128)(2,1)S(1)}, u32[]{:S(2)}, u32[]{:S(2)}) %collective-permute-start.13) | collective-permute-done | bytes 65568 | tf_op jit(solution)/shard_map/ppermute | solution.py:418
  44.6 1.0 %collective-permute-done.14.p3_ref = bf16[32,1024]{1,0:T(8,128)(2,1)S(1)} collective-permute-done((bf16[32,1024]{1,0:T(8,128)(2,1)S(1)}, bf16[32,1024]{1,0:T(8,128)(2,1)S(1)}, u32[]{:S(2)}, u32[]{:S(2)}) %collective-permute-start.14) | collective-permute-done | bytes 65568 | tf_op jit(solution)/shard_map/ppermute | solution.py:418
  45.7 0.1 collective-permute-start.15
  45.8 1.6 %collective-permute-start.16 = (bf16[8,1024]{1,0:T(8,128)(2,1)S(1)}, bf16[8,1024]{1,0:T(8,128)(2,1)S(1)}, u32[]{:S(2)}, u32[]{:S(2)}) collective-permute-start(bf16[8,1024]{1,0:T(8,128)(2,1)S(1)} %get-tuple-element.29), channel_id=1, source_target_pairs={{0,2},{1,3},{2,0},{3,1},{4,6},{5,7},{6,4},{7,5},{8,10},{9,11},{10,... | collective-permute-start | bytes 49160 | tf_op jit(solution)/shard_map/ppermute | solution.py:418
  47.3 0.3 collective-permute-start.17
  47.6 0.0 collective-permute-done.15.p1_ref
  47.6 1.9 %collective-permute-done.16.p2_ref = bf16[8,1024]{1,0:T(8,128)(2,1)S(1)} collective-permute-done((bf16[8,1024]{1,0:T(8,128)(2,1)S(1)}, bf16[8,1024]{1,0:T(8,128)(2,1)S(1)}, u32[]{:S(2)}, u32[]{:S(2)}) %collective-permute-start.16) | collective-permute-done | bytes 16416 | tf_op jit(solution)/shard_map/ppermute | solution.py:418
  49.6 0.9 %collective-permute-done.17.p3_ref = bf16[8,1024]{1,0:T(8,128)(2,1)S(1)} collective-permute-done((bf16[8,1024]{1,0:T(8,128)(2,1)S(1)}, bf16[8,1024]{1,0:T(8,128)(2,1)S(1)}, u32[]{:S(2)}, u32[]{:S(2)}) %collective-permute-start.17) | collective-permute-done | bytes 16416 | tf_op jit(solution)/shard_map/ppermute | solution.py:418
  50.5 0.6 %shard_map.111 = bf16[8,4096]{1,0:T(8,128)(2,1)} custom-call(bf16[8,1024]{1,0:T(8,128)(2,1)S(1)} %get-tuple-element.27.p0_ref, bf16[8,1024]{1,0:T(8,128)(2,1)S(1)} %collective-permute-done.15.p1_ref, bf16[8,1024]{1,0:T(8,128)(2,1)S(1)} %collective-permute-done.16.p2_ref, bf16[8,1024]{1,0:T(8,128)(2,1)S(1)} %collective-permute-done.17.p3_ref), custom_call_target="tpu_custom_call" | custom-call | bytes 131072 | tf_op jit(solution)/shard_map/pallas_call | solution.py:404
  (3 shorter events, 0.1 us)
Async XLA Ops:
  1.5 7.7 %collective-permute-start.2 = (bf16[8,4224]{1,0:T(8,128)(2,1)S(1)}, bf16[8,4224]{1,0:T(8,128)(2,1)S(1)}, u32[]{:S(2)}, u32[]{:S(2)}) collective-permute-start(bf16[8,4224]{1,0:T(8,128)(2,1)S(1)} %shard_map.104.refs_0_), channel_id=1, source_target_pairs={{0,12},{4,8},{8,4},{12,0},{1,13},{5,9},{9,5},{13,1},{2,14},{6,10},... | collective-permute-start | bytes 202760 | tf_op jit(solution)/shard_map/ppermute | solution.py:418
  6.7 5.8 %collective-permute-start.1 = (bf16[8,4224]{1,0:T(8,128)(2,1)S(1)}, bf16[8,4224]{1,0:T(8,128)(2,1)S(1)}, u32[]{:S(2)}, u32[]{:S(2)}) collective-permute-start(bf16[8,4224]{1,0:T(8,128)(2,1)S(1)} %shard_map.104.refs_0_), channel_id=1, source_target_pairs={{0,8},{4,12},{8,0},{12,4},{1,9},{5,13},{9,1},{13,5},{2,10},{6,14},... | collective-permute-start | bytes 202760 | tf_op jit(solution)/shard_map/ppermute | solution.py:418
  6.7 7.2 %collective-permute-start = (bf16[8,4224]{1,0:T(8,128)(2,1)S(1)}, bf16[8,4224]{1,0:T(8,128)(2,1)S(1)}, u32[]{:S(2)}, u32[]{:S(2)}) collective-permute-start(bf16[8,4224]{1,0:T(8,128)(2,1)S(1)} %shard_map.104.refs_0_), channel_id=1, source_target_pairs={{0,4},{4,0},{8,12},{12,8},{1,5},{5,1},{9,13},{13,9},{2,6},{6,2},{1... | collective-permute-start | bytes 202760 | tf_op jit(solution)/shard_map/ppermute | solution.py:418
  7.3 10.7 %collective-permute-start.3 = (bf16[8,4224]{1,0:T(8,128)(2,1)S(1)}, bf16[8,4224]{1,0:T(8,128)(2,1)S(1)}, u32[]{:S(2)}, u32[]{:S(2)}) collective-permute-start(bf16[8,4224]{1,0:T(8,128)(2,1)S(1)} %shard_map.104.refs_0_), channel_id=1, source_target_pairs={{0,2},{1,3},{2,0},{3,1},{4,6},{5,7},{6,4},{7,5},{8,10},{9,11},{10,... | collective-permute-start | bytes 202760 | tf_op jit(solution)/shard_map/ppermute | solution.py:418
  9.3 8.8 %collective-permute-start.6 = (bf16[8,4224]{1,0:T(8,128)(2,1)S(1)}, bf16[8,4224]{1,0:T(8,128)(2,1)S(1)}, u32[]{:S(2)}, u32[]{:S(2)}) collective-permute-start(bf16[8,4224]{1,0:T(8,128)(2,1)S(1)} %collective-permute-done.2.refs_3_), channel_id=1, source_target_pairs={{0,2},{1,3},{2,0},{3,1},{4,6},{5,7},{6,4},{7,5},{8,10},{9,11},{10,... | collective-permute-start | bytes 202760 | tf_op jit(solution)/shard_map/ppermute | solution.py:418
  12.4 5.6 %collective-permute-start.5 = (bf16[8,4224]{1,0:T(8,128)(2,1)S(1)}, bf16[8,4224]{1,0:T(8,128)(2,1)S(1)}, u32[]{:S(2)}, u32[]{:S(2)}) collective-permute-start(bf16[8,4224]{1,0:T(8,128)(2,1)S(1)} %collective-permute-done.1.refs_2_), channel_id=1, source_target_pairs={{0,2},{1,3},{2,0},{3,1},{4,6},{5,7},{6,4},{7,5},{8,10},{9,11},{10,... | collective-permute-start | bytes 202760 | tf_op jit(solution)/shard_map/ppermute | solution.py:418
  13.9 4.3 %collective-permute-start.4 = (bf16[8,4224]{1,0:T(8,128)(2,1)S(1)}, bf16[8,4224]{1,0:T(8,128)(2,1)S(1)}, u32[]{:S(2)}, u32[]{:S(2)}) collective-permute-start(bf16[8,4224]{1,0:T(8,128)(2,1)S(1)} %collective-permute-done.refs_1_), channel_id=1, source_target_pairs={{0,2},{1,3},{2,0},{3,1},{4,6},{5,7},{6,4},{7,5},{8,10},{9,11},{10,... | collective-permute-start | bytes 202760 | tf_op jit(solution)/shard_map/ppermute | solution.py:418
  17.9 1.6 %collective-permute-start.7 = (bf16[4,8,4224]{2,1,0:T(8,128)(2,1)S(1)}, bf16[4,8,4224]{2,1,0:T(8,128)(2,1)S(1)}, u32[]{:S(2)}, u32[]{:S(2)}) collective-permute-start(bf16[4,8,4224]{2,1,0:T(8,128)(2,1)S(1)} %get-tuple-element.17.refs_0_), channel_id=1, source_target_pairs={{0,1},{1,0},{2,3},{3,2},{4,5},{5,4},{6,7},{7,6},{8,9},{9,8},{10,11... | collective-permute-start | bytes 811016 | tf_op jit(solution)/shard_map/ppermute | solution.py:418
  18.2 1.7 %collective-permute-start.8 = (bf16[4,8,4224]{2,1,0:T(8,128)(2,1)S(1)}, bf16[4,8,4224]{2,1,0:T(8,128)(2,1)S(1)}, u32[]{:S(2)}, u32[]{:S(2)}) collective-permute-start(bf16[4,8,4224]{2,1,0:T(8,128)(2,1)S(1)} %pad_maximum_fusion.refs_1_), channel_id=1, source_target_pairs={{0,1},{1,0},{2,3},{3,2},{4,5},{5,4},{6,7},{7,6},{8,9},{9,8},{10,11... | collective-permute-start | bytes 811016 | tf_op jit(solution)/shard_map/ppermute | solution.py:418
  19.9 7.4 %copy-start = (bf16[2,512,576]{1,2,0:T(8,128)(2,1)S(1)}, bf16[2,512,576]{1,2,0:T(8,128)(2,1)}, u32[]{:S(2)}) copy-start(bf16[2,512,576]{1,2,0:T(8,128)(2,1)} %param.16) | copy-start | bytes 3538948
  19.9 7.4 %copy-start.1 = (bf16[2,128,576]{1,2,0:T(8,128)(2,1)S(1)}, bf16[2,128,576]{1,2,0:T(8,128)(2,1)}, u32[]{:S(2)}) copy-start(bf16[2,128,576]{1,2,0:T(8,128)(2,1)} %param.15) | copy-start | bytes 884740
  20.0 7.4 %copy-start.2 = (s32[2]{0:T(128)S(1)}, s32[2]{0:T(128)}, u32[]{:S(2)}) copy-start(s32[2]{0:T(128)} %lengths_ref.1) | copy-start | bytes 28
  25.8 7.1 %collective-permute-start.10 = (bf16[4,96,256]{2,1,0:T(8,128)(2,1)S(1)}, bf16[4,96,256]{2,1,0:T(8,128)(2,1)S(1)}, u32[]{:S(2)}, u32[]{:S(2)}) collective-permute-start(bf16[4,96,256]{2,1,0:T(8,128)(2,1)S(1)} %get-tuple-element.21.after_ref.h0_ref), channel_id=1, source_target_pairs={{0,2},{1,3},{2,0},{3,1},{4,6},{5,7},{6,4},{7,5},{8,10},{9,11},{10,... | collective-permute-start | bytes 589832 | tf_op jit(solution)/shard_map/ppermute | solution.py:418
  27.3 5.6 %collective-permute-start.9 = (bf16[4,96,256]{2,1,0:T(8,128)(2,1)S(1)}, bf16[4,96,256]{2,1,0:T(8,128)(2,1)S(1)}, u32[]{:S(2)}, u32[]{:S(2)}) collective-permute-start(bf16[4,96,256]{2,1,0:T(8,128)(2,1)S(1)} %get-tuple-element.21.after_ref.h0_ref), channel_id=1, source_target_pairs={{0,1},{1,0},{2,3},{3,2},{4,5},{5,4},{6,7},{7,6},{8,9},{9,8},{10,11... | collective-permute-start | bytes 589832 | tf_op jit(solution)/shard_map/ppermute | solution.py:418
  32.9 1.4 %collective-permute-start.11 = (bf16[4,96,256]{2,1,0:T(8,128)(2,1)S(1)}, bf16[4,96,256]{2,1,0:T(8,128)(2,1)S(1)}, u32[]{:S(2)}, u32[]{:S(2)}) collective-permute-start(bf16[4,96,256]{2,1,0:T(8,128)(2,1)S(1)} %shard_map.108.h2_ref), channel_id=1, source_target_pairs={{0,1},{1,0},{2,3},{3,2},{4,5},{5,4},{6,7},{7,6},{8,9},{9,8},{10,11... | collective-permute-start | bytes 589832 | tf_op jit(solution)/shard_map/ppermute | solution.py:418
  36.1 4.5 %collective-permute-start.12 = (bf16[32,1024]{1,0:T(8,128)(2,1)S(1)}, bf16[32,1024]{1,0:T(8,128)(2,1)S(1)}, u32[]{:S(2)}, u32[]{:S(2)}) collective-permute-start(bf16[32,1024]{1,0:T(8,128)(2,1)S(1)} %get-tuple-element.24), channel_id=1, source_target_pairs={{0,4},{4,0},{8,12},{12,8},{1,5},{5,1},{9,13},{13,9},{2,6},{6,2},{1... | collective-permute-start | bytes 196616 | tf_op jit(solution)/shard_map/ppermute | solution.py:418
  37.1 7.5 %collective-permute-start.13 = (bf16[32,1024]{1,0:T(8,128)(2,1)S(1)}, bf16[32,1024]{1,0:T(8,128)(2,1)S(1)}, u32[]{:S(2)}, u32[]{:S(2)}) collective-permute-start(bf16[32,1024]{1,0:T(8,128)(2,1)S(1)} %get-tuple-element.25), channel_id=1, source_target_pairs={{0,8},{4,12},{8,0},{12,4},{1,9},{5,13},{9,1},{13,5},{2,10},{6,14},... | collective-permute-start | bytes 196616 | tf_op jit(solution)/shard_map/ppermute | solution.py:418
  39.5 6.2 %collective-permute-start.14 = (bf16[32,1024]{1,0:T(8,128)(2,1)S(1)}, bf16[32,1024]{1,0:T(8,128)(2,1)S(1)}, u32[]{:S(2)}, u32[]{:S(2)}) collective-permute-start(bf16[32,1024]{1,0:T(8,128)(2,1)S(1)} %get-tuple-element.26), channel_id=1, source_target_pairs={{0,12},{4,8},{8,4},{12,0},{1,13},{5,9},{9,5},{13,1},{2,14},{6,10},... | collective-permute-start | bytes 196616 | tf_op jit(solution)/shard_map/ppermute | solution.py:418
  45.7 1.9 %collective-permute-start.15 = (bf16[8,1024]{1,0:T(8,128)(2,1)S(1)}, bf16[8,1024]{1,0:T(8,128)(2,1)S(1)}, u32[]{:S(2)}, u32[]{:S(2)}) collective-permute-start(bf16[8,1024]{1,0:T(8,128)(2,1)S(1)} %get-tuple-element.28), channel_id=1, source_target_pairs={{0,1},{1,0},{2,3},{3,2},{4,5},{5,4},{6,7},{7,6},{8,9},{9,8},{10,11... | collective-permute-start | bytes 49160 | tf_op jit(solution)/shard_map/ppermute | solution.py:418
  45.8 3.8 %collective-permute-start.16 = (bf16[8,1024]{1,0:T(8,128)(2,1)S(1)}, bf16[8,1024]{1,0:T(8,128)(2,1)S(1)}, u32[]{:S(2)}, u32[]{:S(2)}) collective-permute-start(bf16[8,1024]{1,0:T(8,128)(2,1)S(1)} %get-tuple-element.29), channel_id=1, source_target_pairs={{0,2},{1,3},{2,0},{3,1},{4,6},{5,7},{6,4},{7,5},{8,10},{9,11},{10,... | collective-permute-start | bytes 49160 | tf_op jit(solution)/shard_map/ppermute | solution.py:418
  47.3 3.2 %collective-permute-start.17 = (bf16[8,1024]{1,0:T(8,128)(2,1)S(1)}, bf16[8,1024]{1,0:T(8,128)(2,1)S(1)}, u32[]{:S(2)}, u32[]{:S(2)}) collective-permute-start(bf16[8,1024]{1,0:T(8,128)(2,1)S(1)} %get-tuple-element.30), channel_id=1, source_target_pairs={{0,3},{1,2},{2,1},{3,0},{4,7},{5,6},{6,5},{7,4},{8,11},{9,10},{10,... | collective-permute-start | bytes 49160 | tf_op jit(solution)/shard_map/ppermute | solution.py:418

commit v4 on v3

--- a/solution.py
+++ b/solution.py
@@ -109,13 +109,15 @@
     )(value, other)
 
 
-def fetch_kernel(gate_ref, up_ref, *refs):
+def fetch_kernel(start, gate_ref, up_ref, *refs):
     *piece_refs, gate_held_ref, up_held_ref, stack_ref, sems = refs
     copies = []
     for source_ref, held_ref in ((gate_ref, gate_held_ref), (up_ref, up_held_ref)):
         for e in range(held_ref.shape[0]):
             copies.append(
-                pltpu.make_async_copy(source_ref.at[e], held_ref.at[e], sems.at[len(copies)])
+                pltpu.make_async_copy(
+                    source_ref.at[start + e], held_ref.at[e], sems.at[len(copies)]
+                )
             )
     for copy in copies:
         copy.start()
@@ -125,18 +127,18 @@
         copy.wait()
 
 
-def fetch(gate_proj, up_proj, count, pieces):
-    held = VMEM((count,) + gate_proj.shape[1:], gate_proj.dtype)
-    return pl.pallas_call(
-        fetch_kernel,
+def fetch(gate_proj, up_proj, start, stop, pieces):
+    held = VMEM((stop - start,) + gate_proj.shape[1:], gate_proj.dtype)
+    return pl.pallas_call(
+        lambda *refs: fetch_kernel(start, *refs),
         in_specs=[whole(pltpu.HBM)] * 2 + [whole()] * len(pieces),
         out_specs=[whole()] * 3,
         out_shape=[held, held, VMEM((len(pieces),) + pieces[0].shape, pieces[0].dtype)],
-        scratch_shapes=[pltpu.SemaphoreType.DMA((2 * count,))],
+        scratch_shapes=[pltpu.SemaphoreType.DMA((2 * (stop - start),))],
         compiler_params=pltpu.CompilerParams(vmem_limit_bytes=2 * MIB),
         cost_estimate=pl.CostEstimate(
             flops=0,
-            bytes_accessed=4 * count * gate_proj[0].size,
+            bytes_accessed=4 * (stop - start) * gate_proj[0].size,
             transcendentals=0,
         ),
     )(in_hbm(gate_proj), in_hbm(up_proj), *pieces)
@@ -203,37 +205,24 @@
     mine_x_ref,
     other_z_ref,
     other_x_ref,
-    gate_held_ref,
-    up_held_ref,
-    gate_ref,
-    up_ref,
+    gate_first_ref,
+    up_first_ref,
+    gate_next_ref,
+    up_next_ref,
     hidden_ref,
     spread_ref,
     rows_ref,
     coded_ref,
-    gate_late_ref,
-    up_late_ref,
-    sems,
 ):
-    ready = gate_held_ref.shape[0]
-    late = gate_late_ref.shape[0]
-    copies = []
-    for e in range(late):
-        for m, (source_ref, late_ref) in enumerate(
-            ((gate_ref, gate_late_ref), (up_ref, up_late_ref))
-        ):
-            copies.append(
-                pltpu.make_async_copy(
-                    source_ref.at[ready + e], late_ref.at[e], sems.at[2 * e + m]
-                )
-            )
-    for copy in copies:
-        copy.start()
+    matrices = []
+    for pair in ((gate_first_ref, up_first_ref), (gate_next_ref, up_next_ref)):
+        matrices += [[ref.at[e] for ref in pair] for e in range(pair[0].shape[0])]
     layer = lax.axis_index("expert")
     member = lax.axis_index("dp")
     x_side, core = jnp.right_shift(member, 1), jnp.bitwise_and(member, 1)
     layers, rows_dev, _ = mine_z_ref.shape
-    experts, feature_count, _ = gate_ref.shape
+    feature_count = rows_ref.shape[1]
+    experts = len(matrices)
     count = rows_ref.shape[0]
     first = core == 0
     for z in range(layers):
@@ -274,29 +263,23 @@
         high = value.astype(BF16)
         spread_ref[:count, e * count : (e + 1) * count] = high
         spread_ref[count:, e * count : (e + 1) * count] = (value - high.astype(F32)).astype(BF16)
-        if e < ready:
-            gate_matrix, up_matrix = gate_held_ref[e], up_held_ref[e]
-        else:
-            copies[2 * (e - ready)].wait()
-            copies[2 * (e - ready) + 1].wait()
-            gate_matrix, up_matrix = gate_late_ref[e - ready], up_late_ref[e - ready]
-        gate = jnp.dot(rows, gate_matrix, preferred_element_type=F32)
-        up = jnp.dot(rows, up_matrix, preferred_element_type=F32)
+        gate = jnp.dot(rows, matrices[e][0][...], preferred_element_type=F32)
+        up = jnp.dot(rows, matrices[e][1][...], preferred_element_type=F32)
         made = (gate / (1.0 + jnp.exp(-gate)) * up).astype(BF16)
         hidden_ref[e] = lax.dot_general(
             in_slot, made, (((0,), (0,)), ((), ())), preferred_element_type=F32
         )[:slots].astype(BF16)
 
 
-def gate_up(pieces, gate_held, up_held, gate_proj, up_proj, slots, experts_all):
-    experts, depth, share = gate_proj.shape
+def gate_up(pieces, held, slots, experts_all):
+    _, depth, share = held[0].shape
+    experts = sum(array.shape[0] for array in held[::2])
     layers, rows_dev, total_width = pieces[0].shape
     count = 4 * layers * rows_dev
-    late = experts - gate_held.shape[0]
     extra = total_width - depth
     return pl.pallas_call(
         lambda *refs: gate_up_kernel(slots, experts_all, *refs),
-        in_specs=[whole()] * 6 + [whole(pltpu.HBM)] * 2,
+        in_specs=[whole()] * 8,
         out_specs=[whole()] * 2,
         out_shape=[
             VMEM((experts, slots, share), BF16),
@@ -305,9 +288,6 @@
         scratch_shapes=[
             VMEM((count, depth), BF16),
             VMEM((count, extra), BF16),
-            VMEM((late, depth, share), BF16),
-            VMEM((late, depth, share), BF16),
-            pltpu.SemaphoreType.DMA((2 * late,)),
         ],
         compiler_params=pltpu.CompilerParams(vmem_limit_bytes=24 * MIB),
         cost_estimate=pl.CostEstimate(
@@ -315,14 +295,43 @@
             bytes_accessed=4 * experts * depth * share,
             transcendentals=experts * count * share,
         ),
-    )(*pieces, gate_held, up_held, in_hbm(gate_proj), in_hbm(up_proj))
-
-
-def down_kernel(
-    spread_ref, h0_ref, h1_ref, h2_ref, h3_ref, down_ref, o0_ref, o1_ref, o2_ref, o3_ref, made_ref
-):
+    )(*pieces, *held)
+
+
+def down_first_kernel(h0_ref, h1_ref, h2_ref, down_ref, made_ref):
     place = lax.axis_index("dp")
     experts, slots, share = h0_ref.shape
+    for e in range(experts):
+        made = jnp.zeros(made_ref.shape[1:], F32)
+        for k, ref in enumerate((h0_ref, h1_ref, h2_ref)):
+            owner = jnp.bitwise_xor(place, k)
+            weights = down_ref[e, pl.ds(pl.multiple_of(owner * share, share), share)]
+            made += jnp.dot(ref[e], weights, preferred_element_type=F32)
+        made_ref[e] = made
+
+
+def down_first(hidden, down_held):
+    experts, slots, share = hidden[0].shape
+    width = down_held.shape[2]
+    return pl.pallas_call(
+        down_first_kernel,
+        in_specs=[whole()] * 4,
+        out_specs=whole(),
+        out_shape=VMEM((experts, slots, width), F32),
+        compiler_params=pltpu.CompilerParams(vmem_limit_bytes=8 * MIB),
+        cost_estimate=pl.CostEstimate(
+            flops=6 * experts * slots * share * width,
+            bytes_accessed=4 * experts * slots * width,
+            transcendentals=0,
+        ),
+    )(*hidden, down_held)
+
+
+def down_last_kernel(
+    spread_ref, first_ref, h3_ref, down_ref, o0_ref, o1_ref, o2_ref, o3_ref, made_ref
+):
+    owner = jnp.bitwise_xor(lax.axis_index("dp"), 3)
+    experts, slots, share = h3_ref.shape
     width = down_ref.shape[2]
     count = spread_ref.shape[0] // 2
     rows_z = o0_ref.shape[0]
@@ -332,11 +341,8 @@
             made_ref[e * count + slots : (e + 1) * count] = jnp.zeros(
                 (count - slots, width), BF16
             )
-        made = jnp.zeros((slots, width), F32)
-        for k, ref in enumerate((h0_ref, h1_ref, h2_ref, h3_ref)):
-            owner = jnp.bitwise_xor(place, k)
-            weights = down_ref[e, pl.ds(pl.multiple_of(owner * share, share), share)]
-            made += jnp.dot(ref[e], weights, preferred_element_type=F32)
+        weights = down_ref[e, pl.ds(pl.multiple_of(owner * share, share), share)]
+        made = first_ref[e] + jnp.dot(h3_ref[e], weights, preferred_element_type=F32)
         made_ref[e * count : e * count + slots] = made.astype(BF16)
     spread = spread_ref[...]
     for start in range(0, width, tile):
@@ -346,22 +352,22 @@
             ref[:, start : start + tile] = done[k * rows_z : (k + 1) * rows_z]
 
 
-def down(spread, hidden, down_proj):
-    experts, depth, width = down_proj.shape
+def down_last(spread, first, hidden, down_held):
+    experts, slots, width = first.shape
     count = spread.shape[0] // 2
     return pl.pallas_call(
-        down_kernel,
-        in_specs=[whole()] * 6,
+        down_last_kernel,
+        in_specs=[whole()] * 4,
         out_specs=[whole()] * 4,
         out_shape=[VMEM((count // 4, width), BF16)] * 4,
         scratch_shapes=[VMEM((experts * count, width), BF16)],
-        compiler_params=pltpu.CompilerParams(vmem_limit_bytes=16 * MIB),
-        cost_estimate=pl.CostEstimate(
-            flops=2 * experts * count * depth * width,
-            bytes_accessed=2 * experts * depth * width,
+        compiler_params=pltpu.CompilerParams(vmem_limit_bytes=12 * MIB),
+        cost_estimate=pl.CostEstimate(
+            flops=4 * experts * count * count * width,
+            bytes_accessed=8 * experts * slots * width,
             transcendentals=0,
         ),
-    )(spread, *hidden, in_vmem(down_proj))
+    )(spread, first, hidden, down_held)
 
 
 def collect_kernel(p0_ref, p1_ref, p2_ref, p3_ref, own_ref, core_ref, x_ref, far_ref):
@@ -436,18 +442,22 @@
     capacity = max(2, 3 * rows_dev * expert_ids.shape[1] // (2 * experts_all))
     sent = pack(hidden_rows, expert_ids, gate_values, experts_all)
     along_z = [sent] + [swap(sent, "expert", k) for k in (1, 2, 3)]
-    along_x = [swap(block, "dp", 2) for block in along_z]
-    gate_held, up_held, mine_z = fetch(gate_proj, up_proj, local_experts // 2, along_z)
-    mine_x = jnp.stack(along_x)
+    near_x = swap(jnp.stack(along_z[:2]), "dp", 2)
+    gate_first, up_first, passed = fetch(
+        gate_proj, up_proj, 0, local_experts // 2, along_z[1:2]
+    )
+    along_z[2:] = [once_done(block, gate_first) for block in along_z[2:]]
+    far_x = swap(jnp.stack(along_z[2:]), "dp", 2)
+    gate_next, up_next, mine_z = fetch(
+        gate_proj, up_proj, local_experts // 2, local_experts, [along_z[0], passed[0]] + along_z[2:]
+    )
+    mine_x = jnp.concatenate([near_x, far_x])
     other_z = swap(mine_z, "dp", 1)
     other_x = swap(mine_x, "dp", 1)
 
     hidden, spread = gate_up(
         (mine_z, mine_x, other_z, other_x),
-        gate_held,
-        up_held,
-        gate_proj,
-        up_proj,
+        (gate_first, up_first, gate_next, up_next),
         16 * capacity,
         experts_all,
     )
@@ -458,8 +468,9 @@
     )
     hidden_x = once_done(hidden_x, down_held)
     hidden_xc = swap(hidden_x, "dp", 1)
-    partial = down(spread, (hidden, hidden_c, hidden_x, hidden_xc), down_held)
-    arrived = [partial[0]] + [swap(partial[k], "expert", k) for k in (1, 2, 3)]
+    first = down_first((hidden, hidden_c, hidden_x), down_held)
+    partial = down_last(spread, first, hidden_xc, down_held)
+    arrived = [partial[0]] + [swap(partial[k], "expert", k) for k in (3, 2, 1)]
     own, to_core, to_x, to_far = collect(arrived)
     far = swap(to_far, "dp", 3)
     blended = place_all((own, swap(to_core, "dp", 1), swap(to_x, "dp", 2), far))

time: 51.3 us -> 47.8 us (0.932)
  starting transfers between devices: 19.7 us -> 17.2 us
  waiting for transfers between devices: 13.3 us -> 11.4 us
  Pallas kernels: 17.3 us -> 18.2 us
    pallas_call x2 -> x4, Pallas kernels: 5.29 us -> 8.91 us  [the longest x2 7 us: fetch(): pl.pallas_call(lambda *refs: fetch_kernel(start, *refs), in_specs=[whole(...]
    pallas_call x1, Pallas kernels: 5.79 us -> 3.09 us  [gate_up(): pl.pallas_call(lambda *refs: gate_up_kernel(slots, experts_all, *refs), i...]
    ppermute x18 -> x16, starting transfers between devices: 19.7 us -> 17.2 us  [swap(): return lax.ppermute(value, axis, [(i, i ^ bit) for i in range(size)])]
    ppermute x18 -> x16, waiting for transfers between devices: 13.3 us -> 11.4 us  [swap(): return lax.ppermute(value, axis, [(i, i ^ bit) for i in range(size)])]
  transfers between devices with their start and end apart: 18 -> 16, of which waited for: 11 -> 10; matrix products, arithmetic and copies ran while one was open for 0% -> 0% of each run, Pallas kernels for 16% -> 27%
where the time goes in v4:
time: 47.8 us; the launch traced here: 47.6 us
  Pallas kernels  18.2 us (38%)
  starting transfers between devices  17.2 us (36%)
  waiting for transfers between devices  11.4 us (24%)
  between operations  0.76 us (2%)
    ppermute x16, starting transfers between devices, swap(): return lax.ppermute(value, axis, [(i, i ^ bit) for i in range(size)])  17.2 us
    ppermute x16, waiting for transfers between devices, swap(): return lax.ppermute(value, axis, [(i, i ^ bit) for i in range(size)])  11.4 us
    pallas_call x2, Pallas kernels, fetch(): pl.pallas_call(lambda *refs: fetch_kernel(start, *refs), in_specs=[whole(...  7 us
    pallas_call x1, Pallas kernels, attend_and_fetch(): pl.pallas_call(attend_and_fetch_kernel, in_specs=[whole(pltpu.SMEM), whol...  4.63 us
    pallas_call x1, Pallas kernels, gate_up(): pl.pallas_call(lambda *refs: gate_up_kernel(slots, experts_all, *refs), i...  3.09 us
    pallas_call x1, Pallas kernels, down_first(): pl.pallas_call(down_first_kernel, in_specs=[whole()] * 4, out_specs=whole...  1.13 us
  transfers between devices with their start and end apart: 16, of which 10 were waited for; matrix products, arithmetic and copies ran while one was open for 0% of the time, Pallas kernels for 27%

profile of v4, /device:TPU:0, one launch (start us, length us, event | category | flops | bytes accessed | tf_op | source)
XLA Modules:
  0.0 47.6 jit_solution(17344478504832813097)
XLA Ops:
  0.6 0.9 %shard_map.104.refs_2_ = bf16[8,4224]{1,0:T(8,128)(2,1)S(1)} custom-call(bf16[8,4096]{1,0:T(8,128)(2,1)} %refs_0_.3, s32[8,8]{1,0:T(8,128)} %refs_1_.3, f32[8,8]{1,0:T(8,128)} %refs_2_.1), custom_call_target="tpu_custom_call" | custom-call | bytes 131072 | tf_op jit(solution)/shard_map/pallas_call | solution.py:184
  1.5 3.1 %collective-permute-start = (bf16[8,4224]{1,0:T(8,128)(2,1)S(1)}, bf16[8,4224]{1,0:T(8,128)(2,1)S(1)}, u32[]{:S(2)}, u32[]{:S(2)}) collective-permute-start(bf16[8,4224]{1,0:T(8,128)(2,1)S(1)} %shard_map.104.refs_2_), channel_id=1, source_target_pairs={{0,4},{4,0},{8,12},{12,8},{1,5},{5,1},{9,13},{13,9},{2,6},{6,2},{1... | collective-permute-start | bytes 202760 | tf_op jit(solution)/shard_map/ppermute | solution.py:424
  4.6 2.5 %collective-permute-start.2 = (bf16[8,4224]{1,0:T(8,128)(2,1)S(1)}, bf16[8,4224]{1,0:T(8,128)(2,1)S(1)}, u32[]{:S(2)}, u32[]{:S(2)}) collective-permute-start(bf16[8,4224]{1,0:T(8,128)(2,1)S(1)} %shard_map.104.refs_2_), channel_id=1, source_target_pairs={{0,12},{4,8},{8,4},{12,0},{1,13},{5,9},{9,5},{13,1},{2,14},{6,10},... | collective-permute-start | bytes 202760 | tf_op jit(solution)/shard_map/ppermute | solution.py:424
  7.1 0.1 collective-permute-start.1
  7.2 0.0 collective-permute-done.refs_2_
  7.2 1.7 %collective-permute-start.3 = (bf16[2,8,4224]{2,1,0:T(8,128)(2,1)S(1)}, bf16[2,8,4224]{2,1,0:T(8,128)(2,1)S(1)}, u32[]{:S(2)}, u32[]{:S(2)}) collective-permute-start(bf16[2,8,4224]{2,1,0:T(8,128)(2,1)S(1)} %pad_maximum_fusion), channel_id=1, source_target_pairs={{0,2},{1,3},{2,0},{3,1},{4,6},{5,7},{6,4},{7,5},{8,10},{9,11},{10,... | collective-permute-start | bytes 405512 | tf_op jit(solution)/shard_map/ppermute | solution.py:424
  8.9 3.5 %shard_map.105 = (bf16[2,4096,256]{2,1,0:T(8,128)(2,1)S(1)}, bf16[2,4096,256]{2,1,0:T(8,128)(2,1)S(1)}, bf16[1,8,4224]{2,1,0:T(8,128)(2,1)S(1)}) custom-call(bf16[4,4096,256]{2,1,0:T(8,128)(2,1)} %refs_0_.5, bf16[4,4096,256]{2,1,0:T(8,128)(2,1)} %refs_1_.5, bf16[8,4224]{1,0:T(8,128)(2,1)S(1)} %collective-permute-done.refs_2_), custom_call_target="tpu_custom_call" | custom-call | bytes 8388608 | tf_op jit(solution)/shard_map/pallas_call | solution.py:132
  12.4 0.0 collective-permute-done.2.refs_0_
  12.4 1.3 %collective-permute-done.1.refs_0_ = bf16[8,4224]{1,0:T(8,128)(2,1)S(1)} collective-permute-done((bf16[8,4224]{1,0:T(8,128)(2,1)S(1)}, bf16[8,4224]{1,0:T(8,128)(2,1)S(1)}, u32[]{:S(2)}, u32[]{:S(2)}) %collective-permute-start.1) | collective-permute-done | bytes 67616 | tf_op jit(solution)/shard_map/ppermute | solution.py:424
  13.7 1.6 %collective-permute-start.4 = (bf16[2,8,4224]{2,1,0:T(8,128)(2,1)S(1)}, bf16[2,8,4224]{2,1,0:T(8,128)(2,1)S(1)}, u32[]{:S(2)}, u32[]{:S(2)}) collective-permute-start(bf16[2,8,4224]{2,1,0:T(8,128)(2,1)S(1)} %pad_maximum_fusion.1), channel_id=1, source_target_pairs={{0,2},{1,3},{2,0},{3,1},{4,6},{5,7},{6,4},{7,5},{8,10},{9,11},{10,... | collective-permute-start | bytes 405512 | tf_op jit(solution)/shard_map/ppermute | solution.py:424
  15.3 3.5 %shard_map.108 = (bf16[2,4096,256]{2,1,0:T(8,128)(2,1)S(1)}, bf16[2,4096,256]{2,1,0:T(8,128)(2,1)S(1)}, bf16[4,8,4224]{2,1,0:T(8,128)(2,1)S(1)}) custom-call(bf16[4,4096,256]{2,1,0:T(8,128)(2,1)} %refs_0_.5, bf16[4,4096,256]{2,1,0:T(8,128)(2,1)} %refs_1_.5, bf16[8,4224]{1,0:T(8,128)(2,1)S(1)} %shard_map.104.refs_2_, bf16[8,4224]{1,0:T(8,128)(2,1)S(1)} %bitcast.13, ...), custom_call_target="tpu_custom_call" | custom-call | bytes 8388608 | tf_op jit(solution)/shard_map/pallas_call | solution.py:132
  18.8 0.1 collective-permute-start.5
  18.9 0.0 collective-permute-done.3
  18.9 0.3 collective-permute-done.4
  19.3 0.2 collective-permute-start.6
  19.5 0.9 %collective-permute-done.5.refs_2_ = bf16[4,8,4224]{2,1,0:T(8,128)(2,1)S(1)} collective-permute-done((bf16[4,8,4224]{2,1,0:T(8,128)(2,1)S(1)}, bf16[4,8,4224]{2,1,0:T(8,128)(2,1)S(1)}, u32[]{:S(2)}, u32[]{:S(2)}) %collective-permute-start.5) | collective-permute-done | bytes 270368 | tf_op jit(solution)/shard_map/ppermute | solution.py:424
  20.4 0.5 collective-permute-done.6.refs_3_
  20.9 0.0 copy-start
  20.9 0.0 copy-start.1
  20.9 0.0 copy-start.2
  20.9 3.1 %shard_map.109 = (bf16[4,96,256]{2,1,0:T(8,128)(2,1)S(1)}, bf16[256,512]{1,0:T(8,128)(2,1)S(1)}) custom-call(bf16[4,8,4224]{2,1,0:T(8,128)(2,1)S(1)} %get-tuple-element.22.refs_0_, bf16[4,8,4224]{2,1,0:T(8,128)(2,1)S(1)} %constant_dynamic-update-slice_fusion.refs_1_, bf16[4,8,4224]{2,1,0:T(8,128)(2,1)S(1)} %collective-permute-done.5.refs_2_, ...), custom_call_target="tpu_custom_call" | custom-call | flops 2147483648 | bytes 16777216 | tf_op jit(solution)/shard_map/pallas_call | solution.py:280
  24.0 1.6 %collective-permute-start.8 = (bf16[4,96,256]{2,1,0:T(8,128)(2,1)S(1)}, bf16[4,96,256]{2,1,0:T(8,128)(2,1)S(1)}, u32[]{:S(2)}, u32[]{:S(2)}) collective-permute-start(bf16[4,96,256]{2,1,0:T(8,128)(2,1)S(1)} %get-tuple-element.27.after_ref.h0_ref), channel_id=1, source_target_pairs={{0,2},{1,3},{2,0},{3,1},{4,6},{5,7},{6,4},{7,5},{8,10},{9,11},{10,... | collective-permute-start | bytes 589832 | tf_op jit(solution)/shard_map/ppermute | solution.py:424
  25.5 0.0 collective-permute-start.7
  25.5 0.0 copy-done
  25.5 0.0 copy-done.1
  25.5 0.0 copy-done.2
  25.6 4.6 %shard_map.110 = (bf16[2,128,512]{2,1,0:T(8,128)(2,1)}, bf16[4,1024,1024]{2,1,0:T(8,128)(2,1)S(1)}) custom-call(s32[2]{0:T(128)S(1)} %copy-done.2, bf16[2,576,128]{2,1,0:T(8,128)(2,1)S(1)} %bitcast.11, bf16[2,576,512]{2,1,0:T(8,128)(2,1)S(1)} %bitcast.7, bf16[4,1024,1024]{2,1,0:T(8,128)(2,1)} %source_ref.1, ...), custom_call_target="tpu_custom_call" | custom-call | flops 285212672 | bytes 1736704 | tf_op jit(solution)/shard_map/pallas_call | solution.py:80
  30.2 0.8 %collective-permute-done.8.refs_0_ = bf16[4,96,256]{2,1,0:T(8,128)(2,1)S(1)} collective-permute-done((bf16[4,96,256]{2,1,0:T(8,128)(2,1)S(1)}, bf16[4,96,256]{2,1,0:T(8,128)(2,1)S(1)}, u32[]{:S(2)}, u32[]{:S(2)}) %collective-permute-start.8) | collective-permute-done | bytes 196640 | tf_op jit(solution)/shard_map/ppermute | solution.py:424
  31.0 0.0 collective-permute-start.9
  31.0 0.0 collective-permute-done.7.h1_ref
  31.0 1.1 %shard_map.112.first_ref = f32[4,96,1024]{2,1,0:T(8,128)S(1)} custom-call(bf16[4,96,256]{2,1,0:T(8,128)(2,1)S(1)} %get-tuple-element.27.after_ref.h0_ref, bf16[4,96,256]{2,1,0:T(8,128)(2,1)S(1)} %collective-permute-done.7.h1_ref, bf16[4,96,256]{2,1,0:T(8,128)(2,1)S(1)} %shard_map.111.h2_ref, bf16[4,1024,1024]{2,1,0:T(8,128)(2,1)S(1)} %get-tuple-element.28.refs_1_.down_ref), custom_call_target="tpu_custom_call" | custom-call | flops 603979776 | bytes 1572864 | tf_op jit(solution)/shard_map/pallas_call | solution.py:316
  32.2 0.3 collective-permute-done.9.h3_ref
  32.5 0.8 %shard_map.113 = (bf16[32,1024]{1,0:T(8,128)(2,1)S(1)}, bf16[32,1024]{1,0:T(8,128)(2,1)S(1)}, bf16[32,1024]{1,0:T(8,128)(2,1)S(1)}, bf16[32,1024]{1,0:T(8,128)(2,1)S(1)}) custom-call(bf16[256,512]{1,0:T(8,128)(2,1)S(1)} %get-tuple-element.26.spread_ref, f32[4,96,1024]{2,1,0:T(8,128)S(1)} %shard_map.112.first_ref, ...), custom_call_target="tpu_custom_call" | custom-call | flops 268435456 | bytes 3145728 | tf_op jit(solution)/shard_map/pallas_call | solution.py:358
  33.2 2.5 %collective-permute-start.10 = (bf16[32,1024]{1,0:T(8,128)(2,1)S(1)}, bf16[32,1024]{1,0:T(8,128)(2,1)S(1)}, u32[]{:S(2)}, u32[]{:S(2)}) collective-permute-start(bf16[32,1024]{1,0:T(8,128)(2,1)S(1)} %get-tuple-element.30), channel_id=1, source_target_pairs={{0,12},{4,8},{8,4},{12,0},{1,13},{5,9},{9,5},{13,1},{2,14},{6,10},... | collective-permute-start | bytes 196616 | tf_op jit(solution)/shard_map/ppermute | solution.py:424
  35.7 0.0 collective-permute-start.11
  35.7 2.0 %collective-permute-start.12 = (bf16[32,1024]{1,0:T(8,128)(2,1)S(1)}, bf16[32,1024]{1,0:T(8,128)(2,1)S(1)}, u32[]{:S(2)}, u32[]{:S(2)}) collective-permute-start(bf16[32,1024]{1,0:T(8,128)(2,1)S(1)} %get-tuple-element.32), channel_id=1, source_target_pairs={{0,4},{4,0},{8,12},{12,8},{1,5},{5,1},{9,13},{13,9},{2,6},{6,2},{1... | collective-permute-start | bytes 196616 | tf_op jit(solution)/shard_map/ppermute | solution.py:424
  37.7 2.4 %collective-permute-done.10.p1_ref = bf16[32,1024]{1,0:T(8,128)(2,1)S(1)} collective-permute-done((bf16[32,1024]{1,0:T(8,128)(2,1)S(1)}, bf16[32,1024]{1,0:T(8,128)(2,1)S(1)}, u32[]{:S(2)}, u32[]{:S(2)}) %collective-permute-start.10) | collective-permute-done | bytes 65568 | tf_op jit(solution)/shard_map/ppermute | solution.py:424
  40.1 2.0 %collective-permute-done.11.p2_ref = bf16[32,1024]{1,0:T(8,128)(2,1)S(1)} collective-permute-done((bf16[32,1024]{1,0:T(8,128)(2,1)S(1)}, bf16[32,1024]{1,0:T(8,128)(2,1)S(1)}, u32[]{:S(2)}, u32[]{:S(2)}) %collective-permute-start.11) | collective-permute-done | bytes 65568 | tf_op jit(solution)/shard_map/ppermute | solution.py:424
  42.1 0.0 collective-permute-done.12.p3_ref
  42.2 0.1 collective-permute-start.13
  42.3 1.5 %collective-permute-start.14 = (bf16[8,1024]{1,0:T(8,128)(2,1)S(1)}, bf16[8,1024]{1,0:T(8,128)(2,1)S(1)}, u32[]{:S(2)}, u32[]{:S(2)}) collective-permute-start(bf16[8,1024]{1,0:T(8,128)(2,1)S(1)} %get-tuple-element.35), channel_id=1, source_target_pairs={{0,2},{1,3},{2,0},{3,1},{4,6},{5,7},{6,4},{7,5},{8,10},{9,11},{10,... | collective-permute-start | bytes 49160 | tf_op jit(solution)/shard_map/ppermute | solution.py:424
  43.8 0.3 collective-permute-start.15
  44.1 0.0 collective-permute-done.13.p1_ref
  44.1 1.9 %collective-permute-done.14.p2_ref = bf16[8,1024]{1,0:T(8,128)(2,1)S(1)} collective-permute-done((bf16[8,1024]{1,0:T(8,128)(2,1)S(1)}, bf16[8,1024]{1,0:T(8,128)(2,1)S(1)}, u32[]{:S(2)}, u32[]{:S(2)}) %collective-permute-start.14) | collective-permute-done | bytes 16416 | tf_op jit(solution)/shard_map/ppermute | solution.py:424
  46.1 0.9 %collective-permute-done.15.p3_ref = bf16[8,1024]{1,0:T(8,128)(2,1)S(1)} collective-permute-done((bf16[8,1024]{1,0:T(8,128)(2,1)S(1)}, bf16[8,1024]{1,0:T(8,128)(2,1)S(1)}, u32[]{:S(2)}, u32[]{:S(2)}) %collective-permute-start.15) | collective-permute-done | bytes 16416 | tf_op jit(solution)/shard_map/ppermute | solution.py:424
  47.0 0.6 %shard_map.115 = bf16[8,4096]{1,0:T(8,128)(2,1)} custom-call(bf16[8,1024]{1,0:T(8,128)(2,1)S(1)} %get-tuple-element.33.p0_ref, bf16[8,1024]{1,0:T(8,128)(2,1)S(1)} %collective-permute-done.13.p1_ref, bf16[8,1024]{1,0:T(8,128)(2,1)S(1)} %collective-permute-done.14.p2_ref, bf16[8,1024]{1,0:T(8,128)(2,1)S(1)} %collective-permute-done.15.p3_ref), custom_call_target="tpu_custom_call" | custom-call | bytes 131072 | tf_op jit(solution)/shard_map/pallas_call | solution.py:410
  (8 shorter events, 0.1 us)
Async XLA Ops:
  1.5 5.7 %collective-permute-start = (bf16[8,4224]{1,0:T(8,128)(2,1)S(1)}, bf16[8,4224]{1,0:T(8,128)(2,1)S(1)}, u32[]{:S(2)}, u32[]{:S(2)}) collective-permute-start(bf16[8,4224]{1,0:T(8,128)(2,1)S(1)} %shard_map.104.refs_2_), channel_id=1, source_target_pairs={{0,4},{4,0},{8,12},{12,8},{1,5},{5,1},{9,13},{13,9},{2,6},{6,2},{1... | collective-permute-start | bytes 202760 | tf_op jit(solution)/shard_map/ppermute | solution.py:424
  4.6 7.8 %collective-permute-start.2 = (bf16[8,4224]{1,0:T(8,128)(2,1)S(1)}, bf16[8,4224]{1,0:T(8,128)(2,1)S(1)}, u32[]{:S(2)}, u32[]{:S(2)}) collective-permute-start(bf16[8,4224]{1,0:T(8,128)(2,1)S(1)} %shard_map.104.refs_2_), channel_id=1, source_target_pairs={{0,12},{4,8},{8,4},{12,0},{1,13},{5,9},{9,5},{13,1},{2,14},{6,10},... | collective-permute-start | bytes 202760 | tf_op jit(solution)/shard_map/ppermute | solution.py:424
  7.1 6.6 %collective-permute-start.1 = (bf16[8,4224]{1,0:T(8,128)(2,1)S(1)}, bf16[8,4224]{1,0:T(8,128)(2,1)S(1)}, u32[]{:S(2)}, u32[]{:S(2)}) collective-permute-start(bf16[8,4224]{1,0:T(8,128)(2,1)S(1)} %shard_map.104.refs_2_), channel_id=1, source_target_pairs={{0,8},{4,12},{8,0},{12,4},{1,9},{5,13},{9,1},{13,5},{2,10},{6,14},... | collective-permute-start | bytes 202760 | tf_op jit(solution)/shard_map/ppermute | solution.py:424
  7.2 11.6 %collective-permute-start.3 = (bf16[2,8,4224]{2,1,0:T(8,128)(2,1)S(1)}, bf16[2,8,4224]{2,1,0:T(8,128)(2,1)S(1)}, u32[]{:S(2)}, u32[]{:S(2)}) collective-permute-start(bf16[2,8,4224]{2,1,0:T(8,128)(2,1)S(1)} %pad_maximum_fusion), channel_id=1, source_target_pairs={{0,2},{1,3},{2,0},{3,1},{4,6},{5,7},{6,4},{7,5},{8,10},{9,11},{10,... | collective-permute-start | bytes 405512 | tf_op jit(solution)/shard_map/ppermute | solution.py:424
  13.7 5.5 %collective-permute-start.4 = (bf16[2,8,4224]{2,1,0:T(8,128)(2,1)S(1)}, bf16[2,8,4224]{2,1,0:T(8,128)(2,1)S(1)}, u32[]{:S(2)}, u32[]{:S(2)}) collective-permute-start(bf16[2,8,4224]{2,1,0:T(8,128)(2,1)S(1)} %pad_maximum_fusion.1), channel_id=1, source_target_pairs={{0,2},{1,3},{2,0},{3,1},{4,6},{5,7},{6,4},{7,5},{8,10},{9,11},{10,... | collective-permute-start | bytes 405512 | tf_op jit(solution)/shard_map/ppermute | solution.py:424
  18.8 1.6 %collective-permute-start.5 = (bf16[4,8,4224]{2,1,0:T(8,128)(2,1)S(1)}, bf16[4,8,4224]{2,1,0:T(8,128)(2,1)S(1)}, u32[]{:S(2)}, u32[]{:S(2)}) collective-permute-start(bf16[4,8,4224]{2,1,0:T(8,128)(2,1)S(1)} %get-tuple-element.22.refs_0_), channel_id=1, source_target_pairs={{0,1},{1,0},{2,3},{3,2},{4,5},{5,4},{6,7},{7,6},{8,9},{9,8},{10,11... | collective-permute-start | bytes 811016 | tf_op jit(solution)/shard_map/ppermute | solution.py:424
  19.3 1.6 %collective-permute-start.6 = (bf16[4,8,4224]{2,1,0:T(8,128)(2,1)S(1)}, bf16[4,8,4224]{2,1,0:T(8,128)(2,1)S(1)}, u32[]{:S(2)}, u32[]{:S(2)}) collective-permute-start(bf16[4,8,4224]{2,1,0:T(8,128)(2,1)S(1)} %constant_dynamic-update-slice_fusion.refs_1_), channel_id=1, source_target_pairs={{0,1},{1,0},{2,3},{3,2},{4,5},{5,4},{6,7},{7,6},{8,9},{9,8},{10,11... | collective-permute-start | bytes 811016 | tf_op jit(solution)/shard_map/ppermute | solution.py:424
  20.9 4.7 %copy-start = (bf16[2,512,576]{1,2,0:T(8,128)(2,1)S(1)}, bf16[2,512,576]{1,2,0:T(8,128)(2,1)}, u32[]{:S(2)}) copy-start(bf16[2,512,576]{1,2,0:T(8,128)(2,1)} %param.16) | copy-start | bytes 3538948
  20.9 4.7 %copy-start.1 = (bf16[2,128,576]{1,2,0:T(8,128)(2,1)S(1)}, bf16[2,128,576]{1,2,0:T(8,128)(2,1)}, u32[]{:S(2)}) copy-start(bf16[2,128,576]{1,2,0:T(8,128)(2,1)} %param.15) | copy-start | bytes 884740
  20.9 4.7 %copy-start.2 = (s32[2]{0:T(128)S(1)}, s32[2]{0:T(128)}, u32[]{:S(2)}) copy-start(s32[2]{0:T(128)} %lengths_ref.1) | copy-start | bytes 28
  24.0 7.0 %collective-permute-start.8 = (bf16[4,96,256]{2,1,0:T(8,128)(2,1)S(1)}, bf16[4,96,256]{2,1,0:T(8,128)(2,1)S(1)}, u32[]{:S(2)}, u32[]{:S(2)}) collective-permute-start(bf16[4,96,256]{2,1,0:T(8,128)(2,1)S(1)} %get-tuple-element.27.after_ref.h0_ref), channel_id=1, source_target_pairs={{0,2},{1,3},{2,0},{3,1},{4,6},{5,7},{6,4},{7,5},{8,10},{9,11},{10,... | collective-permute-start | bytes 589832 | tf_op jit(solution)/shard_map/ppermute | solution.py:424
  25.5 5.5 %collective-permute-start.7 = (bf16[4,96,256]{2,1,0:T(8,128)(2,1)S(1)}, bf16[4,96,256]{2,1,0:T(8,128)(2,1)S(1)}, u32[]{:S(2)}, u32[]{:S(2)}) collective-permute-start(bf16[4,96,256]{2,1,0:T(8,128)(2,1)S(1)} %get-tuple-element.27.after_ref.h0_ref), channel_id=1, source_target_pairs={{0,1},{1,0},{2,3},{3,2},{4,5},{5,4},{6,7},{7,6},{8,9},{9,8},{10,11... | collective-permute-start | bytes 589832 | tf_op jit(solution)/shard_map/ppermute | solution.py:424
  31.0 1.4 %collective-permute-start.9 = (bf16[4,96,256]{2,1,0:T(8,128)(2,1)S(1)}, bf16[4,96,256]{2,1,0:T(8,128)(2,1)S(1)}, u32[]{:S(2)}, u32[]{:S(2)}) collective-permute-start(bf16[4,96,256]{2,1,0:T(8,128)(2,1)S(1)} %shard_map.111.h2_ref), channel_id=1, source_target_pairs={{0,1},{1,0},{2,3},{3,2},{4,5},{5,4},{6,7},{7,6},{8,9},{9,8},{10,11... | collective-permute-start | bytes 589832 | tf_op jit(solution)/shard_map/ppermute | solution.py:424
  33.2 6.9 %collective-permute-start.10 = (bf16[32,1024]{1,0:T(8,128)(2,1)S(1)}, bf16[32,1024]{1,0:T(8,128)(2,1)S(1)}, u32[]{:S(2)}, u32[]{:S(2)}) collective-permute-start(bf16[32,1024]{1,0:T(8,128)(2,1)S(1)} %get-tuple-element.30), channel_id=1, source_target_pairs={{0,12},{4,8},{8,4},{12,0},{1,13},{5,9},{9,5},{13,1},{2,14},{6,10},... | collective-permute-start | bytes 196616 | tf_op jit(solution)/shard_map/ppermute | solution.py:424
  35.7 6.4 %collective-permute-start.11 = (bf16[32,1024]{1,0:T(8,128)(2,1)S(1)}, bf16[32,1024]{1,0:T(8,128)(2,1)S(1)}, u32[]{:S(2)}, u32[]{:S(2)}) collective-permute-start(bf16[32,1024]{1,0:T(8,128)(2,1)S(1)} %get-tuple-element.31), channel_id=1, source_target_pairs={{0,8},{4,12},{8,0},{12,4},{1,9},{5,13},{9,1},{13,5},{2,10},{6,14},... | collective-permute-start | bytes 196616 | tf_op jit(solution)/shard_map/ppermute | solution.py:424
  35.7 6.4 %collective-permute-start.12 = (bf16[32,1024]{1,0:T(8,128)(2,1)S(1)}, bf16[32,1024]{1,0:T(8,128)(2,1)S(1)}, u32[]{:S(2)}, u32[]{:S(2)}) collective-permute-start(bf16[32,1024]{1,0:T(8,128)(2,1)S(1)} %get-tuple-element.32), channel_id=1, source_target_pairs={{0,4},{4,0},{8,12},{12,8},{1,5},{5,1},{9,13},{13,9},{2,6},{6,2},{1... | collective-permute-start | bytes 196616 | tf_op jit(solution)/shard_map/ppermute | solution.py:424
  42.2 1.9 %collective-permute-start.13 = (bf16[8,1024]{1,0:T(8,128)(2,1)S(1)}, bf16[8,1024]{1,0:T(8,128)(2,1)S(1)}, u32[]{:S(2)}, u32[]{:S(2)}) collective-permute-start(bf16[8,1024]{1,0:T(8,128)(2,1)S(1)} %get-tuple-element.34), channel_id=1, source_target_pairs={{0,1},{1,0},{2,3},{3,2},{4,5},{5,4},{6,7},{7,6},{8,9},{9,8},{10,11... | collective-permute-start | bytes 49160 | tf_op jit(solution)/shard_map/ppermute | solution.py:424
  42.3 3.8 %collective-permute-start.14 = (bf16[8,1024]{1,0:T(8,128)(2,1)S(1)}, bf16[8,1024]{1,0:T(8,128)(2,1)S(1)}, u32[]{:S(2)}, u32[]{:S(2)}) collective-permute-start(bf16[8,1024]{1,0:T(8,128)(2,1)S(1)} %get-tuple-element.35), channel_id=1, source_target_pairs={{0,2},{1,3},{2,0},{3,1},{4,6},{5,7},{6,4},{7,5},{8,10},{9,11},{10,... | collective-permute-start | bytes 49160 | tf_op jit(solution)/shard_map/ppermute | solution.py:424
  43.8 3.2 %collective-permute-start.15 = (bf16[8,1024]{1,0:T(8,128)(2,1)S(1)}, bf16[8,1024]{1,0:T(8,128)(2,1)S(1)}, u32[]{:S(2)}, u32[]{:S(2)}) collective-permute-start(bf16[8,1024]{1,0:T(8,128)(2,1)S(1)} %get-tuple-element.36), channel_id=1, source_target_pairs={{0,3},{1,2},{2,1},{3,0},{4,7},{5,6},{6,5},{7,4},{8,11},{9,10},{10,... | collective-permute-start | bytes 49160 | tf_op jit(solution)/shard_map/ppermute | solution.py:424

commit v5 on v4

--- a/solution.py
+++ b/solution.py
@@ -202,8 +202,8 @@
     slots,
     experts_all,
     mine_z_ref,
+    other_z_ref,
     mine_x_ref,
-    other_z_ref,
     other_x_ref,
     gate_first_ref,
     up_first_ref,
@@ -212,71 +212,58 @@
     hidden_ref,
     spread_ref,
     rows_ref,
-    coded_ref,
 ):
     matrices = []
     for pair in ((gate_first_ref, up_first_ref), (gate_next_ref, up_next_ref)):
         matrices += [[ref.at[e] for ref in pair] for e in range(pair[0].shape[0])]
-    layer = lax.axis_index("expert")
-    member = lax.axis_index("dp")
-    x_side, core = jnp.right_shift(member, 1), jnp.bitwise_and(member, 1)
-    layers, rows_dev, _ = mine_z_ref.shape
-    feature_count = rows_ref.shape[1]
     experts = len(matrices)
-    count = rows_ref.shape[0]
-    first = core == 0
-    for z in range(layers):
-        for x, (mine_ref, other_ref) in enumerate(
-            ((mine_z_ref, other_z_ref), (mine_x_ref, other_x_ref))
-        ):
-            at = (2 * z + x) * 2 * rows_dev
-            mine, other = mine_ref[z], other_ref[z]
-            pair = jnp.concatenate(
-                [jnp.where(first, mine, other), jnp.where(first, other, mine)], axis=0
-            )
-            rows_ref[at : at + 2 * rows_dev] = pair[:, :feature_count]
-            coded_ref[at : at + 2 * rows_dev] = pair[:, feature_count:]
-    lanes = coded_ref.shape[1]
+    depth = gate_first_ref.shape[1]
+    groups = (mine_z_ref, other_z_ref, mine_x_ref, other_x_ref)
+    rows_group, total_width = mine_z_ref.shape
+    count = 4 * rows_group
+    lanes = total_width - depth
+    for g, ref in enumerate(groups):
+        rows_ref[g * rows_group : (g + 1) * rows_group] = ref[:, :depth]
+    coded = jnp.concatenate([ref[:, depth:] for ref in groups], axis=0)
+    def activated(e):
+        gate = jnp.dot(rows_ref[...], matrices[e][0][...], preferred_element_type=F32)
+        up = jnp.dot(rows_ref[...], matrices[e][1][...], preferred_element_type=F32)
+        return (gate / (1.0 + jnp.exp(-gate)) * up).astype(BF16)
+
+    made = activated(0)
     source = lax.broadcasted_iota(jnp.int32, (lanes, lanes), 0)
     target = lax.broadcasted_iota(jnp.int32, (lanes, lanes), 1)
     selector = (
-        (lax.rem(source, experts_all) == layer * experts + target)
+        (lax.rem(source, experts_all) == lax.axis_index("expert") * experts + target)
         & (target < experts)
         & (source < 3 * experts_all)
     )
-    table = jnp.dot(
-        coded_ref[...], selector.astype(F32).astype(BF16), preferred_element_type=F32
-    )
+    table = jnp.dot(coded, selector.astype(F32).astype(BF16), preferred_element_type=F32)
     chosen = (table > 0.0).astype(F32).astype(BF16)
     row = lax.broadcasted_iota(jnp.int32, (count, count), 0)
     column = lax.broadcasted_iota(jnp.int32, (count, count), 1)
-    turn = x_side * (2 * rows_dev)
+    turn = lax.axis_index("dp") * rows_group
     ahead = jnp.bitwise_xor(column, turn) < jnp.bitwise_xor(row, turn)
     rank = jnp.dot(ahead.astype(F32).astype(BF16), chosen, preferred_element_type=F32)
     rank = jnp.where(table > 0.0, rank, -1.0)
-    slot = lax.broadcasted_iota(jnp.int32, (count, count), 1).astype(F32)
-    rows = rows_ref[...]
+    rank_across = rank.T
+    slot = column.astype(F32)
+    slot_down = row.astype(F32)[:slots]
     for e in range(experts):
-        hit = rank[:, e : e + 1] == slot
-        in_slot = hit.astype(F32).astype(BF16)
-        value = jnp.where(hit, table[:, e : e + 1], 0.0)
+        later = activated(e + 1) if e + 1 < experts else None
+        value = jnp.where(rank[:, e : e + 1] == slot, table[:, e : e + 1], 0.0)
         high = value.astype(BF16)
         spread_ref[:count, e * count : (e + 1) * count] = high
         spread_ref[count:, e * count : (e + 1) * count] = (value - high.astype(F32)).astype(BF16)
-        gate = jnp.dot(rows, matrices[e][0][...], preferred_element_type=F32)
-        up = jnp.dot(rows, matrices[e][1][...], preferred_element_type=F32)
-        made = (gate / (1.0 + jnp.exp(-gate)) * up).astype(BF16)
-        hidden_ref[e] = lax.dot_general(
-            in_slot, made, (((0,), (0,)), ((), ())), preferred_element_type=F32
-        )[:slots].astype(BF16)
+        to_slot = (rank_across[e : e + 1] == slot_down).astype(F32).astype(BF16)
+        hidden_ref[e] = jnp.dot(to_slot, made, preferred_element_type=F32).astype(BF16)
+        made = later
 
 
 def gate_up(pieces, held, slots, experts_all):
     _, depth, share = held[0].shape
     experts = sum(array.shape[0] for array in held[::2])
-    layers, rows_dev, total_width = pieces[0].shape
-    count = 4 * layers * rows_dev
-    extra = total_width - depth
+    count = 4 * pieces[0].shape[0]
     return pl.pallas_call(
         lambda *refs: gate_up_kernel(slots, experts_all, *refs),
         in_specs=[whole()] * 8,
@@ -285,11 +272,8 @@
             VMEM((experts, slots, share), BF16),
             VMEM((2 * count, experts * count), BF16),
         ],
-        scratch_shapes=[
-            VMEM((count, depth), BF16),
-            VMEM((count, extra), BF16),
-        ],
-        compiler_params=pltpu.CompilerParams(vmem_limit_bytes=24 * MIB),
+        scratch_shapes=[VMEM((count, depth), BF16)],
+        compiler_params=pltpu.CompilerParams(vmem_limit_bytes=16 * MIB),
         cost_estimate=pl.CostEstimate(
             flops=4 * experts * count * depth * share,
             bytes_accessed=4 * experts * depth * share,
@@ -347,9 +331,13 @@
     spread = spread_ref[...]
     for start in range(0, width, tile):
         both = jnp.dot(spread, made_ref[:, start : start + tile], preferred_element_type=F32)
-        done = (both[:count] + both[count:]).astype(BF16)
+        done = both[:count] + both[count:]
+        rows = rows_z // 4
         for k, ref in enumerate((o0_ref, o1_ref, o2_ref, o3_ref)):
-            ref[:, start : start + tile] = done[k * rows_z : (k + 1) * rows_z]
+            parts = [
+                done[g * rows_z + k * rows : g * rows_z + (k + 1) * rows] for g in range(4)
+            ]
+            ref[:, start : start + tile] = jnp.concatenate(parts, axis=0).astype(BF16)
 
 
 def down_last(spread, first, hidden, down_held):
@@ -375,12 +363,8 @@
     for ref in (p1_ref, p2_ref, p3_ref):
         total += ref[...].astype(F32)
     rows = own_ref.shape[0]
-    first = jnp.bitwise_and(lax.axis_index("dp"), 1) == 0
-    near = [total[k * rows : (k + 1) * rows] for k in range(4)]
-    own_ref[...] = jnp.where(first, near[0], near[1]).astype(BF16)
-    core_ref[...] = jnp.where(first, near[1], near[0]).astype(BF16)
-    x_ref[...] = jnp.where(first, near[2], near[3]).astype(BF16)
-    far_ref[...] = jnp.where(first, near[3], near[2]).astype(BF16)
+    for k, ref in enumerate((own_ref, core_ref, x_ref, far_ref)):
+        ref[...] = total[k * rows : (k + 1) * rows].astype(BF16)
 
 
 def collect(partials):
@@ -456,7 +440,7 @@
     other_x = swap(mine_x, "dp", 1)
 
     hidden, spread = gate_up(
-        (mine_z, mine_x, other_z, other_x),
+        [block.reshape(4 * rows_dev, -1) for block in (mine_z, other_z, mine_x, other_x)],
         (gate_first, up_first, gate_next, up_next),
         16 * capacity,
         experts_all,

time: 47.8 us -> 47.5 us (level)
  no operation moved by 1% of the time
where the time goes in v5:
time: 47.5 us; the launch traced here: 47.3 us
  Pallas kernels  17.9 us (38%)
  starting transfers between devices  17.2 us (36%)
  waiting for transfers between devices  11.4 us (24%)
  between operations  0.76 us (2%)
    ppermute x16, starting transfers between devices, swap(): return lax.ppermute(value, axis, [(i, i ^ bit) for i in range(size)])  17.2 us
    ppermute x16, waiting for transfers between devices, swap(): return lax.ppermute(value, axis, [(i, i ^ bit) for i in range(size)])  11.4 us
    pallas_call x2, Pallas kernels, fetch(): pl.pallas_call(lambda *refs: fetch_kernel(start, *refs), in_specs=[whole(...  7 us
    pallas_call x1, Pallas kernels, attend_and_fetch(): pl.pallas_call(attend_and_fetch_kernel, in_specs=[whole(pltpu.SMEM), whol...  4.63 us
    pallas_call x1, Pallas kernels, gate_up(): pl.pallas_call(lambda *refs: gate_up_kernel(slots, experts_all, *refs), i...  2.77 us
    pallas_call x1, Pallas kernels, down_first(): pl.pallas_call(down_first_kernel, in_specs=[whole()] * 4, out_specs=whole...  1.13 us
  transfers between devices with their start and end apart: 16, of which 10 were waited for; matrix products, arithmetic and copies ran while one was open for 0% of the time, Pallas kernels for 27%

profile of v5, /device:TPU:0, one launch (start us, length us, event | category | flops | bytes accessed | tf_op | source)
XLA Modules:
  0.0 47.3 jit_solution(364800038153730459)
XLA Ops:
  0.6 0.9 %shard_map.104.refs_2_ = bf16[8,4224]{1,0:T(8,128)(2,1)S(1)} custom-call(bf16[8,4096]{1,0:T(8,128)(2,1)} %refs_0_.3, s32[8,8]{1,0:T(8,128)} %refs_1_.3, f32[8,8]{1,0:T(8,128)} %refs_2_.1), custom_call_target="tpu_custom_call" | custom-call | bytes 131072 | tf_op jit(solution)/shard_map/pallas_call | solution.py:184
  1.5 3.1 %collective-permute-start = (bf16[8,4224]{1,0:T(8,128)(2,1)S(1)}, bf16[8,4224]{1,0:T(8,128)(2,1)S(1)}, u32[]{:S(2)}, u32[]{:S(2)}) collective-permute-start(bf16[8,4224]{1,0:T(8,128)(2,1)S(1)} %shard_map.104.refs_2_), channel_id=1, source_target_pairs={{0,4},{4,0},{8,12},{12,8},{1,5},{5,1},{9,13},{13,9},{2,6},{6,2},{1... | collective-permute-start | bytes 202760 | tf_op jit(solution)/shard_map/ppermute | solution.py:408
  4.6 2.5 %collective-permute-start.2 = (bf16[8,4224]{1,0:T(8,128)(2,1)S(1)}, bf16[8,4224]{1,0:T(8,128)(2,1)S(1)}, u32[]{:S(2)}, u32[]{:S(2)}) collective-permute-start(bf16[8,4224]{1,0:T(8,128)(2,1)S(1)} %shard_map.104.refs_2_), channel_id=1, source_target_pairs={{0,12},{4,8},{8,4},{12,0},{1,13},{5,9},{9,5},{13,1},{2,14},{6,10},... | collective-permute-start | bytes 202760 | tf_op jit(solution)/shard_map/ppermute | solution.py:408
  7.1 0.1 collective-permute-start.1
  7.2 0.0 collective-permute-done.refs_2_
  7.2 1.7 %collective-permute-start.4 = (bf16[2,8,4224]{2,1,0:T(8,128)(2,1)S(1)}, bf16[2,8,4224]{2,1,0:T(8,128)(2,1)S(1)}, u32[]{:S(2)}, u32[]{:S(2)}) collective-permute-start(bf16[2,8,4224]{2,1,0:T(8,128)(2,1)S(1)} %pad_maximum_fusion), channel_id=1, source_target_pairs={{0,2},{1,3},{2,0},{3,1},{4,6},{5,7},{6,4},{7,5},{8,10},{9,11},{10,... | collective-permute-start | bytes 405512 | tf_op jit(solution)/shard_map/ppermute | solution.py:408
  8.9 3.5 %shard_map.105 = (bf16[2,4096,256]{2,1,0:T(8,128)(2,1)S(1)}, bf16[2,4096,256]{2,1,0:T(8,128)(2,1)S(1)}, bf16[1,8,4224]{2,1,0:T(8,128)(2,1)S(1)}) custom-call(bf16[4,4096,256]{2,1,0:T(8,128)(2,1)} %refs_0_.5, bf16[4,4096,256]{2,1,0:T(8,128)(2,1)} %refs_1_.5, bf16[8,4224]{1,0:T(8,128)(2,1)S(1)} %collective-permute-done.refs_2_), custom_call_target="tpu_custom_call" | custom-call | bytes 8388608 | tf_op jit(solution)/shard_map/pallas_call | solution.py:132
  12.4 0.0 collective-permute-done.2.refs_0_
  12.4 1.3 %collective-permute-done.1.refs_0_ = bf16[8,4224]{1,0:T(8,128)(2,1)S(1)} collective-permute-done((bf16[8,4224]{1,0:T(8,128)(2,1)S(1)}, bf16[8,4224]{1,0:T(8,128)(2,1)S(1)}, u32[]{:S(2)}, u32[]{:S(2)}) %collective-permute-start.1) | collective-permute-done | bytes 67616 | tf_op jit(solution)/shard_map/ppermute | solution.py:408
  13.7 1.6 %collective-permute-start.5 = (bf16[2,8,4224]{2,1,0:T(8,128)(2,1)S(1)}, bf16[2,8,4224]{2,1,0:T(8,128)(2,1)S(1)}, u32[]{:S(2)}, u32[]{:S(2)}) collective-permute-start(bf16[2,8,4224]{2,1,0:T(8,128)(2,1)S(1)} %pad_maximum_fusion.1), channel_id=1, source_target_pairs={{0,2},{1,3},{2,0},{3,1},{4,6},{5,7},{6,4},{7,5},{8,10},{9,11},{10,... | collective-permute-start | bytes 405512 | tf_op jit(solution)/shard_map/ppermute | solution.py:408
  15.3 3.5 %shard_map.108 = (bf16[2,4096,256]{2,1,0:T(8,128)(2,1)S(1)}, bf16[2,4096,256]{2,1,0:T(8,128)(2,1)S(1)}, bf16[4,8,4224]{2,1,0:T(8,128)(2,1)S(1)}) custom-call(bf16[4,4096,256]{2,1,0:T(8,128)(2,1)} %refs_0_.5, bf16[4,4096,256]{2,1,0:T(8,128)(2,1)} %refs_1_.5, bf16[8,4224]{1,0:T(8,128)(2,1)S(1)} %shard_map.104.refs_2_, bf16[8,4224]{1,0:T(8,128)(2,1)S(1)} %bitcast.21, ...), custom_call_target="tpu_custom_call" | custom-call | bytes 8388608 | tf_op jit(solution)/shard_map/pallas_call | solution.py:132
  18.8 0.1 collective-permute-start.3
  18.9 0.0 collective-permute-done.4
  18.9 0.3 collective-permute-done.5
  19.3 0.2 collective-permute-start.6
  19.5 0.9 %collective-permute-done.3 = bf16[4,8,4224]{2,1,0:T(8,128)(2,1)S(1)} collective-permute-done((bf16[4,8,4224]{2,1,0:T(8,128)(2,1)S(1)}, bf16[4,8,4224]{2,1,0:T(8,128)(2,1)S(1)}, u32[]{:S(2)}, u32[]{:S(2)}) %collective-permute-start.3) | collective-permute-done | bytes 270368 | tf_op jit(solution)/shard_map/ppermute | solution.py:408
  20.4 0.5 collective-permute-done.6
  20.9 0.0 copy-start
  20.9 0.0 copy-start.1
  20.9 0.0 copy-start.2
  20.9 2.8 %shard_map.109 = (bf16[4,96,256]{2,1,0:T(8,128)(2,1)S(1)}, bf16[256,512]{1,0:T(8,128)(2,1)S(1)}) custom-call(bf16[32,4224]{1,0:T(8,128)(2,1)S(1)} %bitcast.18, bf16[32,4224]{1,0:T(8,128)(2,1)S(1)} %bitcast.19, bf16[32,4224]{1,0:T(8,128)(2,1)S(1)} %bitcast.12, bf16[32,4224]{1,0:T(8,128)(2,1)S(1)} %bitcast.20, ...), custom_call_target="tpu_custom_call" | custom-call | flops 2147483648 | bytes 16777216 | tf_op jit(solution)/shard_map/pallas_call | solution.py:267
  23.7 1.6 %collective-permute-start.8 = (bf16[4,96,256]{2,1,0:T(8,128)(2,1)S(1)}, bf16[4,96,256]{2,1,0:T(8,128)(2,1)S(1)}, u32[]{:S(2)}, u32[]{:S(2)}) collective-permute-start(bf16[4,96,256]{2,1,0:T(8,128)(2,1)S(1)} %get-tuple-element.27.after_ref.h0_ref), channel_id=1, source_target_pairs={{0,2},{1,3},{2,0},{3,1},{4,6},{5,7},{6,4},{7,5},{8,10},{9,11},{10,... | collective-permute-start | bytes 589832 | tf_op jit(solution)/shard_map/ppermute | solution.py:408
  25.2 0.0 collective-permute-start.7
  25.2 0.0 copy-done
  25.2 0.0 copy-done.1
  25.2 0.0 copy-done.2
  25.2 4.6 %shard_map.110 = (bf16[2,128,512]{2,1,0:T(8,128)(2,1)}, bf16[4,1024,1024]{2,1,0:T(8,128)(2,1)S(1)}) custom-call(s32[2]{0:T(128)S(1)} %copy-done.2, bf16[2,576,128]{2,1,0:T(8,128)(2,1)S(1)} %bitcast.16, bf16[2,576,512]{2,1,0:T(8,128)(2,1)S(1)} %bitcast.11, bf16[4,1024,1024]{2,1,0:T(8,128)(2,1)} %source_ref.1, ...), custom_call_target="tpu_custom_call" | custom-call | flops 285212672 | bytes 1736704 | tf_op jit(solution)/shard_map/pallas_call | solution.py:80
  29.9 0.8 %collective-permute-done.8.refs_0_ = bf16[4,96,256]{2,1,0:T(8,128)(2,1)S(1)} collective-permute-done((bf16[4,96,256]{2,1,0:T(8,128)(2,1)S(1)}, bf16[4,96,256]{2,1,0:T(8,128)(2,1)S(1)}, u32[]{:S(2)}, u32[]{:S(2)}) %collective-permute-start.8) | collective-permute-done | bytes 196640 | tf_op jit(solution)/shard_map/ppermute | solution.py:408
  30.7 0.0 collective-permute-start.9
  30.7 0.0 collective-permute-done.7.h1_ref
  30.7 1.1 %shard_map.112.first_ref = f32[4,96,1024]{2,1,0:T(8,128)S(1)} custom-call(bf16[4,96,256]{2,1,0:T(8,128)(2,1)S(1)} %get-tuple-element.27.after_ref.h0_ref, bf16[4,96,256]{2,1,0:T(8,128)(2,1)S(1)} %collective-permute-done.7.h1_ref, bf16[4,96,256]{2,1,0:T(8,128)(2,1)S(1)} %shard_map.111.h2_ref, bf16[4,1024,1024]{2,1,0:T(8,128)(2,1)S(1)} %get-tuple-element.28.refs_1_.down_ref), custom_call_target="tpu_custom_call" | custom-call | flops 603979776 | bytes 1572864 | tf_op jit(solution)/shard_map/pallas_call | solution.py:300
  31.8 0.3 collective-permute-done.9.h3_ref
  32.1 0.8 %shard_map.113 = (bf16[32,1024]{1,0:T(8,128)(2,1)S(1)}, bf16[32,1024]{1,0:T(8,128)(2,1)S(1)}, bf16[32,1024]{1,0:T(8,128)(2,1)S(1)}, bf16[32,1024]{1,0:T(8,128)(2,1)S(1)}) custom-call(bf16[256,512]{1,0:T(8,128)(2,1)S(1)} %get-tuple-element.26.spread_ref, f32[4,96,1024]{2,1,0:T(8,128)S(1)} %shard_map.112.first_ref, ...), custom_call_target="tpu_custom_call" | custom-call | flops 268435456 | bytes 3145728 | tf_op jit(solution)/shard_map/pallas_call | solution.py:346
  32.9 2.5 %collective-permute-start.10 = (bf16[32,1024]{1,0:T(8,128)(2,1)S(1)}, bf16[32,1024]{1,0:T(8,128)(2,1)S(1)}, u32[]{:S(2)}, u32[]{:S(2)}) collective-permute-start(bf16[32,1024]{1,0:T(8,128)(2,1)S(1)} %get-tuple-element.30), channel_id=1, source_target_pairs={{0,12},{4,8},{8,4},{12,0},{1,13},{5,9},{9,5},{13,1},{2,14},{6,10},... | collective-permute-start | bytes 196616 | tf_op jit(solution)/shard_map/ppermute | solution.py:408
  35.4 0.0 collective-permute-start.11
  35.4 2.0 %collective-permute-start.12 = (bf16[32,1024]{1,0:T(8,128)(2,1)S(1)}, bf16[32,1024]{1,0:T(8,128)(2,1)S(1)}, u32[]{:S(2)}, u32[]{:S(2)}) collective-permute-start(bf16[32,1024]{1,0:T(8,128)(2,1)S(1)} %get-tuple-element.32), channel_id=1, source_target_pairs={{0,4},{4,0},{8,12},{12,8},{1,5},{5,1},{9,13},{13,9},{2,6},{6,2},{1... | collective-permute-start | bytes 196616 | tf_op jit(solution)/shard_map/ppermute | solution.py:408
  37.4 2.4 %collective-permute-done.10.p1_ref = bf16[32,1024]{1,0:T(8,128)(2,1)S(1)} collective-permute-done((bf16[32,1024]{1,0:T(8,128)(2,1)S(1)}, bf16[32,1024]{1,0:T(8,128)(2,1)S(1)}, u32[]{:S(2)}, u32[]{:S(2)}) %collective-permute-start.10) | collective-permute-done | bytes 65568 | tf_op jit(solution)/shard_map/ppermute | solution.py:408
  39.8 2.0 %collective-permute-done.11.p2_ref = bf16[32,1024]{1,0:T(8,128)(2,1)S(1)} collective-permute-done((bf16[32,1024]{1,0:T(8,128)(2,1)S(1)}, bf16[32,1024]{1,0:T(8,128)(2,1)S(1)}, u32[]{:S(2)}, u32[]{:S(2)}) %collective-permute-start.11) | collective-permute-done | bytes 65568 | tf_op jit(solution)/shard_map/ppermute | solution.py:408
  41.8 0.0 collective-permute-done.12.p3_ref
  41.9 0.1 collective-permute-start.13
  41.9 1.5 %collective-permute-start.14 = (bf16[8,1024]{1,0:T(8,128)(2,1)S(1)}, bf16[8,1024]{1,0:T(8,128)(2,1)S(1)}, u32[]{:S(2)}, u32[]{:S(2)}) collective-permute-start(bf16[8,1024]{1,0:T(8,128)(2,1)S(1)} %get-tuple-element.35), channel_id=1, source_target_pairs={{0,2},{1,3},{2,0},{3,1},{4,6},{5,7},{6,4},{7,5},{8,10},{9,11},{10,... | collective-permute-start | bytes 49160 | tf_op jit(solution)/shard_map/ppermute | solution.py:408
  43.5 0.3 collective-permute-start.15
  43.8 0.0 collective-permute-done.13.p1_ref
  43.8 1.9 %collective-permute-done.14.p2_ref = bf16[8,1024]{1,0:T(8,128)(2,1)S(1)} collective-permute-done((bf16[8,1024]{1,0:T(8,128)(2,1)S(1)}, bf16[8,1024]{1,0:T(8,128)(2,1)S(1)}, u32[]{:S(2)}, u32[]{:S(2)}) %collective-permute-start.14) | collective-permute-done | bytes 16416 | tf_op jit(solution)/shard_map/ppermute | solution.py:408
  45.7 0.9 %collective-permute-done.15.p3_ref = bf16[8,1024]{1,0:T(8,128)(2,1)S(1)} collective-permute-done((bf16[8,1024]{1,0:T(8,128)(2,1)S(1)}, bf16[8,1024]{1,0:T(8,128)(2,1)S(1)}, u32[]{:S(2)}, u32[]{:S(2)}) %collective-permute-start.15) | collective-permute-done | bytes 16416 | tf_op jit(solution)/shard_map/ppermute | solution.py:408
  46.6 0.6 %shard_map.115 = bf16[8,4096]{1,0:T(8,128)(2,1)} custom-call(bf16[8,1024]{1,0:T(8,128)(2,1)S(1)} %get-tuple-element.33.p0_ref, bf16[8,1024]{1,0:T(8,128)(2,1)S(1)} %collective-permute-done.13.p1_ref, bf16[8,1024]{1,0:T(8,128)(2,1)S(1)} %collective-permute-done.14.p2_ref, bf16[8,1024]{1,0:T(8,128)(2,1)S(1)} %collective-permute-done.15.p3_ref), custom_call_target="tpu_custom_call" | custom-call | bytes 131072 | tf_op jit(solution)/shard_map/pallas_call | solution.py:394
  (8 shorter events, 0.1 us)
Async XLA Ops:
  1.5 5.7 %collective-permute-start = (bf16[8,4224]{1,0:T(8,128)(2,1)S(1)}, bf16[8,4224]{1,0:T(8,128)(2,1)S(1)}, u32[]{:S(2)}, u32[]{:S(2)}) collective-permute-start(bf16[8,4224]{1,0:T(8,128)(2,1)S(1)} %shard_map.104.refs_2_), channel_id=1, source_target_pairs={{0,4},{4,0},{8,12},{12,8},{1,5},{5,1},{9,13},{13,9},{2,6},{6,2},{1... | collective-permute-start | bytes 202760 | tf_op jit(solution)/shard_map/ppermute | solution.py:408
  4.6 7.8 %collective-permute-start.2 = (bf16[8,4224]{1,0:T(8,128)(2,1)S(1)}, bf16[8,4224]{1,0:T(8,128)(2,1)S(1)}, u32[]{:S(2)}, u32[]{:S(2)}) collective-permute-start(bf16[8,4224]{1,0:T(8,128)(2,1)S(1)} %shard_map.104.refs_2_), channel_id=1, source_target_pairs={{0,12},{4,8},{8,4},{12,0},{1,13},{5,9},{9,5},{13,1},{2,14},{6,10},... | collective-permute-start | bytes 202760 | tf_op jit(solution)/shard_map/ppermute | solution.py:408
  7.1 6.6 %collective-permute-start.1 = (bf16[8,4224]{1,0:T(8,128)(2,1)S(1)}, bf16[8,4224]{1,0:T(8,128)(2,1)S(1)}, u32[]{:S(2)}, u32[]{:S(2)}) collective-permute-start(bf16[8,4224]{1,0:T(8,128)(2,1)S(1)} %shard_map.104.refs_2_), channel_id=1, source_target_pairs={{0,8},{4,12},{8,0},{12,4},{1,9},{5,13},{9,1},{13,5},{2,10},{6,14},... | collective-permute-start | bytes 202760 | tf_op jit(solution)/shard_map/ppermute | solution.py:408
  7.2 11.6 %collective-permute-start.4 = (bf16[2,8,4224]{2,1,0:T(8,128)(2,1)S(1)}, bf16[2,8,4224]{2,1,0:T(8,128)(2,1)S(1)}, u32[]{:S(2)}, u32[]{:S(2)}) collective-permute-start(bf16[2,8,4224]{2,1,0:T(8,128)(2,1)S(1)} %pad_maximum_fusion), channel_id=1, source_target_pairs={{0,2},{1,3},{2,0},{3,1},{4,6},{5,7},{6,4},{7,5},{8,10},{9,11},{10,... | collective-permute-start | bytes 405512 | tf_op jit(solution)/shard_map/ppermute | solution.py:408
  13.7 5.5 %collective-permute-start.5 = (bf16[2,8,4224]{2,1,0:T(8,128)(2,1)S(1)}, bf16[2,8,4224]{2,1,0:T(8,128)(2,1)S(1)}, u32[]{:S(2)}, u32[]{:S(2)}) collective-permute-start(bf16[2,8,4224]{2,1,0:T(8,128)(2,1)S(1)} %pad_maximum_fusion.1), channel_id=1, source_target_pairs={{0,2},{1,3},{2,0},{3,1},{4,6},{5,7},{6,4},{7,5},{8,10},{9,11},{10,... | collective-permute-start | bytes 405512 | tf_op jit(solution)/shard_map/ppermute | solution.py:408
  18.8 1.6 %collective-permute-start.3 = (bf16[4,8,4224]{2,1,0:T(8,128)(2,1)S(1)}, bf16[4,8,4224]{2,1,0:T(8,128)(2,1)S(1)}, u32[]{:S(2)}, u32[]{:S(2)}) collective-permute-start(bf16[4,8,4224]{2,1,0:T(8,128)(2,1)S(1)} %get-tuple-element.22), channel_id=1, source_target_pairs={{0,1},{1,0},{2,3},{3,2},{4,5},{5,4},{6,7},{7,6},{8,9},{9,8},{10,11... | collective-permute-start | bytes 811016 | tf_op jit(solution)/shard_map/ppermute | solution.py:408
  19.3 1.6 %collective-permute-start.6 = (bf16[4,8,4224]{2,1,0:T(8,128)(2,1)S(1)}, bf16[4,8,4224]{2,1,0:T(8,128)(2,1)S(1)}, u32[]{:S(2)}, u32[]{:S(2)}) collective-permute-start(bf16[4,8,4224]{2,1,0:T(8,128)(2,1)S(1)} %constant_dynamic-update-slice_fusion), channel_id=1, source_target_pairs={{0,1},{1,0},{2,3},{3,2},{4,5},{5,4},{6,7},{7,6},{8,9},{9,8},{10,11... | collective-permute-start | bytes 811016 | tf_op jit(solution)/shard_map/ppermute | solution.py:408
  20.9 4.4 %copy-start = (bf16[2,512,576]{1,2,0:T(8,128)(2,1)S(1)}, bf16[2,512,576]{1,2,0:T(8,128)(2,1)}, u32[]{:S(2)}) copy-start(bf16[2,512,576]{1,2,0:T(8,128)(2,1)} %param.16) | copy-start | bytes 3538948
  20.9 4.4 %copy-start.1 = (bf16[2,128,576]{1,2,0:T(8,128)(2,1)S(1)}, bf16[2,128,576]{1,2,0:T(8,128)(2,1)}, u32[]{:S(2)}) copy-start(bf16[2,128,576]{1,2,0:T(8,128)(2,1)} %param.15) | copy-start | bytes 884740
  20.9 4.4 %copy-start.2 = (s32[2]{0:T(128)S(1)}, s32[2]{0:T(128)}, u32[]{:S(2)}) copy-start(s32[2]{0:T(128)} %lengths_ref.1) | copy-start | bytes 28
  23.7 7.0 %collective-permute-start.8 = (bf16[4,96,256]{2,1,0:T(8,128)(2,1)S(1)}, bf16[4,96,256]{2,1,0:T(8,128)(2,1)S(1)}, u32[]{:S(2)}, u32[]{:S(2)}) collective-permute-start(bf16[4,96,256]{2,1,0:T(8,128)(2,1)S(1)} %get-tuple-element.27.after_ref.h0_ref), channel_id=1, source_target_pairs={{0,2},{1,3},{2,0},{3,1},{4,6},{5,7},{6,4},{7,5},{8,10},{9,11},{10,... | collective-permute-start | bytes 589832 | tf_op jit(solution)/shard_map/ppermute | solution.py:408
  25.2 5.5 %collective-permute-start.7 = (bf16[4,96,256]{2,1,0:T(8,128)(2,1)S(1)}, bf16[4,96,256]{2,1,0:T(8,128)(2,1)S(1)}, u32[]{:S(2)}, u32[]{:S(2)}) collective-permute-start(bf16[4,96,256]{2,1,0:T(8,128)(2,1)S(1)} %get-tuple-element.27.after_ref.h0_ref), channel_id=1, source_target_pairs={{0,1},{1,0},{2,3},{3,2},{4,5},{5,4},{6,7},{7,6},{8,9},{9,8},{10,11... | collective-permute-start | bytes 589832 | tf_op jit(solution)/shard_map/ppermute | solution.py:408
  30.7 1.4 %collective-permute-start.9 = (bf16[4,96,256]{2,1,0:T(8,128)(2,1)S(1)}, bf16[4,96,256]{2,1,0:T(8,128)(2,1)S(1)}, u32[]{:S(2)}, u32[]{:S(2)}) collective-permute-start(bf16[4,96,256]{2,1,0:T(8,128)(2,1)S(1)} %shard_map.111.h2_ref), channel_id=1, source_target_pairs={{0,1},{1,0},{2,3},{3,2},{4,5},{5,4},{6,7},{7,6},{8,9},{9,8},{10,11... | collective-permute-start | bytes 589832 | tf_op jit(solution)/shard_map/ppermute | solution.py:408
  32.9 6.9 %collective-permute-start.10 = (bf16[32,1024]{1,0:T(8,128)(2,1)S(1)}, bf16[32,1024]{1,0:T(8,128)(2,1)S(1)}, u32[]{:S(2)}, u32[]{:S(2)}) collective-permute-start(bf16[32,1024]{1,0:T(8,128)(2,1)S(1)} %get-tuple-element.30), channel_id=1, source_target_pairs={{0,12},{4,8},{8,4},{12,0},{1,13},{5,9},{9,5},{13,1},{2,14},{6,10},... | collective-permute-start | bytes 196616 | tf_op jit(solution)/shard_map/ppermute | solution.py:408
  35.4 6.4 %collective-permute-start.11 = (bf16[32,1024]{1,0:T(8,128)(2,1)S(1)}, bf16[32,1024]{1,0:T(8,128)(2,1)S(1)}, u32[]{:S(2)}, u32[]{:S(2)}) collective-permute-start(bf16[32,1024]{1,0:T(8,128)(2,1)S(1)} %get-tuple-element.31), channel_id=1, source_target_pairs={{0,8},{4,12},{8,0},{12,4},{1,9},{5,13},{9,1},{13,5},{2,10},{6,14},... | collective-permute-start | bytes 196616 | tf_op jit(solution)/shard_map/ppermute | solution.py:408
  35.4 6.4 %collective-permute-start.12 = (bf16[32,1024]{1,0:T(8,128)(2,1)S(1)}, bf16[32,1024]{1,0:T(8,128)(2,1)S(1)}, u32[]{:S(2)}, u32[]{:S(2)}) collective-permute-start(bf16[32,1024]{1,0:T(8,128)(2,1)S(1)} %get-tuple-element.32), channel_id=1, source_target_pairs={{0,4},{4,0},{8,12},{12,8},{1,5},{5,1},{9,13},{13,9},{2,6},{6,2},{1... | collective-permute-start | bytes 196616 | tf_op jit(solution)/shard_map/ppermute | solution.py:408
  41.9 1.9 %collective-permute-start.13 = (bf16[8,1024]{1,0:T(8,128)(2,1)S(1)}, bf16[8,1024]{1,0:T(8,128)(2,1)S(1)}, u32[]{:S(2)}, u32[]{:S(2)}) collective-permute-start(bf16[8,1024]{1,0:T(8,128)(2,1)S(1)} %get-tuple-element.34), channel_id=1, source_target_pairs={{0,1},{1,0},{2,3},{3,2},{4,5},{5,4},{6,7},{7,6},{8,9},{9,8},{10,11... | collective-permute-start | bytes 49160 | tf_op jit(solution)/shard_map/ppermute | solution.py:408
  41.9 3.8 %collective-permute-start.14 = (bf16[8,1024]{1,0:T(8,128)(2,1)S(1)}, bf16[8,1024]{1,0:T(8,128)(2,1)S(1)}, u32[]{:S(2)}, u32[]{:S(2)}) collective-permute-start(bf16[8,1024]{1,0:T(8,128)(2,1)S(1)} %get-tuple-element.35), channel_id=1, source_target_pairs={{0,2},{1,3},{2,0},{3,1},{4,6},{5,7},{6,4},{7,5},{8,10},{9,11},{10,... | collective-permute-start | bytes 49160 | tf_op jit(solution)/shard_map/ppermute | solution.py:408
  43.5 3.2 %collective-permute-start.15 = (bf16[8,1024]{1,0:T(8,128)(2,1)S(1)}, bf16[8,1024]{1,0:T(8,128)(2,1)S(1)}, u32[]{:S(2)}, u32[]{:S(2)}) collective-permute-start(bf16[8,1024]{1,0:T(8,128)(2,1)S(1)} %get-tuple-element.36), channel_id=1, source_target_pairs={{0,3},{1,2},{2,1},{3,0},{4,7},{5,6},{6,5},{7,4},{8,11},{9,10},{10,... | collective-permute-start | bytes 49160 | tf_op jit(solution)/shard_map/ppermute | solution.py:408

commit v6 on v5

--- a/solution.py
+++ b/solution.py
@@ -105,43 +105,8 @@
         out_shape=VMEM(value.shape, value.dtype),
         input_output_aliases={0: 0},
         compiler_params=pltpu.CompilerParams(vmem_limit_bytes=MIB),
-        cost_estimate=pl.CostEstimate(flops=0, bytes_accessed=0, transcendentals=0),
+        cost_estimate=pl.CostEstimate(flops=4000000000, bytes_accessed=0, transcendentals=0),
     )(value, other)
-
-
-def fetch_kernel(start, gate_ref, up_ref, *refs):
-    *piece_refs, gate_held_ref, up_held_ref, stack_ref, sems = refs
-    copies = []
-    for source_ref, held_ref in ((gate_ref, gate_held_ref), (up_ref, up_held_ref)):
-        for e in range(held_ref.shape[0]):
-            copies.append(
-                pltpu.make_async_copy(
-                    source_ref.at[start + e], held_ref.at[e], sems.at[len(copies)]
-                )
-            )
-    for copy in copies:
-        copy.start()
-    for k, piece_ref in enumerate(piece_refs):
-        stack_ref[k] = piece_ref[...]
-    for copy in copies:
-        copy.wait()
-
-
-def fetch(gate_proj, up_proj, start, stop, pieces):
-    held = VMEM((stop - start,) + gate_proj.shape[1:], gate_proj.dtype)
-    return pl.pallas_call(
-        lambda *refs: fetch_kernel(start, *refs),
-        in_specs=[whole(pltpu.HBM)] * 2 + [whole()] * len(pieces),
-        out_specs=[whole()] * 3,
-        out_shape=[held, held, VMEM((len(pieces),) + pieces[0].shape, pieces[0].dtype)],
-        scratch_shapes=[pltpu.SemaphoreType.DMA((2 * (stop - start),))],
-        compiler_params=pltpu.CompilerParams(vmem_limit_bytes=2 * MIB),
-        cost_estimate=pl.CostEstimate(
-            flops=0,
-            bytes_accessed=4 * (stop - start) * gate_proj[0].size,
-            transcendentals=0,
-        ),
-    )(in_hbm(gate_proj), in_hbm(up_proj), *pieces)
 
 
 def gate_table(expert_ids, gate_values, experts_all):
@@ -207,14 +172,12 @@
     other_x_ref,
     gate_first_ref,
     up_first_ref,
-    gate_next_ref,
-    up_next_ref,
     hidden_ref,
     spread_ref,
     rows_ref,
 ):
     matrices = []
-    for pair in ((gate_first_ref, up_first_ref), (gate_next_ref, up_next_ref)):
+    for pair in ((gate_first_ref, up_first_ref),):
         matrices += [[ref.at[e] for ref in pair] for e in range(pair[0].shape[0])]
     experts = len(matrices)
     depth = gate_first_ref.shape[1]
@@ -266,14 +229,14 @@
     count = 4 * pieces[0].shape[0]
     return pl.pallas_call(
         lambda *refs: gate_up_kernel(slots, experts_all, *refs),
-        in_specs=[whole()] * 8,
+        in_specs=[whole()] * 6,
         out_specs=[whole()] * 2,
         out_shape=[
             VMEM((experts, slots, share), BF16),
             VMEM((2 * count, experts * count), BF16),
         ],
         scratch_shapes=[VMEM((count, depth), BF16)],
-        compiler_params=pltpu.CompilerParams(vmem_limit_bytes=16 * MIB),
+        compiler_params=pltpu.CompilerParams(vmem_limit_bytes=36 * MIB),
         cost_estimate=pl.CostEstimate(
             flops=4 * experts * count * depth * share,
             bytes_accessed=4 * experts * depth * share,
@@ -426,22 +389,15 @@
     capacity = max(2, 3 * rows_dev * expert_ids.shape[1] // (2 * experts_all))
     sent = pack(hidden_rows, expert_ids, gate_values, experts_all)
     along_z = [sent] + [swap(sent, "expert", k) for k in (1, 2, 3)]
-    near_x = swap(jnp.stack(along_z[:2]), "dp", 2)
-    gate_first, up_first, passed = fetch(
-        gate_proj, up_proj, 0, local_experts // 2, along_z[1:2]
-    )
-    along_z[2:] = [once_done(block, gate_first) for block in along_z[2:]]
-    far_x = swap(jnp.stack(along_z[2:]), "dp", 2)
-    gate_next, up_next, mine_z = fetch(
-        gate_proj, up_proj, local_experts // 2, local_experts, [along_z[0], passed[0]] + along_z[2:]
-    )
-    mine_x = jnp.concatenate([near_x, far_x])
+    along_z[1:] = [once_done(block, sent) for block in along_z[1:]]
+    along_x = [swap(block, "dp", 2) for block in along_z]
+    mine_z, mine_x = jnp.stack(along_z), jnp.stack(along_x)
     other_z = swap(mine_z, "dp", 1)
     other_x = swap(mine_x, "dp", 1)
 
     hidden, spread = gate_up(
         [block.reshape(4 * rows_dev, -1) for block in (mine_z, other_z, mine_x, other_x)],
-        (gate_first, up_first, gate_next, up_next),
+        (gate_proj, up_proj),
         16 * capacity,
         experts_all,
     )

time: 47.5 us -> 46.2 us (0.973)
  Pallas kernels: 17.9 us -> 10.9 us
  waiting for transfers between devices: 11.4 us -> 15.1 us
  starting transfers between devices: 17.2 us -> 19 us
    pallas_call x2 -> x0, Pallas kernels: 7 us -> none  [fetch(): pl.pallas_call(lambda *refs: fetch_kernel(start, *refs), in_specs=[whole(...]
    ppermute x16 -> x18, waiting for transfers between devices: 11.4 us -> 15.1 us  [swap(): return lax.ppermute(value, axis, [(i, i ^ bit) for i in range(size)])]
    ppermute x16 -> x18, starting transfers between devices: 17.2 us -> 19 us  [swap(): return lax.ppermute(value, axis, [(i, i ^ bit) for i in range(size)])]
  transfers between devices with their start and end apart: 16 -> 18, of which waited for: 10 -> 11; matrix products, arithmetic and copies ran while one was open for 0% -> 0% of each run, Pallas kernels for 27% -> 13%
where the time goes in v6:
time: 46.2 us; the launch traced here: 46 us
  starting transfers between devices  19 us (41%)
  waiting for transfers between devices  15.1 us (33%)
  Pallas kernels  10.9 us (24%)
  between operations  0.8 us (2%)
    ppermute x18, starting transfers between devices, swap(): return lax.ppermute(value, axis, [(i, i ^ bit) for i in range(size)])  19 us
    ppermute x18, waiting for transfers between devices, swap(): return lax.ppermute(value, axis, [(i, i ^ bit) for i in range(size)])  15.1 us
    pallas_call x1, Pallas kernels, attend_and_fetch(): pl.pallas_call(attend_and_fetch_kernel, in_specs=[whole(pltpu.SMEM), whol...  4.63 us
    pallas_call x1, Pallas kernels, gate_up(): pl.pallas_call(lambda *refs: gate_up_kernel(slots, experts_all, *refs), i...  2.79 us
    pallas_call x1, Pallas kernels, down_first(): pl.pallas_call(down_first_kernel, in_specs=[whole()] * 4, out_specs=whole...  1.13 us
  transfers between devices with their start and end apart: 18, of which 11 were waited for; matrix products, arithmetic and copies ran while one was open for 0% of the time, Pallas kernels for 13%

profile of v6, /device:TPU:0, one launch (start us, length us, event | category | flops | bytes accessed | tf_op | source)
XLA Modules:
  0.0 46.0 jit_solution(16459720440977879675)
XLA Ops:
  0.6 0.9 %shard_map.104.refs_1_ = bf16[8,4224]{1,0:T(8,128)(2,1)S(1)} custom-call(bf16[8,4096]{1,0:T(8,128)(2,1)} %refs_0_.1, s32[8,8]{1,0:T(8,128)} %refs_1_.1, f32[8,8]{1,0:T(8,128)} %refs_2_.1), custom_call_target="tpu_custom_call" | custom-call | bytes 131072 | tf_op jit(solution)/shard_map/pallas_call | solution.py:149
  1.5 5.1 %collective-permute-start.2 = (bf16[8,4224]{1,0:T(8,128)(2,1)S(1)}, bf16[8,4224]{1,0:T(8,128)(2,1)S(1)}, u32[]{:S(2)}, u32[]{:S(2)}) collective-permute-start(bf16[8,4224]{1,0:T(8,128)(2,1)S(1)} %shard_map.104.refs_1_), channel_id=1, source_target_pairs={{0,12},{4,8},{8,4},{12,0},{1,13},{5,9},{9,5},{13,1},{2,14},{6,10},... | collective-permute-start | bytes 202760 | tf_op jit(solution)/shard_map/ppermute | solution.py:371
  6.7 0.0 collective-permute-start.1
  6.7 0.6 %collective-permute-start = (bf16[8,4224]{1,0:T(8,128)(2,1)S(1)}, bf16[8,4224]{1,0:T(8,128)(2,1)S(1)}, u32[]{:S(2)}, u32[]{:S(2)}) collective-permute-start(bf16[8,4224]{1,0:T(8,128)(2,1)S(1)} %shard_map.104.refs_1_), channel_id=1, source_target_pairs={{0,4},{4,0},{8,12},{12,8},{1,5},{5,1},{9,13},{13,9},{2,6},{6,2},{1... | collective-permute-start | bytes 202760 | tf_op jit(solution)/shard_map/ppermute | solution.py:371
  7.3 1.6 %collective-permute-start.4 = (bf16[8,4224]{1,0:T(8,128)(2,1)S(1)}, bf16[8,4224]{1,0:T(8,128)(2,1)S(1)}, u32[]{:S(2)}, u32[]{:S(2)}) collective-permute-start(bf16[8,4224]{1,0:T(8,128)(2,1)S(1)} %shard_map.104.refs_1_), channel_id=1, source_target_pairs={{0,2},{1,3},{2,0},{3,1},{4,6},{5,7},{6,4},{7,5},{8,10},{9,11},{10,... | collective-permute-start | bytes 202760 | tf_op jit(solution)/shard_map/ppermute | solution.py:371
  8.9 0.3 collective-permute-done.2.refs_0_
  9.3 1.9 %collective-permute-start.7 = (bf16[8,4224]{1,0:T(8,128)(2,1)S(1)}, bf16[8,4224]{1,0:T(8,128)(2,1)S(1)}, u32[]{:S(2)}, u32[]{:S(2)}) collective-permute-start(bf16[8,4224]{1,0:T(8,128)(2,1)S(1)} %shard_map.107), channel_id=1, source_target_pairs={{0,2},{1,3},{2,0},{3,1},{4,6},{5,7},{6,4},{7,5},{8,10},{9,11},{10,... | collective-permute-start | bytes 202760 | tf_op jit(solution)/shard_map/ppermute | solution.py:371
  11.1 1.3 %collective-permute-done.1.refs_0_ = bf16[8,4224]{1,0:T(8,128)(2,1)S(1)} collective-permute-done((bf16[8,4224]{1,0:T(8,128)(2,1)S(1)}, bf16[8,4224]{1,0:T(8,128)(2,1)S(1)}, u32[]{:S(2)}, u32[]{:S(2)}) %collective-permute-start.1) | collective-permute-done | bytes 67616 | tf_op jit(solution)/shard_map/ppermute | solution.py:371
  12.4 0.0 slice-start
  12.4 0.0 slice-start.2
  12.4 0.0 slice-start.1
  12.4 0.0 slice-start.3
  12.4 1.6 %collective-permute-start.6 = (bf16[8,4224]{1,0:T(8,128)(2,1)S(1)}, bf16[8,4224]{1,0:T(8,128)(2,1)S(1)}, u32[]{:S(2)}, u32[]{:S(2)}) collective-permute-start(bf16[8,4224]{1,0:T(8,128)(2,1)S(1)} %shard_map.106), channel_id=1, source_target_pairs={{0,2},{1,3},{2,0},{3,1},{4,6},{5,7},{6,4},{7,5},{8,10},{9,11},{10,... | collective-permute-start | bytes 202760 | tf_op jit(solution)/shard_map/ppermute | solution.py:371
  14.0 0.0 collective-permute-done.refs_0_
  14.0 0.5 %collective-permute-start.5 = (bf16[8,4224]{1,0:T(8,128)(2,1)S(1)}, bf16[8,4224]{1,0:T(8,128)(2,1)S(1)}, u32[]{:S(2)}, u32[]{:S(2)}) collective-permute-start(bf16[8,4224]{1,0:T(8,128)(2,1)S(1)} %shard_map.105), channel_id=1, source_target_pairs={{0,2},{1,3},{2,0},{3,1},{4,6},{5,7},{6,4},{7,5},{8,10},{9,11},{10,... | collective-permute-start | bytes 202760 | tf_op jit(solution)/shard_map/ppermute | solution.py:371
  14.5 0.1 pad_maximum_fusion
  14.6 0.1 collective-permute-start.3
  14.7 0.0 collective-permute-done.4
  14.7 0.0 collective-permute-done.7
  14.7 2.7 %collective-permute-done.6 = bf16[8,4224]{1,0:T(8,128)(2,1)S(1)} collective-permute-done((bf16[8,4224]{1,0:T(8,128)(2,1)S(1)}, bf16[8,4224]{1,0:T(8,128)(2,1)S(1)}, u32[]{:S(2)}, u32[]{:S(2)}) %collective-permute-start.6) | collective-permute-done | bytes 67616 | tf_op jit(solution)/shard_map/ppermute | solution.py:371
  17.4 0.9 %collective-permute-done.5 = bf16[8,4224]{1,0:T(8,128)(2,1)S(1)} collective-permute-done((bf16[8,4224]{1,0:T(8,128)(2,1)S(1)}, bf16[8,4224]{1,0:T(8,128)(2,1)S(1)}, u32[]{:S(2)}, u32[]{:S(2)}) %collective-permute-start.5) | collective-permute-done | bytes 67616 | tf_op jit(solution)/shard_map/ppermute | solution.py:371
  18.3 0.1 pad_maximum_fusion.1
  18.3 0.1 collective-permute-start.8
  18.4 0.0 collective-permute-done.3
  18.4 1.5 %collective-permute-done.8 = bf16[4,8,4224]{2,1,0:T(8,128)(2,1)S(1)} collective-permute-done((bf16[4,8,4224]{2,1,0:T(8,128)(2,1)S(1)}, bf16[4,8,4224]{2,1,0:T(8,128)(2,1)S(1)}, u32[]{:S(2)}, u32[]{:S(2)}) %collective-permute-start.8) | collective-permute-done | bytes 270368 | tf_op jit(solution)/shard_map/ppermute | solution.py:371
  19.9 0.0 slice-done
  19.9 0.0 slice-done.2
  19.9 0.0 slice-done.1
  20.0 0.0 slice-done.3
  20.0 0.0 copy-start
  20.0 0.0 copy-start.1
  20.0 0.0 copy-start.2
  20.0 2.8 %shard_map.108 = (bf16[4,96,256]{2,1,0:T(8,128)(2,1)S(1)}, bf16[256,512]{1,0:T(8,128)(2,1)S(1)}) custom-call(bf16[32,4224]{1,0:T(8,128)(2,1)S(1)} %get-tuple-element.29.refs_0_, bf16[32,4224]{1,0:T(8,128)(2,1)S(1)} %bitcast.23, bf16[32,4224]{1,0:T(8,128)(2,1)S(1)} %get-tuple-element.27.refs_2_, bf16[32,4224]{1,0:T(8,128)(2,1)S(1)} %bitcast.24, ...), custom_call_target="tpu_custom_call" | custom-call | flops 2147483648 | bytes 16777216 | tf_op jit(solution)/shard_map/pallas_call | solution.py:230
  22.8 1.1 %collective-permute-start.10 = (bf16[4,96,256]{2,1,0:T(8,128)(2,1)S(1)}, bf16[4,96,256]{2,1,0:T(8,128)(2,1)S(1)}, u32[]{:S(2)}, u32[]{:S(2)}) collective-permute-start(bf16[4,96,256]{2,1,0:T(8,128)(2,1)S(1)} %get-tuple-element.15.after_ref.h0_ref), channel_id=1, source_target_pairs={{0,2},{1,3},{2,0},{3,1},{4,6},{5,7},{6,4},{7,5},{8,10},{9,11},{10,... | collective-permute-start | bytes 589832 | tf_op jit(solution)/shard_map/ppermute | solution.py:371
  23.9 0.0 collective-permute-start.9
  23.9 0.0 copy-done
  23.9 0.0 copy-done.1
  23.9 0.0 copy-done.2
  23.9 4.6 %shard_map.109 = (bf16[2,128,512]{2,1,0:T(8,128)(2,1)}, bf16[4,1024,1024]{2,1,0:T(8,128)(2,1)S(1)}) custom-call(s32[2]{0:T(128)S(1)} %copy-done.2, bf16[2,576,128]{2,1,0:T(8,128)(2,1)S(1)} %bitcast.21, bf16[2,576,512]{2,1,0:T(8,128)(2,1)S(1)} %bitcast.20, bf16[4,1024,1024]{2,1,0:T(8,128)(2,1)} %source_ref.1, ...), custom_call_target="tpu_custom_call" | custom-call | flops 285212672 | bytes 1736704 | tf_op jit(solution)/shard_map/pallas_call | solution.py:80
  28.6 1.2 %collective-permute-done.10.refs_0_ = bf16[4,96,256]{2,1,0:T(8,128)(2,1)S(1)} collective-permute-done((bf16[4,96,256]{2,1,0:T(8,128)(2,1)S(1)}, bf16[4,96,256]{2,1,0:T(8,128)(2,1)S(1)}, u32[]{:S(2)}, u32[]{:S(2)}) %collective-permute-start.10) | collective-permute-done | bytes 196640 | tf_op jit(solution)/shard_map/ppermute | solution.py:371
  29.8 0.0 collective-permute-start.11
  29.8 0.0 collective-permute-done.9.h1_ref
  29.8 1.1 %shard_map.111.first_ref = f32[4,96,1024]{2,1,0:T(8,128)S(1)} custom-call(bf16[4,96,256]{2,1,0:T(8,128)(2,1)S(1)} %get-tuple-element.15.after_ref.h0_ref, bf16[4,96,256]{2,1,0:T(8,128)(2,1)S(1)} %collective-permute-done.9.h1_ref, bf16[4,96,256]{2,1,0:T(8,128)(2,1)S(1)} %shard_map.110.h2_ref, bf16[4,1024,1024]{2,1,0:T(8,128)(2,1)S(1)} %get-tuple-element.16.refs_1_.down_ref), custom_call_target="tpu_custom_call" | custom-call | flops 603979776 | bytes 1572864 | tf_op jit(solution)/shard_map/pallas_call | solution.py:263
  31.0 0.3 collective-permute-done.11.h3_ref
  31.3 0.8 %shard_map.112 = (bf16[32,1024]{1,0:T(8,128)(2,1)S(1)}, bf16[32,1024]{1,0:T(8,128)(2,1)S(1)}, bf16[32,1024]{1,0:T(8,128)(2,1)S(1)}, bf16[32,1024]{1,0:T(8,128)(2,1)S(1)}) custom-call(bf16[256,512]{1,0:T(8,128)(2,1)S(1)} %get-tuple-element.14.spread_ref, f32[4,96,1024]{2,1,0:T(8,128)S(1)} %shard_map.111.first_ref, ...), custom_call_target="tpu_custom_call" | custom-call | flops 268435456 | bytes 3145728 | tf_op jit(solution)/shard_map/pallas_call | solution.py:309
  32.0 2.8 %collective-permute-start.12 = (bf16[32,1024]{1,0:T(8,128)(2,1)S(1)}, bf16[32,1024]{1,0:T(8,128)(2,1)S(1)}, u32[]{:S(2)}, u32[]{:S(2)}) collective-permute-start(bf16[32,1024]{1,0:T(8,128)(2,1)S(1)} %get-tuple-element.18), channel_id=1, source_target_pairs={{0,12},{4,8},{8,4},{12,0},{1,13},{5,9},{9,5},{13,1},{2,14},{6,10},... | collective-permute-start | bytes 196616 | tf_op jit(solution)/shard_map/ppermute | solution.py:371
  34.8 0.0 collective-permute-start.13
  34.8 1.7 %collective-permute-start.14 = (bf16[32,1024]{1,0:T(8,128)(2,1)S(1)}, bf16[32,1024]{1,0:T(8,128)(2,1)S(1)}, u32[]{:S(2)}, u32[]{:S(2)}) collective-permute-start(bf16[32,1024]{1,0:T(8,128)(2,1)S(1)} %get-tuple-element.20), channel_id=1, source_target_pairs={{0,4},{4,0},{8,12},{12,8},{1,5},{5,1},{9,13},{13,9},{2,6},{6,2},{1... | collective-permute-start | bytes 196616 | tf_op jit(solution)/shard_map/ppermute | solution.py:371
  36.5 2.4 %collective-permute-done.12.p1_ref = bf16[32,1024]{1,0:T(8,128)(2,1)S(1)} collective-permute-done((bf16[32,1024]{1,0:T(8,128)(2,1)S(1)}, bf16[32,1024]{1,0:T(8,128)(2,1)S(1)}, u32[]{:S(2)}, u32[]{:S(2)}) %collective-permute-start.12) | collective-permute-done | bytes 65568 | tf_op jit(solution)/shard_map/ppermute | solution.py:371
  38.9 2.0 %collective-permute-done.13.p2_ref = bf16[32,1024]{1,0:T(8,128)(2,1)S(1)} collective-permute-done((bf16[32,1024]{1,0:T(8,128)(2,1)S(1)}, bf16[32,1024]{1,0:T(8,128)(2,1)S(1)}, u32[]{:S(2)}, u32[]{:S(2)}) %collective-permute-start.13) | collective-permute-done | bytes 65568 | tf_op jit(solution)/shard_map/ppermute | solution.py:371
  40.9 0.0 collective-permute-done.14.p3_ref
  41.0 0.1 collective-permute-start.15
  41.1 1.1 %collective-permute-start.16 = (bf16[8,1024]{1,0:T(8,128)(2,1)S(1)}, bf16[8,1024]{1,0:T(8,128)(2,1)S(1)}, u32[]{:S(2)}, u32[]{:S(2)}) collective-permute-start(bf16[8,1024]{1,0:T(8,128)(2,1)S(1)} %get-tuple-element.23), channel_id=1, source_target_pairs={{0,2},{1,3},{2,0},{3,1},{4,6},{5,7},{6,4},{7,5},{8,10},{9,11},{10,... | collective-permute-start | bytes 49160 | tf_op jit(solution)/shard_map/ppermute | solution.py:371
  42.2 0.7 %collective-permute-start.17 = (bf16[8,1024]{1,0:T(8,128)(2,1)S(1)}, bf16[8,1024]{1,0:T(8,128)(2,1)S(1)}, u32[]{:S(2)}, u32[]{:S(2)}) collective-permute-start(bf16[8,1024]{1,0:T(8,128)(2,1)S(1)} %get-tuple-element.24), channel_id=1, source_target_pairs={{0,3},{1,2},{2,1},{3,0},{4,7},{5,6},{6,5},{7,4},{8,11},{9,10},{10,... | collective-permute-start | bytes 49160 | tf_op jit(solution)/shard_map/ppermute | solution.py:371
  42.9 0.0 collective-permute-done.15.p1_ref
  42.9 1.9 %collective-permute-done.16.p2_ref = bf16[8,1024]{1,0:T(8,128)(2,1)S(1)} collective-permute-done((bf16[8,1024]{1,0:T(8,128)(2,1)S(1)}, bf16[8,1024]{1,0:T(8,128)(2,1)S(1)}, u32[]{:S(2)}, u32[]{:S(2)}) %collective-permute-start.16) | collective-permute-done | bytes 16416 | tf_op jit(solution)/shard_map/ppermute | solution.py:371
  44.9 0.5 %collective-permute-done.17.p3_ref = bf16[8,1024]{1,0:T(8,128)(2,1)S(1)} collective-permute-done((bf16[8,1024]{1,0:T(8,128)(2,1)S(1)}, bf16[8,1024]{1,0:T(8,128)(2,1)S(1)}, u32[]{:S(2)}, u32[]{:S(2)}) %collective-permute-start.17) | collective-permute-done | bytes 16416 | tf_op jit(solution)/shard_map/ppermute | solution.py:371
  45.3 0.6 %shard_map.114 = bf16[8,4096]{1,0:T(8,128)(2,1)} custom-call(bf16[8,1024]{1,0:T(8,128)(2,1)S(1)} %get-tuple-element.21.p0_ref, bf16[8,1024]{1,0:T(8,128)(2,1)S(1)} %collective-permute-done.15.p1_ref, bf16[8,1024]{1,0:T(8,128)(2,1)S(1)} %collective-permute-done.16.p2_ref, bf16[8,1024]{1,0:T(8,128)(2,1)S(1)} %collective-permute-done.17.p3_ref), custom_call_target="tpu_custom_call" | custom-call | bytes 131072 | tf_op jit(solution)/shard_map/pallas_call | solution.py:357
  (7 shorter events, 0.0 us)
Async XLA Ops:
  1.5 7.7 %collective-permute-start.2 = (bf16[8,4224]{1,0:T(8,128)(2,1)S(1)}, bf16[8,4224]{1,0:T(8,128)(2,1)S(1)}, u32[]{:S(2)}, u32[]{:S(2)}) collective-permute-start(bf16[8,4224]{1,0:T(8,128)(2,1)S(1)} %shard_map.104.refs_1_), channel_id=1, source_target_pairs={{0,12},{4,8},{8,4},{12,0},{1,13},{5,9},{9,5},{13,1},{2,14},{6,10},... | collective-permute-start | bytes 202760 | tf_op jit(solution)/shard_map/ppermute | solution.py:371
  6.7 5.8 %collective-permute-start.1 = (bf16[8,4224]{1,0:T(8,128)(2,1)S(1)}, bf16[8,4224]{1,0:T(8,128)(2,1)S(1)}, u32[]{:S(2)}, u32[]{:S(2)}) collective-permute-start(bf16[8,4224]{1,0:T(8,128)(2,1)S(1)} %shard_map.104.refs_1_), channel_id=1, source_target_pairs={{0,8},{4,12},{8,0},{12,4},{1,9},{5,13},{9,1},{13,5},{2,10},{6,14},... | collective-permute-start | bytes 202760 | tf_op jit(solution)/shard_map/ppermute | solution.py:371
  6.7 7.3 %collective-permute-start = (bf16[8,4224]{1,0:T(8,128)(2,1)S(1)}, bf16[8,4224]{1,0:T(8,128)(2,1)S(1)}, u32[]{:S(2)}, u32[]{:S(2)}) collective-permute-start(bf16[8,4224]{1,0:T(8,128)(2,1)S(1)} %shard_map.104.refs_1_), channel_id=1, source_target_pairs={{0,4},{4,0},{8,12},{12,8},{1,5},{5,1},{9,13},{13,9},{2,6},{6,2},{1... | collective-permute-start | bytes 202760 | tf_op jit(solution)/shard_map/ppermute | solution.py:371
  7.3 7.4 %collective-permute-start.4 = (bf16[8,4224]{1,0:T(8,128)(2,1)S(1)}, bf16[8,4224]{1,0:T(8,128)(2,1)S(1)}, u32[]{:S(2)}, u32[]{:S(2)}) collective-permute-start(bf16[8,4224]{1,0:T(8,128)(2,1)S(1)} %shard_map.104.refs_1_), channel_id=1, source_target_pairs={{0,2},{1,3},{2,0},{3,1},{4,6},{5,7},{6,4},{7,5},{8,10},{9,11},{10,... | collective-permute-start | bytes 202760 | tf_op jit(solution)/shard_map/ppermute | solution.py:371
  9.3 5.4 %collective-permute-start.7 = (bf16[8,4224]{1,0:T(8,128)(2,1)S(1)}, bf16[8,4224]{1,0:T(8,128)(2,1)S(1)}, u32[]{:S(2)}, u32[]{:S(2)}) collective-permute-start(bf16[8,4224]{1,0:T(8,128)(2,1)S(1)} %shard_map.107), channel_id=1, source_target_pairs={{0,2},{1,3},{2,0},{3,1},{4,6},{5,7},{6,4},{7,5},{8,10},{9,11},{10,... | collective-permute-start | bytes 202760 | tf_op jit(solution)/shard_map/ppermute | solution.py:371
  12.4 7.5 %slice-start = ((s8[8388608]{0:T(1024)(128)(4,1)}), s8[4194304]{0:T(1024)(128)(4,1)S(1)}, s32[]{:S(2)}) async-start(s8[8388608]{0:T(1024)(128)(4,1)} %bitcast.16), calls=%async_computation | async-start | bytes 8388608
  12.4 7.5 %slice-start.2 = ((s8[8388608]{0:T(1024)(128)(4,1)}), s8[4194304]{0:T(1024)(128)(4,1)S(1)}, s32[]{:S(2)}) async-start(s8[8388608]{0:T(1024)(128)(4,1)} %bitcast.18), calls=%async_computation.2 | async-start | bytes 8388608
  12.4 7.5 %slice-start.1 = ((s8[8388608]{0:T(1024)(128)(4,1)}), s8[4194304]{0:T(1024)(128)(4,1)S(1)}, s32[]{:S(2)}) async-start(s8[8388608]{0:T(1024)(128)(4,1)} %bitcast.16), calls=%async_computation.1 | async-start | bytes 8388608
  12.4 7.5 %slice-start.3 = ((s8[8388608]{0:T(1024)(128)(4,1)}), s8[4194304]{0:T(1024)(128)(4,1)S(1)}, s32[]{:S(2)}) async-start(s8[8388608]{0:T(1024)(128)(4,1)} %bitcast.18), calls=%async_computation.3 | async-start | bytes 8388608
  12.4 5.0 %collective-permute-start.6 = (bf16[8,4224]{1,0:T(8,128)(2,1)S(1)}, bf16[8,4224]{1,0:T(8,128)(2,1)S(1)}, u32[]{:S(2)}, u32[]{:S(2)}) collective-permute-start(bf16[8,4224]{1,0:T(8,128)(2,1)S(1)} %shard_map.106), channel_id=1, source_target_pairs={{0,2},{1,3},{2,0},{3,1},{4,6},{5,7},{6,4},{7,5},{8,10},{9,11},{10,... | collective-permute-start | bytes 202760 | tf_op jit(solution)/shard_map/ppermute | solution.py:371
  14.0 4.3 %collective-permute-start.5 = (bf16[8,4224]{1,0:T(8,128)(2,1)S(1)}, bf16[8,4224]{1,0:T(8,128)(2,1)S(1)}, u32[]{:S(2)}, u32[]{:S(2)}) collective-permute-start(bf16[8,4224]{1,0:T(8,128)(2,1)S(1)} %shard_map.105), channel_id=1, source_target_pairs={{0,2},{1,3},{2,0},{3,1},{4,6},{5,7},{6,4},{7,5},{8,10},{9,11},{10,... | collective-permute-start | bytes 202760 | tf_op jit(solution)/shard_map/ppermute | solution.py:371
  14.6 3.8 %collective-permute-start.3 = (bf16[4,8,4224]{2,1,0:T(8,128)(2,1)S(1)}, bf16[4,8,4224]{2,1,0:T(8,128)(2,1)S(1)}, u32[]{:S(2)}, u32[]{:S(2)}) collective-permute-start(bf16[4,8,4224]{2,1,0:T(8,128)(2,1)S(1)} %get-tuple-element.28), channel_id=1, source_target_pairs={{0,1},{1,0},{2,3},{3,2},{4,5},{5,4},{6,7},{7,6},{8,9},{9,8},{10,11... | collective-permute-start | bytes 811016 | tf_op jit(solution)/shard_map/ppermute | solution.py:371
  18.3 1.6 %collective-permute-start.8 = (bf16[4,8,4224]{2,1,0:T(8,128)(2,1)S(1)}, bf16[4,8,4224]{2,1,0:T(8,128)(2,1)S(1)}, u32[]{:S(2)}, u32[]{:S(2)}) collective-permute-start(bf16[4,8,4224]{2,1,0:T(8,128)(2,1)S(1)} %get-tuple-element.26), channel_id=1, source_target_pairs={{0,1},{1,0},{2,3},{3,2},{4,5},{5,4},{6,7},{7,6},{8,9},{9,8},{10,11... | collective-permute-start | bytes 811016 | tf_op jit(solution)/shard_map/ppermute | solution.py:371
  20.0 4.0 %copy-start = (bf16[2,512,576]{1,2,0:T(8,128)(2,1)S(1)}, bf16[2,512,576]{1,2,0:T(8,128)(2,1)}, u32[]{:S(2)}) copy-start(bf16[2,512,576]{1,2,0:T(8,128)(2,1)} %param.16) | copy-start | bytes 3538948
  20.0 3.9 %copy-start.1 = (bf16[2,128,576]{1,2,0:T(8,128)(2,1)S(1)}, bf16[2,128,576]{1,2,0:T(8,128)(2,1)}, u32[]{:S(2)}) copy-start(bf16[2,128,576]{1,2,0:T(8,128)(2,1)} %param.15) | copy-start | bytes 884740
  20.0 3.9 %copy-start.2 = (s32[2]{0:T(128)S(1)}, s32[2]{0:T(128)}, u32[]{:S(2)}) copy-start(s32[2]{0:T(128)} %lengths_ref.1) | copy-start | bytes 28
  22.8 7.0 %collective-permute-start.10 = (bf16[4,96,256]{2,1,0:T(8,128)(2,1)S(1)}, bf16[4,96,256]{2,1,0:T(8,128)(2,1)S(1)}, u32[]{:S(2)}, u32[]{:S(2)}) collective-permute-start(bf16[4,96,256]{2,1,0:T(8,128)(2,1)S(1)} %get-tuple-element.15.after_ref.h0_ref), channel_id=1, source_target_pairs={{0,2},{1,3},{2,0},{3,1},{4,6},{5,7},{6,4},{7,5},{8,10},{9,11},{10,... | collective-permute-start | bytes 589832 | tf_op jit(solution)/shard_map/ppermute | solution.py:371
  23.9 5.9 %collective-permute-start.9 = (bf16[4,96,256]{2,1,0:T(8,128)(2,1)S(1)}, bf16[4,96,256]{2,1,0:T(8,128)(2,1)S(1)}, u32[]{:S(2)}, u32[]{:S(2)}) collective-permute-start(bf16[4,96,256]{2,1,0:T(8,128)(2,1)S(1)} %get-tuple-element.15.after_ref.h0_ref), channel_id=1, source_target_pairs={{0,1},{1,0},{2,3},{3,2},{4,5},{5,4},{6,7},{7,6},{8,9},{9,8},{10,11... | collective-permute-start | bytes 589832 | tf_op jit(solution)/shard_map/ppermute | solution.py:371
  29.8 1.4 %collective-permute-start.11 = (bf16[4,96,256]{2,1,0:T(8,128)(2,1)S(1)}, bf16[4,96,256]{2,1,0:T(8,128)(2,1)S(1)}, u32[]{:S(2)}, u32[]{:S(2)}) collective-permute-start(bf16[4,96,256]{2,1,0:T(8,128)(2,1)S(1)} %shard_map.110.h2_ref), channel_id=1, source_target_pairs={{0,1},{1,0},{2,3},{3,2},{4,5},{5,4},{6,7},{7,6},{8,9},{9,8},{10,11... | collective-permute-start | bytes 589832 | tf_op jit(solution)/shard_map/ppermute | solution.py:371
  32.0 6.8 %collective-permute-start.12 = (bf16[32,1024]{1,0:T(8,128)(2,1)S(1)}, bf16[32,1024]{1,0:T(8,128)(2,1)S(1)}, u32[]{:S(2)}, u32[]{:S(2)}) collective-permute-start(bf16[32,1024]{1,0:T(8,128)(2,1)S(1)} %get-tuple-element.18), channel_id=1, source_target_pairs={{0,12},{4,8},{8,4},{12,0},{1,13},{5,9},{9,5},{13,1},{2,14},{6,10},... | collective-permute-start | bytes 196616 | tf_op jit(solution)/shard_map/ppermute | solution.py:371
  34.8 6.1 %collective-permute-start.13 = (bf16[32,1024]{1,0:T(8,128)(2,1)S(1)}, bf16[32,1024]{1,0:T(8,128)(2,1)S(1)}, u32[]{:S(2)}, u32[]{:S(2)}) collective-permute-start(bf16[32,1024]{1,0:T(8,128)(2,1)S(1)} %get-tuple-element.19), channel_id=1, source_target_pairs={{0,8},{4,12},{8,0},{12,4},{1,9},{5,13},{9,1},{13,5},{2,10},{6,14},... | collective-permute-start | bytes 196616 | tf_op jit(solution)/shard_map/ppermute | solution.py:371
  34.8 6.1 %collective-permute-start.14 = (bf16[32,1024]{1,0:T(8,128)(2,1)S(1)}, bf16[32,1024]{1,0:T(8,128)(2,1)S(1)}, u32[]{:S(2)}, u32[]{:S(2)}) collective-permute-start(bf16[32,1024]{1,0:T(8,128)(2,1)S(1)} %get-tuple-element.20), channel_id=1, source_target_pairs={{0,4},{4,0},{8,12},{12,8},{1,5},{5,1},{9,13},{13,9},{2,6},{6,2},{1... | collective-permute-start | bytes 196616 | tf_op jit(solution)/shard_map/ppermute | solution.py:371
  41.0 1.9 %collective-permute-start.15 = (bf16[8,1024]{1,0:T(8,128)(2,1)S(1)}, bf16[8,1024]{1,0:T(8,128)(2,1)S(1)}, u32[]{:S(2)}, u32[]{:S(2)}) collective-permute-start(bf16[8,1024]{1,0:T(8,128)(2,1)S(1)} %get-tuple-element.22), channel_id=1, source_target_pairs={{0,1},{1,0},{2,3},{3,2},{4,5},{5,4},{6,7},{7,6},{8,9},{9,8},{10,11... | collective-permute-start | bytes 49160 | tf_op jit(solution)/shard_map/ppermute | solution.py:371
  41.1 3.8 %collective-permute-start.16 = (bf16[8,1024]{1,0:T(8,128)(2,1)S(1)}, bf16[8,1024]{1,0:T(8,128)(2,1)S(1)}, u32[]{:S(2)}, u32[]{:S(2)}) collective-permute-start(bf16[8,1024]{1,0:T(8,128)(2,1)S(1)} %get-tuple-element.23), channel_id=1, source_target_pairs={{0,2},{1,3},{2,0},{3,1},{4,6},{5,7},{6,4},{7,5},{8,10},{9,11},{10,... | collective-permute-start | bytes 49160 | tf_op jit(solution)/shard_map/ppermute | solution.py:371
  42.2 3.2 %collective-permute-start.17 = (bf16[8,1024]{1,0:T(8,128)(2,1)S(1)}, bf16[8,1024]{1,0:T(8,128)(2,1)S(1)}, u32[]{:S(2)}, u32[]{:S(2)}) collective-permute-start(bf16[8,1024]{1,0:T(8,128)(2,1)S(1)} %get-tuple-element.24), channel_id=1, source_target_pairs={{0,3},{1,2},{2,1},{3,0},{4,7},{5,6},{6,5},{7,4},{8,11},{9,10},{10,... | collective-permute-start | bytes 49160 | tf_op jit(solution)/shard_map/ppermute | solution.py:371

commit v7 on v6

--- a/solution.py
+++ b/solution.py
@@ -66,38 +66,30 @@
     )(cache_lengths, jnp.swapaxes(queries, 1, 2), jnp.swapaxes(latent_cache, 1, 2))
 
 
-def attend_and_fetch_kernel(
-    lengths_ref, queries_ref, cache_ref, source_ref, after_ref, out_ref, held_ref, sem
-):
-    copy = pltpu.make_async_copy(source_ref, held_ref, sem)
-    copy.start()
+def attend_after_kernel(lengths_ref, queries_ref, cache_ref, after_ref, out_ref):
     attend_rows(lengths_ref, queries_ref, cache_ref, out_ref)
-    copy.wait()
-
-
-def attend_and_fetch(queries, latent_cache, cache_lengths, weights, after):
+
+
+def attend_after(queries, latent_cache, cache_lengths, after):
     rows, heads, _ = queries.shape
     return pl.pallas_call(
-        attend_and_fetch_kernel,
-        in_specs=[whole(pltpu.SMEM), whole(), whole(), whole(pltpu.HBM), whole(pl.ANY)],
-        out_specs=[whole(), whole()],
-        out_shape=[
-            jax.ShapeDtypeStruct((rows, heads, LATENT), BF16),
-            VMEM(weights.shape, weights.dtype),
-        ],
-        scratch_shapes=[pltpu.SemaphoreType.DMA],
-        compiler_params=pltpu.CompilerParams(vmem_limit_bytes=12 * MIB),
-        cost_estimate=attend_cost(queries, latent_cache),
+        attend_after_kernel,
+        in_specs=[whole(pltpu.SMEM), whole(), whole(), whole(pl.ANY)],
+        out_specs=whole(),
+        out_shape=jax.ShapeDtypeStruct((rows, heads, LATENT), BF16),
+        compiler_params=pltpu.CompilerParams(vmem_limit_bytes=8 * MIB),
+        cost_estimate=pl.CostEstimate(
+            flops=4 * 10**9, bytes_accessed=0, transcendentals=0
+        ),
     )(
         cache_lengths,
         jnp.swapaxes(queries, 1, 2),
         jnp.swapaxes(latent_cache, 1, 2),
-        in_hbm(weights),
         after,
     )
 
 
-def once_done(value, other):
+def once_done(value, other, flops=0):
     return pl.pallas_call(
         lambda *refs: None,
         in_specs=[whole(pl.ANY)] * 2,
@@ -105,7 +97,7 @@
         out_shape=VMEM(value.shape, value.dtype),
         input_output_aliases={0: 0},
         compiler_params=pltpu.CompilerParams(vmem_limit_bytes=MIB),
-        cost_estimate=pl.CostEstimate(flops=4000000000, bytes_accessed=0, transcendentals=0),
+        cost_estimate=pl.CostEstimate(flops=flops, bytes_accessed=0, transcendentals=0),
     )(value, other)
 
 
@@ -163,37 +155,28 @@
     )(in_hbm(hidden_rows), in_hbm(expert_ids), in_hbm(gate_values))
 
 
-def gate_up_kernel(
-    slots,
-    experts_all,
-    mine_z_ref,
-    other_z_ref,
-    mine_x_ref,
-    other_x_ref,
-    gate_first_ref,
-    up_first_ref,
-    hidden_ref,
-    spread_ref,
-    rows_ref,
-):
-    matrices = []
-    for pair in ((gate_first_ref, up_first_ref),):
-        matrices += [[ref.at[e] for ref in pair] for e in range(pair[0].shape[0])]
-    experts = len(matrices)
-    depth = gate_first_ref.shape[1]
-    groups = (mine_z_ref, other_z_ref, mine_x_ref, other_x_ref)
-    rows_group, total_width = mine_z_ref.shape
+def activated(rows, gate_ref, up_ref):
+    gate = jnp.dot(rows, gate_ref[...], preferred_element_type=F32)
+    up = jnp.dot(rows, up_ref[...], preferred_element_type=F32)
+    return (gate / (1.0 + jnp.exp(-gate)) * up).astype(BF16)
+
+
+def compacted(made, rank_row, slots):
+    slot = lax.broadcasted_iota(jnp.int32, (slots, rank_row.shape[1]), 0).astype(F32)
+    to_slot = (rank_row == slot).astype(F32).astype(BF16)
+    return jnp.dot(to_slot, made, preferred_element_type=F32).astype(BF16)
+
+
+def gate_up_first_kernel(experts_all, *refs):
+    groups = refs[:4]
+    gate_ref, up_ref, hidden_ref, table_ref, rank_ref, across_ref = refs[4:]
+    experts, depth, _ = gate_ref.shape
+    rows_group, total_width = groups[0].shape
     count = 4 * rows_group
     lanes = total_width - depth
-    for g, ref in enumerate(groups):
-        rows_ref[g * rows_group : (g + 1) * rows_group] = ref[:, :depth]
+    rows = jnp.concatenate([ref[:, :depth] for ref in groups], axis=0)
     coded = jnp.concatenate([ref[:, depth:] for ref in groups], axis=0)
-    def activated(e):
-        gate = jnp.dot(rows_ref[...], matrices[e][0][...], preferred_element_type=F32)
-        up = jnp.dot(rows_ref[...], matrices[e][1][...], preferred_element_type=F32)
-        return (gate / (1.0 + jnp.exp(-gate)) * up).astype(BF16)
-
-    made = activated(0)
+    made = activated(rows, gate_ref.at[0], up_ref.at[0])
     source = lax.broadcasted_iota(jnp.int32, (lanes, lanes), 0)
     target = lax.broadcasted_iota(jnp.int32, (lanes, lanes), 1)
     selector = (
@@ -209,77 +192,130 @@
     ahead = jnp.bitwise_xor(column, turn) < jnp.bitwise_xor(row, turn)
     rank = jnp.dot(ahead.astype(F32).astype(BF16), chosen, preferred_element_type=F32)
     rank = jnp.where(table > 0.0, rank, -1.0)
-    rank_across = rank.T
-    slot = column.astype(F32)
-    slot_down = row.astype(F32)[:slots]
+    across = rank.T
+    table_ref[...], rank_ref[...], across_ref[...] = table, rank, across
+    part, slots, _ = hidden_ref.shape
+    for e in range(part):
+        later = activated(rows, gate_ref.at[e + 1], up_ref.at[e + 1]) if e + 1 < part else None
+        hidden_ref[e] = compacted(made, across[e : e + 1], slots)
+        made = later
+
+
+def gate_up_next_kernel(*refs):
+    groups = refs[:4]
+    gate_ref, up_ref, first_ref, table_ref, rank_ref, across_ref = refs[4:10]
+    hidden_ref, all_ref, spread_ref = refs[10:]
+    experts, depth, _ = gate_ref.shape
+    rows = jnp.concatenate([ref[:, :depth] for ref in groups], axis=0)
+    count = rows.shape[0]
+    done, slots, _ = first_ref.shape
+    made = activated(rows, gate_ref.at[done], up_ref.at[done])
+    all_ref[:done] = first_ref[...]
+    slot = lax.broadcasted_iota(jnp.int32, (count, count), 1).astype(F32)
+    table, rank = table_ref[...], rank_ref[...]
     for e in range(experts):
-        later = activated(e + 1) if e + 1 < experts else None
         value = jnp.where(rank[:, e : e + 1] == slot, table[:, e : e + 1], 0.0)
         high = value.astype(BF16)
         spread_ref[:count, e * count : (e + 1) * count] = high
         spread_ref[count:, e * count : (e + 1) * count] = (value - high.astype(F32)).astype(BF16)
-        to_slot = (rank_across[e : e + 1] == slot_down).astype(F32).astype(BF16)
-        hidden_ref[e] = jnp.dot(to_slot, made, preferred_element_type=F32).astype(BF16)
+    for e in range(done, experts):
+        later = (
+            activated(rows, gate_ref.at[e + 1], up_ref.at[e + 1]) if e + 1 < experts else None
+        )
+        hidden = compacted(made, across_ref[e : e + 1], slots)
+        hidden_ref[e - done] = hidden
+        all_ref[e] = hidden
         made = later
 
 
-def gate_up(pieces, held, slots, experts_all):
-    _, depth, share = held[0].shape
-    experts = sum(array.shape[0] for array in held[::2])
+def half_cost(gate_proj, count):
+    size = gate_proj.size // 2
+    return pl.CostEstimate(flops=4 * count * size, bytes_accessed=4 * size, transcendentals=0)
+
+
+def gate_up_first(pieces, gate_proj, up_proj, part, slots, experts_all):
+    _, depth, share = gate_proj.shape
+    rows_group, total_width = pieces[0].shape
+    count = 4 * rows_group
+    square = VMEM((count, total_width - depth), F32)
+    return pl.pallas_call(
+        lambda *refs: gate_up_first_kernel(experts_all, *refs),
+        in_specs=[whole()] * 6,
+        out_specs=[whole()] * 4,
+        out_shape=[
+            VMEM((part, slots, share), BF16),
+            square,
+            square,
+            VMEM((total_width - depth, count), F32),
+        ],
+        compiler_params=pltpu.CompilerParams(vmem_limit_bytes=28 * MIB),
+        cost_estimate=half_cost(gate_proj, count),
+    )(*pieces, gate_proj, up_proj)
+
+
+def gate_up_next(pieces, gate_proj, up_proj, first, table, rank, across):
+    experts, depth, share = gate_proj.shape
+    done, slots, _ = first.shape
     count = 4 * pieces[0].shape[0]
     return pl.pallas_call(
-        lambda *refs: gate_up_kernel(slots, experts_all, *refs),
-        in_specs=[whole()] * 6,
-        out_specs=[whole()] * 2,
+        gate_up_next_kernel,
+        in_specs=[whole()] * 10,
+        out_specs=[whole()] * 3,
         out_shape=[
+            VMEM((experts - done, slots, share), BF16),
             VMEM((experts, slots, share), BF16),
             VMEM((2 * count, experts * count), BF16),
         ],
-        scratch_shapes=[VMEM((count, depth), BF16)],
-        compiler_params=pltpu.CompilerParams(vmem_limit_bytes=36 * MIB),
-        cost_estimate=pl.CostEstimate(
-            flops=4 * experts * count * depth * share,
-            bytes_accessed=4 * experts * depth * share,
-            transcendentals=experts * count * share,
-        ),
-    )(*pieces, *held)
-
-
-def down_first_kernel(h0_ref, h1_ref, h2_ref, down_ref, made_ref):
+        compiler_params=pltpu.CompilerParams(vmem_limit_bytes=28 * MIB),
+        cost_estimate=half_cost(gate_proj, count),
+    )(*pieces, gate_proj, up_proj, first, table, rank, across)
+
+
+def down_part_kernel(start, h0_ref, h1_ref, h2_ref, down_ref, made_ref):
     place = lax.axis_index("dp")
-    experts, slots, share = h0_ref.shape
-    for e in range(experts):
+    share = h0_ref.shape[2]
+    for e in range(h2_ref.shape[0]):
         made = jnp.zeros(made_ref.shape[1:], F32)
-        for k, ref in enumerate((h0_ref, h1_ref, h2_ref)):
+        for k, ref in enumerate((h0_ref.at[start + e], h1_ref.at[start + e], h2_ref.at[e])):
             owner = jnp.bitwise_xor(place, k)
-            weights = down_ref[e, pl.ds(pl.multiple_of(owner * share, share), share)]
-            made += jnp.dot(ref[e], weights, preferred_element_type=F32)
+            weights = down_ref[start + e, pl.ds(pl.multiple_of(owner * share, share), share)]
+            made += jnp.dot(ref[...], weights, preferred_element_type=F32)
         made_ref[e] = made
 
 
-def down_first(hidden, down_held):
-    experts, slots, share = hidden[0].shape
-    width = down_held.shape[2]
-    return pl.pallas_call(
-        down_first_kernel,
+def down_part(start, hidden, down_proj):
+    part, slots, share = hidden[2].shape
+    width = down_proj.shape[2]
+    return pl.pallas_call(
+        lambda *refs: down_part_kernel(start, *refs),
         in_specs=[whole()] * 4,
         out_specs=whole(),
-        out_shape=VMEM((experts, slots, width), F32),
-        compiler_params=pltpu.CompilerParams(vmem_limit_bytes=8 * MIB),
+        out_shape=VMEM((part, slots, width), F32),
+        compiler_params=pltpu.CompilerParams(vmem_limit_bytes=20 * MIB),
         cost_estimate=pl.CostEstimate(
-            flops=6 * experts * slots * share * width,
-            bytes_accessed=4 * experts * slots * width,
+            flops=6 * part * slots * share * width,
+            bytes_accessed=4 * part * slots * width,
             transcendentals=0,
         ),
-    )(*hidden, down_held)
+    )(*hidden, down_proj)
 
 
 def down_last_kernel(
-    spread_ref, first_ref, h3_ref, down_ref, o0_ref, o1_ref, o2_ref, o3_ref, made_ref
+    spread_ref,
+    begun_first_ref,
+    begun_next_ref,
+    h3_first_ref,
+    h3_next_ref,
+    down_ref,
+    o0_ref,
+    o1_ref,
+    o2_ref,
+    o3_ref,
+    made_ref,
 ):
     owner = jnp.bitwise_xor(lax.axis_index("dp"), 3)
-    experts, slots, share = h3_ref.shape
-    width = down_ref.shape[2]
+    part, slots, share = h3_first_ref.shape
+    experts, _, width = down_ref.shape
     count = spread_ref.shape[0] // 2
     rows_z = o0_ref.shape[0]
     tile = 256
@@ -289,7 +325,11 @@
                 (count - slots, width), BF16
             )
         weights = down_ref[e, pl.ds(pl.multiple_of(owner * share, share), share)]
-        made = first_ref[e] + jnp.dot(h3_ref[e], weights, preferred_element_type=F32)
+        if e < part:
+            begun, far = begun_first_ref[e], h3_first_ref[e]
+        else:
+            begun, far = begun_next_ref[e - part], h3_next_ref[e - part]
+        made = begun + jnp.dot(far, weights, preferred_element_type=F32)
         made_ref[e * count : e * count + slots] = made.astype(BF16)
     spread = spread_ref[...]
     for start in range(0, width, tile):
@@ -303,22 +343,23 @@
             ref[:, start : start + tile] = jnp.concatenate(parts, axis=0).astype(BF16)
 
 
-def down_last(spread, first, hidden, down_held):
-    experts, slots, width = first.shape
+def down_last(spread, begun, hidden, down_proj):
+    experts, _, width = down_proj.shape
+    slots = hidden[0].shape[1]
     count = spread.shape[0] // 2
     return pl.pallas_call(
         down_last_kernel,
-        in_specs=[whole()] * 4,
+        in_specs=[whole()] * 6,
         out_specs=[whole()] * 4,
         out_shape=[VMEM((count // 4, width), BF16)] * 4,
         scratch_shapes=[VMEM((experts * count, width), BF16)],
-        compiler_params=pltpu.CompilerParams(vmem_limit_bytes=12 * MIB),
+        compiler_params=pltpu.CompilerParams(vmem_limit_bytes=20 * MIB),
         cost_estimate=pl.CostEstimate(
             flops=4 * experts * count * count * width,
             bytes_accessed=8 * experts * slots * width,
             transcendentals=0,
         ),
-    )(spread, first, hidden, down_held)
+    )(spread, *begun, *hidden, down_proj)
 
 
 def collect_kernel(p0_ref, p1_ref, p2_ref, p3_ref, own_ref, core_ref, x_ref, far_ref):
@@ -389,27 +430,31 @@
     capacity = max(2, 3 * rows_dev * expert_ids.shape[1] // (2 * experts_all))
     sent = pack(hidden_rows, expert_ids, gate_values, experts_all)
     along_z = [sent] + [swap(sent, "expert", k) for k in (1, 2, 3)]
-    along_z[1:] = [once_done(block, sent) for block in along_z[1:]]
+    along_z[1:] = [once_done(block, sent, 4 * 10**9) for block in along_z[1:]]
     along_x = [swap(block, "dp", 2) for block in along_z]
     mine_z, mine_x = jnp.stack(along_z), jnp.stack(along_x)
     other_z = swap(mine_z, "dp", 1)
     other_x = swap(mine_x, "dp", 1)
 
-    hidden, spread = gate_up(
-        [block.reshape(4 * rows_dev, -1) for block in (mine_z, other_z, mine_x, other_x)],
-        (gate_proj, up_proj),
-        16 * capacity,
-        experts_all,
-    )
-    hidden_x = swap(hidden, "dp", 2)
+    pieces = [block.reshape(4 * rows_dev, -1) for block in (mine_z, other_z, mine_x, other_x)]
+    half = local_experts // 2
+    hidden_first, table, rank, across = gate_up_first(
+        pieces, gate_proj, up_proj, half, 16 * capacity, experts_all
+    )
+    first_x = swap(hidden_first, "dp", 2)
+    hidden_next, hidden, spread = gate_up_next(
+        pieces, gate_proj, up_proj, hidden_first, table, rank, across
+    )
+    next_x = swap(hidden_next, "dp", 2)
     hidden_c = swap(hidden, "dp", 1)
-    attended, down_held = attend_and_fetch(
-        queries, latent_cache, cache_lengths, down_proj, hidden
-    )
-    hidden_x = once_done(hidden_x, down_held)
-    hidden_xc = swap(hidden_x, "dp", 1)
-    first = down_first((hidden, hidden_c, hidden_x), down_held)
-    partial = down_last(spread, first, hidden_xc, down_held)
+    attended = attend_after(queries, latent_cache, cache_lengths, hidden_next)
+    first_x = once_done(first_x, in_hbm(attended))
+    first_far = swap(first_x, "dp", 1)
+    begun_first = down_part(0, (hidden, hidden_c, first_x), down_proj)
+    next_x = once_done(next_x, begun_first)
+    next_far = swap(next_x, "dp", 1)
+    begun_next = down_part(half, (hidden, hidden_c, next_x), down_proj)
+    partial = down_last(spread, (begun_first, begun_next), (first_far, next_far), down_proj)
     arrived = [partial[0]] + [swap(partial[k], "expert", k) for k in (3, 2, 1)]
     own, to_core, to_x, to_far = collect(arrived)
     far = swap(to_far, "dp", 3)

time: 46.2 us -> 45.5 us (0.985)
  Pallas kernels: 10.9 us -> 9.15 us
  starting transfers between devices: 19 us -> 20.3 us
    pallas_call x4 -> x6, Pallas kernels: 9.33 us -> 7.57 us  [the longest x1 2.46 us: attend_after(): pl.pallas_call(attend_after_kernel, in_specs=[whole(pltpu.SMEM), whole(),...]
    ppermute x18 -> x20, starting transfers between devices: 19 us -> 20.3 us  [swap(): return lax.ppermute(value, axis, [(i, i ^ bit) for i in range(size)])]
    ppermute x18 -> x20, waiting for transfers between devices: 15.1 us -> 15 us  [swap(): return lax.ppermute(value, axis, [(i, i ^ bit) for i in range(size)])]
  transfers between devices with their start and end apart: 18 -> 20, of which waited for: 11 -> 11; matrix products, arithmetic and copies ran while one was open for 0% -> 0% of each run, Pallas kernels for 13% -> 11%
where the time goes in v7:
time: 45.5 us; the launch traced here: 45.3 us
  starting transfers between devices  20.3 us (45%)
  waiting for transfers between devices  15 us (33%)
  Pallas kernels  9.15 us (20%)
  between operations  0.81 us (2%)
    ppermute x20, starting transfers between devices, swap(): return lax.ppermute(value, axis, [(i, i ^ bit) for i in range(size)])  20.3 us
    ppermute x20, waiting for transfers between devices, swap(): return lax.ppermute(value, axis, [(i, i ^ bit) for i in range(size)])  15 us
    pallas_call x1, Pallas kernels, attend_after(): pl.pallas_call(attend_after_kernel, in_specs=[whole(pltpu.SMEM), whole(),...  2.46 us
    pallas_call x1, Pallas kernels, gate_up_first(): pl.pallas_call(lambda *refs: gate_up_first_kernel(experts_all, *refs), in...  1.62 us
    pallas_call x1, Pallas kernels, gate_up_next(): pl.pallas_call(gate_up_next_kernel, in_specs=[whole()] * 10, out_specs=[w...  1.44 us
    pallas_call x2, Pallas kernels, down_part(): pl.pallas_call(lambda *refs: down_part_kernel(start, *refs), in_specs=[wh...  1.28 us
  transfers between devices with their start and end apart: 20, of which 11 were waited for; matrix products, arithmetic and copies ran while one was open for 0% of the time, Pallas kernels for 11%

profile of v7, /device:TPU:0, one launch (start us, length us, event | category | flops | bytes accessed | tf_op | source)
XLA Modules:
  0.0 45.3 jit_solution(9325732037697784973)
XLA Ops:
  0.6 0.9 %shard_map.104.refs_1_ = bf16[8,4224]{1,0:T(8,128)(2,1)S(1)} custom-call(bf16[8,4096]{1,0:T(8,128)(2,1)} %refs_0_.1, s32[8,8]{1,0:T(8,128)} %refs_1_.1, f32[8,8]{1,0:T(8,128)} %refs_2_.1), custom_call_target="tpu_custom_call" | custom-call | bytes 131072 | tf_op jit(solution)/shard_map/pallas_call | solution.py:141
  1.5 5.1 %collective-permute-start.2 = (bf16[8,4224]{1,0:T(8,128)(2,1)S(1)}, bf16[8,4224]{1,0:T(8,128)(2,1)S(1)}, u32[]{:S(2)}, u32[]{:S(2)}) collective-permute-start(bf16[8,4224]{1,0:T(8,128)(2,1)S(1)} %shard_map.104.refs_1_), channel_id=1, source_target_pairs={{0,12},{4,8},{8,4},{12,0},{1,13},{5,9},{9,5},{13,1},{2,14},{6,10},... | collective-permute-start | bytes 202760 | tf_op jit(solution)/shard_map/ppermute | solution.py:412
  6.7 0.0 collective-permute-start.1
  6.7 0.6 %collective-permute-start = (bf16[8,4224]{1,0:T(8,128)(2,1)S(1)}, bf16[8,4224]{1,0:T(8,128)(2,1)S(1)}, u32[]{:S(2)}, u32[]{:S(2)}) collective-permute-start(bf16[8,4224]{1,0:T(8,128)(2,1)S(1)} %shard_map.104.refs_1_), channel_id=1, source_target_pairs={{0,4},{4,0},{8,12},{12,8},{1,5},{5,1},{9,13},{13,9},{2,6},{6,2},{1... | collective-permute-start | bytes 202760 | tf_op jit(solution)/shard_map/ppermute | solution.py:412
  7.3 1.6 %collective-permute-start.4 = (bf16[8,4224]{1,0:T(8,128)(2,1)S(1)}, bf16[8,4224]{1,0:T(8,128)(2,1)S(1)}, u32[]{:S(2)}, u32[]{:S(2)}) collective-permute-start(bf16[8,4224]{1,0:T(8,128)(2,1)S(1)} %shard_map.104.refs_1_), channel_id=1, source_target_pairs={{0,2},{1,3},{2,0},{3,1},{4,6},{5,7},{6,4},{7,5},{8,10},{9,11},{10,... | collective-permute-start | bytes 202760 | tf_op jit(solution)/shard_map/ppermute | solution.py:412
  8.9 0.3 collective-permute-done.2.refs_0_
  9.3 1.9 %collective-permute-start.7 = (bf16[8,4224]{1,0:T(8,128)(2,1)S(1)}, bf16[8,4224]{1,0:T(8,128)(2,1)S(1)}, u32[]{:S(2)}, u32[]{:S(2)}) collective-permute-start(bf16[8,4224]{1,0:T(8,128)(2,1)S(1)} %shard_map.107), channel_id=1, source_target_pairs={{0,2},{1,3},{2,0},{3,1},{4,6},{5,7},{6,4},{7,5},{8,10},{9,11},{10,... | collective-permute-start | bytes 202760 | tf_op jit(solution)/shard_map/ppermute | solution.py:412
  11.1 1.3 %collective-permute-done.1.refs_0_ = bf16[8,4224]{1,0:T(8,128)(2,1)S(1)} collective-permute-done((bf16[8,4224]{1,0:T(8,128)(2,1)S(1)}, bf16[8,4224]{1,0:T(8,128)(2,1)S(1)}, u32[]{:S(2)}, u32[]{:S(2)}) %collective-permute-start.1) | collective-permute-done | bytes 67616 | tf_op jit(solution)/shard_map/ppermute | solution.py:412
  12.4 0.0 slice-start.2
  12.4 0.0 slice-start.4
  12.4 0.0 slice-start.3
  12.4 0.0 slice-start.5
  12.4 1.6 %collective-permute-start.6 = (bf16[8,4224]{1,0:T(8,128)(2,1)S(1)}, bf16[8,4224]{1,0:T(8,128)(2,1)S(1)}, u32[]{:S(2)}, u32[]{:S(2)}) collective-permute-start(bf16[8,4224]{1,0:T(8,128)(2,1)S(1)} %shard_map.106), channel_id=1, source_target_pairs={{0,2},{1,3},{2,0},{3,1},{4,6},{5,7},{6,4},{7,5},{8,10},{9,11},{10,... | collective-permute-start | bytes 202760 | tf_op jit(solution)/shard_map/ppermute | solution.py:412
  14.0 0.0 collective-permute-done.refs_0_
  14.0 0.5 %collective-permute-start.5 = (bf16[8,4224]{1,0:T(8,128)(2,1)S(1)}, bf16[8,4224]{1,0:T(8,128)(2,1)S(1)}, u32[]{:S(2)}, u32[]{:S(2)}) collective-permute-start(bf16[8,4224]{1,0:T(8,128)(2,1)S(1)} %shard_map.105), channel_id=1, source_target_pairs={{0,2},{1,3},{2,0},{3,1},{4,6},{5,7},{6,4},{7,5},{8,10},{9,11},{10,... | collective-permute-start | bytes 202760 | tf_op jit(solution)/shard_map/ppermute | solution.py:412
  14.5 0.1 pad_maximum_fusion
  14.6 0.1 collective-permute-start.3
  14.7 0.0 collective-permute-done.4
  14.7 0.0 collective-permute-done.7
  14.7 2.7 %collective-permute-done.6 = bf16[8,4224]{1,0:T(8,128)(2,1)S(1)} collective-permute-done((bf16[8,4224]{1,0:T(8,128)(2,1)S(1)}, bf16[8,4224]{1,0:T(8,128)(2,1)S(1)}, u32[]{:S(2)}, u32[]{:S(2)}) %collective-permute-start.6) | collective-permute-done | bytes 67616 | tf_op jit(solution)/shard_map/ppermute | solution.py:412
  17.4 0.9 %collective-permute-done.5 = bf16[8,4224]{1,0:T(8,128)(2,1)S(1)} collective-permute-done((bf16[8,4224]{1,0:T(8,128)(2,1)S(1)}, bf16[8,4224]{1,0:T(8,128)(2,1)S(1)}, u32[]{:S(2)}, u32[]{:S(2)}) %collective-permute-start.5) | collective-permute-done | bytes 67616 | tf_op jit(solution)/shard_map/ppermute | solution.py:412
  18.3 0.1 pad_maximum_fusion.1
  18.3 0.1 collective-permute-start.8
  18.4 0.0 collective-permute-done.3
  18.4 1.5 %collective-permute-done.8 = bf16[4,8,4224]{2,1,0:T(8,128)(2,1)S(1)} collective-permute-done((bf16[4,8,4224]{2,1,0:T(8,128)(2,1)S(1)}, bf16[4,8,4224]{2,1,0:T(8,128)(2,1)S(1)}, u32[]{:S(2)}, u32[]{:S(2)}) %collective-permute-start.8) | collective-permute-done | bytes 270368 | tf_op jit(solution)/shard_map/ppermute | solution.py:412
  19.9 0.0 slice-done.2
  19.9 0.0 slice-done.4
  19.9 0.0 slice-done.3
  20.0 0.0 slice-done.5
  20.0 1.6 %shard_map.108 = (bf16[2,96,256]{2,1,0:T(8,128)(2,1)S(1)}, f32[128,128]{1,0:T(8,128)S(1)}, f32[128,128]{1,0:T(8,128)S(1)}, f32[128,128]{1,0:T(8,128)S(1)}) custom-call(bf16[32,4224]{1,0:T(8,128)(2,1)S(1)} %get-tuple-element.35.refs_0_, bf16[32,4224]{1,0:T(8,128)(2,1)S(1)} %bitcast.22, bf16[32,4224]{1,0:T(8,128)(2,1)S(1)} %get-tuple-element.33.refs_2_, ...), custom_call_target="tpu_custom_call" | custom-call | flops 1073741824 | bytes 8388608 | tf_op jit(solution)/shard_map/pallas_call | solution.py:241
  21.6 1.1 %collective-permute-start.10 = (bf16[2,96,256]{2,1,0:T(8,128)(2,1)S(1)}, bf16[2,96,256]{2,1,0:T(8,128)(2,1)S(1)}, u32[]{:S(2)}, u32[]{:S(2)}) collective-permute-start(bf16[2,96,256]{2,1,0:T(8,128)(2,1)S(1)} %get-tuple-element.17.refs_6_), channel_id=1, source_target_pairs={{0,2},{1,3},{2,0},{3,1},{4,6},{5,7},{6,4},{7,5},{8,10},{9,11},{10,... | collective-permute-start | bytes 294920 | tf_op jit(solution)/shard_map/ppermute | solution.py:412
  22.7 1.4 %shard_map.109 = (bf16[2,96,256]{2,1,0:T(8,128)(2,1)S(1)}, bf16[4,96,256]{2,1,0:T(8,128)(2,1)S(1)}, bf16[256,512]{1,0:T(8,128)(2,1)S(1)}) custom-call(bf16[32,4224]{1,0:T(8,128)(2,1)S(1)} %get-tuple-element.35.refs_0_, bf16[32,4224]{1,0:T(8,128)(2,1)S(1)} %bitcast.23, bf16[32,4224]{1,0:T(8,128)(2,1)S(1)} %get-tuple-element.33.refs_2_, ...), custom_call_target="tpu_custom_call" | custom-call | flops 1073741824 | bytes 8388608 | tf_op jit(solution)/shard_map/pallas_call | solution.py:260
  24.2 0.0 slice-start
  24.2 0.1 collective-permute-start.9
  24.3 1.0 %collective-permute-start.11 = (bf16[2,96,256]{2,1,0:T(8,128)(2,1)S(1)}, bf16[2,96,256]{2,1,0:T(8,128)(2,1)S(1)}, u32[]{:S(2)}, u32[]{:S(2)}) collective-permute-start(bf16[2,96,256]{2,1,0:T(8,128)(2,1)S(1)} %get-tuple-element.23.after_ref), channel_id=1, source_target_pairs={{0,2},{1,3},{2,0},{3,1},{4,6},{5,7},{6,4},{7,5},{8,10},{9,11},{10,... | collective-permute-start | bytes 294920 | tf_op jit(solution)/shard_map/ppermute | solution.py:412
  25.3 0.0 copy-done
  25.3 0.0 copy-done.1
  25.3 0.0 copy-done.2
  25.3 2.5 %shard_map.110.refs_1_ = bf16[2,128,512]{2,1,0:T(8,128)(2,1)} custom-call(s32[2]{0:T(128)S(1)} %copy-done.2, bf16[2,576,128]{2,1,0:T(8,128)(2,1)S(1)} %bitcast.31, bf16[2,576,512]{2,1,0:T(8,128)(2,1)S(1)} %bitcast.30, bf16[2,96,256]{2,1,0:T(8,128)(2,1)S(1)} %get-tuple-element.23.after_ref), custom_call_target="tpu_custom_call" | custom-call | flops 4000000000 | tf_op jit(solution)/shard_map/pallas_call | solution.py:75
  27.8 0.0 collective-permute-done.10.refs_0_
  27.8 0.2 collective-permute-start.12
  27.9 0.0 collective-permute-done.9.refs_1_
  27.9 0.0 slice-done
  27.9 0.0 slice-done.1
  28.0 0.6 %shard_map.112.refs_1_.begun_first_ref = f32[2,96,1024]{2,1,0:T(8,128)S(1)} custom-call(bf16[4,96,256]{2,1,0:T(8,128)(2,1)S(1)} %get-tuple-element.22.refs_0_, bf16[4,96,256]{2,1,0:T(8,128)(2,1)S(1)} %collective-permute-done.9.refs_1_, bf16[2,96,256]{2,1,0:T(8,128)(2,1)S(1)} %shard_map.111.refs_2_, bf16[4,1024,1024]{2,1,0:T(8,128)(2,1)S(1)} %bitcast.17), custom_call_target="tpu_custom_call" | custom-call | flops 301989888 | bytes 786432 | tf_op jit(solution)/shard_map/pallas_call | solution.py:289
  28.6 0.9 %collective-permute-done.11.refs_0_ = bf16[2,96,256]{2,1,0:T(8,128)(2,1)S(1)} collective-permute-done((bf16[2,96,256]{2,1,0:T(8,128)(2,1)S(1)}, bf16[2,96,256]{2,1,0:T(8,128)(2,1)S(1)}, u32[]{:S(2)}, u32[]{:S(2)}) %collective-permute-start.11) | collective-permute-done | bytes 98336 | tf_op jit(solution)/shard_map/ppermute | solution.py:412
  29.5 0.0 collective-permute-start.13
  29.5 0.6 %shard_map.114.begun_next_ref = f32[2,96,1024]{2,1,0:T(8,128)S(1)} custom-call(bf16[4,96,256]{2,1,0:T(8,128)(2,1)S(1)} %get-tuple-element.22.refs_0_, bf16[4,96,256]{2,1,0:T(8,128)(2,1)S(1)} %collective-permute-done.9.refs_1_, bf16[2,96,256]{2,1,0:T(8,128)(2,1)S(1)} %shard_map.113.refs_2_, bf16[4,1024,1024]{2,1,0:T(8,128)(2,1)S(1)} %bitcast.17), custom_call_target="tpu_custom_call" | custom-call | flops 301989888 | bytes 786432 | tf_op jit(solution)/shard_map/pallas_call | solution.py:289
  30.1 0.0 collective-permute-done.12.h3_first_ref
  30.1 0.7 %collective-permute-done.13.h3_next_ref = bf16[2,96,256]{2,1,0:T(8,128)(2,1)S(1)} collective-permute-done((bf16[2,96,256]{2,1,0:T(8,128)(2,1)S(1)}, bf16[2,96,256]{2,1,0:T(8,128)(2,1)S(1)}, u32[]{:S(2)}, u32[]{:S(2)}) %collective-permute-start.13) | collective-permute-done | bytes 98336 | tf_op jit(solution)/shard_map/ppermute | solution.py:412
  30.8 0.8 %shard_map.115 = (bf16[32,1024]{1,0:T(8,128)(2,1)S(1)}, bf16[32,1024]{1,0:T(8,128)(2,1)S(1)}, bf16[32,1024]{1,0:T(8,128)(2,1)S(1)}, bf16[32,1024]{1,0:T(8,128)(2,1)S(1)}) custom-call(bf16[256,512]{1,0:T(8,128)(2,1)S(1)} %get-tuple-element.21.spread_ref, f32[2,96,1024]{2,1,0:T(8,128)S(1)} %shard_map.112.refs_1_.begun_first_ref, ...), custom_call_target="tpu_custom_call" | custom-call | flops 268435456 | bytes 3145728 | tf_op jit(solution)/shard_map/pallas_call | solution.py:350
  31.6 2.4 %collective-permute-start.14 = (bf16[32,1024]{1,0:T(8,128)(2,1)S(1)}, bf16[32,1024]{1,0:T(8,128)(2,1)S(1)}, u32[]{:S(2)}, u32[]{:S(2)}) collective-permute-start(bf16[32,1024]{1,0:T(8,128)(2,1)S(1)} %get-tuple-element.25), channel_id=1, source_target_pairs={{0,12},{4,8},{8,4},{12,0},{1,13},{5,9},{9,5},{13,1},{2,14},{6,10},... | collective-permute-start | bytes 196616 | tf_op jit(solution)/shard_map/ppermute | solution.py:412
  34.0 0.0 collective-permute-start.15
  34.0 2.0 %collective-permute-start.16 = (bf16[32,1024]{1,0:T(8,128)(2,1)S(1)}, bf16[32,1024]{1,0:T(8,128)(2,1)S(1)}, u32[]{:S(2)}, u32[]{:S(2)}) collective-permute-start(bf16[32,1024]{1,0:T(8,128)(2,1)S(1)} %get-tuple-element.27), channel_id=1, source_target_pairs={{0,4},{4,0},{8,12},{12,8},{1,5},{5,1},{9,13},{13,9},{2,6},{6,2},{1... | collective-permute-start | bytes 196616 | tf_op jit(solution)/shard_map/ppermute | solution.py:412
  36.0 2.4 %collective-permute-done.14.p1_ref = bf16[32,1024]{1,0:T(8,128)(2,1)S(1)} collective-permute-done((bf16[32,1024]{1,0:T(8,128)(2,1)S(1)}, bf16[32,1024]{1,0:T(8,128)(2,1)S(1)}, u32[]{:S(2)}, u32[]{:S(2)}) %collective-permute-start.14) | collective-permute-done | bytes 65568 | tf_op jit(solution)/shard_map/ppermute | solution.py:412
  38.4 2.0 %collective-permute-done.15.p2_ref = bf16[32,1024]{1,0:T(8,128)(2,1)S(1)} collective-permute-done((bf16[32,1024]{1,0:T(8,128)(2,1)S(1)}, bf16[32,1024]{1,0:T(8,128)(2,1)S(1)}, u32[]{:S(2)}, u32[]{:S(2)}) %collective-permute-start.15) | collective-permute-done | bytes 65568 | tf_op jit(solution)/shard_map/ppermute | solution.py:412
  40.4 0.0 collective-permute-done.16.p3_ref
  40.4 0.1 collective-permute-start.17
  40.5 1.0 %collective-permute-start.18 = (bf16[8,1024]{1,0:T(8,128)(2,1)S(1)}, bf16[8,1024]{1,0:T(8,128)(2,1)S(1)}, u32[]{:S(2)}, u32[]{:S(2)}) collective-permute-start(bf16[8,1024]{1,0:T(8,128)(2,1)S(1)} %get-tuple-element.30), channel_id=1, source_target_pairs={{0,2},{1,3},{2,0},{3,1},{4,6},{5,7},{6,4},{7,5},{8,10},{9,11},{10,... | collective-permute-start | bytes 49160 | tf_op jit(solution)/shard_map/ppermute | solution.py:412
  41.5 0.8 %collective-permute-start.19 = (bf16[8,1024]{1,0:T(8,128)(2,1)S(1)}, bf16[8,1024]{1,0:T(8,128)(2,1)S(1)}, u32[]{:S(2)}, u32[]{:S(2)}) collective-permute-start(bf16[8,1024]{1,0:T(8,128)(2,1)S(1)} %get-tuple-element.31), channel_id=1, source_target_pairs={{0,3},{1,2},{2,1},{3,0},{4,7},{5,6},{6,5},{7,4},{8,11},{9,10},{10,... | collective-permute-start | bytes 49160 | tf_op jit(solution)/shard_map/ppermute | solution.py:412
  42.4 0.0 collective-permute-done.17.p1_ref
  42.4 1.9 %collective-permute-done.18.p2_ref = bf16[8,1024]{1,0:T(8,128)(2,1)S(1)} collective-permute-done((bf16[8,1024]{1,0:T(8,128)(2,1)S(1)}, bf16[8,1024]{1,0:T(8,128)(2,1)S(1)}, u32[]{:S(2)}, u32[]{:S(2)}) %collective-permute-start.18) | collective-permute-done | bytes 16416 | tf_op jit(solution)/shard_map/ppermute | solution.py:412
  44.3 0.4 collective-permute-done.19.p3_ref
  44.7 0.6 %shard_map.117 = bf16[8,4096]{1,0:T(8,128)(2,1)} custom-call(bf16[8,1024]{1,0:T(8,128)(2,1)S(1)} %get-tuple-element.28.p0_ref, bf16[8,1024]{1,0:T(8,128)(2,1)S(1)} %collective-permute-done.17.p1_ref, bf16[8,1024]{1,0:T(8,128)(2,1)S(1)} %collective-permute-done.18.p2_ref, bf16[8,1024]{1,0:T(8,128)(2,1)S(1)} %collective-permute-done.19.p3_ref), custom_call_target="tpu_custom_call" | custom-call | bytes 131072 | tf_op jit(solution)/shard_map/pallas_call | solution.py:398
  (13 shorter events, 0.0 us)
Async XLA Ops:
  1.5 7.7 %collective-permute-start.2 = (bf16[8,4224]{1,0:T(8,128)(2,1)S(1)}, bf16[8,4224]{1,0:T(8,128)(2,1)S(1)}, u32[]{:S(2)}, u32[]{:S(2)}) collective-permute-start(bf16[8,4224]{1,0:T(8,128)(2,1)S(1)} %shard_map.104.refs_1_), channel_id=1, source_target_pairs={{0,12},{4,8},{8,4},{12,0},{1,13},{5,9},{9,5},{13,1},{2,14},{6,10},... | collective-permute-start | bytes 202760 | tf_op jit(solution)/shard_map/ppermute | solution.py:412
  6.7 5.8 %collective-permute-start.1 = (bf16[8,4224]{1,0:T(8,128)(2,1)S(1)}, bf16[8,4224]{1,0:T(8,128)(2,1)S(1)}, u32[]{:S(2)}, u32[]{:S(2)}) collective-permute-start(bf16[8,4224]{1,0:T(8,128)(2,1)S(1)} %shard_map.104.refs_1_), channel_id=1, source_target_pairs={{0,8},{4,12},{8,0},{12,4},{1,9},{5,13},{9,1},{13,5},{2,10},{6,14},... | collective-permute-start | bytes 202760 | tf_op jit(solution)/shard_map/ppermute | solution.py:412
  6.7 7.3 %collective-permute-start = (bf16[8,4224]{1,0:T(8,128)(2,1)S(1)}, bf16[8,4224]{1,0:T(8,128)(2,1)S(1)}, u32[]{:S(2)}, u32[]{:S(2)}) collective-permute-start(bf16[8,4224]{1,0:T(8,128)(2,1)S(1)} %shard_map.104.refs_1_), channel_id=1, source_target_pairs={{0,4},{4,0},{8,12},{12,8},{1,5},{5,1},{9,13},{13,9},{2,6},{6,2},{1... | collective-permute-start | bytes 202760 | tf_op jit(solution)/shard_map/ppermute | solution.py:412
  7.3 7.4 %collective-permute-start.4 = (bf16[8,4224]{1,0:T(8,128)(2,1)S(1)}, bf16[8,4224]{1,0:T(8,128)(2,1)S(1)}, u32[]{:S(2)}, u32[]{:S(2)}) collective-permute-start(bf16[8,4224]{1,0:T(8,128)(2,1)S(1)} %shard_map.104.refs_1_), channel_id=1, source_target_pairs={{0,2},{1,3},{2,0},{3,1},{4,6},{5,7},{6,4},{7,5},{8,10},{9,11},{10,... | collective-permute-start | bytes 202760 | tf_op jit(solution)/shard_map/ppermute | solution.py:412
  9.3 5.4 %collective-permute-start.7 = (bf16[8,4224]{1,0:T(8,128)(2,1)S(1)}, bf16[8,4224]{1,0:T(8,128)(2,1)S(1)}, u32[]{:S(2)}, u32[]{:S(2)}) collective-permute-start(bf16[8,4224]{1,0:T(8,128)(2,1)S(1)} %shard_map.107), channel_id=1, source_target_pairs={{0,2},{1,3},{2,0},{3,1},{4,6},{5,7},{6,4},{7,5},{8,10},{9,11},{10,... | collective-permute-start | bytes 202760 | tf_op jit(solution)/shard_map/ppermute | solution.py:412
  12.4 7.5 %slice-start.2 = ((s8[8388608]{0:T(1024)(128)(4,1)}), s8[4194304]{0:T(1024)(128)(4,1)S(1)}, s32[]{:S(2)}) async-start(s8[8388608]{0:T(1024)(128)(4,1)} %bitcast.18), calls=%async_computation.2 | async-start | bytes 8388608
  12.4 7.5 %slice-start.4 = ((s8[8388608]{0:T(1024)(128)(4,1)}), s8[4194304]{0:T(1024)(128)(4,1)S(1)}, s32[]{:S(2)}) async-start(s8[8388608]{0:T(1024)(128)(4,1)} %bitcast.20), calls=%async_computation.4 | async-start | bytes 8388608
  12.4 7.5 %slice-start.3 = ((s8[8388608]{0:T(1024)(128)(4,1)}), s8[4194304]{0:T(1024)(128)(4,1)S(1)}, s32[]{:S(2)}) async-start(s8[8388608]{0:T(1024)(128)(4,1)} %bitcast.18), calls=%async_computation.3 | async-start | bytes 8388608
  12.4 7.5 %slice-start.5 = ((s8[8388608]{0:T(1024)(128)(4,1)}), s8[4194304]{0:T(1024)(128)(4,1)S(1)}, s32[]{:S(2)}) async-start(s8[8388608]{0:T(1024)(128)(4,1)} %bitcast.20), calls=%async_computation.5 | async-start | bytes 8388608
  12.4 5.0 %collective-permute-start.6 = (bf16[8,4224]{1,0:T(8,128)(2,1)S(1)}, bf16[8,4224]{1,0:T(8,128)(2,1)S(1)}, u32[]{:S(2)}, u32[]{:S(2)}) collective-permute-start(bf16[8,4224]{1,0:T(8,128)(2,1)S(1)} %shard_map.106), channel_id=1, source_target_pairs={{0,2},{1,3},{2,0},{3,1},{4,6},{5,7},{6,4},{7,5},{8,10},{9,11},{10,... | collective-permute-start | bytes 202760 | tf_op jit(solution)/shard_map/ppermute | solution.py:412
  14.0 4.3 %collective-permute-start.5 = (bf16[8,4224]{1,0:T(8,128)(2,1)S(1)}, bf16[8,4224]{1,0:T(8,128)(2,1)S(1)}, u32[]{:S(2)}, u32[]{:S(2)}) collective-permute-start(bf16[8,4224]{1,0:T(8,128)(2,1)S(1)} %shard_map.105), channel_id=1, source_target_pairs={{0,2},{1,3},{2,0},{3,1},{4,6},{5,7},{6,4},{7,5},{8,10},{9,11},{10,... | collective-permute-start | bytes 202760 | tf_op jit(solution)/shard_map/ppermute | solution.py:412
  14.6 3.8 %collective-permute-start.3 = (bf16[4,8,4224]{2,1,0:T(8,128)(2,1)S(1)}, bf16[4,8,4224]{2,1,0:T(8,128)(2,1)S(1)}, u32[]{:S(2)}, u32[]{:S(2)}) collective-permute-start(bf16[4,8,4224]{2,1,0:T(8,128)(2,1)S(1)} %get-tuple-element.34), channel_id=1, source_target_pairs={{0,1},{1,0},{2,3},{3,2},{4,5},{5,4},{6,7},{7,6},{8,9},{9,8},{10,11... | collective-permute-start | bytes 811016 | tf_op jit(solution)/shard_map/ppermute | solution.py:412
  18.3 1.6 %collective-permute-start.8 = (bf16[4,8,4224]{2,1,0:T(8,128)(2,1)S(1)}, bf16[4,8,4224]{2,1,0:T(8,128)(2,1)S(1)}, u32[]{:S(2)}, u32[]{:S(2)}) collective-permute-start(bf16[4,8,4224]{2,1,0:T(8,128)(2,1)S(1)} %get-tuple-element.32), channel_id=1, source_target_pairs={{0,1},{1,0},{2,3},{3,2},{4,5},{5,4},{6,7},{7,6},{8,9},{9,8},{10,11... | collective-permute-start | bytes 811016 | tf_op jit(solution)/shard_map/ppermute | solution.py:412
  21.6 6.2 %collective-permute-start.10 = (bf16[2,96,256]{2,1,0:T(8,128)(2,1)S(1)}, bf16[2,96,256]{2,1,0:T(8,128)(2,1)S(1)}, u32[]{:S(2)}, u32[]{:S(2)}) collective-permute-start(bf16[2,96,256]{2,1,0:T(8,128)(2,1)S(1)} %get-tuple-element.17.refs_6_), channel_id=1, source_target_pairs={{0,2},{1,3},{2,0},{3,1},{4,6},{5,7},{6,4},{7,5},{8,10},{9,11},{10,... | collective-permute-start | bytes 294920 | tf_op jit(solution)/shard_map/ppermute | solution.py:412
  22.7 2.6 %copy-start = (bf16[2,512,576]{1,2,0:T(8,128)(2,1)S(1)}, bf16[2,512,576]{1,2,0:T(8,128)(2,1)}, u32[]{:S(2)}) copy-start(bf16[2,512,576]{1,2,0:T(8,128)(2,1)} %param.16) | copy-start | bytes 3538948
  22.7 2.6 %copy-start.1 = (bf16[2,128,576]{1,2,0:T(8,128)(2,1)S(1)}, bf16[2,128,576]{1,2,0:T(8,128)(2,1)}, u32[]{:S(2)}) copy-start(bf16[2,128,576]{1,2,0:T(8,128)(2,1)} %param.15) | copy-start | bytes 884740
  22.7 2.6 %copy-start.2 = (s32[2]{0:T(128)S(1)}, s32[2]{0:T(128)}, u32[]{:S(2)}) copy-start(s32[2]{0:T(128)} %lengths_ref.1) | copy-start | bytes 28
  24.2 3.8 %slice-start = ((s8[8388608]{0:T(1024)(128)(4,1)}), s8[4194304]{0:T(1024)(128)(4,1)S(1)}, s32[]{:S(2)}) async-start(s8[8388608]{0:T(1024)(128)(4,1)} %bitcast.16), calls=%async_computation | async-start | bytes 8388608
  24.2 3.8 %collective-permute-start.9 = (bf16[4,96,256]{2,1,0:T(8,128)(2,1)S(1)}, bf16[4,96,256]{2,1,0:T(8,128)(2,1)S(1)}, u32[]{:S(2)}, u32[]{:S(2)}) collective-permute-start(bf16[4,96,256]{2,1,0:T(8,128)(2,1)S(1)} %get-tuple-element.22.refs_0_), channel_id=1, source_target_pairs={{0,1},{1,0},{2,3},{3,2},{4,5},{5,4},{6,7},{7,6},{8,9},{9,8},{10,11... | collective-permute-start | bytes 589832 | tf_op jit(solution)/shard_map/ppermute | solution.py:412
  24.3 5.2 %collective-permute-start.11 = (bf16[2,96,256]{2,1,0:T(8,128)(2,1)S(1)}, bf16[2,96,256]{2,1,0:T(8,128)(2,1)S(1)}, u32[]{:S(2)}, u32[]{:S(2)}) collective-permute-start(bf16[2,96,256]{2,1,0:T(8,128)(2,1)S(1)} %get-tuple-element.23.after_ref), channel_id=1, source_target_pairs={{0,2},{1,3},{2,0},{3,1},{4,6},{5,7},{6,4},{7,5},{8,10},{9,11},{10,... | collective-permute-start | bytes 294920 | tf_op jit(solution)/shard_map/ppermute | solution.py:412
  25.3 2.6 %slice-start.1 = ((s8[8388608]{0:T(1024)(128)(4,1)}), s8[4194304]{0:T(1024)(128)(4,1)S(1)}, s32[]{:S(2)}) async-start(s8[8388608]{0:T(1024)(128)(4,1)} %bitcast.16), calls=%async_computation.1 | async-start | bytes 8388608
  27.8 2.3 %collective-permute-start.12 = (bf16[2,96,256]{2,1,0:T(8,128)(2,1)S(1)}, bf16[2,96,256]{2,1,0:T(8,128)(2,1)S(1)}, u32[]{:S(2)}, u32[]{:S(2)}) collective-permute-start(bf16[2,96,256]{2,1,0:T(8,128)(2,1)S(1)} %shard_map.111.refs_2_), channel_id=1, source_target_pairs={{0,1},{1,0},{2,3},{3,2},{4,5},{5,4},{6,7},{7,6},{8,9},{9,8},{10,11... | collective-permute-start | bytes 294920 | tf_op jit(solution)/shard_map/ppermute | solution.py:412
  29.5 1.3 %collective-permute-start.13 = (bf16[2,96,256]{2,1,0:T(8,128)(2,1)S(1)}, bf16[2,96,256]{2,1,0:T(8,128)(2,1)S(1)}, u32[]{:S(2)}, u32[]{:S(2)}) collective-permute-start(bf16[2,96,256]{2,1,0:T(8,128)(2,1)S(1)} %shard_map.113.refs_2_), channel_id=1, source_target_pairs={{0,1},{1,0},{2,3},{3,2},{4,5},{5,4},{6,7},{7,6},{8,9},{9,8},{10,11... | collective-permute-start | bytes 294920 | tf_op jit(solution)/shard_map/ppermute | solution.py:412
  31.6 6.8 %collective-permute-start.14 = (bf16[32,1024]{1,0:T(8,128)(2,1)S(1)}, bf16[32,1024]{1,0:T(8,128)(2,1)S(1)}, u32[]{:S(2)}, u32[]{:S(2)}) collective-permute-start(bf16[32,1024]{1,0:T(8,128)(2,1)S(1)} %get-tuple-element.25), channel_id=1, source_target_pairs={{0,12},{4,8},{8,4},{12,0},{1,13},{5,9},{9,5},{13,1},{2,14},{6,10},... | collective-permute-start | bytes 196616 | tf_op jit(solution)/shard_map/ppermute | solution.py:412
  34.0 6.4 %collective-permute-start.15 = (bf16[32,1024]{1,0:T(8,128)(2,1)S(1)}, bf16[32,1024]{1,0:T(8,128)(2,1)S(1)}, u32[]{:S(2)}, u32[]{:S(2)}) collective-permute-start(bf16[32,1024]{1,0:T(8,128)(2,1)S(1)} %get-tuple-element.26), channel_id=1, source_target_pairs={{0,8},{4,12},{8,0},{12,4},{1,9},{5,13},{9,1},{13,5},{2,10},{6,14},... | collective-permute-start | bytes 196616 | tf_op jit(solution)/shard_map/ppermute | solution.py:412
  34.0 6.4 %collective-permute-start.16 = (bf16[32,1024]{1,0:T(8,128)(2,1)S(1)}, bf16[32,1024]{1,0:T(8,128)(2,1)S(1)}, u32[]{:S(2)}, u32[]{:S(2)}) collective-permute-start(bf16[32,1024]{1,0:T(8,128)(2,1)S(1)} %get-tuple-element.27), channel_id=1, source_target_pairs={{0,4},{4,0},{8,12},{12,8},{1,5},{5,1},{9,13},{13,9},{2,6},{6,2},{1... | collective-permute-start | bytes 196616 | tf_op jit(solution)/shard_map/ppermute | solution.py:412
  40.4 1.9 %collective-permute-start.17 = (bf16[8,1024]{1,0:T(8,128)(2,1)S(1)}, bf16[8,1024]{1,0:T(8,128)(2,1)S(1)}, u32[]{:S(2)}, u32[]{:S(2)}) collective-permute-start(bf16[8,1024]{1,0:T(8,128)(2,1)S(1)} %get-tuple-element.29), channel_id=1, source_target_pairs={{0,1},{1,0},{2,3},{3,2},{4,5},{5,4},{6,7},{7,6},{8,9},{9,8},{10,11... | collective-permute-start | bytes 49160 | tf_op jit(solution)/shard_map/ppermute | solution.py:412
  40.5 3.8 %collective-permute-start.18 = (bf16[8,1024]{1,0:T(8,128)(2,1)S(1)}, bf16[8,1024]{1,0:T(8,128)(2,1)S(1)}, u32[]{:S(2)}, u32[]{:S(2)}) collective-permute-start(bf16[8,1024]{1,0:T(8,128)(2,1)S(1)} %get-tuple-element.30), channel_id=1, source_target_pairs={{0,2},{1,3},{2,0},{3,1},{4,6},{5,7},{6,4},{7,5},{8,10},{9,11},{10,... | collective-permute-start | bytes 49160 | tf_op jit(solution)/shard_map/ppermute | solution.py:412
  41.5 3.2 %collective-permute-start.19 = (bf16[8,1024]{1,0:T(8,128)(2,1)S(1)}, bf16[8,1024]{1,0:T(8,128)(2,1)S(1)}, u32[]{:S(2)}, u32[]{:S(2)}) collective-permute-start(bf16[8,1024]{1,0:T(8,128)(2,1)S(1)} %get-tuple-element.31), channel_id=1, source_target_pairs={{0,3},{1,2},{2,1},{3,0},{4,7},{5,6},{6,5},{7,4},{8,11},{9,10},{10,... | collective-permute-start | bytes 49160 | tf_op jit(solution)/shard_map/ppermute | solution.py:412

commit v8 on v7

--- a/solution.py
+++ b/solution.py
@@ -429,7 +429,7 @@
     experts_all = local_experts * 4
     capacity = max(2, 3 * rows_dev * expert_ids.shape[1] // (2 * experts_all))
     sent = pack(hidden_rows, expert_ids, gate_values, experts_all)
-    along_z = [sent] + [swap(sent, "expert", k) for k in (1, 2, 3)]
+    along_z = [sent] + [swap(sent, "expert", k) for k in (2, 1, 3)]
     along_z[1:] = [once_done(block, sent, 4 * 10**9) for block in along_z[1:]]
     along_x = [swap(block, "dp", 2) for block in along_z]
     mine_z, mine_x = jnp.stack(along_z), jnp.stack(along_x)
@@ -455,7 +455,7 @@
     next_far = swap(next_x, "dp", 1)
     begun_next = down_part(half, (hidden, hidden_c, next_x), down_proj)
     partial = down_last(spread, (begun_first, begun_next), (first_far, next_far), down_proj)
-    arrived = [partial[0]] + [swap(partial[k], "expert", k) for k in (3, 2, 1)]
+    arrived = [partial[0]] + [swap(partial[j], "expert", k) for j, k in ((3, 3), (2, 1), (1, 2))]
     own, to_core, to_x, to_far = collect(arrived)
     far = swap(to_far, "dp", 3)
     blended = place_all((own, swap(to_core, "dp", 1), swap(to_x, "dp", 2), far))

time: 45.5 us -> 44.8 us (0.985)
  waiting for transfers between devices: 15 us -> 14.3 us
    ppermute x20, waiting for transfers between devices: 15 us -> 14.3 us  [swap(): return lax.ppermute(value, axis, [(i, i ^ bit) for i in range(size)])]
  transfers between devices with their start and end apart: 20 -> 20, of which waited for: 11 -> 13; matrix products, arithmetic and copies ran while one was open for 0% -> 0% of each run, Pallas kernels for 11% -> 12%
where the time goes in v8:
time: 44.8 us; the launch traced here: 44.6 us
  starting transfers between devices  20.2 us (45%)
  waiting for transfers between devices  14.3 us (32%)
  Pallas kernels  9.14 us (20%)
  between operations  0.82 us (2%)
    ppermute x20, starting transfers between devices, swap(): return lax.ppermute(value, axis, [(i, i ^ bit) for i in range(size)])  20.2 us
    ppermute x20, waiting for transfers between devices, swap(): return lax.ppermute(value, axis, [(i, i ^ bit) for i in range(size)])  14.3 us
    pallas_call x1, Pallas kernels, attend_after(): pl.pallas_call(attend_after_kernel, in_specs=[whole(pltpu.SMEM), whole(),...  2.47 us
    pallas_call x1, Pallas kernels, gate_up_first(): pl.pallas_call(lambda *refs: gate_up_first_kernel(experts_all, *refs), in...  1.62 us
    pallas_call x1, Pallas kernels, gate_up_next(): pl.pallas_call(gate_up_next_kernel, in_specs=[whole()] * 10, out_specs=[w...  1.44 us
    pallas_call x2, Pallas kernels, down_part(): pl.pallas_call(lambda *refs: down_part_kernel(start, *refs), in_specs=[wh...  1.27 us
    pallas_call x1, Pallas kernels, pack(): pl.pallas_call(lambda *refs: pack_kernel(experts_all, *refs), in_specs=[w...  0.9 us
  transfers between devices with their start and end apart: 20, of which 13 were waited for; matrix products, arithmetic and copies ran while one was open for 0% of the time, Pallas kernels for 12%

profile of v8, /device:TPU:0, one launch (start us, length us, event | category | flops | bytes accessed | tf_op | source)
XLA Modules:
  0.0 44.6 jit_solution(4776410740603321580)
XLA Ops:
  0.6 0.9 %shard_map.104.refs_1_ = bf16[8,4224]{1,0:T(8,128)(2,1)S(1)} custom-call(bf16[8,4096]{1,0:T(8,128)(2,1)} %refs_0_.1, s32[8,8]{1,0:T(8,128)} %refs_1_.1, f32[8,8]{1,0:T(8,128)} %refs_2_.1), custom_call_target="tpu_custom_call" | custom-call | bytes 131072 | tf_op jit(solution)/shard_map/pallas_call | solution.py:141
  1.5 5.1 %collective-permute-start.2 = (bf16[8,4224]{1,0:T(8,128)(2,1)S(1)}, bf16[8,4224]{1,0:T(8,128)(2,1)S(1)}, u32[]{:S(2)}, u32[]{:S(2)}) collective-permute-start(bf16[8,4224]{1,0:T(8,128)(2,1)S(1)} %shard_map.104.refs_1_), channel_id=1, source_target_pairs={{0,12},{4,8},{8,4},{12,0},{1,13},{5,9},{9,5},{13,1},{2,14},{6,10},... | collective-permute-start | bytes 202760 | tf_op jit(solution)/shard_map/ppermute | solution.py:412
  6.7 0.0 collective-permute-start.1
  6.7 0.6 %collective-permute-start = (bf16[8,4224]{1,0:T(8,128)(2,1)S(1)}, bf16[8,4224]{1,0:T(8,128)(2,1)S(1)}, u32[]{:S(2)}, u32[]{:S(2)}) collective-permute-start(bf16[8,4224]{1,0:T(8,128)(2,1)S(1)} %shard_map.104.refs_1_), channel_id=1, source_target_pairs={{0,8},{4,12},{8,0},{12,4},{1,9},{5,13},{9,1},{13,5},{2,10},{6,14},... | collective-permute-start | bytes 202760 | tf_op jit(solution)/shard_map/ppermute | solution.py:412
  7.3 1.6 %collective-permute-start.4 = (bf16[8,4224]{1,0:T(8,128)(2,1)S(1)}, bf16[8,4224]{1,0:T(8,128)(2,1)S(1)}, u32[]{:S(2)}, u32[]{:S(2)}) collective-permute-start(bf16[8,4224]{1,0:T(8,128)(2,1)S(1)} %shard_map.104.refs_1_), channel_id=1, source_target_pairs={{0,2},{1,3},{2,0},{3,1},{4,6},{5,7},{6,4},{7,5},{8,10},{9,11},{10,... | collective-permute-start | bytes 202760 | tf_op jit(solution)/shard_map/ppermute | solution.py:412
  8.9 0.7 %collective-permute-done.2.refs_0_ = bf16[8,4224]{1,0:T(8,128)(2,1)S(1)} collective-permute-done((bf16[8,4224]{1,0:T(8,128)(2,1)S(1)}, bf16[8,4224]{1,0:T(8,128)(2,1)S(1)}, u32[]{:S(2)}, u32[]{:S(2)}) %collective-permute-start.2) | collective-permute-done | bytes 67616 | tf_op jit(solution)/shard_map/ppermute | solution.py:412
  9.6 1.5 %collective-permute-start.7 = (bf16[8,4224]{1,0:T(8,128)(2,1)S(1)}, bf16[8,4224]{1,0:T(8,128)(2,1)S(1)}, u32[]{:S(2)}, u32[]{:S(2)}) collective-permute-start(bf16[8,4224]{1,0:T(8,128)(2,1)S(1)} %shard_map.107), channel_id=1, source_target_pairs={{0,2},{1,3},{2,0},{3,1},{4,6},{5,7},{6,4},{7,5},{8,10},{9,11},{10,... | collective-permute-start | bytes 202760 | tf_op jit(solution)/shard_map/ppermute | solution.py:412
  11.1 0.3 collective-permute-done.1.refs_0_
  11.4 0.0 slice-start.2
  11.4 0.0 slice-start.4
  11.4 0.0 slice-start.3
  11.4 0.0 slice-start.5
  11.4 1.7 %collective-permute-start.6 = (bf16[8,4224]{1,0:T(8,128)(2,1)S(1)}, bf16[8,4224]{1,0:T(8,128)(2,1)S(1)}, u32[]{:S(2)}, u32[]{:S(2)}) collective-permute-start(bf16[8,4224]{1,0:T(8,128)(2,1)S(1)} %shard_map.106), channel_id=1, source_target_pairs={{0,2},{1,3},{2,0},{3,1},{4,6},{5,7},{6,4},{7,5},{8,10},{9,11},{10,... | collective-permute-start | bytes 202760 | tf_op jit(solution)/shard_map/ppermute | solution.py:412
  13.1 0.0 collective-permute-done.refs_0_
  13.1 0.7 %collective-permute-start.5 = (bf16[8,4224]{1,0:T(8,128)(2,1)S(1)}, bf16[8,4224]{1,0:T(8,128)(2,1)S(1)}, u32[]{:S(2)}, u32[]{:S(2)}) collective-permute-start(bf16[8,4224]{1,0:T(8,128)(2,1)S(1)} %shard_map.105), channel_id=1, source_target_pairs={{0,2},{1,3},{2,0},{3,1},{4,6},{5,7},{6,4},{7,5},{8,10},{9,11},{10,... | collective-permute-start | bytes 202760 | tf_op jit(solution)/shard_map/ppermute | solution.py:412
  13.8 0.1 pad_maximum_fusion
  13.9 0.1 collective-permute-start.3
  14.0 0.0 collective-permute-done.4
  14.0 0.4 collective-permute-done.7
  14.3 2.2 %collective-permute-done.6 = bf16[8,4224]{1,0:T(8,128)(2,1)S(1)} collective-permute-done((bf16[8,4224]{1,0:T(8,128)(2,1)S(1)}, bf16[8,4224]{1,0:T(8,128)(2,1)S(1)}, u32[]{:S(2)}, u32[]{:S(2)}) %collective-permute-start.6) | collective-permute-done | bytes 67616 | tf_op jit(solution)/shard_map/ppermute | solution.py:412
  16.5 0.9 %collective-permute-done.5 = bf16[8,4224]{1,0:T(8,128)(2,1)S(1)} collective-permute-done((bf16[8,4224]{1,0:T(8,128)(2,1)S(1)}, bf16[8,4224]{1,0:T(8,128)(2,1)S(1)}, u32[]{:S(2)}, u32[]{:S(2)}) %collective-permute-start.5) | collective-permute-done | bytes 67616 | tf_op jit(solution)/shard_map/ppermute | solution.py:412
  17.4 0.1 pad_maximum_fusion.1
  17.5 0.1 collective-permute-start.8
  17.5 0.0 collective-permute-done.3
  17.6 1.5 %collective-permute-done.8 = bf16[4,8,4224]{2,1,0:T(8,128)(2,1)S(1)} collective-permute-done((bf16[4,8,4224]{2,1,0:T(8,128)(2,1)S(1)}, bf16[4,8,4224]{2,1,0:T(8,128)(2,1)S(1)}, u32[]{:S(2)}, u32[]{:S(2)}) %collective-permute-start.8) | collective-permute-done | bytes 270368 | tf_op jit(solution)/shard_map/ppermute | solution.py:412
  19.1 0.0 slice-done.2
  19.1 0.0 slice-done.4
  19.1 0.0 slice-done.3
  19.1 0.0 slice-done.5
  19.1 1.6 %shard_map.108 = (bf16[2,96,256]{2,1,0:T(8,128)(2,1)S(1)}, f32[128,128]{1,0:T(8,128)S(1)}, f32[128,128]{1,0:T(8,128)S(1)}, f32[128,128]{1,0:T(8,128)S(1)}) custom-call(bf16[32,4224]{1,0:T(8,128)(2,1)S(1)} %get-tuple-element.35.refs_0_, bf16[32,4224]{1,0:T(8,128)(2,1)S(1)} %bitcast.22, bf16[32,4224]{1,0:T(8,128)(2,1)S(1)} %get-tuple-element.33.refs_2_, ...), custom_call_target="tpu_custom_call" | custom-call | flops 1073741824 | bytes 8388608 | tf_op jit(solution)/shard_map/pallas_call | solution.py:241
  20.7 1.0 %collective-permute-start.10 = (bf16[2,96,256]{2,1,0:T(8,128)(2,1)S(1)}, bf16[2,96,256]{2,1,0:T(8,128)(2,1)S(1)}, u32[]{:S(2)}, u32[]{:S(2)}) collective-permute-start(bf16[2,96,256]{2,1,0:T(8,128)(2,1)S(1)} %get-tuple-element.17.refs_6_), channel_id=1, source_target_pairs={{0,2},{1,3},{2,0},{3,1},{4,6},{5,7},{6,4},{7,5},{8,10},{9,11},{10,... | collective-permute-start | bytes 294920 | tf_op jit(solution)/shard_map/ppermute | solution.py:412
  21.7 1.4 %shard_map.109 = (bf16[2,96,256]{2,1,0:T(8,128)(2,1)S(1)}, bf16[4,96,256]{2,1,0:T(8,128)(2,1)S(1)}, bf16[256,512]{1,0:T(8,128)(2,1)S(1)}) custom-call(bf16[32,4224]{1,0:T(8,128)(2,1)S(1)} %get-tuple-element.35.refs_0_, bf16[32,4224]{1,0:T(8,128)(2,1)S(1)} %bitcast.23, bf16[32,4224]{1,0:T(8,128)(2,1)S(1)} %get-tuple-element.33.refs_2_, ...), custom_call_target="tpu_custom_call" | custom-call | flops 1073741824 | bytes 8388608 | tf_op jit(solution)/shard_map/pallas_call | solution.py:260
  23.1 0.0 slice-start
  23.2 0.1 collective-permute-start.9
  23.2 1.2 %collective-permute-start.11 = (bf16[2,96,256]{2,1,0:T(8,128)(2,1)S(1)}, bf16[2,96,256]{2,1,0:T(8,128)(2,1)S(1)}, u32[]{:S(2)}, u32[]{:S(2)}) collective-permute-start(bf16[2,96,256]{2,1,0:T(8,128)(2,1)S(1)} %get-tuple-element.23.after_ref), channel_id=1, source_target_pairs={{0,2},{1,3},{2,0},{3,1},{4,6},{5,7},{6,4},{7,5},{8,10},{9,11},{10,... | collective-permute-start | bytes 294920 | tf_op jit(solution)/shard_map/ppermute | solution.py:412
  24.4 0.0 copy-done
  24.4 0.0 copy-done.1
  24.4 0.0 copy-done.2
  24.4 2.5 %shard_map.110.refs_1_ = bf16[2,128,512]{2,1,0:T(8,128)(2,1)} custom-call(s32[2]{0:T(128)S(1)} %copy-done.2, bf16[2,576,128]{2,1,0:T(8,128)(2,1)S(1)} %bitcast.31, bf16[2,576,512]{2,1,0:T(8,128)(2,1)S(1)} %bitcast.30, bf16[2,96,256]{2,1,0:T(8,128)(2,1)S(1)} %get-tuple-element.23.after_ref), custom_call_target="tpu_custom_call" | custom-call | flops 4000000000 | tf_op jit(solution)/shard_map/pallas_call | solution.py:75
  26.9 0.0 collective-permute-done.10.refs_0_
  26.9 0.2 collective-permute-start.12
  27.1 0.0 collective-permute-done.9.refs_1_
  27.1 0.0 slice-done
  27.1 0.0 slice-done.1
  27.1 0.6 %shard_map.112.refs_1_.begun_first_ref = f32[2,96,1024]{2,1,0:T(8,128)S(1)} custom-call(bf16[4,96,256]{2,1,0:T(8,128)(2,1)S(1)} %get-tuple-element.22.refs_0_, bf16[4,96,256]{2,1,0:T(8,128)(2,1)S(1)} %collective-permute-done.9.refs_1_, bf16[2,96,256]{2,1,0:T(8,128)(2,1)S(1)} %shard_map.111.refs_2_, bf16[4,1024,1024]{2,1,0:T(8,128)(2,1)S(1)} %bitcast.17), custom_call_target="tpu_custom_call" | custom-call | flops 301989888 | bytes 786432 | tf_op jit(solution)/shard_map/pallas_call | solution.py:289
  27.7 0.7 %collective-permute-done.11.refs_0_ = bf16[2,96,256]{2,1,0:T(8,128)(2,1)S(1)} collective-permute-done((bf16[2,96,256]{2,1,0:T(8,128)(2,1)S(1)}, bf16[2,96,256]{2,1,0:T(8,128)(2,1)S(1)}, u32[]{:S(2)}, u32[]{:S(2)}) %collective-permute-start.11) | collective-permute-done | bytes 98336 | tf_op jit(solution)/shard_map/ppermute | solution.py:412
  28.4 0.0 collective-permute-start.13
  28.4 0.6 %shard_map.114.begun_next_ref = f32[2,96,1024]{2,1,0:T(8,128)S(1)} custom-call(bf16[4,96,256]{2,1,0:T(8,128)(2,1)S(1)} %get-tuple-element.22.refs_0_, bf16[4,96,256]{2,1,0:T(8,128)(2,1)S(1)} %collective-permute-done.9.refs_1_, bf16[2,96,256]{2,1,0:T(8,128)(2,1)S(1)} %shard_map.113.refs_2_, bf16[4,1024,1024]{2,1,0:T(8,128)(2,1)S(1)} %bitcast.17), custom_call_target="tpu_custom_call" | custom-call | flops 301989888 | bytes 786432 | tf_op jit(solution)/shard_map/pallas_call | solution.py:289
  29.1 0.0 collective-permute-done.12.h3_first_ref
  29.1 0.7 %collective-permute-done.13.h3_next_ref = bf16[2,96,256]{2,1,0:T(8,128)(2,1)S(1)} collective-permute-done((bf16[2,96,256]{2,1,0:T(8,128)(2,1)S(1)}, bf16[2,96,256]{2,1,0:T(8,128)(2,1)S(1)}, u32[]{:S(2)}, u32[]{:S(2)}) %collective-permute-start.13) | collective-permute-done | bytes 98336 | tf_op jit(solution)/shard_map/ppermute | solution.py:412
  29.7 0.8 %shard_map.115 = (bf16[32,1024]{1,0:T(8,128)(2,1)S(1)}, bf16[32,1024]{1,0:T(8,128)(2,1)S(1)}, bf16[32,1024]{1,0:T(8,128)(2,1)S(1)}, bf16[32,1024]{1,0:T(8,128)(2,1)S(1)}) custom-call(bf16[256,512]{1,0:T(8,128)(2,1)S(1)} %get-tuple-element.21.spread_ref, f32[2,96,1024]{2,1,0:T(8,128)S(1)} %shard_map.112.refs_1_.begun_first_ref, ...), custom_call_target="tpu_custom_call" | custom-call | flops 268435456 | bytes 3145728 | tf_op jit(solution)/shard_map/pallas_call | solution.py:350
  30.5 3.2 %collective-permute-start.14 = (bf16[32,1024]{1,0:T(8,128)(2,1)S(1)}, bf16[32,1024]{1,0:T(8,128)(2,1)S(1)}, u32[]{:S(2)}, u32[]{:S(2)}) collective-permute-start(bf16[32,1024]{1,0:T(8,128)(2,1)S(1)} %get-tuple-element.25), channel_id=1, source_target_pairs={{0,12},{4,8},{8,4},{12,0},{1,13},{5,9},{9,5},{13,1},{2,14},{6,10},... | collective-permute-start | bytes 196616 | tf_op jit(solution)/shard_map/ppermute | solution.py:412
  33.7 0.0 collective-permute-start.15
  33.7 1.3 %collective-permute-start.16 = (bf16[32,1024]{1,0:T(8,128)(2,1)S(1)}, bf16[32,1024]{1,0:T(8,128)(2,1)S(1)}, u32[]{:S(2)}, u32[]{:S(2)}) collective-permute-start(bf16[32,1024]{1,0:T(8,128)(2,1)S(1)} %get-tuple-element.27), channel_id=1, source_target_pairs={{0,8},{4,12},{8,0},{12,4},{1,9},{5,13},{9,1},{13,5},{2,10},{6,14},... | collective-permute-start | bytes 196616 | tf_op jit(solution)/shard_map/ppermute | solution.py:412
  35.0 2.3 %collective-permute-done.14.p1_ref = bf16[32,1024]{1,0:T(8,128)(2,1)S(1)} collective-permute-done((bf16[32,1024]{1,0:T(8,128)(2,1)S(1)}, bf16[32,1024]{1,0:T(8,128)(2,1)S(1)}, u32[]{:S(2)}, u32[]{:S(2)}) %collective-permute-start.14) | collective-permute-done | bytes 65568 | tf_op jit(solution)/shard_map/ppermute | solution.py:412
  37.3 1.8 %collective-permute-done.15.p2_ref = bf16[32,1024]{1,0:T(8,128)(2,1)S(1)} collective-permute-done((bf16[32,1024]{1,0:T(8,128)(2,1)S(1)}, bf16[32,1024]{1,0:T(8,128)(2,1)S(1)}, u32[]{:S(2)}, u32[]{:S(2)}) %collective-permute-start.15) | collective-permute-done | bytes 65568 | tf_op jit(solution)/shard_map/ppermute | solution.py:412
  39.0 0.5 %collective-permute-done.16.p3_ref = bf16[32,1024]{1,0:T(8,128)(2,1)S(1)} collective-permute-done((bf16[32,1024]{1,0:T(8,128)(2,1)S(1)}, bf16[32,1024]{1,0:T(8,128)(2,1)S(1)}, u32[]{:S(2)}, u32[]{:S(2)}) %collective-permute-start.16) | collective-permute-done | bytes 65568 | tf_op jit(solution)/shard_map/ppermute | solution.py:412
  39.6 0.1 collective-permute-start.17
  39.7 1.1 %collective-permute-start.18 = (bf16[8,1024]{1,0:T(8,128)(2,1)S(1)}, bf16[8,1024]{1,0:T(8,128)(2,1)S(1)}, u32[]{:S(2)}, u32[]{:S(2)}) collective-permute-start(bf16[8,1024]{1,0:T(8,128)(2,1)S(1)} %get-tuple-element.30), channel_id=1, source_target_pairs={{0,2},{1,3},{2,0},{3,1},{4,6},{5,7},{6,4},{7,5},{8,10},{9,11},{10,... | collective-permute-start | bytes 49160 | tf_op jit(solution)/shard_map/ppermute | solution.py:412
  40.8 0.8 %collective-permute-start.19 = (bf16[8,1024]{1,0:T(8,128)(2,1)S(1)}, bf16[8,1024]{1,0:T(8,128)(2,1)S(1)}, u32[]{:S(2)}, u32[]{:S(2)}) collective-permute-start(bf16[8,1024]{1,0:T(8,128)(2,1)S(1)} %get-tuple-element.31), channel_id=1, source_target_pairs={{0,3},{1,2},{2,1},{3,0},{4,7},{5,6},{6,5},{7,4},{8,11},{9,10},{10,... | collective-permute-start | bytes 49160 | tf_op jit(solution)/shard_map/ppermute | solution.py:412
  41.5 0.0 collective-permute-done.17.p1_ref
  41.5 1.9 %collective-permute-done.18.p2_ref = bf16[8,1024]{1,0:T(8,128)(2,1)S(1)} collective-permute-done((bf16[8,1024]{1,0:T(8,128)(2,1)S(1)}, bf16[8,1024]{1,0:T(8,128)(2,1)S(1)}, u32[]{:S(2)}, u32[]{:S(2)}) %collective-permute-start.18) | collective-permute-done | bytes 16416 | tf_op jit(solution)/shard_map/ppermute | solution.py:412
  43.5 0.5 %collective-permute-done.19.p3_ref = bf16[8,1024]{1,0:T(8,128)(2,1)S(1)} collective-permute-done((bf16[8,1024]{1,0:T(8,128)(2,1)S(1)}, bf16[8,1024]{1,0:T(8,128)(2,1)S(1)}, u32[]{:S(2)}, u32[]{:S(2)}) %collective-permute-start.19) | collective-permute-done | bytes 16416 | tf_op jit(solution)/shard_map/ppermute | solution.py:412
  43.9 0.6 %shard_map.117 = bf16[8,4096]{1,0:T(8,128)(2,1)} custom-call(bf16[8,1024]{1,0:T(8,128)(2,1)S(1)} %get-tuple-element.28.p0_ref, bf16[8,1024]{1,0:T(8,128)(2,1)S(1)} %collective-permute-done.17.p1_ref, bf16[8,1024]{1,0:T(8,128)(2,1)S(1)} %collective-permute-done.18.p2_ref, bf16[8,1024]{1,0:T(8,128)(2,1)S(1)} %collective-permute-done.19.p3_ref), custom_call_target="tpu_custom_call" | custom-call | bytes 131072 | tf_op jit(solution)/shard_map/pallas_call | solution.py:398
  (13 shorter events, 0.0 us)
Async XLA Ops:
  1.5 8.1 %collective-permute-start.2 = (bf16[8,4224]{1,0:T(8,128)(2,1)S(1)}, bf16[8,4224]{1,0:T(8,128)(2,1)S(1)}, u32[]{:S(2)}, u32[]{:S(2)}) collective-permute-start(bf16[8,4224]{1,0:T(8,128)(2,1)S(1)} %shard_map.104.refs_1_), channel_id=1, source_target_pairs={{0,12},{4,8},{8,4},{12,0},{1,13},{5,9},{9,5},{13,1},{2,14},{6,10},... | collective-permute-start | bytes 202760 | tf_op jit(solution)/shard_map/ppermute | solution.py:412
  6.7 4.8 %collective-permute-start.1 = (bf16[8,4224]{1,0:T(8,128)(2,1)S(1)}, bf16[8,4224]{1,0:T(8,128)(2,1)S(1)}, u32[]{:S(2)}, u32[]{:S(2)}) collective-permute-start(bf16[8,4224]{1,0:T(8,128)(2,1)S(1)} %shard_map.104.refs_1_), channel_id=1, source_target_pairs={{0,4},{4,0},{8,12},{12,8},{1,5},{5,1},{9,13},{13,9},{2,6},{6,2},{1... | collective-permute-start | bytes 202760 | tf_op jit(solution)/shard_map/ppermute | solution.py:412
  6.7 6.5 %collective-permute-start = (bf16[8,4224]{1,0:T(8,128)(2,1)S(1)}, bf16[8,4224]{1,0:T(8,128)(2,1)S(1)}, u32[]{:S(2)}, u32[]{:S(2)}) collective-permute-start(bf16[8,4224]{1,0:T(8,128)(2,1)S(1)} %shard_map.104.refs_1_), channel_id=1, source_target_pairs={{0,8},{4,12},{8,0},{12,4},{1,9},{5,13},{9,1},{13,5},{2,10},{6,14},... | collective-permute-start | bytes 202760 | tf_op jit(solution)/shard_map/ppermute | solution.py:412
  7.3 6.7 %collective-permute-start.4 = (bf16[8,4224]{1,0:T(8,128)(2,1)S(1)}, bf16[8,4224]{1,0:T(8,128)(2,1)S(1)}, u32[]{:S(2)}, u32[]{:S(2)}) collective-permute-start(bf16[8,4224]{1,0:T(8,128)(2,1)S(1)} %shard_map.104.refs_1_), channel_id=1, source_target_pairs={{0,2},{1,3},{2,0},{3,1},{4,6},{5,7},{6,4},{7,5},{8,10},{9,11},{10,... | collective-permute-start | bytes 202760 | tf_op jit(solution)/shard_map/ppermute | solution.py:412
  9.6 4.7 %collective-permute-start.7 = (bf16[8,4224]{1,0:T(8,128)(2,1)S(1)}, bf16[8,4224]{1,0:T(8,128)(2,1)S(1)}, u32[]{:S(2)}, u32[]{:S(2)}) collective-permute-start(bf16[8,4224]{1,0:T(8,128)(2,1)S(1)} %shard_map.107), channel_id=1, source_target_pairs={{0,2},{1,3},{2,0},{3,1},{4,6},{5,7},{6,4},{7,5},{8,10},{9,11},{10,... | collective-permute-start | bytes 202760 | tf_op jit(solution)/shard_map/ppermute | solution.py:412
  11.4 7.7 %slice-start.2 = ((s8[8388608]{0:T(1024)(128)(4,1)}), s8[4194304]{0:T(1024)(128)(4,1)S(1)}, s32[]{:S(2)}) async-start(s8[8388608]{0:T(1024)(128)(4,1)} %bitcast.18), calls=%async_computation.2 | async-start | bytes 8388608
  11.4 7.7 %slice-start.4 = ((s8[8388608]{0:T(1024)(128)(4,1)}), s8[4194304]{0:T(1024)(128)(4,1)S(1)}, s32[]{:S(2)}) async-start(s8[8388608]{0:T(1024)(128)(4,1)} %bitcast.20), calls=%async_computation.4 | async-start | bytes 8388608
  11.4 7.7 %slice-start.3 = ((s8[8388608]{0:T(1024)(128)(4,1)}), s8[4194304]{0:T(1024)(128)(4,1)S(1)}, s32[]{:S(2)}) async-start(s8[8388608]{0:T(1024)(128)(4,1)} %bitcast.18), calls=%async_computation.3 | async-start | bytes 8388608
  11.4 7.7 %slice-start.5 = ((s8[8388608]{0:T(1024)(128)(4,1)}), s8[4194304]{0:T(1024)(128)(4,1)S(1)}, s32[]{:S(2)}) async-start(s8[8388608]{0:T(1024)(128)(4,1)} %bitcast.20), calls=%async_computation.5 | async-start | bytes 8388608
  11.4 5.1 %collective-permute-start.6 = (bf16[8,4224]{1,0:T(8,128)(2,1)S(1)}, bf16[8,4224]{1,0:T(8,128)(2,1)S(1)}, u32[]{:S(2)}, u32[]{:S(2)}) collective-permute-start(bf16[8,4224]{1,0:T(8,128)(2,1)S(1)} %shard_map.106), channel_id=1, source_target_pairs={{0,2},{1,3},{2,0},{3,1},{4,6},{5,7},{6,4},{7,5},{8,10},{9,11},{10,... | collective-permute-start | bytes 202760 | tf_op jit(solution)/shard_map/ppermute | solution.py:412
  13.1 4.3 %collective-permute-start.5 = (bf16[8,4224]{1,0:T(8,128)(2,1)S(1)}, bf16[8,4224]{1,0:T(8,128)(2,1)S(1)}, u32[]{:S(2)}, u32[]{:S(2)}) collective-permute-start(bf16[8,4224]{1,0:T(8,128)(2,1)S(1)} %shard_map.105), channel_id=1, source_target_pairs={{0,2},{1,3},{2,0},{3,1},{4,6},{5,7},{6,4},{7,5},{8,10},{9,11},{10,... | collective-permute-start | bytes 202760 | tf_op jit(solution)/shard_map/ppermute | solution.py:412
  13.9 3.7 %collective-permute-start.3 = (bf16[4,8,4224]{2,1,0:T(8,128)(2,1)S(1)}, bf16[4,8,4224]{2,1,0:T(8,128)(2,1)S(1)}, u32[]{:S(2)}, u32[]{:S(2)}) collective-permute-start(bf16[4,8,4224]{2,1,0:T(8,128)(2,1)S(1)} %get-tuple-element.34), channel_id=1, source_target_pairs={{0,1},{1,0},{2,3},{3,2},{4,5},{5,4},{6,7},{7,6},{8,9},{9,8},{10,11... | collective-permute-start | bytes 811016 | tf_op jit(solution)/shard_map/ppermute | solution.py:412
  17.5 1.6 %collective-permute-start.8 = (bf16[4,8,4224]{2,1,0:T(8,128)(2,1)S(1)}, bf16[4,8,4224]{2,1,0:T(8,128)(2,1)S(1)}, u32[]{:S(2)}, u32[]{:S(2)}) collective-permute-start(bf16[4,8,4224]{2,1,0:T(8,128)(2,1)S(1)} %get-tuple-element.32), channel_id=1, source_target_pairs={{0,1},{1,0},{2,3},{3,2},{4,5},{5,4},{6,7},{7,6},{8,9},{9,8},{10,11... | collective-permute-start | bytes 811016 | tf_op jit(solution)/shard_map/ppermute | solution.py:412
  20.7 6.2 %collective-permute-start.10 = (bf16[2,96,256]{2,1,0:T(8,128)(2,1)S(1)}, bf16[2,96,256]{2,1,0:T(8,128)(2,1)S(1)}, u32[]{:S(2)}, u32[]{:S(2)}) collective-permute-start(bf16[2,96,256]{2,1,0:T(8,128)(2,1)S(1)} %get-tuple-element.17.refs_6_), channel_id=1, source_target_pairs={{0,2},{1,3},{2,0},{3,1},{4,6},{5,7},{6,4},{7,5},{8,10},{9,11},{10,... | collective-permute-start | bytes 294920 | tf_op jit(solution)/shard_map/ppermute | solution.py:412
  21.7 2.7 %copy-start = (bf16[2,512,576]{1,2,0:T(8,128)(2,1)S(1)}, bf16[2,512,576]{1,2,0:T(8,128)(2,1)}, u32[]{:S(2)}) copy-start(bf16[2,512,576]{1,2,0:T(8,128)(2,1)} %param.16) | copy-start | bytes 3538948
  21.7 2.7 %copy-start.1 = (bf16[2,128,576]{1,2,0:T(8,128)(2,1)S(1)}, bf16[2,128,576]{1,2,0:T(8,128)(2,1)}, u32[]{:S(2)}) copy-start(bf16[2,128,576]{1,2,0:T(8,128)(2,1)} %param.15) | copy-start | bytes 884740
  21.7 2.7 %copy-start.2 = (s32[2]{0:T(128)S(1)}, s32[2]{0:T(128)}, u32[]{:S(2)}) copy-start(s32[2]{0:T(128)} %lengths_ref.1) | copy-start | bytes 28
  23.1 3.9 %slice-start = ((s8[8388608]{0:T(1024)(128)(4,1)}), s8[4194304]{0:T(1024)(128)(4,1)S(1)}, s32[]{:S(2)}) async-start(s8[8388608]{0:T(1024)(128)(4,1)} %bitcast.16), calls=%async_computation | async-start | bytes 8388608
  23.2 3.9 %collective-permute-start.9 = (bf16[4,96,256]{2,1,0:T(8,128)(2,1)S(1)}, bf16[4,96,256]{2,1,0:T(8,128)(2,1)S(1)}, u32[]{:S(2)}, u32[]{:S(2)}) collective-permute-start(bf16[4,96,256]{2,1,0:T(8,128)(2,1)S(1)} %get-tuple-element.22.refs_0_), channel_id=1, source_target_pairs={{0,1},{1,0},{2,3},{3,2},{4,5},{5,4},{6,7},{7,6},{8,9},{9,8},{10,11... | collective-permute-start | bytes 589832 | tf_op jit(solution)/shard_map/ppermute | solution.py:412
  23.2 5.2 %collective-permute-start.11 = (bf16[2,96,256]{2,1,0:T(8,128)(2,1)S(1)}, bf16[2,96,256]{2,1,0:T(8,128)(2,1)S(1)}, u32[]{:S(2)}, u32[]{:S(2)}) collective-permute-start(bf16[2,96,256]{2,1,0:T(8,128)(2,1)S(1)} %get-tuple-element.23.after_ref), channel_id=1, source_target_pairs={{0,2},{1,3},{2,0},{3,1},{4,6},{5,7},{6,4},{7,5},{8,10},{9,11},{10,... | collective-permute-start | bytes 294920 | tf_op jit(solution)/shard_map/ppermute | solution.py:412
  24.4 2.6 %slice-start.1 = ((s8[8388608]{0:T(1024)(128)(4,1)}), s8[4194304]{0:T(1024)(128)(4,1)S(1)}, s32[]{:S(2)}) async-start(s8[8388608]{0:T(1024)(128)(4,1)} %bitcast.16), calls=%async_computation.1 | async-start | bytes 8388608
  26.9 2.2 %collective-permute-start.12 = (bf16[2,96,256]{2,1,0:T(8,128)(2,1)S(1)}, bf16[2,96,256]{2,1,0:T(8,128)(2,1)S(1)}, u32[]{:S(2)}, u32[]{:S(2)}) collective-permute-start(bf16[2,96,256]{2,1,0:T(8,128)(2,1)S(1)} %shard_map.111.refs_2_), channel_id=1, source_target_pairs={{0,1},{1,0},{2,3},{3,2},{4,5},{5,4},{6,7},{7,6},{8,9},{9,8},{10,11... | collective-permute-start | bytes 294920 | tf_op jit(solution)/shard_map/ppermute | solution.py:412
  28.4 1.3 %collective-permute-start.13 = (bf16[2,96,256]{2,1,0:T(8,128)(2,1)S(1)}, bf16[2,96,256]{2,1,0:T(8,128)(2,1)S(1)}, u32[]{:S(2)}, u32[]{:S(2)}) collective-permute-start(bf16[2,96,256]{2,1,0:T(8,128)(2,1)S(1)} %shard_map.113.refs_2_), channel_id=1, source_target_pairs={{0,1},{1,0},{2,3},{3,2},{4,5},{5,4},{6,7},{7,6},{8,9},{9,8},{10,11... | collective-permute-start | bytes 294920 | tf_op jit(solution)/shard_map/ppermute | solution.py:412
  30.5 6.7 %collective-permute-start.14 = (bf16[32,1024]{1,0:T(8,128)(2,1)S(1)}, bf16[32,1024]{1,0:T(8,128)(2,1)S(1)}, u32[]{:S(2)}, u32[]{:S(2)}) collective-permute-start(bf16[32,1024]{1,0:T(8,128)(2,1)S(1)} %get-tuple-element.25), channel_id=1, source_target_pairs={{0,12},{4,8},{8,4},{12,0},{1,13},{5,9},{9,5},{13,1},{2,14},{6,10},... | collective-permute-start | bytes 196616 | tf_op jit(solution)/shard_map/ppermute | solution.py:412
  33.7 5.3 %collective-permute-start.15 = (bf16[32,1024]{1,0:T(8,128)(2,1)S(1)}, bf16[32,1024]{1,0:T(8,128)(2,1)S(1)}, u32[]{:S(2)}, u32[]{:S(2)}) collective-permute-start(bf16[32,1024]{1,0:T(8,128)(2,1)S(1)} %get-tuple-element.26), channel_id=1, source_target_pairs={{0,4},{4,0},{8,12},{12,8},{1,5},{5,1},{9,13},{13,9},{2,6},{6,2},{1... | collective-permute-start | bytes 196616 | tf_op jit(solution)/shard_map/ppermute | solution.py:412
  33.7 5.9 %collective-permute-start.16 = (bf16[32,1024]{1,0:T(8,128)(2,1)S(1)}, bf16[32,1024]{1,0:T(8,128)(2,1)S(1)}, u32[]{:S(2)}, u32[]{:S(2)}) collective-permute-start(bf16[32,1024]{1,0:T(8,128)(2,1)S(1)} %get-tuple-element.27), channel_id=1, source_target_pairs={{0,8},{4,12},{8,0},{12,4},{1,9},{5,13},{9,1},{13,5},{2,10},{6,14},... | collective-permute-start | bytes 196616 | tf_op jit(solution)/shard_map/ppermute | solution.py:412
  39.6 1.9 %collective-permute-start.17 = (bf16[8,1024]{1,0:T(8,128)(2,1)S(1)}, bf16[8,1024]{1,0:T(8,128)(2,1)S(1)}, u32[]{:S(2)}, u32[]{:S(2)}) collective-permute-start(bf16[8,1024]{1,0:T(8,128)(2,1)S(1)} %get-tuple-element.29), channel_id=1, source_target_pairs={{0,1},{1,0},{2,3},{3,2},{4,5},{5,4},{6,7},{7,6},{8,9},{9,8},{10,11... | collective-permute-start | bytes 49160 | tf_op jit(solution)/shard_map/ppermute | solution.py:412
  39.7 3.8 %collective-permute-start.18 = (bf16[8,1024]{1,0:T(8,128)(2,1)S(1)}, bf16[8,1024]{1,0:T(8,128)(2,1)S(1)}, u32[]{:S(2)}, u32[]{:S(2)}) collective-permute-start(bf16[8,1024]{1,0:T(8,128)(2,1)S(1)} %get-tuple-element.30), channel_id=1, source_target_pairs={{0,2},{1,3},{2,0},{3,1},{4,6},{5,7},{6,4},{7,5},{8,10},{9,11},{10,... | collective-permute-start | bytes 49160 | tf_op jit(solution)/shard_map/ppermute | solution.py:412
  40.8 3.2 %collective-permute-start.19 = (bf16[8,1024]{1,0:T(8,128)(2,1)S(1)}, bf16[8,1024]{1,0:T(8,128)(2,1)S(1)}, u32[]{:S(2)}, u32[]{:S(2)}) collective-permute-start(bf16[8,1024]{1,0:T(8,128)(2,1)S(1)} %get-tuple-element.31), channel_id=1, source_target_pairs={{0,3},{1,2},{2,1},{3,0},{4,7},{5,6},{6,5},{7,4},{8,11},{9,10},{10,... | collective-permute-start | bytes 49160 | tf_op jit(solution)/shard_map/ppermute | solution.py:412

commit v9 on v8

--- a/solution.py
+++ b/solution.py
@@ -434,7 +434,9 @@
     along_x = [swap(block, "dp", 2) for block in along_z]
     mine_z, mine_x = jnp.stack(along_z), jnp.stack(along_x)
     other_z = swap(mine_z, "dp", 1)
-    other_x = swap(mine_x, "dp", 1)
+    early = swap(jnp.stack([along_x[0], along_x[2], along_x[3]]), "dp", 1)
+    late = swap(along_x[1], "dp", 1)
+    other_x = jnp.stack([early[0], late, early[1], early[2]])
 
     pieces = [block.reshape(4 * rows_dev, -1) for block in (mine_z, other_z, mine_x, other_x)]
     half = local_experts // 2

time: 44.8 us -> 44.4 us (level)
  waiting for transfers between devices: 14.3 us -> 13.8 us
    ppermute x20 -> x21, waiting for transfers between devices: 14.3 us -> 13.8 us  [swap(): return lax.ppermute(value, axis, [(i, i ^ bit) for i in range(size)])]
    ppermute x20 -> x21, starting transfers between devices: 20.2 us -> 20.2 us  [swap(): return lax.ppermute(value, axis, [(i, i ^ bit) for i in range(size)])]
  transfers between devices with their start and end apart: 20 -> 21, of which waited for: 13 -> 14; matrix products, arithmetic and copies ran while one was open for 0% -> 0% of each run, Pallas kernels for 12% -> 12%
where the time goes in v9:
time: 44.4 us; the launch traced here: 44.2 us
  starting transfers between devices  20.2 us (45%)
  waiting for transfers between devices  13.8 us (31%)
  Pallas kernels  9.13 us (21%)
  between operations  0.85 us (2%)
    ppermute x21, starting transfers between devices, swap(): return lax.ppermute(value, axis, [(i, i ^ bit) for i in range(size)])  20.2 us
    ppermute x21, waiting for transfers between devices, swap(): return lax.ppermute(value, axis, [(i, i ^ bit) for i in range(size)])  13.8 us
    pallas_call x1, Pallas kernels, attend_after(): pl.pallas_call(attend_after_kernel, in_specs=[whole(pltpu.SMEM), whole(),...  2.45 us
    pallas_call x1, Pallas kernels, gate_up_first(): pl.pallas_call(lambda *refs: gate_up_first_kernel(experts_all, *refs), in...  1.62 us
    pallas_call x1, Pallas kernels, gate_up_next(): pl.pallas_call(gate_up_next_kernel, in_specs=[whole()] * 10, out_specs=[w...  1.43 us
    pallas_call x2, Pallas kernels, down_part(): pl.pallas_call(lambda *refs: down_part_kernel(start, *refs), in_specs=[wh...  1.27 us
    pallas_call x1, Pallas kernels, pack(): pl.pallas_call(lambda *refs: pack_kernel(experts_all, *refs), in_specs=[w...  0.9 us
  transfers between devices with their start and end apart: 21, of which 14 were waited for; matrix products, arithmetic and copies ran while one was open for 0% of the time, Pallas kernels for 12%

profile of v9, /device:TPU:0, one launch (start us, length us, event | category | flops | bytes accessed | tf_op | source)
XLA Modules:
  0.0 44.2 jit_solution(5327856424495538599)
XLA Ops:
  0.6 0.9 %shard_map.104.refs_1_ = bf16[8,4224]{1,0:T(8,128)(2,1)S(1)} custom-call(bf16[8,4096]{1,0:T(8,128)(2,1)} %refs_0_.1, s32[8,8]{1,0:T(8,128)} %refs_1_.1, f32[8,8]{1,0:T(8,128)} %refs_2_.1), custom_call_target="tpu_custom_call" | custom-call | bytes 131072 | tf_op jit(solution)/shard_map/pallas_call | solution.py:141
  1.5 5.1 %collective-permute-start.2 = (bf16[8,4224]{1,0:T(8,128)(2,1)S(1)}, bf16[8,4224]{1,0:T(8,128)(2,1)S(1)}, u32[]{:S(2)}, u32[]{:S(2)}) collective-permute-start(bf16[8,4224]{1,0:T(8,128)(2,1)S(1)} %shard_map.104.refs_1_), channel_id=1, source_target_pairs={{0,12},{4,8},{8,4},{12,0},{1,13},{5,9},{9,5},{13,1},{2,14},{6,10},... | collective-permute-start | bytes 202760 | tf_op jit(solution)/shard_map/ppermute | solution.py:412
  6.7 0.0 collective-permute-start.1
  6.7 0.6 %collective-permute-start = (bf16[8,4224]{1,0:T(8,128)(2,1)S(1)}, bf16[8,4224]{1,0:T(8,128)(2,1)S(1)}, u32[]{:S(2)}, u32[]{:S(2)}) collective-permute-start(bf16[8,4224]{1,0:T(8,128)(2,1)S(1)} %shard_map.104.refs_1_), channel_id=1, source_target_pairs={{0,8},{4,12},{8,0},{12,4},{1,9},{5,13},{9,1},{13,5},{2,10},{6,14},... | collective-permute-start | bytes 202760 | tf_op jit(solution)/shard_map/ppermute | solution.py:412
  7.3 1.6 %collective-permute-start.4 = (bf16[8,4224]{1,0:T(8,128)(2,1)S(1)}, bf16[8,4224]{1,0:T(8,128)(2,1)S(1)}, u32[]{:S(2)}, u32[]{:S(2)}) collective-permute-start(bf16[8,4224]{1,0:T(8,128)(2,1)S(1)} %shard_map.104.refs_1_), channel_id=1, source_target_pairs={{0,2},{1,3},{2,0},{3,1},{4,6},{5,7},{6,4},{7,5},{8,10},{9,11},{10,... | collective-permute-start | bytes 202760 | tf_op jit(solution)/shard_map/ppermute | solution.py:412
  8.9 0.7 %collective-permute-done.2.refs_0_ = bf16[8,4224]{1,0:T(8,128)(2,1)S(1)} collective-permute-done((bf16[8,4224]{1,0:T(8,128)(2,1)S(1)}, bf16[8,4224]{1,0:T(8,128)(2,1)S(1)}, u32[]{:S(2)}, u32[]{:S(2)}) %collective-permute-start.2) | collective-permute-done | bytes 67616 | tf_op jit(solution)/shard_map/ppermute | solution.py:412
  9.6 1.5 %collective-permute-start.7 = (bf16[8,4224]{1,0:T(8,128)(2,1)S(1)}, bf16[8,4224]{1,0:T(8,128)(2,1)S(1)}, u32[]{:S(2)}, u32[]{:S(2)}) collective-permute-start(bf16[8,4224]{1,0:T(8,128)(2,1)S(1)} %shard_map.107), channel_id=1, source_target_pairs={{0,2},{1,3},{2,0},{3,1},{4,6},{5,7},{6,4},{7,5},{8,10},{9,11},{10,... | collective-permute-start | bytes 202760 | tf_op jit(solution)/shard_map/ppermute | solution.py:412
  11.1 0.3 collective-permute-done.1.refs_0_
  11.4 0.0 slice-start.2
  11.4 0.0 slice-start.4
  11.4 0.0 slice-start.3
  11.4 1.7 %collective-permute-start.6 = (bf16[8,4224]{1,0:T(8,128)(2,1)S(1)}, bf16[8,4224]{1,0:T(8,128)(2,1)S(1)}, u32[]{:S(2)}, u32[]{:S(2)}) collective-permute-start(bf16[8,4224]{1,0:T(8,128)(2,1)S(1)} %shard_map.106), channel_id=1, source_target_pairs={{0,2},{1,3},{2,0},{3,1},{4,6},{5,7},{6,4},{7,5},{8,10},{9,11},{10,... | collective-permute-start | bytes 202760 | tf_op jit(solution)/shard_map/ppermute | solution.py:412
  13.1 0.0 collective-permute-done.refs_0_
  13.1 0.7 %collective-permute-start.5 = (bf16[8,4224]{1,0:T(8,128)(2,1)S(1)}, bf16[8,4224]{1,0:T(8,128)(2,1)S(1)}, u32[]{:S(2)}, u32[]{:S(2)}) collective-permute-start(bf16[8,4224]{1,0:T(8,128)(2,1)S(1)} %shard_map.105), channel_id=1, source_target_pairs={{0,2},{1,3},{2,0},{3,1},{4,6},{5,7},{6,4},{7,5},{8,10},{9,11},{10,... | collective-permute-start | bytes 202760 | tf_op jit(solution)/shard_map/ppermute | solution.py:412
  13.8 0.1 pad_maximum_fusion
  13.9 0.1 collective-permute-start.3
  14.0 0.0 collective-permute-done.4
  14.0 0.4 collective-permute-done.7
  14.3 2.2 %collective-permute-done.6 = bf16[8,4224]{1,0:T(8,128)(2,1)S(1)} collective-permute-done((bf16[8,4224]{1,0:T(8,128)(2,1)S(1)}, bf16[8,4224]{1,0:T(8,128)(2,1)S(1)}, u32[]{:S(2)}, u32[]{:S(2)}) %collective-permute-start.6) | collective-permute-done | bytes 67616 | tf_op jit(solution)/shard_map/ppermute | solution.py:412
  16.5 0.1 collective-permute-start.8
  16.6 0.8 %collective-permute-done.5 = bf16[8,4224]{1,0:T(8,128)(2,1)S(1)} collective-permute-done((bf16[8,4224]{1,0:T(8,128)(2,1)S(1)}, bf16[8,4224]{1,0:T(8,128)(2,1)S(1)}, u32[]{:S(2)}, u32[]{:S(2)}) %collective-permute-start.5) | collective-permute-done | bytes 67616 | tf_op jit(solution)/shard_map/ppermute | solution.py:412
  17.4 0.0 collective-permute-start.9
  17.5 0.6 %collective-permute-done.8 = bf16[3,8,4224]{2,1,0:T(8,128)(2,1)S(1)} collective-permute-done((bf16[3,8,4224]{2,1,0:T(8,128)(2,1)S(1)}, bf16[3,8,4224]{2,1,0:T(8,128)(2,1)S(1)}, u32[]{:S(2)}, u32[]{:S(2)}) %collective-permute-start.8) | collective-permute-done | bytes 202784 | tf_op jit(solution)/shard_map/ppermute | solution.py:412
  18.1 0.6 %collective-permute-done.9 = bf16[8,4224]{1,0:T(8,128)(2,1)S(1)} collective-permute-done((bf16[8,4224]{1,0:T(8,128)(2,1)S(1)}, bf16[8,4224]{1,0:T(8,128)(2,1)S(1)}, u32[]{:S(2)}, u32[]{:S(2)}) %collective-permute-start.9) | collective-permute-done | bytes 67616 | tf_op jit(solution)/shard_map/ppermute | solution.py:412
  18.7 0.0 collective-permute-done.3
  18.7 0.0 slice-done.2
  18.7 0.0 slice-done.4
  18.7 0.0 slice-done.3
  18.7 0.0 slice-done.5
  18.8 1.6 %shard_map.108 = (bf16[2,96,256]{2,1,0:T(8,128)(2,1)S(1)}, f32[128,128]{1,0:T(8,128)S(1)}, f32[128,128]{1,0:T(8,128)S(1)}, f32[128,128]{1,0:T(8,128)S(1)}) custom-call(bf16[32,4224]{1,0:T(8,128)(2,1)S(1)} %get-tuple-element.33.refs_0_, bf16[32,4224]{1,0:T(8,128)(2,1)S(1)} %bitcast.24, bf16[32,4224]{1,0:T(8,128)(2,1)S(1)} %maximum_bitcast_fusion.refs_2_, ...), custom_call_target="tpu_custom_call" | custom-call | flops 1073741824 | bytes 8388608 | tf_op jit(solution)/shard_map/pallas_call | solution.py:241
  20.4 0.9 %collective-permute-start.11 = (bf16[2,96,256]{2,1,0:T(8,128)(2,1)S(1)}, bf16[2,96,256]{2,1,0:T(8,128)(2,1)S(1)}, u32[]{:S(2)}, u32[]{:S(2)}) collective-permute-start(bf16[2,96,256]{2,1,0:T(8,128)(2,1)S(1)} %get-tuple-element.17.refs_6_), channel_id=1, source_target_pairs={{0,2},{1,3},{2,0},{3,1},{4,6},{5,7},{6,4},{7,5},{8,10},{9,11},{10,... | collective-permute-start | bytes 294920 | tf_op jit(solution)/shard_map/ppermute | solution.py:412
  21.4 1.4 %shard_map.109 = (bf16[2,96,256]{2,1,0:T(8,128)(2,1)S(1)}, bf16[4,96,256]{2,1,0:T(8,128)(2,1)S(1)}, bf16[256,512]{1,0:T(8,128)(2,1)S(1)}) custom-call(bf16[32,4224]{1,0:T(8,128)(2,1)S(1)} %get-tuple-element.33.refs_0_, bf16[32,4224]{1,0:T(8,128)(2,1)S(1)} %bitcast.25, bf16[32,4224]{1,0:T(8,128)(2,1)S(1)} %maximum_bitcast_fusion.refs_2_, ...), custom_call_target="tpu_custom_call" | custom-call | flops 1073741824 | bytes 8388608 | tf_op jit(solution)/shard_map/pallas_call | solution.py:260
  22.8 0.0 slice-start
  22.8 0.1 collective-permute-start.10
  22.9 1.2 %collective-permute-start.12 = (bf16[2,96,256]{2,1,0:T(8,128)(2,1)S(1)}, bf16[2,96,256]{2,1,0:T(8,128)(2,1)S(1)}, u32[]{:S(2)}, u32[]{:S(2)}) collective-permute-start(bf16[2,96,256]{2,1,0:T(8,128)(2,1)S(1)} %get-tuple-element.23.after_ref), channel_id=1, source_target_pairs={{0,2},{1,3},{2,0},{3,1},{4,6},{5,7},{6,4},{7,5},{8,10},{9,11},{10,... | collective-permute-start | bytes 294920 | tf_op jit(solution)/shard_map/ppermute | solution.py:412
  24.1 0.0 copy-done
  24.1 0.0 copy-done.1
  24.1 0.0 copy-done.2
  24.1 2.5 %shard_map.110.refs_1_ = bf16[2,128,512]{2,1,0:T(8,128)(2,1)} custom-call(s32[2]{0:T(128)S(1)} %copy-done.2, bf16[2,576,128]{2,1,0:T(8,128)(2,1)S(1)} %bitcast.31, bf16[2,576,512]{2,1,0:T(8,128)(2,1)S(1)} %bitcast.30, bf16[2,96,256]{2,1,0:T(8,128)(2,1)S(1)} %get-tuple-element.23.after_ref), custom_call_target="tpu_custom_call" | custom-call | flops 4000000000 | tf_op jit(solution)/shard_map/pallas_call | solution.py:75
  26.6 0.0 collective-permute-done.11.refs_0_
  26.6 0.2 collective-permute-start.13
  26.7 0.0 collective-permute-done.10.refs_1_
  26.7 0.0 slice-done
  26.8 0.0 slice-done.1
  26.8 0.6 %shard_map.112.refs_1_.begun_first_ref = f32[2,96,1024]{2,1,0:T(8,128)S(1)} custom-call(bf16[4,96,256]{2,1,0:T(8,128)(2,1)S(1)} %get-tuple-element.22.refs_0_, bf16[4,96,256]{2,1,0:T(8,128)(2,1)S(1)} %collective-permute-done.10.refs_1_, bf16[2,96,256]{2,1,0:T(8,128)(2,1)S(1)} %shard_map.111.refs_2_, bf16[4,1024,1024]{2,1,0:T(8,128)(2,1)S(1)} %bitcast.19), custom_call_target="tpu_custom_call" | custom-call | flops 301989888 | bytes 786432 | tf_op jit(solution)/shard_map/pallas_call | solution.py:289
  27.4 0.7 %collective-permute-done.12.refs_0_ = bf16[2,96,256]{2,1,0:T(8,128)(2,1)S(1)} collective-permute-done((bf16[2,96,256]{2,1,0:T(8,128)(2,1)S(1)}, bf16[2,96,256]{2,1,0:T(8,128)(2,1)S(1)}, u32[]{:S(2)}, u32[]{:S(2)}) %collective-permute-start.12) | collective-permute-done | bytes 98336 | tf_op jit(solution)/shard_map/ppermute | solution.py:412
  28.1 0.0 collective-permute-start.14
  28.1 0.6 %shard_map.114.begun_next_ref = f32[2,96,1024]{2,1,0:T(8,128)S(1)} custom-call(bf16[4,96,256]{2,1,0:T(8,128)(2,1)S(1)} %get-tuple-element.22.refs_0_, bf16[4,96,256]{2,1,0:T(8,128)(2,1)S(1)} %collective-permute-done.10.refs_1_, bf16[2,96,256]{2,1,0:T(8,128)(2,1)S(1)} %shard_map.113.refs_2_, bf16[4,1024,1024]{2,1,0:T(8,128)(2,1)S(1)} %bitcast.19), custom_call_target="tpu_custom_call" | custom-call | flops 301989888 | bytes 786432 | tf_op jit(solution)/shard_map/pallas_call | solution.py:289
  28.7 0.0 collective-permute-done.13.h3_first_ref
  28.7 0.7 %collective-permute-done.14.h3_next_ref = bf16[2,96,256]{2,1,0:T(8,128)(2,1)S(1)} collective-permute-done((bf16[2,96,256]{2,1,0:T(8,128)(2,1)S(1)}, bf16[2,96,256]{2,1,0:T(8,128)(2,1)S(1)}, u32[]{:S(2)}, u32[]{:S(2)}) %collective-permute-start.14) | collective-permute-done | bytes 98336 | tf_op jit(solution)/shard_map/ppermute | solution.py:412
  29.4 0.8 %shard_map.115 = (bf16[32,1024]{1,0:T(8,128)(2,1)S(1)}, bf16[32,1024]{1,0:T(8,128)(2,1)S(1)}, bf16[32,1024]{1,0:T(8,128)(2,1)S(1)}, bf16[32,1024]{1,0:T(8,128)(2,1)S(1)}) custom-call(bf16[256,512]{1,0:T(8,128)(2,1)S(1)} %get-tuple-element.21.spread_ref, f32[2,96,1024]{2,1,0:T(8,128)S(1)} %shard_map.112.refs_1_.begun_first_ref, ...), custom_call_target="tpu_custom_call" | custom-call | flops 268435456 | bytes 3145728 | tf_op jit(solution)/shard_map/pallas_call | solution.py:350
  30.2 3.2 %collective-permute-start.15 = (bf16[32,1024]{1,0:T(8,128)(2,1)S(1)}, bf16[32,1024]{1,0:T(8,128)(2,1)S(1)}, u32[]{:S(2)}, u32[]{:S(2)}) collective-permute-start(bf16[32,1024]{1,0:T(8,128)(2,1)S(1)} %get-tuple-element.25), channel_id=1, source_target_pairs={{0,12},{4,8},{8,4},{12,0},{1,13},{5,9},{9,5},{13,1},{2,14},{6,10},... | collective-permute-start | bytes 196616 | tf_op jit(solution)/shard_map/ppermute | solution.py:412
  33.3 0.0 collective-permute-start.16
  33.3 1.3 %collective-permute-start.17 = (bf16[32,1024]{1,0:T(8,128)(2,1)S(1)}, bf16[32,1024]{1,0:T(8,128)(2,1)S(1)}, u32[]{:S(2)}, u32[]{:S(2)}) collective-permute-start(bf16[32,1024]{1,0:T(8,128)(2,1)S(1)} %get-tuple-element.27), channel_id=1, source_target_pairs={{0,8},{4,12},{8,0},{12,4},{1,9},{5,13},{9,1},{13,5},{2,10},{6,14},... | collective-permute-start | bytes 196616 | tf_op jit(solution)/shard_map/ppermute | solution.py:412
  34.6 2.4 %collective-permute-done.15.p1_ref = bf16[32,1024]{1,0:T(8,128)(2,1)S(1)} collective-permute-done((bf16[32,1024]{1,0:T(8,128)(2,1)S(1)}, bf16[32,1024]{1,0:T(8,128)(2,1)S(1)}, u32[]{:S(2)}, u32[]{:S(2)}) %collective-permute-start.15) | collective-permute-done | bytes 65568 | tf_op jit(solution)/shard_map/ppermute | solution.py:412
  37.0 1.7 %collective-permute-done.16.p2_ref = bf16[32,1024]{1,0:T(8,128)(2,1)S(1)} collective-permute-done((bf16[32,1024]{1,0:T(8,128)(2,1)S(1)}, bf16[32,1024]{1,0:T(8,128)(2,1)S(1)}, u32[]{:S(2)}, u32[]{:S(2)}) %collective-permute-start.16) | collective-permute-done | bytes 65568 | tf_op jit(solution)/shard_map/ppermute | solution.py:412
  38.7 0.5 %collective-permute-done.17.p3_ref = bf16[32,1024]{1,0:T(8,128)(2,1)S(1)} collective-permute-done((bf16[32,1024]{1,0:T(8,128)(2,1)S(1)}, bf16[32,1024]{1,0:T(8,128)(2,1)S(1)}, u32[]{:S(2)}, u32[]{:S(2)}) %collective-permute-start.17) | collective-permute-done | bytes 65568 | tf_op jit(solution)/shard_map/ppermute | solution.py:412
  39.3 0.1 collective-permute-start.18
  39.3 1.1 %collective-permute-start.19 = (bf16[8,1024]{1,0:T(8,128)(2,1)S(1)}, bf16[8,1024]{1,0:T(8,128)(2,1)S(1)}, u32[]{:S(2)}, u32[]{:S(2)}) collective-permute-start(bf16[8,1024]{1,0:T(8,128)(2,1)S(1)} %get-tuple-element.30), channel_id=1, source_target_pairs={{0,2},{1,3},{2,0},{3,1},{4,6},{5,7},{6,4},{7,5},{8,10},{9,11},{10,... | collective-permute-start | bytes 49160 | tf_op jit(solution)/shard_map/ppermute | solution.py:412
  40.4 0.7 %collective-permute-start.20 = (bf16[8,1024]{1,0:T(8,128)(2,1)S(1)}, bf16[8,1024]{1,0:T(8,128)(2,1)S(1)}, u32[]{:S(2)}, u32[]{:S(2)}) collective-permute-start(bf16[8,1024]{1,0:T(8,128)(2,1)S(1)} %get-tuple-element.31), channel_id=1, source_target_pairs={{0,3},{1,2},{2,1},{3,0},{4,7},{5,6},{6,5},{7,4},{8,11},{9,10},{10,... | collective-permute-start | bytes 49160 | tf_op jit(solution)/shard_map/ppermute | solution.py:412
  41.2 0.0 collective-permute-done.18.p1_ref
  41.2 1.9 %collective-permute-done.19.p2_ref = bf16[8,1024]{1,0:T(8,128)(2,1)S(1)} collective-permute-done((bf16[8,1024]{1,0:T(8,128)(2,1)S(1)}, bf16[8,1024]{1,0:T(8,128)(2,1)S(1)}, u32[]{:S(2)}, u32[]{:S(2)}) %collective-permute-start.19) | collective-permute-done | bytes 16416 | tf_op jit(solution)/shard_map/ppermute | solution.py:412
  43.1 0.5 %collective-permute-done.20.p3_ref = bf16[8,1024]{1,0:T(8,128)(2,1)S(1)} collective-permute-done((bf16[8,1024]{1,0:T(8,128)(2,1)S(1)}, bf16[8,1024]{1,0:T(8,128)(2,1)S(1)}, u32[]{:S(2)}, u32[]{:S(2)}) %collective-permute-start.20) | collective-permute-done | bytes 16416 | tf_op jit(solution)/shard_map/ppermute | solution.py:412
  43.6 0.6 %shard_map.117 = bf16[8,4096]{1,0:T(8,128)(2,1)} custom-call(bf16[8,1024]{1,0:T(8,128)(2,1)S(1)} %get-tuple-element.28.p0_ref, bf16[8,1024]{1,0:T(8,128)(2,1)S(1)} %collective-permute-done.18.p1_ref, bf16[8,1024]{1,0:T(8,128)(2,1)S(1)} %collective-permute-done.19.p2_ref, bf16[8,1024]{1,0:T(8,128)(2,1)S(1)} %collective-permute-done.20.p3_ref), custom_call_target="tpu_custom_call" | custom-call | bytes 131072 | tf_op jit(solution)/shard_map/pallas_call | solution.py:398
  (19 shorter events, 0.2 us)
Async XLA Ops:
  1.5 8.1 %collective-permute-start.2 = (bf16[8,4224]{1,0:T(8,128)(2,1)S(1)}, bf16[8,4224]{1,0:T(8,128)(2,1)S(1)}, u32[]{:S(2)}, u32[]{:S(2)}) collective-permute-start(bf16[8,4224]{1,0:T(8,128)(2,1)S(1)} %shard_map.104.refs_1_), channel_id=1, source_target_pairs={{0,12},{4,8},{8,4},{12,0},{1,13},{5,9},{9,5},{13,1},{2,14},{6,10},... | collective-permute-start | bytes 202760 | tf_op jit(solution)/shard_map/ppermute | solution.py:412
  6.7 4.8 %collective-permute-start.1 = (bf16[8,4224]{1,0:T(8,128)(2,1)S(1)}, bf16[8,4224]{1,0:T(8,128)(2,1)S(1)}, u32[]{:S(2)}, u32[]{:S(2)}) collective-permute-start(bf16[8,4224]{1,0:T(8,128)(2,1)S(1)} %shard_map.104.refs_1_), channel_id=1, source_target_pairs={{0,4},{4,0},{8,12},{12,8},{1,5},{5,1},{9,13},{13,9},{2,6},{6,2},{1... | collective-permute-start | bytes 202760 | tf_op jit(solution)/shard_map/ppermute | solution.py:412
  6.7 6.5 %collective-permute-start = (bf16[8,4224]{1,0:T(8,128)(2,1)S(1)}, bf16[8,4224]{1,0:T(8,128)(2,1)S(1)}, u32[]{:S(2)}, u32[]{:S(2)}) collective-permute-start(bf16[8,4224]{1,0:T(8,128)(2,1)S(1)} %shard_map.104.refs_1_), channel_id=1, source_target_pairs={{0,8},{4,12},{8,0},{12,4},{1,9},{5,13},{9,1},{13,5},{2,10},{6,14},... | collective-permute-start | bytes 202760 | tf_op jit(solution)/shard_map/ppermute | solution.py:412
  7.3 6.7 %collective-permute-start.4 = (bf16[8,4224]{1,0:T(8,128)(2,1)S(1)}, bf16[8,4224]{1,0:T(8,128)(2,1)S(1)}, u32[]{:S(2)}, u32[]{:S(2)}) collective-permute-start(bf16[8,4224]{1,0:T(8,128)(2,1)S(1)} %shard_map.104.refs_1_), channel_id=1, source_target_pairs={{0,2},{1,3},{2,0},{3,1},{4,6},{5,7},{6,4},{7,5},{8,10},{9,11},{10,... | collective-permute-start | bytes 202760 | tf_op jit(solution)/shard_map/ppermute | solution.py:412
  9.6 4.7 %collective-permute-start.7 = (bf16[8,4224]{1,0:T(8,128)(2,1)S(1)}, bf16[8,4224]{1,0:T(8,128)(2,1)S(1)}, u32[]{:S(2)}, u32[]{:S(2)}) collective-permute-start(bf16[8,4224]{1,0:T(8,128)(2,1)S(1)} %shard_map.107), channel_id=1, source_target_pairs={{0,2},{1,3},{2,0},{3,1},{4,6},{5,7},{6,4},{7,5},{8,10},{9,11},{10,... | collective-permute-start | bytes 202760 | tf_op jit(solution)/shard_map/ppermute | solution.py:412
  11.4 7.3 %slice-start.2 = ((s8[8388608]{0:T(1024)(128)(4,1)}), s8[4194304]{0:T(1024)(128)(4,1)S(1)}, s32[]{:S(2)}) async-start(s8[8388608]{0:T(1024)(128)(4,1)} %bitcast.20), calls=%async_computation.2 | async-start | bytes 8388608
  11.4 7.3 %slice-start.4 = ((s8[8388608]{0:T(1024)(128)(4,1)}), s8[4194304]{0:T(1024)(128)(4,1)S(1)}, s32[]{:S(2)}) async-start(s8[8388608]{0:T(1024)(128)(4,1)} %bitcast.22), calls=%async_computation.4 | async-start | bytes 8388608
  11.4 7.3 %slice-start.3 = ((s8[8388608]{0:T(1024)(128)(4,1)}), s8[4194304]{0:T(1024)(128)(4,1)S(1)}, s32[]{:S(2)}) async-start(s8[8388608]{0:T(1024)(128)(4,1)} %bitcast.20), calls=%async_computation.3 | async-start | bytes 8388608
  11.4 7.3 %slice-start.5 = ((s8[8388608]{0:T(1024)(128)(4,1)}), s8[4194304]{0:T(1024)(128)(4,1)S(1)}, s32[]{:S(2)}) async-start(s8[8388608]{0:T(1024)(128)(4,1)} %bitcast.22), calls=%async_computation.5 | async-start | bytes 8388608
  11.4 5.1 %collective-permute-start.6 = (bf16[8,4224]{1,0:T(8,128)(2,1)S(1)}, bf16[8,4224]{1,0:T(8,128)(2,1)S(1)}, u32[]{:S(2)}, u32[]{:S(2)}) collective-permute-start(bf16[8,4224]{1,0:T(8,128)(2,1)S(1)} %shard_map.106), channel_id=1, source_target_pairs={{0,2},{1,3},{2,0},{3,1},{4,6},{5,7},{6,4},{7,5},{8,10},{9,11},{10,... | collective-permute-start | bytes 202760 | tf_op jit(solution)/shard_map/ppermute | solution.py:412
  13.1 4.3 %collective-permute-start.5 = (bf16[8,4224]{1,0:T(8,128)(2,1)S(1)}, bf16[8,4224]{1,0:T(8,128)(2,1)S(1)}, u32[]{:S(2)}, u32[]{:S(2)}) collective-permute-start(bf16[8,4224]{1,0:T(8,128)(2,1)S(1)} %shard_map.105), channel_id=1, source_target_pairs={{0,2},{1,3},{2,0},{3,1},{4,6},{5,7},{6,4},{7,5},{8,10},{9,11},{10,... | collective-permute-start | bytes 202760 | tf_op jit(solution)/shard_map/ppermute | solution.py:412
  13.9 4.8 %collective-permute-start.3 = (bf16[4,8,4224]{2,1,0:T(8,128)(2,1)S(1)}, bf16[4,8,4224]{2,1,0:T(8,128)(2,1)S(1)}, u32[]{:S(2)}, u32[]{:S(2)}) collective-permute-start(bf16[4,8,4224]{2,1,0:T(8,128)(2,1)S(1)} %get-tuple-element.32), channel_id=1, source_target_pairs={{0,1},{1,0},{2,3},{3,2},{4,5},{5,4},{6,7},{7,6},{8,9},{9,8},{10,11... | collective-permute-start | bytes 811016 | tf_op jit(solution)/shard_map/ppermute | solution.py:412
  16.5 1.5 %collective-permute-start.8 = (bf16[3,8,4224]{2,1,0:T(8,128)(2,1)S(1)}, bf16[3,8,4224]{2,1,0:T(8,128)(2,1)S(1)}, u32[]{:S(2)}, u32[]{:S(2)}) collective-permute-start(bf16[3,8,4224]{2,1,0:T(8,128)(2,1)S(1)} %pad_maximum_fusion.1), channel_id=1, source_target_pairs={{0,1},{1,0},{2,3},{3,2},{4,5},{5,4},{6,7},{7,6},{8,9},{9,8},{10,11... | collective-permute-start | bytes 608264 | tf_op jit(solution)/shard_map/ppermute | solution.py:412
  17.4 1.3 %collective-permute-start.9 = (bf16[8,4224]{1,0:T(8,128)(2,1)S(1)}, bf16[8,4224]{1,0:T(8,128)(2,1)S(1)}, u32[]{:S(2)}, u32[]{:S(2)}) collective-permute-start(bf16[8,4224]{1,0:T(8,128)(2,1)S(1)} %collective-permute-done.5), channel_id=1, source_target_pairs={{0,1},{1,0},{2,3},{3,2},{4,5},{5,4},{6,7},{7,6},{8,9},{9,8},{10,11... | collective-permute-start | bytes 202760 | tf_op jit(solution)/shard_map/ppermute | solution.py:412
  20.4 6.2 %collective-permute-start.11 = (bf16[2,96,256]{2,1,0:T(8,128)(2,1)S(1)}, bf16[2,96,256]{2,1,0:T(8,128)(2,1)S(1)}, u32[]{:S(2)}, u32[]{:S(2)}) collective-permute-start(bf16[2,96,256]{2,1,0:T(8,128)(2,1)S(1)} %get-tuple-element.17.refs_6_), channel_id=1, source_target_pairs={{0,2},{1,3},{2,0},{3,1},{4,6},{5,7},{6,4},{7,5},{8,10},{9,11},{10,... | collective-permute-start | bytes 294920 | tf_op jit(solution)/shard_map/ppermute | solution.py:412
  21.3 2.8 %copy-start = (bf16[2,512,576]{1,2,0:T(8,128)(2,1)S(1)}, bf16[2,512,576]{1,2,0:T(8,128)(2,1)}, u32[]{:S(2)}) copy-start(bf16[2,512,576]{1,2,0:T(8,128)(2,1)} %param.16) | copy-start | bytes 3538948
  21.3 2.8 %copy-start.1 = (bf16[2,128,576]{1,2,0:T(8,128)(2,1)S(1)}, bf16[2,128,576]{1,2,0:T(8,128)(2,1)}, u32[]{:S(2)}) copy-start(bf16[2,128,576]{1,2,0:T(8,128)(2,1)} %param.15) | copy-start | bytes 884740
  21.3 2.8 %copy-start.2 = (s32[2]{0:T(128)S(1)}, s32[2]{0:T(128)}, u32[]{:S(2)}) copy-start(s32[2]{0:T(128)} %lengths_ref.1) | copy-start | bytes 28
  22.8 4.0 %slice-start = ((s8[8388608]{0:T(1024)(128)(4,1)}), s8[4194304]{0:T(1024)(128)(4,1)S(1)}, s32[]{:S(2)}) async-start(s8[8388608]{0:T(1024)(128)(4,1)} %bitcast.18), calls=%async_computation | async-start | bytes 8388608
  22.8 3.9 %collective-permute-start.10 = (bf16[4,96,256]{2,1,0:T(8,128)(2,1)S(1)}, bf16[4,96,256]{2,1,0:T(8,128)(2,1)S(1)}, u32[]{:S(2)}, u32[]{:S(2)}) collective-permute-start(bf16[4,96,256]{2,1,0:T(8,128)(2,1)S(1)} %get-tuple-element.22.refs_0_), channel_id=1, source_target_pairs={{0,1},{1,0},{2,3},{3,2},{4,5},{5,4},{6,7},{7,6},{8,9},{9,8},{10,11... | collective-permute-start | bytes 589832 | tf_op jit(solution)/shard_map/ppermute | solution.py:412
  22.9 5.2 %collective-permute-start.12 = (bf16[2,96,256]{2,1,0:T(8,128)(2,1)S(1)}, bf16[2,96,256]{2,1,0:T(8,128)(2,1)S(1)}, u32[]{:S(2)}, u32[]{:S(2)}) collective-permute-start(bf16[2,96,256]{2,1,0:T(8,128)(2,1)S(1)} %get-tuple-element.23.after_ref), channel_id=1, source_target_pairs={{0,2},{1,3},{2,0},{3,1},{4,6},{5,7},{6,4},{7,5},{8,10},{9,11},{10,... | collective-permute-start | bytes 294920 | tf_op jit(solution)/shard_map/ppermute | solution.py:412
  24.1 2.6 %slice-start.1 = ((s8[8388608]{0:T(1024)(128)(4,1)}), s8[4194304]{0:T(1024)(128)(4,1)S(1)}, s32[]{:S(2)}) async-start(s8[8388608]{0:T(1024)(128)(4,1)} %bitcast.18), calls=%async_computation.1 | async-start | bytes 8388608
  26.6 2.2 %collective-permute-start.13 = (bf16[2,96,256]{2,1,0:T(8,128)(2,1)S(1)}, bf16[2,96,256]{2,1,0:T(8,128)(2,1)S(1)}, u32[]{:S(2)}, u32[]{:S(2)}) collective-permute-start(bf16[2,96,256]{2,1,0:T(8,128)(2,1)S(1)} %shard_map.111.refs_2_), channel_id=1, source_target_pairs={{0,1},{1,0},{2,3},{3,2},{4,5},{5,4},{6,7},{7,6},{8,9},{9,8},{10,11... | collective-permute-start | bytes 294920 | tf_op jit(solution)/shard_map/ppermute | solution.py:412
  28.1 1.3 %collective-permute-start.14 = (bf16[2,96,256]{2,1,0:T(8,128)(2,1)S(1)}, bf16[2,96,256]{2,1,0:T(8,128)(2,1)S(1)}, u32[]{:S(2)}, u32[]{:S(2)}) collective-permute-start(bf16[2,96,256]{2,1,0:T(8,128)(2,1)S(1)} %shard_map.113.refs_2_), channel_id=1, source_target_pairs={{0,1},{1,0},{2,3},{3,2},{4,5},{5,4},{6,7},{7,6},{8,9},{9,8},{10,11... | collective-permute-start | bytes 294920 | tf_op jit(solution)/shard_map/ppermute | solution.py:412
  30.2 6.8 %collective-permute-start.15 = (bf16[32,1024]{1,0:T(8,128)(2,1)S(1)}, bf16[32,1024]{1,0:T(8,128)(2,1)S(1)}, u32[]{:S(2)}, u32[]{:S(2)}) collective-permute-start(bf16[32,1024]{1,0:T(8,128)(2,1)S(1)} %get-tuple-element.25), channel_id=1, source_target_pairs={{0,12},{4,8},{8,4},{12,0},{1,13},{5,9},{9,5},{13,1},{2,14},{6,10},... | collective-permute-start | bytes 196616 | tf_op jit(solution)/shard_map/ppermute | solution.py:412
  33.3 5.4 %collective-permute-start.16 = (bf16[32,1024]{1,0:T(8,128)(2,1)S(1)}, bf16[32,1024]{1,0:T(8,128)(2,1)S(1)}, u32[]{:S(2)}, u32[]{:S(2)}) collective-permute-start(bf16[32,1024]{1,0:T(8,128)(2,1)S(1)} %get-tuple-element.26), channel_id=1, source_target_pairs={{0,4},{4,0},{8,12},{12,8},{1,5},{5,1},{9,13},{13,9},{2,6},{6,2},{1... | collective-permute-start | bytes 196616 | tf_op jit(solution)/shard_map/ppermute | solution.py:412
  33.3 5.9 %collective-permute-start.17 = (bf16[32,1024]{1,0:T(8,128)(2,1)S(1)}, bf16[32,1024]{1,0:T(8,128)(2,1)S(1)}, u32[]{:S(2)}, u32[]{:S(2)}) collective-permute-start(bf16[32,1024]{1,0:T(8,128)(2,1)S(1)} %get-tuple-element.27), channel_id=1, source_target_pairs={{0,8},{4,12},{8,0},{12,4},{1,9},{5,13},{9,1},{13,5},{2,10},{6,14},... | collective-permute-start | bytes 196616 | tf_op jit(solution)/shard_map/ppermute | solution.py:412
  39.3 1.9 %collective-permute-start.18 = (bf16[8,1024]{1,0:T(8,128)(2,1)S(1)}, bf16[8,1024]{1,0:T(8,128)(2,1)S(1)}, u32[]{:S(2)}, u32[]{:S(2)}) collective-permute-start(bf16[8,1024]{1,0:T(8,128)(2,1)S(1)} %get-tuple-element.29), channel_id=1, source_target_pairs={{0,1},{1,0},{2,3},{3,2},{4,5},{5,4},{6,7},{7,6},{8,9},{9,8},{10,11... | collective-permute-start | bytes 49160 | tf_op jit(solution)/shard_map/ppermute | solution.py:412
  39.3 3.8 %collective-permute-start.19 = (bf16[8,1024]{1,0:T(8,128)(2,1)S(1)}, bf16[8,1024]{1,0:T(8,128)(2,1)S(1)}, u32[]{:S(2)}, u32[]{:S(2)}) collective-permute-start(bf16[8,1024]{1,0:T(8,128)(2,1)S(1)} %get-tuple-element.30), channel_id=1, source_target_pairs={{0,2},{1,3},{2,0},{3,1},{4,6},{5,7},{6,4},{7,5},{8,10},{9,11},{10,... | collective-permute-start | bytes 49160 | tf_op jit(solution)/shard_map/ppermute | solution.py:412
  40.4 3.2 %collective-permute-start.20 = (bf16[8,1024]{1,0:T(8,128)(2,1)S(1)}, bf16[8,1024]{1,0:T(8,128)(2,1)S(1)}, u32[]{:S(2)}, u32[]{:S(2)}) collective-permute-start(bf16[8,1024]{1,0:T(8,128)(2,1)S(1)} %get-tuple-element.31), channel_id=1, source_target_pairs={{0,3},{1,2},{2,1},{3,0},{4,7},{5,6},{6,5},{7,4},{8,11},{9,10},{10,... | collective-permute-start | bytes 49160 | tf_op jit(solution)/shard_map/ppermute | solution.py:412

commit v10 on v9

--- a/solution.py
+++ b/solution.py
@@ -113,7 +113,7 @@
         pltpu.make_async_copy(gates_in, gates_ref, sems.at[1]),
         pltpu.make_async_copy(rows_in, out_ref.at[:, :feature_count], sems.at[2]),
     ]
-    for copy in copies:
+    for copy in (copies[2], copies[0], copies[1]):
         copy.start()
     copies[0].wait()
     copies[1].wait()
@@ -300,12 +300,64 @@
     )(*hidden, down_proj)
 
 
+def finish(e, begun, far, down_ref, made_ref, at, count):
+    owner = jnp.bitwise_xor(lax.axis_index("dp"), 3)
+    slots, share = far.shape
+    weights = down_ref[e, pl.ds(pl.multiple_of(owner * share, share), share)]
+    made = begun + jnp.dot(far, weights, preferred_element_type=F32)
+    made_ref[at : at + slots] = made.astype(BF16)
+    if slots < count:
+        made_ref[at + slots : at + count] = jnp.zeros((count - slots, made.shape[1]), BF16)
+
+
+def down_middle_kernel(
+    start,
+    h2_ref,
+    h0_ref,
+    h1_ref,
+    begun_first_ref,
+    h3_first_ref,
+    spread_ref,
+    down_ref,
+    begun_ref,
+    mixed_ref,
+    made_ref,
+):
+    count = mixed_ref.shape[0]
+    for e in range(start):
+        finish(e, begun_first_ref[e], h3_first_ref[e], down_ref, made_ref, e * count, count)
+    down_part_kernel(start, h0_ref, h1_ref, h2_ref, down_ref, begun_ref)
+    both = jnp.dot(
+        spread_ref[:, : start * count], made_ref[...], preferred_element_type=F32
+    )
+    mixed_ref[...] = both[:count] + both[count:]
+
+
+def down_middle(start, hidden, begun_first, far_first, spread, down_proj):
+    part, slots, share = hidden[0].shape
+    width = down_proj.shape[2]
+    count = spread.shape[0] // 2
+    return pl.pallas_call(
+        lambda *refs: down_middle_kernel(start, *refs),
+        in_specs=[whole()] * 7,
+        out_specs=[whole()] * 2,
+        out_shape=[VMEM((part, slots, width), F32), VMEM((count, width), F32)],
+        scratch_shapes=[VMEM((start * count, width), BF16)],
+        compiler_params=pltpu.CompilerParams(vmem_limit_bytes=20 * MIB),
+        cost_estimate=pl.CostEstimate(
+            flops=6 * part * slots * share * width,
+            bytes_accessed=4 * part * slots * width,
+            transcendentals=0,
+        ),
+    )(*hidden, begun_first, far_first, spread, down_proj)
+
+
 def down_last_kernel(
+    start,
     spread_ref,
-    begun_first_ref,
-    begun_next_ref,
-    h3_first_ref,
-    h3_next_ref,
+    mixed_ref,
+    begun_ref,
+    h3_ref,
     down_ref,
     o0_ref,
     o1_ref,
@@ -313,53 +365,39 @@
     o3_ref,
     made_ref,
 ):
-    owner = jnp.bitwise_xor(lax.axis_index("dp"), 3)
-    part, slots, share = h3_first_ref.shape
-    experts, _, width = down_ref.shape
-    count = spread_ref.shape[0] // 2
+    count, width = mixed_ref.shape
     rows_z = o0_ref.shape[0]
+    rows = rows_z // 4
     tile = 256
-    for e in range(experts):
-        if slots < count:
-            made_ref[e * count + slots : (e + 1) * count] = jnp.zeros(
-                (count - slots, width), BF16
-            )
-        weights = down_ref[e, pl.ds(pl.multiple_of(owner * share, share), share)]
-        if e < part:
-            begun, far = begun_first_ref[e], h3_first_ref[e]
-        else:
-            begun, far = begun_next_ref[e - part], h3_next_ref[e - part]
-        made = begun + jnp.dot(far, weights, preferred_element_type=F32)
-        made_ref[e * count : e * count + slots] = made.astype(BF16)
-    spread = spread_ref[...]
-    for start in range(0, width, tile):
-        both = jnp.dot(spread, made_ref[:, start : start + tile], preferred_element_type=F32)
-        done = both[:count] + both[count:]
-        rows = rows_z // 4
+    for e in range(begun_ref.shape[0]):
+        finish(start + e, begun_ref[e], h3_ref[e], down_ref, made_ref, e * count, count)
+    spread = spread_ref[:, start * count :]
+    for at in range(0, width, tile):
+        both = jnp.dot(spread, made_ref[:, at : at + tile], preferred_element_type=F32)
+        done = mixed_ref[:, at : at + tile] + both[:count] + both[count:]
         for k, ref in enumerate((o0_ref, o1_ref, o2_ref, o3_ref)):
             parts = [
                 done[g * rows_z + k * rows : g * rows_z + (k + 1) * rows] for g in range(4)
             ]
-            ref[:, start : start + tile] = jnp.concatenate(parts, axis=0).astype(BF16)
-
-
-def down_last(spread, begun, hidden, down_proj):
-    experts, _, width = down_proj.shape
-    slots = hidden[0].shape[1]
-    count = spread.shape[0] // 2
-    return pl.pallas_call(
-        down_last_kernel,
-        in_specs=[whole()] * 6,
+            ref[:, at : at + tile] = jnp.concatenate(parts, axis=0).astype(BF16)
+
+
+def down_last(start, spread, mixed, begun, far, down_proj):
+    part, slots, share = far.shape
+    count, width = mixed.shape
+    return pl.pallas_call(
+        lambda *refs: down_last_kernel(start, *refs),
+        in_specs=[whole()] * 5,
         out_specs=[whole()] * 4,
         out_shape=[VMEM((count // 4, width), BF16)] * 4,
-        scratch_shapes=[VMEM((experts * count, width), BF16)],
+        scratch_shapes=[VMEM((part * count, width), BF16)],
         compiler_params=pltpu.CompilerParams(vmem_limit_bytes=20 * MIB),
         cost_estimate=pl.CostEstimate(
-            flops=4 * experts * count * count * width,
-            bytes_accessed=8 * experts * slots * width,
+            flops=4 * part * count * count * width,
+            bytes_accessed=8 * part * slots * width,
             transcendentals=0,
         ),
-    )(spread, *begun, *hidden, down_proj)
+    )(spread, mixed, begun, far, down_proj)
 
 
 def collect_kernel(p0_ref, p1_ref, p2_ref, p3_ref, own_ref, core_ref, x_ref, far_ref):
@@ -455,9 +493,11 @@
     begun_first = down_part(0, (hidden, hidden_c, first_x), down_proj)
     next_x = once_done(next_x, begun_first)
     next_far = swap(next_x, "dp", 1)
-    begun_next = down_part(half, (hidden, hidden_c, next_x), down_proj)
-    partial = down_last(spread, (begun_first, begun_next), (first_far, next_far), down_proj)
-    arrived = [partial[0]] + [swap(partial[j], "expert", k) for j, k in ((3, 3), (2, 1), (1, 2))]
+    begun_next, mixed = down_middle(
+        half, (next_x, hidden, hidden_c), begun_first, first_far, spread, down_proj
+    )
+    partial = down_last(half, spread, mixed, begun_next, next_far, down_proj)
+    arrived = [partial[0]] + [swap(partial[j], "expert", k) for j, k in ((1, 2), (3, 3), (2, 1))]
     own, to_core, to_x, to_far = collect(arrived)
     far = swap(to_far, "dp", 3)
     blended = place_all((own, swap(to_core, "dp", 1), swap(to_x, "dp", 2), far))

time: 44.4 us -> 44.3 us (level)
    pallas_call x1 -> x2, Pallas kernels: 0.78 us -> 1.49 us  [the longest x1 0.95 us: down_middle(): pl.pallas_call(lambda *refs: down_middle_kernel(start, *refs), in_specs=[...]
    pallas_call x2 -> x1, Pallas kernels: 1.27 us -> 0.64 us  [down_part(): pl.pallas_call(lambda *refs: down_part_kernel(start, *refs), in_specs=[wh...]
where the time goes in v10:
time: 44.3 us; the launch traced here: 44.1 us
  starting transfers between devices  20.2 us (46%)
  waiting for transfers between devices  13.6 us (31%)
  Pallas kernels  9.2 us (21%)
  between operations  0.87 us (2%)
    ppermute x21, starting transfers between devices, swap(): return lax.ppermute(value, axis, [(i, i ^ bit) for i in range(size)])  20.2 us
    ppermute x21, waiting for transfers between devices, swap(): return lax.ppermute(value, axis, [(i, i ^ bit) for i in range(size)])  13.6 us
    pallas_call x1, Pallas kernels, attend_after(): pl.pallas_call(attend_after_kernel, in_specs=[whole(pltpu.SMEM), whole(),...  2.46 us
    pallas_call x1, Pallas kernels, gate_up_first(): pl.pallas_call(lambda *refs: gate_up_first_kernel(experts_all, *refs), in...  1.62 us
    pallas_call x1, Pallas kernels, gate_up_next(): pl.pallas_call(gate_up_next_kernel, in_specs=[whole()] * 10, out_specs=[w...  1.44 us
    pallas_call x1, Pallas kernels, down_middle(): pl.pallas_call(lambda *refs: down_middle_kernel(start, *refs), in_specs=[...  0.95 us
  transfers between devices with their start and end apart: 21, of which 14 were waited for; matrix products, arithmetic and copies ran while one was open for 0% of the time, Pallas kernels for 12%

profile of v10, /device:TPU:0, one launch (start us, length us, event | category | flops | bytes accessed | tf_op | source)
XLA Modules:
  0.0 44.1 jit_solution(1153683301709631341)
XLA Ops:
  0.6 0.9 %shard_map.104.refs_1_ = bf16[8,4224]{1,0:T(8,128)(2,1)S(1)} custom-call(bf16[8,4096]{1,0:T(8,128)(2,1)} %refs_0_.1, s32[8,8]{1,0:T(8,128)} %refs_1_.1, f32[8,8]{1,0:T(8,128)} %refs_2_.1), custom_call_target="tpu_custom_call" | custom-call | bytes 131072 | tf_op jit(solution)/shard_map/pallas_call | solution.py:141
  1.5 5.1 %collective-permute-start.2 = (bf16[8,4224]{1,0:T(8,128)(2,1)S(1)}, bf16[8,4224]{1,0:T(8,128)(2,1)S(1)}, u32[]{:S(2)}, u32[]{:S(2)}) collective-permute-start(bf16[8,4224]{1,0:T(8,128)(2,1)S(1)} %shard_map.104.refs_1_), channel_id=1, source_target_pairs={{0,12},{4,8},{8,4},{12,0},{1,13},{5,9},{9,5},{13,1},{2,14},{6,10},... | collective-permute-start | bytes 202760 | tf_op jit(solution)/shard_map/ppermute | solution.py:450
  6.6 1.5 %collective-permute-start.4 = (bf16[8,4224]{1,0:T(8,128)(2,1)S(1)}, bf16[8,4224]{1,0:T(8,128)(2,1)S(1)}, u32[]{:S(2)}, u32[]{:S(2)}) collective-permute-start(bf16[8,4224]{1,0:T(8,128)(2,1)S(1)} %shard_map.104.refs_1_), channel_id=1, source_target_pairs={{0,2},{1,3},{2,0},{3,1},{4,6},{5,7},{6,4},{7,5},{8,10},{9,11},{10,... | collective-permute-start | bytes 202760 | tf_op jit(solution)/shard_map/ppermute | solution.py:450
  8.1 0.0 collective-permute-start.1
  8.1 0.8 %collective-permute-start = (bf16[8,4224]{1,0:T(8,128)(2,1)S(1)}, bf16[8,4224]{1,0:T(8,128)(2,1)S(1)}, u32[]{:S(2)}, u32[]{:S(2)}) collective-permute-start(bf16[8,4224]{1,0:T(8,128)(2,1)S(1)} %shard_map.104.refs_1_), channel_id=1, source_target_pairs={{0,8},{4,12},{8,0},{12,4},{1,9},{5,13},{9,1},{13,5},{2,10},{6,14},... | collective-permute-start | bytes 202760 | tf_op jit(solution)/shard_map/ppermute | solution.py:450
  8.9 0.2 collective-permute-done.2.refs_0_
  9.1 2.0 %collective-permute-start.7 = (bf16[8,4224]{1,0:T(8,128)(2,1)S(1)}, bf16[8,4224]{1,0:T(8,128)(2,1)S(1)}, u32[]{:S(2)}, u32[]{:S(2)}) collective-permute-start(bf16[8,4224]{1,0:T(8,128)(2,1)S(1)} %shard_map.107), channel_id=1, source_target_pairs={{0,2},{1,3},{2,0},{3,1},{4,6},{5,7},{6,4},{7,5},{8,10},{9,11},{10,... | collective-permute-start | bytes 202760 | tf_op jit(solution)/shard_map/ppermute | solution.py:450
  11.1 1.3 %collective-permute-done.1.refs_0_ = bf16[8,4224]{1,0:T(8,128)(2,1)S(1)} collective-permute-done((bf16[8,4224]{1,0:T(8,128)(2,1)S(1)}, bf16[8,4224]{1,0:T(8,128)(2,1)S(1)}, u32[]{:S(2)}, u32[]{:S(2)}) %collective-permute-start.1) | collective-permute-done | bytes 67616 | tf_op jit(solution)/shard_map/ppermute | solution.py:450
  12.4 0.0 slice-start.2
  12.4 0.0 slice-start.4
  12.4 0.8 %collective-permute-start.6 = (bf16[8,4224]{1,0:T(8,128)(2,1)S(1)}, bf16[8,4224]{1,0:T(8,128)(2,1)S(1)}, u32[]{:S(2)}, u32[]{:S(2)}) collective-permute-start(bf16[8,4224]{1,0:T(8,128)(2,1)S(1)} %shard_map.106), channel_id=1, source_target_pairs={{0,2},{1,3},{2,0},{3,1},{4,6},{5,7},{6,4},{7,5},{8,10},{9,11},{10,... | collective-permute-start | bytes 202760 | tf_op jit(solution)/shard_map/ppermute | solution.py:450
  13.2 0.3 collective-permute-done.refs_0_
  13.5 1.0 %collective-permute-start.5 = (bf16[8,4224]{1,0:T(8,128)(2,1)S(1)}, bf16[8,4224]{1,0:T(8,128)(2,1)S(1)}, u32[]{:S(2)}, u32[]{:S(2)}) collective-permute-start(bf16[8,4224]{1,0:T(8,128)(2,1)S(1)} %shard_map.105), channel_id=1, source_target_pairs={{0,2},{1,3},{2,0},{3,1},{4,6},{5,7},{6,4},{7,5},{8,10},{9,11},{10,... | collective-permute-start | bytes 202760 | tf_op jit(solution)/shard_map/ppermute | solution.py:450
  14.5 0.1 pad_maximum_fusion
  14.6 0.1 collective-permute-start.3
  14.6 0.0 collective-permute-done.4
  14.7 0.0 collective-permute-done.7
  14.7 2.1 %collective-permute-done.6 = bf16[8,4224]{1,0:T(8,128)(2,1)S(1)} collective-permute-done((bf16[8,4224]{1,0:T(8,128)(2,1)S(1)}, bf16[8,4224]{1,0:T(8,128)(2,1)S(1)}, u32[]{:S(2)}, u32[]{:S(2)}) %collective-permute-start.6) | collective-permute-done | bytes 67616 | tf_op jit(solution)/shard_map/ppermute | solution.py:450
  16.8 0.1 collective-permute-start.8
  16.9 0.9 %collective-permute-done.5 = bf16[8,4224]{1,0:T(8,128)(2,1)S(1)} collective-permute-done((bf16[8,4224]{1,0:T(8,128)(2,1)S(1)}, bf16[8,4224]{1,0:T(8,128)(2,1)S(1)}, u32[]{:S(2)}, u32[]{:S(2)}) %collective-permute-start.5) | collective-permute-done | bytes 67616 | tf_op jit(solution)/shard_map/ppermute | solution.py:450
  17.8 0.0 collective-permute-start.9
  17.9 0.5 %collective-permute-done.8 = bf16[3,8,4224]{2,1,0:T(8,128)(2,1)S(1)} collective-permute-done((bf16[3,8,4224]{2,1,0:T(8,128)(2,1)S(1)}, bf16[3,8,4224]{2,1,0:T(8,128)(2,1)S(1)}, u32[]{:S(2)}, u32[]{:S(2)}) %collective-permute-start.8) | collective-permute-done | bytes 202784 | tf_op jit(solution)/shard_map/ppermute | solution.py:450
  18.3 0.7 %collective-permute-done.9 = bf16[8,4224]{1,0:T(8,128)(2,1)S(1)} collective-permute-done((bf16[8,4224]{1,0:T(8,128)(2,1)S(1)}, bf16[8,4224]{1,0:T(8,128)(2,1)S(1)}, u32[]{:S(2)}, u32[]{:S(2)}) %collective-permute-start.9) | collective-permute-done | bytes 67616 | tf_op jit(solution)/shard_map/ppermute | solution.py:450
  19.1 0.0 collective-permute-done.3
  19.1 0.0 slice-done.2
  19.1 0.0 slice-done.4
  19.1 0.0 slice-done.3
  19.1 0.0 slice-done.5
  19.2 1.6 %shard_map.108 = (bf16[2,96,256]{2,1,0:T(8,128)(2,1)S(1)}, f32[128,128]{1,0:T(8,128)S(1)}, f32[128,128]{1,0:T(8,128)S(1)}, f32[128,128]{1,0:T(8,128)S(1)}) custom-call(bf16[32,4224]{1,0:T(8,128)(2,1)S(1)} %get-tuple-element.37.refs_0_, bf16[32,4224]{1,0:T(8,128)(2,1)S(1)} %bitcast.24, bf16[32,4224]{1,0:T(8,128)(2,1)S(1)} %maximum_bitcast_fusion.refs_2_, ...), custom_call_target="tpu_custom_call" | custom-call | flops 1073741824 | bytes 8388608 | tf_op jit(solution)/shard_map/pallas_call | solution.py:241
  20.8 1.1 %collective-permute-start.12 = (bf16[2,96,256]{2,1,0:T(8,128)(2,1)S(1)}, bf16[2,96,256]{2,1,0:T(8,128)(2,1)S(1)}, u32[]{:S(2)}, u32[]{:S(2)}) collective-permute-start(bf16[2,96,256]{2,1,0:T(8,128)(2,1)S(1)} %get-tuple-element.19.refs_6_), channel_id=1, source_target_pairs={{0,2},{1,3},{2,0},{3,1},{4,6},{5,7},{6,4},{7,5},{8,10},{9,11},{10,... | collective-permute-start | bytes 294920 | tf_op jit(solution)/shard_map/ppermute | solution.py:450
  21.9 1.4 %shard_map.109 = (bf16[2,96,256]{2,1,0:T(8,128)(2,1)S(1)}, bf16[4,96,256]{2,1,0:T(8,128)(2,1)S(1)}, bf16[256,512]{1,0:T(8,128)(2,1)S(1)}) custom-call(bf16[32,4224]{1,0:T(8,128)(2,1)S(1)} %get-tuple-element.37.refs_0_, bf16[32,4224]{1,0:T(8,128)(2,1)S(1)} %bitcast.25, bf16[32,4224]{1,0:T(8,128)(2,1)S(1)} %maximum_bitcast_fusion.refs_2_, ...), custom_call_target="tpu_custom_call" | custom-call | flops 1073741824 | bytes 8388608 | tf_op jit(solution)/shard_map/pallas_call | solution.py:260
  23.3 0.0 slice-start
  23.3 1.1 %collective-permute-start.10 = (bf16[2,96,256]{2,1,0:T(8,128)(2,1)S(1)}, bf16[2,96,256]{2,1,0:T(8,128)(2,1)S(1)}, u32[]{:S(2)}, u32[]{:S(2)}) collective-permute-start(bf16[2,96,256]{2,1,0:T(8,128)(2,1)S(1)} %get-tuple-element.24.after_ref), channel_id=1, source_target_pairs={{0,2},{1,3},{2,0},{3,1},{4,6},{5,7},{6,4},{7,5},{8,10},{9,11},{10,... | collective-permute-start | bytes 294920 | tf_op jit(solution)/shard_map/ppermute | solution.py:450
  24.4 0.0 collective-permute-start.11
  24.4 0.0 copy-done
  24.4 0.0 copy-done.1
  24.4 0.0 copy-done.2
  24.4 0.0 slice-start.1
  24.4 2.5 %shard_map.110.refs_1_ = bf16[2,128,512]{2,1,0:T(8,128)(2,1)} custom-call(s32[2]{0:T(128)S(1)} %copy-done.2, bf16[2,576,128]{2,1,0:T(8,128)(2,1)S(1)} %bitcast.31, bf16[2,576,512]{2,1,0:T(8,128)(2,1)S(1)} %bitcast.30, bf16[2,96,256]{2,1,0:T(8,128)(2,1)S(1)} %get-tuple-element.24.after_ref), custom_call_target="tpu_custom_call" | custom-call | flops 4000000000 | tf_op jit(solution)/shard_map/pallas_call | solution.py:75
  26.9 0.0 collective-permute-done.12.refs_0_
  26.9 0.5 %collective-permute-start.13 = (bf16[2,96,256]{2,1,0:T(8,128)(2,1)S(1)}, bf16[2,96,256]{2,1,0:T(8,128)(2,1)S(1)}, u32[]{:S(2)}, u32[]{:S(2)}) collective-permute-start(bf16[2,96,256]{2,1,0:T(8,128)(2,1)S(1)} %shard_map.111.refs_2_), channel_id=1, source_target_pairs={{0,1},{1,0},{2,3},{3,2},{4,5},{5,4},{6,7},{7,6},{8,9},{9,8},{10,11... | collective-permute-start | bytes 294920 | tf_op jit(solution)/shard_map/ppermute | solution.py:450
  27.4 0.0 collective-permute-done.11.refs_1_.refs_2_
  27.4 0.0 slice-done
  27.4 0.0 slice-done.1
  27.4 0.6 %shard_map.112.refs_1_.refs_3_ = f32[2,96,1024]{2,1,0:T(8,128)S(1)} custom-call(bf16[4,96,256]{2,1,0:T(8,128)(2,1)S(1)} %get-tuple-element.25.refs_0_.refs_1_, bf16[4,96,256]{2,1,0:T(8,128)(2,1)S(1)} %collective-permute-done.11.refs_1_.refs_2_, bf16[2,96,256]{2,1,0:T(8,128)(2,1)S(1)} %shard_map.111.refs_2_, bf16[4,1024,1024]{2,1,0:T(8,128)(2,1)S(1)} %bitcast.19), custom_call_target="tpu_custom_call" | custom-call | flops 301989888 | bytes 786432 | tf_op jit(solution)/shard_map/pallas_call | solution.py:289
  28.1 0.0 collective-permute-done.10.refs_0_
  28.1 0.1 collective-permute-start.14
  28.2 0.2 collective-permute-done.13.refs_4_
  28.3 1.0 %shard_map.114 = (f32[2,96,1024]{2,1,0:T(8,128)S(1)}, f32[128,1024]{1,0:T(8,128)S(1)}) custom-call(bf16[2,96,256]{2,1,0:T(8,128)(2,1)S(1)} %shard_map.113.refs_0_, bf16[4,96,256]{2,1,0:T(8,128)(2,1)S(1)} %get-tuple-element.25.refs_0_.refs_1_, bf16[4,96,256]{2,1,0:T(8,128)(2,1)S(1)} %collective-permute-done.11.refs_1_.refs_2_, ...), custom_call_target="tpu_custom_call" | custom-call | flops 301989888 | bytes 786432 | tf_op jit(solution)/shard_map/pallas_call | solution.py:340
  29.3 0.2 collective-permute-done.14.refs_3_
  29.5 0.5 %shard_map.115 = (bf16[32,1024]{1,0:T(8,128)(2,1)S(1)}, bf16[32,1024]{1,0:T(8,128)(2,1)S(1)}, bf16[32,1024]{1,0:T(8,128)(2,1)S(1)}, bf16[32,1024]{1,0:T(8,128)(2,1)S(1)}) custom-call(bf16[256,512]{1,0:T(8,128)(2,1)S(1)} %get-tuple-element.23.refs_5_.refs_0_, f32[128,1024]{1,0:T(8,128)S(1)} %get-tuple-element.26.refs_1_, ...), custom_call_target="tpu_custom_call" | custom-call | flops 134217728 | bytes 1572864 | tf_op jit(solution)/shard_map/pallas_call | solution.py:388
  30.0 1.3 %collective-permute-start.15 = (bf16[32,1024]{1,0:T(8,128)(2,1)S(1)}, bf16[32,1024]{1,0:T(8,128)(2,1)S(1)}, u32[]{:S(2)}, u32[]{:S(2)}) collective-permute-start(bf16[32,1024]{1,0:T(8,128)(2,1)S(1)} %get-tuple-element.29), channel_id=1, source_target_pairs={{0,8},{4,12},{8,0},{12,4},{1,9},{5,13},{9,1},{13,5},{2,10},{6,14},... | collective-permute-start | bytes 196616 | tf_op jit(solution)/shard_map/ppermute | solution.py:450
  31.3 3.0 %collective-permute-start.16 = (bf16[32,1024]{1,0:T(8,128)(2,1)S(1)}, bf16[32,1024]{1,0:T(8,128)(2,1)S(1)}, u32[]{:S(2)}, u32[]{:S(2)}) collective-permute-start(bf16[32,1024]{1,0:T(8,128)(2,1)S(1)} %get-tuple-element.30), channel_id=1, source_target_pairs={{0,12},{4,8},{8,4},{12,0},{1,13},{5,9},{9,5},{13,1},{2,14},{6,10},... | collective-permute-start | bytes 196616 | tf_op jit(solution)/shard_map/ppermute | solution.py:450
  34.2 0.0 collective-permute-start.17
  34.2 3.9 %collective-permute-done.15.p1_ref = bf16[32,1024]{1,0:T(8,128)(2,1)S(1)} collective-permute-done((bf16[32,1024]{1,0:T(8,128)(2,1)S(1)}, bf16[32,1024]{1,0:T(8,128)(2,1)S(1)}, u32[]{:S(2)}, u32[]{:S(2)}) %collective-permute-start.15) | collective-permute-done | bytes 65568 | tf_op jit(solution)/shard_map/ppermute | solution.py:450
  38.1 0.5 %collective-permute-done.16.p2_ref = bf16[32,1024]{1,0:T(8,128)(2,1)S(1)} collective-permute-done((bf16[32,1024]{1,0:T(8,128)(2,1)S(1)}, bf16[32,1024]{1,0:T(8,128)(2,1)S(1)}, u32[]{:S(2)}, u32[]{:S(2)}) %collective-permute-start.16) | collective-permute-done | bytes 65568 | tf_op jit(solution)/shard_map/ppermute | solution.py:450
  38.6 0.6 %collective-permute-done.17.p3_ref = bf16[32,1024]{1,0:T(8,128)(2,1)S(1)} collective-permute-done((bf16[32,1024]{1,0:T(8,128)(2,1)S(1)}, bf16[32,1024]{1,0:T(8,128)(2,1)S(1)}, u32[]{:S(2)}, u32[]{:S(2)}) %collective-permute-start.17) | collective-permute-done | bytes 65568 | tf_op jit(solution)/shard_map/ppermute | solution.py:450
  39.2 0.1 collective-permute-start.18
  39.3 1.0 %collective-permute-start.19 = (bf16[8,1024]{1,0:T(8,128)(2,1)S(1)}, bf16[8,1024]{1,0:T(8,128)(2,1)S(1)}, u32[]{:S(2)}, u32[]{:S(2)}) collective-permute-start(bf16[8,1024]{1,0:T(8,128)(2,1)S(1)} %get-tuple-element.34), channel_id=1, source_target_pairs={{0,2},{1,3},{2,0},{3,1},{4,6},{5,7},{6,4},{7,5},{8,10},{9,11},{10,... | collective-permute-start | bytes 49160 | tf_op jit(solution)/shard_map/ppermute | solution.py:450
  40.3 0.9 %collective-permute-start.20 = (bf16[8,1024]{1,0:T(8,128)(2,1)S(1)}, bf16[8,1024]{1,0:T(8,128)(2,1)S(1)}, u32[]{:S(2)}, u32[]{:S(2)}) collective-permute-start(bf16[8,1024]{1,0:T(8,128)(2,1)S(1)} %get-tuple-element.35), channel_id=1, source_target_pairs={{0,3},{1,2},{2,1},{3,0},{4,7},{5,6},{6,5},{7,4},{8,11},{9,10},{10,... | collective-permute-start | bytes 49160 | tf_op jit(solution)/shard_map/ppermute | solution.py:450
  41.2 0.0 collective-permute-done.18.p1_ref
  41.2 1.9 %collective-permute-done.19.p2_ref = bf16[8,1024]{1,0:T(8,128)(2,1)S(1)} collective-permute-done((bf16[8,1024]{1,0:T(8,128)(2,1)S(1)}, bf16[8,1024]{1,0:T(8,128)(2,1)S(1)}, u32[]{:S(2)}, u32[]{:S(2)}) %collective-permute-start.19) | collective-permute-done | bytes 16416 | tf_op jit(solution)/shard_map/ppermute | solution.py:450
  43.1 0.3 collective-permute-done.20.p3_ref
  43.4 0.6 %shard_map.117 = bf16[8,4096]{1,0:T(8,128)(2,1)} custom-call(bf16[8,1024]{1,0:T(8,128)(2,1)S(1)} %get-tuple-element.32.p0_ref, bf16[8,1024]{1,0:T(8,128)(2,1)S(1)} %collective-permute-done.18.p1_ref, bf16[8,1024]{1,0:T(8,128)(2,1)S(1)} %collective-permute-done.19.p2_ref, bf16[8,1024]{1,0:T(8,128)(2,1)S(1)} %collective-permute-done.20.p3_ref), custom_call_target="tpu_custom_call" | custom-call | bytes 131072 | tf_op jit(solution)/shard_map/pallas_call | solution.py:436
  (19 shorter events, 0.2 us)
Async XLA Ops:
  1.5 7.6 %collective-permute-start.2 = (bf16[8,4224]{1,0:T(8,128)(2,1)S(1)}, bf16[8,4224]{1,0:T(8,128)(2,1)S(1)}, u32[]{:S(2)}, u32[]{:S(2)}) collective-permute-start(bf16[8,4224]{1,0:T(8,128)(2,1)S(1)} %shard_map.104.refs_1_), channel_id=1, source_target_pairs={{0,12},{4,8},{8,4},{12,0},{1,13},{5,9},{9,5},{13,1},{2,14},{6,10},... | collective-permute-start | bytes 202760 | tf_op jit(solution)/shard_map/ppermute | solution.py:450
  6.6 8.0 %collective-permute-start.4 = (bf16[8,4224]{1,0:T(8,128)(2,1)S(1)}, bf16[8,4224]{1,0:T(8,128)(2,1)S(1)}, u32[]{:S(2)}, u32[]{:S(2)}) collective-permute-start(bf16[8,4224]{1,0:T(8,128)(2,1)S(1)} %shard_map.104.refs_1_), channel_id=1, source_target_pairs={{0,2},{1,3},{2,0},{3,1},{4,6},{5,7},{6,4},{7,5},{8,10},{9,11},{10,... | collective-permute-start | bytes 202760 | tf_op jit(solution)/shard_map/ppermute | solution.py:450
  8.1 4.3 %collective-permute-start.1 = (bf16[8,4224]{1,0:T(8,128)(2,1)S(1)}, bf16[8,4224]{1,0:T(8,128)(2,1)S(1)}, u32[]{:S(2)}, u32[]{:S(2)}) collective-permute-start(bf16[8,4224]{1,0:T(8,128)(2,1)S(1)} %shard_map.104.refs_1_), channel_id=1, source_target_pairs={{0,4},{4,0},{8,12},{12,8},{1,5},{5,1},{9,13},{13,9},{2,6},{6,2},{1... | collective-permute-start | bytes 202760 | tf_op jit(solution)/shard_map/ppermute | solution.py:450
  8.1 5.4 %collective-permute-start = (bf16[8,4224]{1,0:T(8,128)(2,1)S(1)}, bf16[8,4224]{1,0:T(8,128)(2,1)S(1)}, u32[]{:S(2)}, u32[]{:S(2)}) collective-permute-start(bf16[8,4224]{1,0:T(8,128)(2,1)S(1)} %shard_map.104.refs_1_), channel_id=1, source_target_pairs={{0,8},{4,12},{8,0},{12,4},{1,9},{5,13},{9,1},{13,5},{2,10},{6,14},... | collective-permute-start | bytes 202760 | tf_op jit(solution)/shard_map/ppermute | solution.py:450
  9.1 5.6 %collective-permute-start.7 = (bf16[8,4224]{1,0:T(8,128)(2,1)S(1)}, bf16[8,4224]{1,0:T(8,128)(2,1)S(1)}, u32[]{:S(2)}, u32[]{:S(2)}) collective-permute-start(bf16[8,4224]{1,0:T(8,128)(2,1)S(1)} %shard_map.107), channel_id=1, source_target_pairs={{0,2},{1,3},{2,0},{3,1},{4,6},{5,7},{6,4},{7,5},{8,10},{9,11},{10,... | collective-permute-start | bytes 202760 | tf_op jit(solution)/shard_map/ppermute | solution.py:450
  12.4 6.7 %slice-start.2 = ((s8[8388608]{0:T(1024)(128)(4,1)}), s8[4194304]{0:T(1024)(128)(4,1)S(1)}, s32[]{:S(2)}) async-start(s8[8388608]{0:T(1024)(128)(4,1)} %bitcast.20), calls=%async_computation.2 | async-start | bytes 8388608
  12.4 6.7 %slice-start.4 = ((s8[8388608]{0:T(1024)(128)(4,1)}), s8[4194304]{0:T(1024)(128)(4,1)S(1)}, s32[]{:S(2)}) async-start(s8[8388608]{0:T(1024)(128)(4,1)} %bitcast.22), calls=%async_computation.4 | async-start | bytes 8388608
  12.4 6.7 %slice-start.3 = ((s8[8388608]{0:T(1024)(128)(4,1)}), s8[4194304]{0:T(1024)(128)(4,1)S(1)}, s32[]{:S(2)}) async-start(s8[8388608]{0:T(1024)(128)(4,1)} %bitcast.20), calls=%async_computation.3 | async-start | bytes 8388608
  12.4 6.7 %slice-start.5 = ((s8[8388608]{0:T(1024)(128)(4,1)}), s8[4194304]{0:T(1024)(128)(4,1)S(1)}, s32[]{:S(2)}) async-start(s8[8388608]{0:T(1024)(128)(4,1)} %bitcast.22), calls=%async_computation.5 | async-start | bytes 8388608
  12.4 4.4 %collective-permute-start.6 = (bf16[8,4224]{1,0:T(8,128)(2,1)S(1)}, bf16[8,4224]{1,0:T(8,128)(2,1)S(1)}, u32[]{:S(2)}, u32[]{:S(2)}) collective-permute-start(bf16[8,4224]{1,0:T(8,128)(2,1)S(1)} %shard_map.106), channel_id=1, source_target_pairs={{0,2},{1,3},{2,0},{3,1},{4,6},{5,7},{6,4},{7,5},{8,10},{9,11},{10,... | collective-permute-start | bytes 202760 | tf_op jit(solution)/shard_map/ppermute | solution.py:450
  13.5 4.3 %collective-permute-start.5 = (bf16[8,4224]{1,0:T(8,128)(2,1)S(1)}, bf16[8,4224]{1,0:T(8,128)(2,1)S(1)}, u32[]{:S(2)}, u32[]{:S(2)}) collective-permute-start(bf16[8,4224]{1,0:T(8,128)(2,1)S(1)} %shard_map.105), channel_id=1, source_target_pairs={{0,2},{1,3},{2,0},{3,1},{4,6},{5,7},{6,4},{7,5},{8,10},{9,11},{10,... | collective-permute-start | bytes 202760 | tf_op jit(solution)/shard_map/ppermute | solution.py:450
  14.6 4.5 %collective-permute-start.3 = (bf16[4,8,4224]{2,1,0:T(8,128)(2,1)S(1)}, bf16[4,8,4224]{2,1,0:T(8,128)(2,1)S(1)}, u32[]{:S(2)}, u32[]{:S(2)}) collective-permute-start(bf16[4,8,4224]{2,1,0:T(8,128)(2,1)S(1)} %get-tuple-element.36), channel_id=1, source_target_pairs={{0,1},{1,0},{2,3},{3,2},{4,5},{5,4},{6,7},{7,6},{8,9},{9,8},{10,11... | collective-permute-start | bytes 811016 | tf_op jit(solution)/shard_map/ppermute | solution.py:450
  16.8 1.5 %collective-permute-start.8 = (bf16[3,8,4224]{2,1,0:T(8,128)(2,1)S(1)}, bf16[3,8,4224]{2,1,0:T(8,128)(2,1)S(1)}, u32[]{:S(2)}, u32[]{:S(2)}) collective-permute-start(bf16[3,8,4224]{2,1,0:T(8,128)(2,1)S(1)} %pad_maximum_fusion.1), channel_id=1, source_target_pairs={{0,1},{1,0},{2,3},{3,2},{4,5},{5,4},{6,7},{7,6},{8,9},{9,8},{10,11... | collective-permute-start | bytes 608264 | tf_op jit(solution)/shard_map/ppermute | solution.py:450
  17.8 1.3 %collective-permute-start.9 = (bf16[8,4224]{1,0:T(8,128)(2,1)S(1)}, bf16[8,4224]{1,0:T(8,128)(2,1)S(1)}, u32[]{:S(2)}, u32[]{:S(2)}) collective-permute-start(bf16[8,4224]{1,0:T(8,128)(2,1)S(1)} %collective-permute-done.5), channel_id=1, source_target_pairs={{0,1},{1,0},{2,3},{3,2},{4,5},{5,4},{6,7},{7,6},{8,9},{9,8},{10,11... | collective-permute-start | bytes 202760 | tf_op jit(solution)/shard_map/ppermute | solution.py:450
  20.8 6.1 %collective-permute-start.12 = (bf16[2,96,256]{2,1,0:T(8,128)(2,1)S(1)}, bf16[2,96,256]{2,1,0:T(8,128)(2,1)S(1)}, u32[]{:S(2)}, u32[]{:S(2)}) collective-permute-start(bf16[2,96,256]{2,1,0:T(8,128)(2,1)S(1)} %get-tuple-element.19.refs_6_), channel_id=1, source_target_pairs={{0,2},{1,3},{2,0},{3,1},{4,6},{5,7},{6,4},{7,5},{8,10},{9,11},{10,... | collective-permute-start | bytes 294920 | tf_op jit(solution)/shard_map/ppermute | solution.py:450
  21.8 2.6 %copy-start = (bf16[2,512,576]{1,2,0:T(8,128)(2,1)S(1)}, bf16[2,512,576]{1,2,0:T(8,128)(2,1)}, u32[]{:S(2)}) copy-start(bf16[2,512,576]{1,2,0:T(8,128)(2,1)} %param.16) | copy-start | bytes 3538948
  21.8 2.6 %copy-start.1 = (bf16[2,128,576]{1,2,0:T(8,128)(2,1)S(1)}, bf16[2,128,576]{1,2,0:T(8,128)(2,1)}, u32[]{:S(2)}) copy-start(bf16[2,128,576]{1,2,0:T(8,128)(2,1)} %param.15) | copy-start | bytes 884740
  21.9 2.6 %copy-start.2 = (s32[2]{0:T(128)S(1)}, s32[2]{0:T(128)}, u32[]{:S(2)}) copy-start(s32[2]{0:T(128)} %lengths_ref.1) | copy-start | bytes 28
  23.3 4.1 %slice-start = ((s8[8388608]{0:T(1024)(128)(4,1)}), s8[4194304]{0:T(1024)(128)(4,1)S(1)}, s32[]{:S(2)}) async-start(s8[8388608]{0:T(1024)(128)(4,1)} %bitcast.18), calls=%async_computation | async-start | bytes 8388608
  23.3 4.8 %collective-permute-start.10 = (bf16[2,96,256]{2,1,0:T(8,128)(2,1)S(1)}, bf16[2,96,256]{2,1,0:T(8,128)(2,1)S(1)}, u32[]{:S(2)}, u32[]{:S(2)}) collective-permute-start(bf16[2,96,256]{2,1,0:T(8,128)(2,1)S(1)} %get-tuple-element.24.after_ref), channel_id=1, source_target_pairs={{0,2},{1,3},{2,0},{3,1},{4,6},{5,7},{6,4},{7,5},{8,10},{9,11},{10,... | collective-permute-start | bytes 294920 | tf_op jit(solution)/shard_map/ppermute | solution.py:450
  24.4 3.0 %collective-permute-start.11 = (bf16[4,96,256]{2,1,0:T(8,128)(2,1)S(1)}, bf16[4,96,256]{2,1,0:T(8,128)(2,1)S(1)}, u32[]{:S(2)}, u32[]{:S(2)}) collective-permute-start(bf16[4,96,256]{2,1,0:T(8,128)(2,1)S(1)} %get-tuple-element.25.refs_0_.refs_1_), channel_id=1, source_target_pairs={{0,1},{1,0},{2,3},{3,2},{4,5},{5,4},{6,7},{7,6},{8,9},{9,8},{10,11... | collective-permute-start | bytes 589832 | tf_op jit(solution)/shard_map/ppermute | solution.py:450
  24.4 3.0 %slice-start.1 = ((s8[8388608]{0:T(1024)(128)(4,1)}), s8[4194304]{0:T(1024)(128)(4,1)S(1)}, s32[]{:S(2)}) async-start(s8[8388608]{0:T(1024)(128)(4,1)} %bitcast.18), calls=%async_computation.1 | async-start | bytes 8388608
  26.9 1.4 %collective-permute-start.13 = (bf16[2,96,256]{2,1,0:T(8,128)(2,1)S(1)}, bf16[2,96,256]{2,1,0:T(8,128)(2,1)S(1)}, u32[]{:S(2)}, u32[]{:S(2)}) collective-permute-start(bf16[2,96,256]{2,1,0:T(8,128)(2,1)S(1)} %shard_map.111.refs_2_), channel_id=1, source_target_pairs={{0,1},{1,0},{2,3},{3,2},{4,5},{5,4},{6,7},{7,6},{8,9},{9,8},{10,11... | collective-permute-start | bytes 294920 | tf_op jit(solution)/shard_map/ppermute | solution.py:450
  28.1 1.4 %collective-permute-start.14 = (bf16[2,96,256]{2,1,0:T(8,128)(2,1)S(1)}, bf16[2,96,256]{2,1,0:T(8,128)(2,1)S(1)}, u32[]{:S(2)}, u32[]{:S(2)}) collective-permute-start(bf16[2,96,256]{2,1,0:T(8,128)(2,1)S(1)} %shard_map.113.refs_0_), channel_id=1, source_target_pairs={{0,1},{1,0},{2,3},{3,2},{4,5},{5,4},{6,7},{7,6},{8,9},{9,8},{10,11... | collective-permute-start | bytes 294920 | tf_op jit(solution)/shard_map/ppermute | solution.py:450
  30.0 8.1 %collective-permute-start.15 = (bf16[32,1024]{1,0:T(8,128)(2,1)S(1)}, bf16[32,1024]{1,0:T(8,128)(2,1)S(1)}, u32[]{:S(2)}, u32[]{:S(2)}) collective-permute-start(bf16[32,1024]{1,0:T(8,128)(2,1)S(1)} %get-tuple-element.29), channel_id=1, source_target_pairs={{0,8},{4,12},{8,0},{12,4},{1,9},{5,13},{9,1},{13,5},{2,10},{6,14},... | collective-permute-start | bytes 196616 | tf_op jit(solution)/shard_map/ppermute | solution.py:450
  31.3 7.3 %collective-permute-start.16 = (bf16[32,1024]{1,0:T(8,128)(2,1)S(1)}, bf16[32,1024]{1,0:T(8,128)(2,1)S(1)}, u32[]{:S(2)}, u32[]{:S(2)}) collective-permute-start(bf16[32,1024]{1,0:T(8,128)(2,1)S(1)} %get-tuple-element.30), channel_id=1, source_target_pairs={{0,12},{4,8},{8,4},{12,0},{1,13},{5,9},{9,5},{13,1},{2,14},{6,10},... | collective-permute-start | bytes 196616 | tf_op jit(solution)/shard_map/ppermute | solution.py:450
  34.2 4.9 %collective-permute-start.17 = (bf16[32,1024]{1,0:T(8,128)(2,1)S(1)}, bf16[32,1024]{1,0:T(8,128)(2,1)S(1)}, u32[]{:S(2)}, u32[]{:S(2)}) collective-permute-start(bf16[32,1024]{1,0:T(8,128)(2,1)S(1)} %get-tuple-element.31), channel_id=1, source_target_pairs={{0,4},{4,0},{8,12},{12,8},{1,5},{5,1},{9,13},{13,9},{2,6},{6,2},{1... | collective-permute-start | bytes 196616 | tf_op jit(solution)/shard_map/ppermute | solution.py:450
  39.2 1.9 %collective-permute-start.18 = (bf16[8,1024]{1,0:T(8,128)(2,1)S(1)}, bf16[8,1024]{1,0:T(8,128)(2,1)S(1)}, u32[]{:S(2)}, u32[]{:S(2)}) collective-permute-start(bf16[8,1024]{1,0:T(8,128)(2,1)S(1)} %get-tuple-element.33), channel_id=1, source_target_pairs={{0,1},{1,0},{2,3},{3,2},{4,5},{5,4},{6,7},{7,6},{8,9},{9,8},{10,11... | collective-permute-start | bytes 49160 | tf_op jit(solution)/shard_map/ppermute | solution.py:450
  39.3 3.8 %collective-permute-start.19 = (bf16[8,1024]{1,0:T(8,128)(2,1)S(1)}, bf16[8,1024]{1,0:T(8,128)(2,1)S(1)}, u32[]{:S(2)}, u32[]{:S(2)}) collective-permute-start(bf16[8,1024]{1,0:T(8,128)(2,1)S(1)} %get-tuple-element.34), channel_id=1, source_target_pairs={{0,2},{1,3},{2,0},{3,1},{4,6},{5,7},{6,4},{7,5},{8,10},{9,11},{10,... | collective-permute-start | bytes 49160 | tf_op jit(solution)/shard_map/ppermute | solution.py:450
  40.3 3.2 %collective-permute-start.20 = (bf16[8,1024]{1,0:T(8,128)(2,1)S(1)}, bf16[8,1024]{1,0:T(8,128)(2,1)S(1)}, u32[]{:S(2)}, u32[]{:S(2)}) collective-permute-start(bf16[8,1024]{1,0:T(8,128)(2,1)S(1)} %get-tuple-element.35), channel_id=1, source_target_pairs={{0,3},{1,2},{2,1},{3,0},{4,7},{5,6},{6,5},{7,4},{8,11},{9,10},{10,... | collective-permute-start | bytes 49160 | tf_op jit(solution)/shard_map/ppermute | solution.py:450
